TPU v7x, 32 devices: a whole 2x2x4 slice. The times are simulated.
32 devices in a mesh: res: 8 (over y, x, core), hid: 4 (over z).
Axes of the slice: x: 2, y: 2, z: 4, core: 2. Of those that a mesh axis runs over, the one named last changes fastest.
Arguments:
- nodes: bfloat16 [1024, 512], P(('res', 'hid')), may hold values from -6 to 6
- edges: bfloat16 [1024, 60, 192], P(('res', 'hid')), may hold values from -6 to 6
- send_rows: int32 [32, 8, 16], P(('res', 'hid')), may hold values from 0 to 31, as said below
- neighbor_slots: int32 [1024, 60], P(('res', 'hid')), may hold values from 0 to 127, as said below
- neighbor_counts: int32 [1024], P(('res', 'hid')), may hold values from 15 to 60
- message_first: bfloat16 [1216, 512], replicated, may hold values from -0.15625 to 0.15625
- message_first_bias: float32 [512], replicated, may hold values from -3 to 3
- message_second: bfloat16 [512, 512], replicated, may hold values from -0.25 to 0.25
- message_second_bias: float32 [512], replicated, may hold values from -3 to 3
- message_third: bfloat16 [512, 512], replicated, may hold values from -0.5 to 0.5
- message_third_bias: float32 [512], replicated, may hold values from -1.75 to 1.75
- message_gain: float32 [512], replicated, may hold values from 0.5 to 1.5
- message_shift: float32 [512], replicated, may hold values from -1.25 to 1.25
- expand_weight: bfloat16 [512, 2048], P(None, 'hid'), may hold values from -0.25 to 0.25
- expand_bias: float32 [2048], P('hid'), may hold values from -3 to 3
- reduce_weight: bfloat16 [2048, 512], P('hid'), may hold values from -0.125 to 0.125
- reduce_bias: float32 [512], replicated, may hold values from -1.75 to 1.75
- feed_gain: float32 [512], replicated, may hold values from 0.5 to 1.5
- feed_shift: float32 [512], replicated, may hold values from -1.25 to 1.25
- edge_first: bfloat16 [1216, 192], replicated, may hold values from -0.15625 to 0.15625
- edge_first_bias: float32 [192], replicated, may hold values from -3 to 3
- edge_second: bfloat16 [192, 192], replicated, may hold values from -0.4375 to 0.4375
- edge_second_bias: float32 [192], replicated, may hold values from -3 to 3
- edge_third: bfloat16 [192, 192], replicated, may hold values from -0.4375 to 0.4375
- edge_third_bias: float32 [192], replicated, may hold values from -1.75 to 1.75
- edge_gain: float32 [192], replicated, may hold values from 0.5 to 1.5
- edge_shift: float32 [192], replicated, may hold values from -1.25 to 1.25
- node_cotangent: bfloat16 [1024, 512], P(('res', 'hid')), may hold values from -6 to 6
- edge_cotangent: bfloat16 [1024, 60, 192], P(('res', 'hid')), may hold values from -6 to 6
Outputs:
- node_result: float32 [1024, 512], P(('res', 'hid'))
- edge_result: float32 [1024, 60, 192], P(('res', 'hid'))
- node_gradient: float32 [1024, 512], P(('res', 'hid'))
- edge_gradient: float32 [1024, 60, 192], P(('res', 'hid'))
- message_first_gradient: float32 [1216, 512], replicated
- message_first_bias_gradient: float32 [512], replicated
- message_second_gradient: float32 [512, 512], replicated
- message_second_bias_gradient: float32 [512], replicated
- message_third_gradient: float32 [512, 512], replicated
- message_third_bias_gradient: float32 [512], replicated
- message_gain_gradient: float32 [512], replicated
- message_shift_gradient: float32 [512], replicated
- expand_weight_gradient: float32 [512, 2048], P(None, 'hid')
- expand_bias_gradient: float32 [2048], P('hid')
- reduce_weight_gradient: float32 [2048, 512], P('hid')
- reduce_bias_gradient: float32 [512], replicated
- feed_gain_gradient: float32 [512], replicated
- feed_shift_gradient: float32 [512], replicated
- edge_first_gradient: float32 [1216, 192], replicated
- edge_first_bias_gradient: float32 [192], replicated
- edge_second_gradient: float32 [192, 192], replicated
- edge_second_bias_gradient: float32 [192], replicated
- edge_third_gradient: float32 [192, 192], replicated
- edge_third_bias_gradient: float32 [192], replicated
- edge_gain_gradient: float32 [192], replicated
- edge_shift_gradient: float32 [192], replicated
Inputs may be any that keep to these rules, and one draw needn't show every extreme that they name: `send_rows`: each row of 16 entries names different rows of its block. `neighbor_slots`: a residue's 60 entries are different.
All inputs are finite; a program needn't handle non-finite values.
Results may differ from a plain program's by a relative error of at most 0.024.
Values may be sent and summed in bfloat16 or wider, within the bound.
No kernel may reach another device: no remote copies, remote signals or barrier semaphores. Data moves between devices by JAX's collectives and lax.ppermute only.
A program may use at most 128 MiB of HBM per device.

v0:
```python
import jax
import jax.numpy as jnp
from jax import lax
from jax.sharding import PartitionSpec as P


def product(left, right):
    return jnp.dot(left, right, preferred_element_type=jnp.float32)


def layer_norm(values, gain, shift):
    center = values - jnp.mean(values, axis=-1, keepdims=True)
    spread = jnp.mean(center * center, axis=-1, keepdims=True)
    return center * lax.rsqrt(spread + 1e-05) * gain + shift


def norm_back(values, gain, shift, upstream):
    result, pull = jax.vjp(layer_norm, values, gain, shift)
    return pull(upstream)


def smooth_back(values, upstream):
    result, pull = jax.vjp(jax.nn.gelu, values)
    return pull(upstream)[0]


def fetch(rows, weight, table, target):
    peers, slots_each = table.shape
    outgoing = rows[table]
    if target == 0:
        arrived = lax.all_to_all(outgoing, "res", split_axis=0, concat_axis=0, tiled=True)
    else:
        arrived = lax.all_to_all(outgoing, "res", split_axis=0, concat_axis=0, tiled=True)
    flat = arrived.reshape(peers * slots_each, rows.shape[1])
    return product(flat, weight).astype(jnp.bfloat16)


def fetch_back(edge_grads, slots, table, target):
    peers, slots_each = table.shape
    width = edge_grads.shape[-1]
    summed = jnp.zeros((peers * slots_each, width), jnp.float32)
    summed = summed.at[slots.reshape(-1)].add(edge_grads.reshape(-1, width))
    packed = summed.astype(jnp.bfloat16).reshape(peers, slots_each, width)
    if target == 0:
        returned = lax.all_to_all(packed, "res", split_axis=0, concat_axis=0, tiled=True)
    else:
        returned = lax.all_to_all(packed, "res", split_axis=0, concat_axis=0, tiled=True)
    owned = jnp.zeros((slots.shape[0], width), jnp.float32)
    return owned.at[table.reshape(-1)].add(returned.reshape(-1, width).astype(jnp.float32))


def forward(state, edge_state, params, table, slots, counts):
    (
        message_first,
        first_bias,
        message_second,
        second_bias,
        message_third,
        third_bias,
        message_gain,
        message_shift,
        expand_weight,
        expand_bias,
        reduce_weight,
        reduce_bias,
        feed_gain,
        feed_shift,
        edge_first,
        edge_first_bias,
        edge_second,
        edge_second_bias,
        edge_third,
        edge_third_bias,
        edge_gain,
        edge_shift,
    ) = params
    width = state.shape[1]
    rows_here, fanout, edge_width = edge_state.shape
    node_low = state.astype(jnp.bfloat16)
    node_part = product(node_low, message_first[:width])
    hidden_width = node_part.shape[1]
    query_buffer = fetch(node_low, message_first[width : 2 * width], table, 0)
    edge_low = edge_state.astype(jnp.bfloat16).reshape(rows_here * fanout, edge_width)
    slot_flat = slots.reshape(-1)
    neighbor_part = query_buffer[slot_flat].astype(jnp.float32) + product(
        edge_low, message_first[2 * width :]
    )
    first_pre = (
        neighbor_part.reshape(rows_here, fanout, hidden_width) + node_part[:, None, :] + first_bias
    ).reshape(-1, hidden_width)
    first_act = jax.nn.gelu(first_pre).astype(jnp.bfloat16)
    second_pre = product(first_act, message_second) + second_bias
    second_act = jax.nn.gelu(second_pre).astype(jnp.bfloat16)
    message_rows = product(second_act, message_third) + third_bias
    valid = (lax.broadcasted_iota(jnp.int32, (rows_here, fanout), 1) < counts[:, None]).astype(
        jnp.float32
    )
    mean_weights = valid / counts.astype(jnp.float32)[:, None]
    message_mean = jnp.sum(
        message_rows.reshape(rows_here, fanout, width) * mean_weights[:, :, None], axis=1
    )
    first_sum = state + message_mean
    node_mid = layer_norm(first_sum, message_gain, message_shift)
    mid_low = node_mid.astype(jnp.bfloat16)
    gathered = lax.all_gather(mid_low, "hid", axis=0, tiled=True)
    expand_pre = product(gathered, expand_weight) + expand_bias
    expand_act = jax.nn.gelu(expand_pre).astype(jnp.bfloat16)
    feed_out = (
        lax.psum_scatter(
            product(expand_act, reduce_weight).astype(jnp.bfloat16),
            "hid",
            scatter_dimension=0,
            tiled=True,
        ).astype(jnp.float32)
        + reduce_bias
    )
    second_sum = node_mid + feed_out
    node_new = layer_norm(second_sum, feed_gain, feed_shift)
    new_low = node_new.astype(jnp.bfloat16)
    edge_node = product(new_low, edge_first[:width])
    key_buffer = fetch(new_low, edge_first[width : 2 * width], table, 1)
    edge_term = key_buffer[slot_flat].astype(jnp.float32) + product(
        edge_low, edge_first[2 * width :]
    )
    edge_pre = (
        edge_term.reshape(rows_here, fanout, edge_width) + edge_node[:, None, :] + edge_first_bias
    ).reshape(-1, edge_width)
    edge_act = jax.nn.gelu(edge_pre).astype(jnp.bfloat16)
    edge_mid = product(edge_act, edge_second) + edge_second_bias
    edge_mid_act = jax.nn.gelu(edge_mid).astype(jnp.bfloat16)
    update = product(edge_mid_act, edge_third) + edge_third_bias
    edge_sum = edge_state + update.reshape(rows_here, fanout, edge_width)
    edge_new = layer_norm(edge_sum, edge_gain, edge_shift)
    saved = (
        node_low,
        edge_low,
        first_pre,
        first_act,
        second_pre,
        second_act,
        mean_weights,
        first_sum,
        gathered,
        expand_pre,
        expand_act,
        second_sum,
        new_low,
        edge_pre,
        edge_act,
        edge_mid,
        edge_mid_act,
        edge_sum,
    )
    return (node_new, edge_new, saved)


def backward(saved, params, table, slots, node_upstream, edge_upstream):
    (
        message_first,
        first_bias,
        message_second,
        second_bias,
        message_third,
        third_bias,
        message_gain,
        message_shift,
        expand_weight,
        expand_bias,
        reduce_weight,
        reduce_bias,
        feed_gain,
        feed_shift,
        edge_first,
        edge_first_bias,
        edge_second,
        edge_second_bias,
        edge_third,
        edge_third_bias,
        edge_gain,
        edge_shift,
    ) = params
    (
        node_low,
        edge_low,
        first_pre,
        first_act,
        second_pre,
        second_act,
        mean_weights,
        first_sum,
        gathered,
        expand_pre,
        expand_act,
        second_sum,
        new_low,
        edge_pre,
        edge_act,
        edge_mid,
        edge_mid_act,
        edge_sum,
    ) = saved
    width = node_low.shape[1]
    rows_here, fanout = slots.shape
    edge_width = edge_low.shape[1]
    hidden_width = first_pre.shape[1]
    edge_sum_grad, edge_gain_grad, edge_shift_grad = norm_back(
        edge_sum, edge_gain, edge_shift, edge_upstream
    )
    update_grad = edge_sum_grad.reshape(-1, edge_width)
    update_low = update_grad.astype(jnp.bfloat16)
    edge_third_grad = product(edge_mid_act.T, update_low)
    edge_third_bias_grad = jnp.sum(update_grad, axis=0)
    edge_mid_grad = smooth_back(edge_mid, product(update_low, edge_third.T))
    edge_mid_low = edge_mid_grad.astype(jnp.bfloat16)
    edge_second_grad = product(edge_act.T, edge_mid_low)
    edge_second_bias_grad = jnp.sum(edge_mid_grad, axis=0)
    edge_pre_grad = smooth_back(edge_pre, product(edge_mid_low, edge_second.T))
    edge_pre_low = edge_pre_grad.astype(jnp.bfloat16)
    edge_first_bias_grad = jnp.sum(edge_pre_grad, axis=0)
    edge_lower_grad = product(edge_low.T, edge_pre_low)
    edge_low_grad = product(edge_pre_low, edge_first[2 * width :].T)
    edge_node_grad = jnp.sum(edge_pre_grad.reshape(rows_here, fanout, edge_width), axis=1).astype(
        jnp.bfloat16
    )
    edge_upper_grad = product(new_low.T, edge_node_grad)
    key_grad = fetch_back(edge_pre_grad.reshape(rows_here, fanout, edge_width), slots, table, 1)
    key_low = key_grad.astype(jnp.bfloat16)
    edge_middle_grad = product(new_low.T, key_low)
    node_new_grad = (
        node_upstream
        + product(edge_node_grad, edge_first[:width].T)
        + product(key_low, edge_first[width : 2 * width].T)
    )
    second_sum_grad, feed_gain_grad, feed_shift_grad = norm_back(
        second_sum, feed_gain, feed_shift, node_new_grad
    )
    reduce_bias_grad = jnp.sum(second_sum_grad, axis=0)
    feed_low = second_sum_grad.astype(jnp.bfloat16)
    feed_all = lax.all_gather(feed_low, "hid", axis=0, tiled=True)
    reduce_grad = product(expand_act.T, feed_all)
    expand_grad = smooth_back(expand_pre, product(feed_all, reduce_weight.T))
    expand_bias_grad = jnp.sum(expand_grad, axis=0)
    expand_low = expand_grad.astype(jnp.bfloat16)
    expand_weight_grad = product(gathered.T, expand_low)
    node_mid_grad = second_sum_grad + lax.psum_scatter(
        product(expand_low, expand_weight.T).astype(jnp.bfloat16),
        "hid",
        scatter_dimension=0,
        tiled=True,
    ).astype(jnp.float32)
    first_sum_grad, message_gain_grad, message_shift_grad = norm_back(
        first_sum, message_gain, message_shift, node_mid_grad
    )
    rows_grad = (first_sum_grad[:, None, :] * mean_weights[:, :, None]).reshape(-1, width)
    third_bias_grad = jnp.sum(rows_grad, axis=0)
    rows_low = rows_grad.astype(jnp.bfloat16)
    third_grad = product(second_act.T, rows_low)
    second_grad = smooth_back(second_pre, product(rows_low, message_third.T))
    second_bias_grad = jnp.sum(second_grad, axis=0)
    second_low = second_grad.astype(jnp.bfloat16)
    second_weight_grad = product(first_act.T, second_low)
    first_grad = smooth_back(first_pre, product(second_low, message_second.T))
    first_bias_grad = jnp.sum(first_grad, axis=0)
    first_low = first_grad.astype(jnp.bfloat16)
    first_lower_grad = product(edge_low.T, first_low)
    edge_low_grad = edge_low_grad + product(first_low, message_first[2 * width :].T)
    node_part_grad = jnp.sum(first_grad.reshape(rows_here, fanout, hidden_width), axis=1).astype(
        jnp.bfloat16
    )
    first_upper_grad = product(node_low.T, node_part_grad)
    query_grad = fetch_back(first_grad.reshape(rows_here, fanout, hidden_width), slots, table, 0)
    query_low = query_grad.astype(jnp.bfloat16)
    first_middle_grad = product(node_low.T, query_low)
    node_gradient = (
        first_sum_grad
        + product(node_part_grad, message_first[:width].T)
        + product(query_low, message_first[width : 2 * width].T)
    )
    edge_gradient = edge_sum_grad + edge_low_grad.reshape(rows_here, fanout, edge_width)
    first_weight_grad = jnp.concatenate(
        [first_upper_grad, first_middle_grad, first_lower_grad], axis=0
    )
    edge_first_grad = jnp.concatenate([edge_upper_grad, edge_middle_grad, edge_lower_grad], axis=0)
    shared = lax.psum(
        (
            first_weight_grad,
            first_bias_grad,
            second_weight_grad,
            second_bias_grad,
            third_grad,
            third_bias_grad,
            message_gain_grad,
            message_shift_grad,
            reduce_bias_grad,
            feed_gain_grad,
            feed_shift_grad,
            edge_first_grad,
            edge_first_bias_grad,
            edge_second_grad,
            edge_second_bias_grad,
            edge_third_grad,
            edge_third_bias_grad,
            edge_gain_grad,
            edge_shift_grad,
        ),
        ("res", "hid"),
    )
    sharded = (
        lax.psum(expand_weight_grad.astype(jnp.bfloat16), "res").astype(jnp.float32),
        lax.psum(expand_bias_grad.astype(jnp.bfloat16), "res").astype(jnp.float32),
        lax.psum(reduce_grad.astype(jnp.bfloat16), "res").astype(jnp.float32),
    )
    return (
        node_gradient,
        edge_gradient,
        shared[0],
        shared[1],
        shared[2],
        shared[3],
        shared[4],
        shared[5],
        shared[6],
        shared[7],
        sharded[0],
        sharded[1],
        sharded[2],
        shared[8],
        shared[9],
        shared[10],
        shared[11],
        shared[12],
        shared[13],
        shared[14],
        shared[15],
        shared[16],
        shared[17],
        shared[18],
    )


def body(
    nodes,
    edges,
    send_rows,
    neighbor_slots,
    neighbor_counts,
    message_first,
    message_first_bias,
    message_second,
    message_second_bias,
    message_third,
    message_third_bias,
    message_gain,
    message_shift,
    expand_weight,
    expand_bias,
    reduce_weight,
    reduce_bias,
    feed_gain,
    feed_shift,
    edge_first,
    edge_first_bias,
    edge_second,
    edge_second_bias,
    edge_third,
    edge_third_bias,
    edge_gain,
    edge_shift,
    node_cotangent,
    edge_cotangent,
):
    params = (
        message_first,
        message_first_bias,
        message_second,
        message_second_bias,
        message_third,
        message_third_bias,
        message_gain,
        message_shift,
        expand_weight,
        expand_bias,
        reduce_weight,
        reduce_bias,
        feed_gain,
        feed_shift,
        edge_first,
        edge_first_bias,
        edge_second,
        edge_second_bias,
        edge_third,
        edge_third_bias,
        edge_gain,
        edge_shift,
    )
    table = send_rows[0]
    recycled_nodes, recycled_edges, unused = forward(
        nodes.astype(jnp.float32),
        edges.astype(jnp.float32),
        params,
        table,
        neighbor_slots,
        neighbor_counts,
    )
    node_result, edge_result, saved = forward(
        recycled_nodes, recycled_edges, params, table, neighbor_slots, neighbor_counts
    )
    grads = backward(
        saved,
        params,
        table,
        neighbor_slots,
        node_cotangent.astype(jnp.float32),
        edge_cotangent.astype(jnp.float32),
    )
    return (
        node_result,
        edge_result,
        grads[0],
        grads[1],
        grads[2],
        grads[3],
        grads[4],
        grads[5],
        grads[6],
        grads[7],
        grads[8],
        grads[9],
        grads[10],
        grads[11],
        grads[12],
        grads[13],
        grads[14],
        grads[15],
        grads[16],
        grads[17],
        grads[18],
        grads[19],
        grads[20],
        grads[21],
        grads[22],
        grads[23],
    )


def solution(mesh):
    placed = (
        P(("res", "hid"), None),
        P(("res", "hid"), None, None),
        P(("res", "hid"), None, None),
        P(("res", "hid"), None),
        P(("res", "hid")),
        P(),
        P(),
        P(),
        P(),
        P(),
        P(),
        P(),
        P(),
        P(None, "hid"),
        P("hid"),
        P("hid", None),
        P(),
        P(),
        P(),
        P(),
        P(),
        P(),
        P(),
        P(),
        P(),
        P(),
        P(),
        P(("res", "hid"), None),
        P(("res", "hid"), None, None),
    )
    return jax.shard_map(
        body,
        mesh=mesh,
        in_specs=placed,
        out_specs=(
            P(("res", "hid"), None),
            P(("res", "hid"), None, None),
            P(("res", "hid"), None),
            P(("res", "hid"), None, None),
            P(),
            P(),
            P(),
            P(),
            P(),
            P(),
            P(),
            P(),
            P(None, "hid"),
            P("hid"),
            P("hid", None),
            P(),
            P(),
            P(),
            P(),
            P(),
            P(),
            P(),
            P(),
            P(),
            P(),
            P(),
        ),
        check_vma=False,
    )
```

profile of v0, /device:TPU:1, one launch (start us, length us, event | category | flops | bytes accessed | tf_op | source)
XLA Modules:
  0.0 564.6 jit_solution(6188259784374282043)
XLA Ops:
  10.4 5.2 all-to-all-start
  23.6 5.1 add.486
  29.0 6.8 %gather_fusion.1 = bf16[1920,512]{1,0:T(8,128)(2,1)} fusion(bf16[128,512]{1,0:T(8,128)(2,1)S(1)} %convolution_convert_fusion.6, s32[2048]{0:T(1024)S(1)} %pad_clamp_fusion), kind=kCustom, calls=%fused_computation.1 | custom fusion | bytes 3939840 | tf_op jit(solution)/shard_map/gather | solution.py:85
  35.8 6.4 %fusion.27 = bf16[1920,512]{1,0:T(8,128)(2,1)} fusion(bf16[512,512]{1,0:T(8,128)(2,1)S(1)} %copy-done, f32[1920,512]{1,0:T(8,128)} %add.486, bf16[1920,512]{1,0:T(8,128)(2,1)} %gather_fusion.1, bf16[1920,192]{1,0:T(8,128)(2,1)S(1)} %copy-done.33, f32[512]{0:T(512)S(1)} %copy-done.113, f32[512]{0:T(512)S(1)} %copy-done.87, bf16[1216,512]{1,0:T(8,128)(2,1)S(1)} %copy-done.14), kind=kOutput, calls=%fused_computation.47 | convolution fusion | flops 1406730240 | bytes 9572352 | tf_op jit(solution)/shard_map/dot_general | solution.py:8
  42.2 4.6 convolution_add_fusion.1
  46.8 5.0 reshape.404
  51.8 3.0 multiply_reduce_fusion.2
  55.3 11.1 %all_gather.9 = bf16[128,512]{1,0:T(8,128)(2,1)S(1)} all-gather(bf16[32,512]{1,0:T(8,128)(2,1)S(1)} %fusion.151), channel_id=1, replica_groups=mesh['res'=8,'hid'=4] {'hid'}, dimensions={0}, use_global_device_ids=true | all-gather | bytes 163840 | tf_op jit(solution)/shard_map/all_gather | solution.py:105
  68.6 20.4 %reduce-scatter.4.cloned.1.call-done = bf16[32,512]{1,0:T(8,128)(2,1)} async-done(((bf16[128,512]{1,0:T(8,128)(2,1)}), bf16[32,512]{1,0:T(8,128)(2,1)}) %reduce-scatter.4.cloned.1.call-update) | async-done | bytes 32784 | tf_op jit(solution)/shard_map/reduce_scatter | solution.py:109
  92.1 6.6 %all-to-all-start.1 = ((bf16[8,16,512]{2,1,0:T(8,128)(2,1)}), bf16[8,16,512]{2,1,0:T(8,128)(2,1)S(1)}, u32[]{:S(2)}, u32[]{:S(2)}) async-start(bf16[8,16,512]{2,1,0:T(8,128)(2,1)} %bitcast.3), calls=%async_computation.2 | async-start | bytes 262144 | tf_op jit(solution)/shard_map/all_to_all | solution.py:31
  105.9 5.0 add.532
  112.5 6.4 %gather_fusion.4 = bf16[1920,192]{1,0:T(8,128)(2,1)S(1)} fusion(bf16[128,192]{1,0:T(8,128)(2,1)S(1)} %copy.66, s32[2048]{0:T(1024)S(1)} %pad_clamp_fusion), kind=kCustom, calls=%fused_computation.4 | custom fusion | bytes 1482240 | tf_op jit(solution)/shard_map/gather | solution.py:122
  120.3 6.8 %gather_fusion.3 = bf16[1920,512]{1,0:T(8,128)(2,1)} fusion(bf16[128,512]{1,0:T(8,128)(2,1)S(1)} %convolution_convert_fusion.4, s32[2048]{0:T(1024)S(1)} %pad_clamp_fusion), kind=kCustom, calls=%fused_computation.3 | custom fusion | bytes 3939840 | tf_op jit(solution)/shard_map/gather | solution.py:85
  127.2 3.8 fusion.70
  144.8 3.1 add_add_fusion
  148.0 3.9 multiply_convert_fusion.1
  153.1 3.1 convolution_add_fusion
  156.2 5.4 reshape.408
  161.7 3.0 multiply_reduce_fusion.1
  165.3 10.6 %all_gather.10 = bf16[128,512]{1,0:T(8,128)(2,1)S(1)} all-gather(bf16[32,512]{1,0:T(8,128)(2,1)S(1)} %fusion.150), channel_id=1, replica_groups=mesh['res'=8,'hid'=4] {'hid'}, dimensions={0}, use_global_device_ids=true | all-gather | bytes 163840 | tf_op jit(solution)/shard_map/all_gather | solution.py:105
  178.4 16.8 %reduce-scatter.6.cloned.1.call-done = bf16[32,512]{1,0:T(8,128)(2,1)} async-done(((bf16[128,512]{1,0:T(8,128)(2,1)}), bf16[32,512]{1,0:T(8,128)(2,1)}) %reduce-scatter.6.cloned.1.call-update) | async-done | bytes 32784 | tf_op jit(solution)/shard_map/reduce_scatter | solution.py:109
  198.6 6.7 %all-to-all-start.2 = ((bf16[8,16,512]{2,1,0:T(8,128)(2,1)}), bf16[8,16,512]{2,1,0:T(8,128)(2,1)S(1)}, u32[]{:S(2)}, u32[]{:S(2)}) async-start(bf16[8,16,512]{2,1,0:T(8,128)(2,1)} %bitcast.5), calls=%async_computation.4 | async-start | bytes 262144 | tf_op jit(solution)/shard_map/all_to_all | solution.py:33
  212.7 6.4 %gather_fusion.6 = bf16[1920,192]{1,0:T(8,128)(2,1)S(1)} fusion(bf16[128,192]{1,0:T(8,128)(2,1)S(1)} %copy.70, s32[2048]{0:T(1024)S(1)} %pad_clamp_fusion), kind=kCustom, calls=%fused_computation.6 | custom fusion | bytes 1482240 | tf_op jit(solution)/shard_map/gather | solution.py:122
  230.4 3.2 fusion.198
  237.5 4.0 fusion.35
  244.0 3.1 fusion.189
  254.3 2.7 copy.75
  259.7 11.6 %scatter_custom_fusion = f32[128,192]{1,0:T(8,128)} fusion(s32[1920]{0:T(1024)} %copy-done.61, f32[1920,192]{1,0:T(8,128)} %copy.75, f32[]{:T(128)} %constant.30.clone.1), kind=kCustom, calls=%fused_computation.223 | custom fusion | flops 368640 | bytes 98816 | tf_op jit(solution)/shard_map/scatter-add | solution.py:42
  272.8 4.2 all-to-all-start.3
  288.4 10.4 %all_gather.11 = bf16[128,512]{1,0:T(8,128)(2,1)S(1)} all-gather(bf16[32,512]{1,0:T(8,128)(2,1)S(1)} %add_convert_fusion.1), channel_id=1, replica_groups=mesh['res'=8,'hid'=4] {'hid'}, dimensions={0}, use_global_device_ids=true | all-gather | bytes 163840 | tf_op jit(solution)/shard_map/all_gather | solution.py:239
  311.4 11.9 %reduce-scatter.8.cloned.1.call-done = bf16[32,512]{1,0:T(8,128)(2,1)} async-done(((bf16[128,512]{1,0:T(8,128)(2,1)}), bf16[32,512]{1,0:T(8,128)(2,1)}) %reduce-scatter.8.cloned.1.call-update) | async-done | bytes 32784 | tf_op jit(solution)/shard_map/reduce_scatter | solution.py:245
  328.3 5.2 mul.660
  333.5 5.2 fusion.187
  338.7 6.3 %fusion.206 = (f32[512]{0:T(512)}, bf16[1920,512]{1,0:T(8,128)(2,1)S(1)}) fusion(f32[1920,512]{1,0:T(8,128)} %get-tuple-element.108, f32[512]{0:T(512)S(1)} %copy-done.115, bf16[512,512]{1,0:T(8,128)(2,1)S(1)} %copy-done.107, f32[1920,512]{1,0:T(8,128)S(1)} %copy-done.9, f32[1920]{0:T(1024)S(1)} %copy-done.60), kind=kOutput, calls=%fused_computation.316 | convolution fusion | flops 1030225408 | bytes 10366464 | tf_op jit(solution)/shard_map/dot_general | solution.py:8
  347.7 8.4 %fusion.205 = (f32[512]{0:T(512)}, f32[1920,512]{1,0:T(8,128)S(1)}) fusion(f32[1920,512]{1,0:T(8,128)S(1)} %copy-done.17, bf16[512,512]{1,0:T(8,128)(2,1)S(1)} %copy-done, bf16[1920,512]{1,0:T(8,128)(2,1)S(1)} %get-tuple-element.113), kind=kOutput, calls=%fused_computation.315 | convolution fusion | flops 1026293248 | bytes 10356736 | tf_op jit(solution)/shard_map/dot_general | solution.py:8
  359.4 13.3 %scatter_custom_fusion.2 = f32[128,512]{1,0:T(8,128)S(1)} fusion(s32[1920]{0:T(1024)} %copy-done.61, f32[1920,512]{1,0:T(8,128)} %copy-done.3, f32[]{:T(128)} %constant.30.clone.1), kind=kCustom, calls=%fused_computation.204 | custom fusion | flops 983040 | bytes 262656 | tf_op jit(solution)/shard_map/scatter-add | solution.py:42
  372.7 5.0 reshape.413
  378.4 6.6 %all-to-all-start.4 = ((bf16[8,16,512]{2,1,0:T(8,128)(2,1)}), bf16[8,16,512]{2,1,0:T(8,128)(2,1)S(1)}, u32[]{:S(2)}, u32[]{:S(2)}) async-start(bf16[8,16,512]{2,1,0:T(8,128)(2,1)} %bitcast.78), calls=%async_computation.7 | async-start | bytes 262144 | tf_op jit(solution)/shard_map/all_to_all | solution.py:45
  385.3 2.8 reduce_sum.351
  391.5 3.0 pad_maximum_fusion
  394.6 4.0 copy.78
  398.6 12.3 %psum.163 = bf16[512]{0:T(512)(128)(2,1)S(1)} all-reduce(bf16[512]{0:T(512)(128)(2,1)S(1)} %copy-done.96), channel_id=1, replica_groups=mesh['res'=8,'hid'=4] {'res'}, use_global_device_ids=true, to_apply=%region_44.0 | all-reduce | flops 512 | bytes 2048 | tf_op jit(solution)/shard_map/psum | solution.py:310
  411.5 3.2 fusion.74
  416.2 2.7 copy.77
  419.0 2.8 reshape.415
  427.5 39.8 %all-reduce = (f32[512]{0:T(512)}, f32[512]{0:T(512)}, f32[512]{0:T(512)}, f32[512]{0:T(512)}, f32[512]{0:T(512)}, /*index=5*/f32[512]{0:T(512)}, f32[512]{0:T(5...) all-reduce(f32[512]{0:T(512)S(1)} %copy-done.93, ...), channel_id=1, replica_groups=mesh['res'=8,'hid'=4] {'res','hid'}, use_global_device_ids=true, to_apply=%region_31.0 | all-reduce | flops 5056 | bytes 40448 | tf_op jit(solution)/shard_map/psum | solution.py:284
  472.8 76.5 %all-reduce.6.cloned.1.call-done = (f32[1216,512]{1,0:T(8,128)}, f32[512,512]{1,0:T(8,128)}, f32[512,512]{1,0:T(8,128)}, f32[1216,192]{0,1:T(8,128)}, f32[192,192]{1,0:T(8,128)}, /*index=5*/f32[192,192]{1,0:T(8,128)}) async-done(((f32[1216,512]{1,0:T(8,128)}, f32[512,512]{1,0:T(8,128)}, f32[512,512]{1,0:T(8,128)}, f32[1216,192]{0,1:T(8,128)}, f32[192,192]{1,0:T(8,128)}, /*index=5*/f32[192,192]{1,0:T(8,128)}), ...) | async-done | bytes 5816336 | tf_op jit(solution)/shard_map/psum | solution.py:284
  549.3 3.5 copy.105
  (382 shorter events, 142.2 us)
Async XLA Ops:
  7.2 28.6 %copy-start = (bf16[512,512]{1,0:T(8,128)(2,1)S(1)}, bf16[512,512]{1,0:T(8,128)(2,1)}, u32[]{:S(2)}) copy-start(bf16[512,512]{1,0:T(8,128)(2,1)} %param.36) | copy-start | bytes 1572868
  7.2 11.9 %copy-start.4 = (bf16[32,60,192]{2,0,1:T(8,128)(2,1)S(1)}, bf16[32,60,192]{2,0,1:T(8,128)(2,1)}, u32[]{:S(2)}) copy-start(bf16[32,60,192]{2,0,1:T(8,128)(2,1)} %param.30) | copy-start | bytes 2211844
  10.4 18.3 %all-to-all-start = ((bf16[8,16,512]{2,1,0:T(8,128)(2,1)}), bf16[8,16,512]{2,1,0:T(8,128)(2,1)S(1)}, u32[]{:S(2)}, u32[]{:S(2)}) async-start(bf16[8,16,512]{2,1,0:T(8,128)(2,1)} %bitcast.1), calls=%async_computation | async-start | bytes 262144 | tf_op jit(solution)/shard_map/all_to_all | solution.py:31
  15.6 73.4 %reduce-scatter.4.cloned.1.call-start = ((), (), s32[]{:S(2)}) async-start(), calls=%async_computation.8 | async-start | bytes 163840 | tf_op jit(solution)/shard_map/reduce_scatter | solution.py:109
  19.2 9.5 %copy-start.61 = (s32[1920]{0:T(1024)}, s32[1920]{0:T(1024)S(1)}, u32[]{:S(2)}) copy-start(s32[1920]{0:T(1024)S(1)} %fusion.169) | copy-start | bytes 23044
  29.0 6.8 %copy-start.33 = (bf16[1920,192]{1,0:T(8,128)(2,1)S(1)}, bf16[1920,192]{1,0:T(8,128)(2,1)}, u32[]{:S(2)}) copy-start(bf16[1920,192]{1,0:T(8,128)(2,1)} %reshape.403) | copy-start | bytes 2211844
  29.0 6.8 %copy-start.87 = (f32[512]{0:T(512)S(1)}, f32[512]{0:T(512)}, u32[]{:S(2)}) copy-start(f32[512]{0:T(512)} %param.35) | copy-start | bytes 6148
  29.0 6.8 %copy-start.113 = (f32[512]{0:T(512)S(1)}, f32[512]{0:T(512)}, u32[]{:S(2)}) copy-start(f32[512]{0:T(512)} %param.37) | copy-start | bytes 6148
  51.8 14.6 %copy-start.20 = (bf16[512,512]{1,0:T(8,128)(2,1)S(1)}, bf16[512,512]{1,0:T(8,128)(2,1)}, u32[]{:S(2)}) copy-start(bf16[512,512]{1,0:T(8,128)(2,1)} %param.42) | copy-start | bytes 1572868
  51.8 14.6 %copy-start.88 = (f32[512]{0:T(512)S(1)}, f32[512]{0:T(512)}, u32[]{:S(2)}) copy-start(f32[512]{0:T(512)} %param.43) | copy-start | bytes 6148
  54.8 34.3 %copy-start.69 = (f32[512]{0:T(512)S(1)}, f32[512]{0:T(512)}, u32[]{:S(2)}) copy-start(f32[512]{0:T(512)} %param.45) | copy-start | bytes 6148
  54.8 35.4 %copy-start.53 = (f32[512]{0:T(512)S(1)}, f32[512]{0:T(512)}, u32[]{:S(2)}) copy-start(f32[512]{0:T(512)} %param.46) | copy-start | bytes 6148
  54.8 35.4 %copy-start.62 = (f32[512]{0:T(512)S(1)}, f32[512]{0:T(512)}, u32[]{:S(2)}) copy-start(f32[512]{0:T(512)} %param.47) | copy-start | bytes 6148
  66.4 32.5 %copy-start.18 = (bf16[1216,192]{0,1:T(8,128)(2,1)S(1)}, bf16[1216,192]{0,1:T(8,128)(2,1)}, u32[]{:S(2)}) copy-start(bf16[1216,192]{0,1:T(8,128)(2,1)} %param.48) | copy-start | bytes 1400836
  90.0 8.8 %copy-start.28 = (f32[32,512]{1,0:T(8,128)}, f32[32,512]{1,0:T(8,128)S(1)}, u32[]{:S(2)}) copy-start(f32[32,512]{1,0:T(8,128)S(1)} %get-tuple-element.102) | copy-start | bytes 196612
  90.0 8.8 %copy-start.80 = (f32[32]{0:T(128)}, f32[32]{0:T(128)S(1)}, u32[]{:S(2)}) copy-start(f32[32]{0:T(128)S(1)} %broadcast_multiply_fusion.4) | copy-start | bytes 388
  90.3 8.6 %copy-start.90 = (f32[32]{0:T(128)}, f32[32]{0:T(128)S(1)}, u32[]{:S(2)}) copy-start(f32[32]{0:T(128)S(1)} %add_rsqrt_fusion.1) | copy-start | bytes 388
  92.1 18.8 %all-to-all-start.1 = ((bf16[8,16,512]{2,1,0:T(8,128)(2,1)}), bf16[8,16,512]{2,1,0:T(8,128)(2,1)S(1)}, u32[]{:S(2)}, u32[]{:S(2)}) async-start(bf16[8,16,512]{2,1,0:T(8,128)(2,1)} %bitcast.3), calls=%async_computation.2 | async-start | bytes 262144 | tf_op jit(solution)/shard_map/all_to_all | solution.py:31
  98.6 96.6 %reduce-scatter.6.cloned.1.call-start = ((), (), s32[]{:S(2)}) async-start(), calls=%async_computation.9 | async-start | bytes 163840 | tf_op jit(solution)/shard_map/reduce_scatter | solution.py:109
  120.3 6.8 %copy-start.108 = (bf16[192,192]{1,0:T(8,128)(2,1)S(1)}, bf16[192,192]{1,0:T(8,128)(2,1)}, u32[]{:S(2)}) copy-start(bf16[192,192]{1,0:T(8,128)(2,1)} %param.50) | copy-start | bytes 221188
  120.3 6.8 %copy-start.116 = (f32[192]{0:T(256)S(1)}, f32[192]{0:T(256)}, u32[]{:S(2)}) copy-start(f32[192]{0:T(256)} %param.51) | copy-start | bytes 2308
  144.8 75.8 %copy-start.6 = (bf16[1920,192]{1,0:T(8,128)(2,1)}, bf16[1920,192]{1,0:T(8,128)(2,1)S(1)}, u32[]{:S(2)}) copy-start(bf16[1920,192]{1,0:T(8,128)(2,1)S(1)} %reshape.407) | copy-start | bytes 2211844
  161.6 14.2 %copy-start.21 = (bf16[512,512]{1,0:T(8,128)(2,1)S(1)}, bf16[512,512]{1,0:T(8,128)(2,1)}, u32[]{:S(2)}) copy-start(bf16[512,512]{1,0:T(8,128)(2,1)} %param.42) | copy-start | bytes 1572868
  161.6 14.2 %copy-start.89 = (f32[512]{0:T(512)S(1)}, f32[512]{0:T(512)}, u32[]{:S(2)}) copy-start(f32[512]{0:T(512)} %param.43) | copy-start | bytes 6148
  161.6 14.5 %copy-start.104 = (bf16[512,512]{1,0:T(8,128)(2,1)S(1)}, bf16[512,512]{1,0:T(8,128)(2,1)}, u32[]{:S(2)}) copy-start(bf16[512,512]{1,0:T(8,128)(2,1)} %param.44) | copy-start | bytes 1572868
  164.7 12.4 %copy-start.64 = (s32[1,8,16]{2,1,0:T(8,128)S(1)}, s32[1,8,16]{2,1,0:T(8,128)}, u32[]{:S(2)}) copy-start(s32[1,8,16]{2,1,0:T(8,128)} %param.31) | copy-start | bytes 1540
  164.7 30.5 %copy-start.70 = (f32[512]{0:T(512)S(1)}, f32[512]{0:T(512)}, u32[]{:S(2)}) copy-start(f32[512]{0:T(512)} %param.45) | copy-start | bytes 6148
  164.9 33.7 %copy-start.65 = (f32[32]{0:T(128)}, f32[32]{0:T(128)S(1)}, u32[]{:S(2)}) copy-start(f32[32]{0:T(128)S(1)} %broadcast_multiply_fusion.3) | copy-start | bytes 388
  165.1 33.5 %copy-start.101 = (f32[32]{0:T(128)}, f32[32]{0:T(128)S(1)}, u32[]{:S(2)}) copy-start(f32[32]{0:T(128)S(1)} %multiply_reduce_fusion.10) | copy-start | bytes 388
  165.2 33.4 %copy-start.71 = (f32[32]{0:T(128)}, f32[32]{0:T(128)S(1)}, u32[]{:S(2)}) copy-start(f32[32]{0:T(128)S(1)} %fusion.172) | copy-start | bytes 388
  165.3 40.0 %copy-start.19 = (bf16[1216,192]{0,1:T(8,128)(2,1)S(1)}, bf16[1216,192]{0,1:T(8,128)(2,1)}, u32[]{:S(2)}) copy-start(bf16[1216,192]{0,1:T(8,128)(2,1)} %param.48) | copy-start | bytes 1400836
  176.1 30.8 %copy-start.27 = (f32[128,512]{1,0:T(8,128)}, f32[128,512]{1,0:T(8,128)S(1)}, u32[]{:S(2)}) copy-start(f32[128,512]{1,0:T(8,128)S(1)} %convolution_add_fusion.9) | copy-start | bytes 786436
  198.6 13.7 %all-to-all-start.2 = ((bf16[8,16,512]{2,1,0:T(8,128)(2,1)}), bf16[8,16,512]{2,1,0:T(8,128)(2,1)S(1)}, u32[]{:S(2)}, u32[]{:S(2)}) async-start(bf16[8,16,512]{2,1,0:T(8,128)(2,1)} %bitcast.5), calls=%async_computation.4 | async-start | bytes 262144 | tf_op jit(solution)/shard_map/all_to_all | solution.py:33
  212.7 7.9 %copy-start.100 = (f32[192]{0:T(256)S(1)}, f32[192]{0:T(256)}, u32[]{:S(2)}) copy-start(f32[192]{0:T(256)} %param.49) | copy-start | bytes 2308
  272.8 9.9 %all-to-all-start.3 = ((bf16[8,16,192]{2,1,0:T(8,128)(2,1)}), bf16[8,16,192]{2,1,0:T(8,128)(2,1)S(1)}, u32[]{:S(2)}, u32[]{:S(2)}) async-start(bf16[8,16,192]{2,1,0:T(8,128)(2,1)} %bitcast.8), calls=%async_computation.5 | async-start | bytes 131072 | tf_op jit(solution)/shard_map/all_to_all | solution.py:47
  277.0 46.3 %reduce-scatter.8.cloned.1.call-start = ((), (), s32[]{:S(2)}) async-start(), calls=%async_computation.10 | async-start | bytes 163840 | tf_op jit(solution)/shard_map/reduce_scatter | solution.py:245
  285.0 17.2 %copy-start.22 = (bf16[512,512]{1,0:T(8,128)(2,1)S(1)}, bf16[512,512]{1,0:T(8,128)(2,1)}, u32[]{:S(2)}) copy-start(bf16[512,512]{1,0:T(8,128)(2,1)} %param.42) | copy-start | bytes 1572868
  288.3 14.9 %copy-start.82 = (f32[32]{0:T(128)}, f32[32]{0:T(128)S(1)}, u32[]{:S(2)}) copy-start(f32[32]{0:T(128)S(1)} %negate_multiply_fusion.2) | copy-start | bytes 388
  305.2 163.3 %all-reduce.8.cloned.1.call-start = ((), (), s32[]{:S(2)}) async-start(), calls=%async_computation.12 | async-start | bytes 2097152 | tf_op jit(solution)/shard_map/psum | solution.py:309
  307.0 16.3 %copy-start.52 = (f32[512]{0:T(512)S(1)}, f32[512]{0:T(512)}, u32[]{:S(2)}) copy-start(f32[512]{0:T(512)} %param.40) | copy-start | bytes 6148
  307.0 16.3 %copy-start.66 = (f32[32]{0:T(128)S(1)}, f32[32]{0:T(128)}, u32[]{:S(2)}) copy-start(f32[32]{0:T(128)} %copy-done.65) | copy-start | bytes 388
  307.0 16.3 %copy-start.72 = (f32[32]{0:T(128)S(1)}, f32[32]{0:T(128)}, u32[]{:S(2)}) copy-start(f32[32]{0:T(128)} %copy-done.71) | copy-start | bytes 388
  307.1 16.3 %copy-start.83 = (f32[32]{0:T(128)S(1)}, f32[32]{0:T(128)}, u32[]{:S(2)}) copy-start(f32[32]{0:T(128)} %copy-done.82) | copy-start | bytes 388
  307.1 17.7 %copy-start.102 = (f32[32]{0:T(128)S(1)}, f32[32]{0:T(128)}, u32[]{:S(2)}) copy-start(f32[32]{0:T(128)} %copy-done.101) | copy-start | bytes 388
  347.7 10.4 %copy-start.8 = (bf16[1920,192]{1,0:T(8,128)(2,1)S(1)}, bf16[1920,192]{1,0:T(8,128)(2,1)}, u32[]{:S(2)}) copy-start(bf16[1920,192]{1,0:T(8,128)(2,1)} %copy-done.6) | copy-start | bytes 2211844
  378.4 11.3 %all-to-all-start.4 = ((bf16[8,16,512]{2,1,0:T(8,128)(2,1)}), bf16[8,16,512]{2,1,0:T(8,128)(2,1)S(1)}, u32[]{:S(2)}, u32[]{:S(2)}) async-start(bf16[8,16,512]{2,1,0:T(8,128)(2,1)} %bitcast.78), calls=%async_computation.7 | async-start | bytes 262144 | tf_op jit(solution)/shard_map/all_to_all | solution.py:45
  385.0 164.3 %all-reduce.6.cloned.1.call-start = ((), (), s32[]{:S(2)}) async-start(), calls=%async_computation.11 | async-start | bytes 11927552 | tf_op jit(solution)/shard_map/psum | solution.py:284
  424.6 42.7 %copy-start.15 = (bf16[1216,512]{1,0:T(8,128)(2,1)S(1)}, bf16[1216,512]{1,0:T(8,128)(2,1)}, u32[]{:S(2)}) copy-start(bf16[1216,512]{1,0:T(8,128)(2,1)} %param.34) | copy-start | bytes 3735556
  (82 other events, 253.0 us)
Sparse Core Ops, SparseCore 0:
  68.7 20.2 reduce-scatter.3
  177.2 17.9 reduce-scatter.5
  305.3 17.9 reduce-scatter.7
  326.7 56.1 all-reduce.7
  394.8 154.4 all-reduce.5
where the time goes:
time: 574 us; the launch traced here: 565 us
  local copies, waits for them, and re-layouts  134 us (23%)
  waiting for transfers between devices  126 us (22%)
  matrix products  92.6 us (16%)
  blocking collectives  84.2 us (15%)
  other arithmetic  82.7 us (14%)
  starting transfers between devices  29.8 us (5%)
  between operations  15.7 us (3%)
    dot_general x45, matrix products, product(): return jnp.dot(left, right, preferred_element_type=jnp.float32)  92.6 us
    psum x1, waiting for transfers between devices, backward(): lax.psum((first_weight_grad, first_bias_grad, second_weight_grad, second_...  76.5 us
    psum x1, blocking collectives, backward(): lax.psum((first_weight_grad, first_bias_grad, second_weight_grad, second_...  39.8 us
    reduce_scatter x2, waiting for transfers between devices, forward(): lax.psum_scatter(product(expand_act, reduce_weight).astype(jnp.bfloat16),...  37.3 us
    scatter-add x2, other arithmetic, fetch_back(): summed = summed.at[slots.reshape(-1)].add(edge_grads.reshape(-1, width))  24.9 us
    unnamed x249, local copies, waits for them, and re-layouts  24.4 us
    all_gather x2, blocking collectives, forward(): gathered = lax.all_gather(mid_low, 'hid', axis=0, tiled=True)  21.7 us
    all_to_all x3, starting transfers between devices, fetch(): lax.all_to_all(outgoing, 'res', split_axis=0, concat_axis=0, tiled=True)  18.4 us
  transfers between devices with their start and end apart: 10, of which 5 were waited for; matrix products, arithmetic and copies ran while one was open for 24% of the time, Pallas kernels for 0%

commit v1 on v0

v1 whole, which is shorter than its diff:
```python
import jax
import jax.numpy as jnp
from jax import lax
from jax.experimental import pallas as pl
from jax.experimental.pallas import tpu as pltpu
from jax.sharding import PartitionSpec as P

BF = jnp.bfloat16
F32 = jnp.float32
LEAN = 0.7978845608028654
CUBE = LEAN * 0.044715
MIB = 1 << 20
KEEP = pl.BlockSpec(memory_space=pltpu.VMEM)


def dot(left, right):
    return jnp.dot(left, right, preferred_element_type=F32)


def dot_nt(left, right):
    return lax.dot_general(left, right, (((1,), (1,)), ((), ())), preferred_element_type=F32)


def dot_tn(left, right):
    return lax.dot_general(left, right, (((0,), (0,)), ((), ())), preferred_element_type=F32)


def smooth(v):
    t = jnp.tanh(v * (LEAN + CUBE * (v * v)))
    half = 0.5 * v
    return half + half * t


def smooth_slope(v):
    v2 = v * v
    t = jnp.tanh(v * (LEAN + CUBE * v2))
    half = 0.5 * v
    slope = (0.5 + 0.5 * t) + (half - half * (t * t)) * (LEAN + (3.0 * CUBE) * v2)
    return half + half * t, slope


def centred(x):
    center = x - jnp.mean(x, axis=-1, keepdims=True)
    rate = lax.rsqrt(jnp.mean(center * center, axis=-1, keepdims=True) + 1e-05)
    return center * rate, rate


def norm_pull(hat, rate, gain, up):
    g = up * gain
    return rate * (
        g - jnp.mean(g, axis=-1, keepdims=True) - hat * jnp.mean(g * hat, axis=-1, keepdims=True)
    )


def tiled_add(rows, part):
    n, width = part.shape
    return (rows.reshape(-1, n, width) + part[None]).reshape(rows.shape)


def fold(rows, n):
    return jnp.sum(rows.reshape(-1, n, rows.shape[-1]), axis=0)


def call(body, outs, args, name, scratch=(), limit=12, spot=None):
    args = jax.tree.map(lambda v: pltpu.with_memory_space_constraint(v, pltpu.VMEM), list(args))
    specs = jax.tree.map(lambda v: KEEP, args)
    if spot is not None:
        args, specs = [spot] + args, [pl.BlockSpec(memory_space=pltpu.SMEM)] + specs
    return pl.pallas_call(
        body,
        out_shape=outs,
        in_specs=specs,
        out_specs=jax.tree.map(lambda v: KEEP, list(outs)),
        scratch_shapes=list(scratch),
        compiler_params=pltpu.CompilerParams(vmem_limit_bytes=limit * MIB),
        name=name,
    )(*args)


def struct(shape, dtype):
    return pltpu.VMEM(shape, dtype)


def feed(mid, we, web, wr, rb, slopes=None):
    mid_low = mid.astype(BF)
    total = mid + rb[...]
    for h in range(we.shape[0]):
        pre = dot(mid_low, we[h]) + web[h : h + 1, :]
        if slopes is None:
            act = smooth(pre)
        else:
            act, slope = smooth_slope(pre)
            slopes[h] = slope.astype(BF)
        total = total + dot(act.astype(BF), wr[h])
    return mid_low, total


def joined(parts):
    if len(parts) == 1:
        return parts[0][...]
    near, far = parts[: len(parts) // 2], parts[len(parts) // 2 :]
    rows = []
    for mine, other in zip(near, far):
        half = mine.shape[0] // 2
        rows += [mine[:half], other[half:]]
    return jnp.concatenate(rows, axis=0)


def dealt(outs, value):
    n = value.shape[0] // len(outs)
    for m, out in enumerate(outs):
        out[...] = value[m * n : (m + 1) * n].astype(out.dtype)


def halved(spot, pay, keep, send):
    n = keep.shape[0]
    keep[...] = pay[pl.ds(pl.multiple_of(spot[0] * n, n), n), :]
    send[...] = pay[pl.ds(pl.multiple_of((1 - spot[0]) * n, n), n), :]


def message_mean(summed, counts, mt, mtb):
    mean = summed / counts
    high = mean.astype(BF)
    rest = (mean - high.astype(F32)).astype(BF)
    return dot(high, mt) + dot(rest, mt) + mtb


def solution(mesh):
    n_res, n_hid = mesh.shape["res"], mesh.shape["hid"]
    tuned = (n_res, n_hid) == (8, 4)
    pair = [(i, i ^ 1) for i in range(n_res)]

    def to_chip(v, m):
        return lax.ppermute(v, "res", [(i, i ^ (2 * m)) for i in range(n_res)])

    def to_core(v):
        return lax.ppermute(v, "res", pair)

    def to_hid(v, m):
        return lax.ppermute(v, "hid", [(i, i ^ m) for i in range(n_hid)])

    def exchange(parts):
        if not tuned:
            n, width = parts[0].shape
            blocks = parts[0].reshape(n_res, n // n_res, width)
            return [lax.all_to_all(blocks, "res", 0, 0, tiled=True).reshape(n, width)]
        near = [parts[0]] + [to_chip(parts[m], m) for m in (1, 2, 3)]
        return near + [to_core(v) for v in near]

    def pass_one(rows, fanout, step):
        span = step * rows

        def kernel(
            arrived, nodes, edges, pick, counts, mf, mfb, ms, msb, mt, mtb, first_out, sums,
        ):
            width = nodes.shape[1]
            query = dot(joined(arrived), mf[width : 2 * width]).astype(BF)
            part = dot(nodes[...], mf[:width]) + mfb[...]
            lower = mf[2 * width :]
            lots = jnp.broadcast_to(counts[...], (rows, ms.shape[1]))
            sums[...] = jnp.zeros_like(sums)

            def chunk(i, carry):
                at = pl.ds(pl.multiple_of(i * span, span), span)
                pre = dot(pick[at, :], query) + dot(edges[at, :], lower)
                act = smooth(tiled_add(pre, part)).astype(BF)
                act = smooth(dot(act, ms[...]) + msb[...])
                total = sums[...]
                for j in range(step):
                    total = total + jnp.where(
                        lots > (i * step + j).astype(F32), act[j * rows : (j + 1) * rows], 0.0
                    )
                sums[...] = total
                return carry

            lax.fori_loop(0, fanout // step, chunk, 0)
            first_out[...] = nodes[...].astype(F32) + message_mean(
                sums[...], counts[...], mt[...], mtb[...]
            )

        return kernel

    def feed_one(first, own, near, far, mg, msh, rb, fg, fsh, send, new_out, low_out, away_out, we, web, wr):
        expand, reduce, bias = own
        if near is None:
            we[...], wr[...], web[...] = expand[...], reduce[...], bias[...]
        else:
            res, n = near[0], near[1][0][0].shape[0] // 9 * 4
            we[0], wr[0] = expand[...], reduce[...]
            web[0:1, :] = bias[...]
            for m in range(1, n_hid):
                for k, piece in enumerate(near[1][m - 1] + far[m - 1]):
                    at = pl.ds(pl.multiple_of((res[3] ^ (k % 4 * 2 + k // 4)) * n, n), n)
                    we[m, at, :] = piece[:n]
                    wr[m, at, :] = piece[n : 2 * n]
                tail = near[1][m - 1][0][2 * n :].astype(F32)
                web[m : m + 1, :] = tail[0:1] + tail[1:2]
        mid = centred(first[...])[0] * mg[...] + msh[...]
        _, second = feed(mid, we, web, wr, rb)
        new = centred(second)[0] * fg[...] + fsh[...]
        new_out[...] = new
        low = new.astype(BF)
        low_out[...] = low
        dealt(away_out, dot(send[...], low))

    def pass_two(rows, fanout, step):
        span = step * rows

        def kernel(
            arrived, state, low, edges, pick, counts, mf, mfb, ms, msb, mt, mtb, mg, msh,
            we, web, wr, rb, fg, fsh, send, ef, efb, es, esb, et, etb, eg, esh,
            edge_out, act_out, slope1_out, slope2_out, first_out, summed_out, mid_out,
            slopes_out, second_out, new_out, low_out, away_out, sums,
        ):
            width = state.shape[1]
            received = joined(arrived)
            key = dot_nt(received, ef[:, width : 2 * width]).astype(BF)
            edge_part = dot_nt(low[...], ef[:, :width]) + efb[...]
            edge_lower = ef[:, 2 * width :]
            query = dot(received, mf[width : 2 * width]).astype(BF)
            part = dot(low[...], mf[:width]) + mfb[...]
            lower = mf[2 * width :]
            lots = jnp.broadcast_to(counts[...], (rows, ms.shape[1]))
            sums[...] = jnp.zeros_like(sums)

            def chunk(i, carry):
                at = pl.ds(pl.multiple_of(i * span, span), span)
                chosen = pick[at, :]
                old = edges[at, :]
                pre = dot(chosen, key) + dot_nt(old, edge_lower)
                act = smooth(tiled_add(pre, edge_part)).astype(BF)
                act = smooth(dot(act, es[...]) + esb[...]).astype(BF)
                total = old.astype(F32) + dot(act, et[...]) + etb[...]
                fresh = centred(total)[0] * eg[...] + esh[...]
                edge_out[at, :] = fresh
                pre = dot(chosen, query) + dot(fresh.astype(BF), lower)
                act, slope = smooth_slope(tiled_add(pre, part))
                act = act.astype(BF)
                act_out[at, :] = act
                slope1_out[at, :] = slope.astype(BF)
                act, slope = smooth_slope(dot(act, ms[...]) + msb[...])
                total = sums[...]
                for j in range(step):
                    valid = lots > (i * step + j).astype(F32)
                    total = total + jnp.where(valid, act[j * rows : (j + 1) * rows], 0.0)
                    slope2_out[pl.ds(pl.multiple_of(i * span + j * rows, rows), rows), :] = jnp.where(
                        valid, slope[j * rows : (j + 1) * rows], 0.0
                    ).astype(BF)
                sums[...] = total
                return carry

            lax.fori_loop(0, fanout // step, chunk, 0)
            summed_out[...] = sums[...].astype(BF)
            first = state[...] + message_mean(sums[...], counts[...], mt[...], mtb[...])
            first_out[...] = first
            mid = centred(first)[0] * mg[...] + msh[...]
            mid_low, second = feed(mid, we, web, wr, rb, slopes_out)
            mid_out[...] = mid_low
            second_out[...] = second
            new = centred(second)[0] * fg[...] + fsh[...]
            new_out[...] = new
            new_low = new.astype(BF)
            low_out[...] = new_low
            dealt(away_out, dot(send[...], new_low))

        return kernel

    def edge_turn(rows, fanout, step):
        span = step * rows

        def kernel(
            arrived, low, edges, up, pick, ef, efb, es, esb, et, etb, eg, esh,
            result_out, grad_out, act1_out, act2_out, top_out, mid_out, bottom_out,
            slot_out, node_out, vec_out, slots, node, marks,
        ):
            width = low.shape[1]
            key = dot_nt(joined(arrived), ef[:, width : 2 * width]).astype(BF)
            edge_part = dot_nt(low[...], ef[:, :width]) + efb[...]
            edge_lower = ef[:, 2 * width :]
            slots[...] = jnp.zeros_like(slots)
            node[...] = jnp.zeros_like(node)
            marks[...] = jnp.zeros_like(marks)

            def chunk(i, carry):
                at = pl.ds(pl.multiple_of(i * span, span), span)
                chosen = pick[at, :]
                old = edges[at, :]
                pre = dot(chosen, key) + dot_nt(old.astype(BF), edge_lower)
                act, slope1 = smooth_slope(tiled_add(pre, edge_part))
                act1 = act.astype(BF)
                act1_out[at, :] = act1
                act, slope2 = smooth_slope(dot(act1, es[...]) + esb[...])
                act2 = act.astype(BF)
                act2_out[at, :] = act2
                total = old + dot(act2, et[...]) + etb[...]
                hat, rate = centred(total)
                result_out[at, :] = hat * eg[...] + esh[...]
                above = up[at, :].astype(F32)
                sum_grad = norm_pull(hat, rate, eg[...], above)
                top = sum_grad.astype(BF)
                top_out[at, :] = top
                mid = dot_nt(top, et[...]) * slope2
                mid_low = mid.astype(BF)
                mid_out[at, :] = mid_low
                bottom = dot_nt(mid_low, es[...]) * slope1
                bottom_low = bottom.astype(BF)
                bottom_out[at, :] = bottom_low
                grad_out[at, :] = sum_grad + dot(bottom_low, edge_lower)
                marks[0] += fold(above * hat, 8)
                marks[1] += fold(above, 8)
                marks[2] += fold(sum_grad, 8)
                marks[3] += fold(mid, 8)
                node[...] += fold(bottom, rows)
                slots[...] += dot_tn(chosen, bottom_low)
                return carry

            lax.fori_loop(0, fanout // step, chunk, 0)
            dealt(slot_out, slots[...])
            node_out[...] = node[...].astype(BF)
            vec_out[...] = jnp.zeros_like(vec_out)
            for j in range(4):
                vec_out[j : j + 1, :] = jnp.sum(marks[j], axis=0, keepdims=True)
            vec_out[4:5, :] = jnp.sum(node[...], axis=0, keepdims=True)

        return kernel

    def edge_weights(arrived, low, edges, act1, act2, top, mid, bottom, slot, node, pack_out):
        n, wide = act1.shape[1], low.shape[1]
        slot = jnp.concatenate([v[...] for v in slot], axis=0)
        pack_out[:n, :] = dot_tn(node[...], low[...]).astype(BF)
        pack_out[n : 2 * n, :] = dot_tn(slot, joined(arrived)).astype(BF)
        pack_out[2 * n :, :] = jnp.zeros((pack_out.shape[0] - 2 * n, wide), BF)
        pack_out[2 * n : 3 * n, :n] = dot_tn(act1[...], mid[...]).astype(BF)
        pack_out[2 * n : 3 * n, 256 : 256 + n] = dot_tn(act2[...], top[...]).astype(BF)
        lower = dot_tn(bottom[...], edges[...].astype(BF)).astype(BF)
        pack_out[3 * n :, :n] = lower[: n // 2]
        pack_out[3 * n :, 256 : 256 + n] = lower[n // 2 :]

    def node_turn(
        spot, returned, up, node, send, second, slopes, first, counts, summed, ef, mt, mg,
        we, wr, fg, pack, edge_vec, feed_out, sum_out, pull_out, pay_out, pay,
    ):
        width = up.shape[1]
        key_low = dot_tn(send[...], joined(returned)).astype(BF)
        new_grad = (
            up[...].astype(F32) + dot(node[...], ef[:, :width]) + dot(key_low, ef[:, width : 2 * width])
        )
        hat, rate = centred(second[...])
        sum_grad = norm_pull(hat, rate, fg[...], new_grad)
        vecs = [sum_grad, new_grad * hat, new_grad]
        low = sum_grad.astype(BF)
        feed_out[...] = low
        mid_grad = sum_grad
        bias = []
        for h in range(we.shape[0]):
            expand = dot_nt(low, wr[h]) * slopes[h].astype(F32)
            bias.append(jnp.sum(expand, axis=0, keepdims=True))
            mid_grad = mid_grad + dot_nt(expand.astype(BF), we[h])
        hat, rate = centred(first[...])
        first_grad = norm_pull(hat, rate, mg[...], mid_grad)
        sum_out[...] = first_grad
        vecs += [mid_grad * hat, mid_grad, first_grad]
        vecs = [jnp.sum(v, axis=0, keepdims=True) for v in vecs]
        rows_low = (first_grad / counts[...]).astype(BF)
        pull_out[...] = dot_nt(rows_low, mt[...])
        third = dot_tn(summed[...], rows_low).astype(BF)
        head, hidden = pack.shape[0], third.shape[0]
        pay[:head, :] = pack[...]
        pay[head : head + hidden, :] = third
        pay[head + hidden :, :] = jnp.zeros((pay.shape[0] - head - hidden, width), BF)
        rows = jnp.concatenate(vecs + [jnp.zeros((10, width), F32)], axis=0)
        at = lax.broadcasted_iota(jnp.int32, rows.shape, 0)
        share = bias[0].shape[1]
        for h, v in enumerate(bias):
            line = 6 + (spot[2] ^ h)
            if share < width:
                v = jnp.concatenate([v, jnp.zeros((1, width - share), F32)], axis=1)
            rows = jnp.where(at == line, v, rows)
        pay[head + hidden : head + hidden + 16, :] = rows.astype(BF)
        pay[head + hidden + 16 : head + hidden + 32, : edge_vec.shape[1]] = jnp.concatenate(
            [edge_vec[...], jnp.zeros_like(edge_vec)], axis=0
        ).astype(BF)
        if len(pay_out) == 1:
            pay_out[0][...] = pay[...]
        else:
            halved(spot, pay, *pay_out)

    def message_turn(rows, fanout, step):
        span = step * rows

        def kernel(
            spot, arrived, low, edges, pick, pull, act, slope1, slope2, ms,
            first_low_out, slot_out, node_out, pay_out,
            second_low, slots, node, marks, pay,
        ):
            width = low.shape[1]
            slots[...] = jnp.zeros_like(slots)
            node[...] = jnp.zeros_like(node)
            marks[...] = jnp.zeros_like(marks)

            def chunk(i, carry):
                at = pl.ds(pl.multiple_of(i * span, span), span)
                second = slope2[at, :].astype(F32).reshape(step, rows, -1) * pull[...][None]
                marks[...] += jnp.sum(second, axis=0)
                second = second.reshape(span, -1).astype(BF)
                second_low[at, :] = second
                first = dot_nt(second, ms[...]) * slope1[at, :].astype(F32)
                node[...] += fold(first, rows)
                first = first.astype(BF)
                first_low_out[at, :] = first
                slots[...] += dot_tn(pick[at, :], first)
                return carry

            lax.fori_loop(0, fanout // step, chunk, 0)
            slot = slots[...].astype(BF)
            dealt(slot_out, slot)
            node_low = node[...].astype(BF)
            node_out[...] = node_low
            hidden, last = ms.shape[0], 2 * width + edges.shape[1]
            pay[:width, :] = dot_tn(low[...], node_low).astype(BF)
            pay[width : 2 * width, :] = dot_tn(joined(arrived), slot).astype(BF)
            pay[2 * width : last, :] = dot_tn(edges[...].astype(BF), first_low_out[...]).astype(BF)
            pay[last : last + hidden, :] = dot_tn(act[...], second_low[...]).astype(BF)
            pay[last + hidden :, :] = jnp.zeros((pay.shape[0] - last - hidden, hidden), BF)
            vecs = [
                jnp.sum(node[...], axis=0, keepdims=True),
                jnp.sum(marks[...], axis=0, keepdims=True),
                jnp.zeros((14, hidden), F32),
            ]
            pay[last + hidden : last + hidden + 16, :] = jnp.concatenate(vecs, axis=0).astype(BF)
            if len(pay_out) == 1:
                pay_out[0][...] = pay[...]
            else:
                halved(spot, pay, *pay_out)

        return kernel

    def feed_weights(spot, mid, up, we, web, wr, pay_out, pay):
        mid = jnp.concatenate([v[...] for v in mid], axis=0)
        up = jnp.concatenate([v[...] for v in up], axis=0)
        act, slope = smooth_slope(dot(mid, we[...]) + web[...])
        expand = dot_nt(up, wr[...]) * slope
        n, share = we.shape
        expand = dot_tn(mid, expand.astype(BF)).astype(BF)
        reduce = dot_tn(act.astype(BF), up).astype(BF)
        if len(pay_out) == 2 and share != n:
            pay_out[0][...], pay_out[1][...] = expand, reduce
        else:
            pay[:n, :] = expand
            pay[n:, :] = reduce
            halved(spot, pay, *pay_out)

    def node_end(returned, send, first_grad, node, mf, out):
        width = out.shape[1]
        query_low = dot_tn(send[...], joined(returned)).astype(BF)
        out[...] = (
            first_grad[...] + dot_nt(node[...], mf[:width]) + dot_nt(query_low, mf[width : 2 * width])
        )

    def edge_end(rows, fanout, step):
        span = step * rows

        def kernel(grad, first_low, mf, out):
            lower = mf[mf.shape[0] - grad.shape[1] :]

            def chunk(i, carry):
                at = pl.ds(pl.multiple_of(i * span, span), span)
                out[at, :] = grad[at, :] + dot_nt(first_low[at, :], lower)
                return carry

            lax.fori_loop(0, fanout // step, chunk, 0)

        return kernel

    def split_chips(spot, keep, got, outs, total):
        total[...] = (keep[...].astype(F32) + got[...].astype(F32)).astype(BF)
        for m, out in enumerate(outs):
            n = out.shape[0]
            out[...] = total[pl.ds(pl.multiple_of((spot[1] ^ m) * n, n), n), :]

    def summed_up(parts):
        total = parts[0][...].astype(F32)
        for v in parts[1:]:
            total = total + v[...].astype(F32)
        return total.astype(BF)

    def split_hid(spot, parts, outs, total):
        total[...] = summed_up(parts)
        for m, out in enumerate(outs):
            n = out.shape[1]
            out[...] = total[:, pl.ds(pl.multiple_of((spot[2] ^ m) * n, n), n)]

    def add_up(parts, out):
        out[...] = summed_up(parts)

    def join_hid(spot, parts, out):
        for m, v in enumerate(parts):
            n = v.shape[1]
            out[:, pl.ds(pl.multiple_of((spot[2] ^ m) * n, n), n)] = v[...]

    def reduced(spot, keep, send, along_hid, name):
        half, width = keep.shape
        n = half // 4
        got = to_core(send)
        (parts,) = call(
            split_chips, [[struct((n, width), BF)] * 4], (keep, got), name + "_chips",
            [pltpu.VMEM((half, width), BF)], spot=spot,
        )
        parts = [parts[0]] + [to_chip(parts[m], m) for m in (1, 2, 3)]
        if along_hid:
            part = struct((n, width // 4), BF)
            (parts,) = call(
                split_hid, [[part] * 4], (parts,), name + "_hid", [pltpu.VMEM((n, width), BF)], spot=spot
            )
            parts = [parts[0]] + [to_hid(parts[m], m) for m in (1, 2, 3)]
            (own,) = call(add_up, [part], (parts,), name + "_sum")
            parts = [own] + [to_hid(own, m) for m in (1, 2, 3)]
            (own,) = call(join_hid, [struct((n, width), BF)], (parts,), name + "_join", spot=spot)
        else:
            (own,) = call(add_up, [struct((n, width), BF)], (parts,), name + "_sum")
        parts = [own] + [to_chip(own, m) for m in (1, 2, 3)]
        return parts + [to_core(v) for v in parts]

    def laid_out(spot, parts, total):
        if len(parts) == 1:
            total[...] = parts[0][...].astype(F32)
            return
        n = parts[0].shape[0]
        for k, v in enumerate(parts):
            at = ((spot[0] ^ (k // 4)) * 4 + (spot[1] ^ (k % 4))) * n
            total[pl.ds(pl.multiple_of(at, n), n), :] = v[...].astype(F32)

    def unpack_early(spot, parts, first_out, second_out, third_out, message_out, vec_out, total):
        laid_out(spot, parts, total)
        n, wide = second_out.shape[0], message_out.shape[1]
        first_out[:, :wide] = total[:n, :]
        first_out[:, wide : 2 * wide] = total[n : 2 * n, :]
        second_out[...] = total[2 * n : 3 * n, :n]
        third_out[...] = total[2 * n : 3 * n, 256 : 256 + n]
        at = 3 * n + n // 2
        first_out[: n // 2, 2 * wide :] = total[3 * n : at, :n]
        first_out[n // 2 :, 2 * wide :] = total[3 * n : at, 256 : 256 + n]
        hidden = message_out.shape[0]
        message_out[...] = total[at : at + hidden, :]
        vec_out[...] = total[at + hidden : at + hidden + 32, :]

    def unpack_late(spot, parts, first_out, second_out, vec_out, total):
        laid_out(spot, parts, total)
        n, hidden = first_out.shape[0], second_out.shape[0]
        first_out[...] = total[:n, :]
        second_out[...] = total[n : n + hidden, :]
        vec_out[...] = total[n + hidden : n + hidden + 16, :]

    def unpack_feed(spot, parts, expand_out, reduce_out, total):
        laid_out(spot, parts, total)
        n = expand_out.shape[0]
        expand_out[...] = total[:n, :]
        reduce_out[...] = total[n:, :]

    def body(
        nodes, edges, send_rows, neighbor_slots, neighbor_counts, mf, mfb, ms, msb, mt, mtb, mg, msh,
        expand_weight, expand_bias, reduce_weight, rb, fg, fsh, ef, efb, es, esb, et, etb, eg, esh,
        node_up, edge_up,
    ):
        rows, fanout, edge_width = edges.shape
        width, hidden = nodes.shape[1], ms.shape[0]
        share = expand_weight.shape[1]
        n_edges = rows * fanout
        step = 10 if fanout % 10 == 0 else 1
        slots_each = send_rows.shape[2]
        buffer = n_res * slots_each
        row = lambda v: v.reshape(1, -1)
        if tuned:
            res, hid = lax.axis_index("res"), lax.axis_index("hid")
            spot = jnp.stack([res % 2, res // 2, hid, res]).astype(jnp.int32)
            table = send_rows[0].reshape(2, 2, 2, slots_each)
            for bit in range(3):
                table = jnp.where((res >> (2 - bit)) % 2 == 1, jnp.flip(table, bit), table)
            slots = neighbor_slots ^ (res * slots_each)
        else:
            spot = jnp.zeros((4,), jnp.int32)
            table, slots = send_rows[0], neighbor_slots
        edges = edges.transpose(1, 0, 2).reshape(n_edges, edge_width)
        edge_up = edge_up.transpose(1, 0, 2).reshape(n_edges, edge_width)
        ef = ef.T
        send = jax.nn.one_hot(table.reshape(-1), rows, dtype=BF)
        pick = jax.nn.one_hot(slots.T.reshape(-1), buffer, dtype=BF)
        counts = neighbor_counts.astype(F32).reshape(-1, 1)
        mfb, msb, mtb, mg, msh, rb, fg, fsh = map(row, (mfb, msb, mtb, mg, msh, rb, fg, fsh))
        efb, esb, etb, eg, esh = map(row, (efb, esb, etb, eg, esh))
        edge_args = (ef, efb, es, esb, et, etb, eg, esh)
        bias = row(expand_bias)

        if tuned:
            deal = [struct((rows, width), BF)] * 4
            away = jnp.split(dot(send, nodes).astype(BF), 4)
        else:
            deal = [struct((buffer, width), BF)]
            away = [dot(send, nodes).astype(BF)]
        arrived = exchange(away)
        if tuned:
            high = bias.astype(BF)
            rest = (bias - high.astype(F32)).astype(BF)
            n = width // 8
            piece = jnp.concatenate(
                [
                    lax.dynamic_slice_in_dim(expand_weight, res * n, n),
                    lax.dynamic_slice_in_dim(reduce_weight, res * n, n),
                    high, rest, jnp.zeros((n // 4 - 2, width), BF),
                ]
            )
            near = []
            for m in (1, 2, 3):
                got = to_hid(piece, m)
                near.append([got] + [to_chip(got, k) for k in (1, 2, 3)])
            far = [[to_core(v) for v in group] for group in near]
            own = (expand_weight, reduce_weight, bias)
        else:
            near, far = None, None
            own = (
                lax.all_gather(expand_weight, "hid"),
                lax.all_gather(reduce_weight, "hid"),
                lax.all_gather(expand_bias, "hid"),
            )
        (first_one,) = call(
            pass_one(rows, fanout, step),
            [struct((rows, width), F32)],
            (arrived, nodes, edges, pick, counts, mf, mfb, ms, msb, mt, mtb),
            "message_one",
            [pltpu.VMEM((rows, hidden), F32)],
        )
        tail = (first_one, own, near, far, mg, msh, rb, fg, fsh, send)
        state, low, away, we, web, wr = call(
            (lambda spot, first, own, near, *more: feed_one(first, own, near and (spot, near), *more)),
            [
                struct((rows, width), F32), struct((rows, width), BF), deal,
                struct((n_hid, width, share), BF), struct((n_hid, share), F32),
                struct((n_hid, share, width), BF),
            ],
            tail,
            "feed_one",
            spot=spot,
        )
        feed_args = (we, web, wr, rb, fg, fsh)
        message_args = (mf, mfb, ms, msb, mt, mtb, mg, msh)
        arrived2, low2 = exchange(away), low
        (
            edge_state, act, slope1, slope2, first, summed, mid_low, slopes, second, node_result, low3, away,
        ) = call(
            pass_two(rows, fanout, step),
            [
                struct((n_edges, edge_width), F32),
                struct((n_edges, hidden), BF),
                struct((n_edges, hidden), BF),
                struct((n_edges, hidden), BF),
                struct((rows, width), F32),
                struct((rows, hidden), BF),
                struct((rows, width), BF),
                struct((n_hid, rows, share), BF),
                struct((rows, width), F32),
                jax.ShapeDtypeStruct((rows, width), F32),
                struct((rows, width), BF),
                deal,
            ],
            (arrived2, state, low2, edges, pick, counts, *message_args, *feed_args, send, *edge_args),
            "layer_two",
            [pltpu.VMEM((rows, hidden), F32)],
        )
        arrived3 = exchange(away)
        wide = lambda dtype: struct((n_edges, edge_width), dtype)
        edge_result, edge_grad, act1, act2, top, mid, bottom, slot, node, edge_vec = call(
            edge_turn(rows, fanout, step),
            [
                jax.ShapeDtypeStruct((n_edges, edge_width), F32),
                wide(F32), wide(BF), wide(BF), wide(BF), wide(BF), wide(BF),
                [struct((buffer // len(deal), edge_width), BF)] * len(deal),
                struct((rows, edge_width), BF),
                struct((8, edge_width), F32),
            ],
            (arrived3, low3, edge_state, edge_up, pick, *edge_args),
            "edge_turn",
            [
                pltpu.VMEM((buffer, edge_width), F32),
                pltpu.VMEM((rows, edge_width), F32),
                pltpu.VMEM((4, 8, edge_width), F32),
            ],
        )
        returned = exchange(slot)
        head = 3 * edge_width + edge_width // 2
        (pack,) = call(
            edge_weights,
            [struct((head, width), BF)],
            (arrived3, low3, edge_state, act1, act2, top, mid, bottom, slot, node),
            "edge_weights",
        )
        sized = lambda n: -(-n // 128) * 128
        n_early, n_late = sized(head + hidden + 32), sized(mf.shape[0] + hidden + 16)
        cut = lambda n: [struct((n // 2, width), BF)] * 2 if tuned else [struct((n, width), BF)]
        feed_low, first_grad, pull, early = call(
            node_turn,
            [struct((rows, width), BF), struct((rows, width), F32), struct((rows, hidden), F32), cut(n_early)],
            (
                returned, node_up, node, send, second, slopes, first, counts, summed, ef, mt, mg, we, wr, fg,
                pack, edge_vec,
            ),
            "node_turn",
            [pltpu.VMEM((n_early, width), BF)],
            spot=spot,
        )
        if tuned:
            mids = [mid_low] + [to_hid(mid_low, m) for m in (1, 2, 3)]
            feeds = [feed_low] + [to_hid(feed_low, m) for m in (1, 2, 3)]
            early = reduced(spot, *early, True, "early")
        else:
            mids = [lax.all_gather(mid_low, "hid", axis=0, tiled=True)]
            feeds = [lax.all_gather(feed_low, "hid", axis=0, tiled=True)]
            early = [lax.psum(early[0].astype(F32), ("res", "hid"))]
        first_low, slot, node, late = call(
            message_turn(rows, fanout, step),
            [
                struct((n_edges, hidden), BF),
                [struct((buffer // len(deal), hidden), BF)] * len(deal),
                struct((rows, hidden), BF),
                cut(n_late),
            ],
            (arrived2, low2, edge_state, pick, pull, act, slope1, slope2, ms),
            "message_turn",
            [
                pltpu.VMEM((n_edges, hidden), BF),
                pltpu.VMEM((buffer, hidden), F32),
                pltpu.VMEM((rows, hidden), F32),
                pltpu.VMEM((rows, hidden), F32),
                pltpu.VMEM((n_late, hidden), BF),
            ],
            limit=16,
            spot=spot,
        )
        returned = exchange(slot)
        (feed_pay,) = call(
            feed_weights,
            [cut(2 * width) if tuned else [struct((width, share), BF), struct((share, width), BF)]],
            (mids, feeds, expand_weight, bias, reduce_weight),
            "feed_weights",
            [pltpu.VMEM((2 * width, width), BF)],
            spot=spot,
        )
        if tuned:
            late = reduced(spot, *late, True, "late")
            feed_parts = reduced(spot, *feed_pay, False, "feed")
        else:
            late = [lax.psum(late[0].astype(F32), ("res", "hid"))]
        (node_gradient,) = call(
            node_end,
            [jax.ShapeDtypeStruct((rows, width), F32)],
            (returned, send, first_grad, node, mf),
            "node_end",
        )
        (edge_gradient,) = call(
            edge_end(rows, fanout, step),
            [jax.ShapeDtypeStruct((n_edges, edge_width), F32)],
            (edge_grad, first_low, mf),
            "edge_end",
        )
        final = lambda *shape: jax.ShapeDtypeStruct(shape, F32)
        edge_first_grad, edge_second_grad, edge_third_grad, third_grad, vec = call(
            unpack_early,
            [
                final(edge_width, ef.shape[1]), final(edge_width, edge_width), final(edge_width, edge_width),
                final(hidden, width), final(32, width),
            ],
            (early,),
            "unpack_early",
            [pltpu.VMEM((n_early, width), F32)],
            spot=spot,
        )
        first_weight_grad, second_weight_grad, message_vec = call(
            unpack_late,
            [final(*mf.shape), final(hidden, hidden), final(16, hidden)],
            (late,),
            "unpack_late",
            [pltpu.VMEM((n_late, width), F32)],
            spot=spot,
        )
        if tuned:
            expand_grad, reduce_grad = call(
                unpack_feed,
                [final(width, share), final(share, width)],
                (feed_parts,),
                "unpack_feed",
                [pltpu.VMEM((2 * width, width), F32)],
                spot=spot,
            )
        else:
            expand_grad, reduce_grad = [lax.psum(v.astype(F32), "res") for v in feed_pay]
        bias_rows = lax.dynamic_index_in_dim(vec, 6 + lax.axis_index("hid"), 0, keepdims=False)
        edge_vecs = vec[16:24, :edge_width]

        back = lambda v: v.reshape(fanout, rows, edge_width).transpose(1, 0, 2)
        return (
            node_result,
            back(edge_result),
            node_gradient,
            back(edge_gradient),
            first_weight_grad,
            message_vec[0],
            second_weight_grad,
            message_vec[1],
            third_grad,
            vec[5],
            vec[3],
            vec[4],
            expand_grad,
            bias_rows[:share],
            reduce_grad,
            vec[0],
            vec[1],
            vec[2],
            edge_first_grad.T,
            edge_vecs[4],
            edge_second_grad,
            edge_vecs[3],
            edge_third_grad,
            edge_vecs[2],
            edge_vecs[0],
            edge_vecs[1],
        )

    both = ("res", "hid")
    rows2, rows3 = P(both, None), P(both, None, None)
    placed = (
        rows2, rows3, rows3, rows2, P(both),
        P(), P(), P(), P(), P(), P(), P(), P(),
        P(None, "hid"), P("hid"), P("hid", None),
        P(), P(), P(), P(), P(), P(), P(), P(), P(), P(), P(),
        rows2, rows3,
    )
    given = (
        rows2, rows3, rows2, rows3,
        P(), P(), P(), P(), P(), P(), P(), P(),
        P(None, "hid"), P("hid"), P("hid", None),
        P(), P(), P(), P(), P(), P(), P(), P(), P(), P(), P(),
    )
    return jax.shard_map(body, mesh=mesh, in_specs=placed, out_specs=given, check_vma=False)
```

time: 574 us -> 242 us (0.42); the launches traced: 565 us -> 241 us
  local copies, waits for them, and re-layouts: 134 us -> 22.8 us
  matrix products: 92.6 us -> 0.98 us
  waiting for transfers between devices: 126 us -> 35.9 us
  blocking collectives: 84.2 us -> 0 us
  starting transfers between devices: 29.8 us -> 113 us
  other arithmetic: 82.7 us -> 3.46 us
  Pallas kernels: 0 us -> 62.9 us
  between operations: 15.7 us -> 1.99 us
    ppermute x0 -> x110, starting transfers between devices: none -> 113 us  [the longest x47 51.5 us: to_core(): return lax.ppermute(v, 'res', pair)]
    dot_general x45 -> x1, matrix products: 92.6 us -> 0.98 us  [dot(): return jnp.dot(left, right, preferred_element_type=F32)]
    psum x2 -> x0, waiting for transfers between devices: 76.5 us -> none  [the longest x1 76.5 us: backward(): lax.psum((first_weight_grad, first_bias_grad, second_weight_grad, second_...]
    pallas_call x0 -> x23, Pallas kernels: none -> 62.9 us  [call(): pl.pallas_call(body, out_shape=outs, in_specs=specs, out_specs=jax.tree.m...]
    psum x2 -> x0, blocking collectives: 52.1 us -> none  [the longest x1 39.8 us: backward(): lax.psum((first_weight_grad, first_bias_grad, second_weight_grad, second_...]
    reduce_scatter x3 -> x0, waiting for transfers between devices: 49.1 us -> none  [the longest x2 37.3 us: forward(): lax.psum_scatter(product(expand_act, reduce_weight).astype(jnp.bfloat16),...]
    ppermute x0 -> x110, waiting for transfers between devices: none -> 35.9 us  [the longest x42 19.5 us: to_chip(): return lax.ppermute(v, 'res', [(i, i ^ 2 * m) for i in range(n_res)])]
    gather x9 -> x0, local copies, waits for them, and re-layouts: 34.5 us -> none  [the longest x4 15.7 us: forward(): key_buffer[slot_flat].astype(jnp.float32)]
  transfers between devices with their start and end apart: 10 -> 110, of which waited for: 5 -> 28; matrix products, arithmetic and copies ran while one was open for 24% -> 2% of each run, Pallas kernels for 0% -> 9%
where the time goes in v1:
time: 242 us; the launch traced here: 241 us
  starting transfers between devices  113 us (47%)
  Pallas kernels  62.9 us (26%)
  waiting for transfers between devices  35.9 us (15%)
  local copies, waits for them, and re-layouts  22.8 us (9%)
  other arithmetic  3.46 us (1%)
    pallas_call x23, Pallas kernels, call(): pl.pallas_call(body, out_shape=outs, in_specs=specs, out_specs=jax.tree.m...  62.9 us
    ppermute x47, starting transfers between devices, to_core(): return lax.ppermute(v, 'res', pair)  51.5 us
    ppermute x42, starting transfers between devices, to_chip(): return lax.ppermute(v, 'res', [(i, i ^ 2 * m) for i in range(n_res)])  38.7 us
    ppermute x21, starting transfers between devices, to_hid(): return lax.ppermute(v, 'hid', [(i, i ^ m) for i in range(n_hid)])  22.3 us
    unnamed x188, local copies, waits for them, and re-layouts  19.5 us
    ppermute x42, waiting for transfers between devices, to_chip(): return lax.ppermute(v, 'res', [(i, i ^ 2 * m) for i in range(n_res)])  19.5 us
    ppermute x21, waiting for transfers between devices, to_hid(): return lax.ppermute(v, 'hid', [(i, i ^ m) for i in range(n_hid)])  13.1 us
  transfers between devices with their start and end apart: 110, of which 28 were waited for; matrix products, arithmetic and copies ran while one was open for 2% of the time, Pallas kernels for 9%

profile of v1, /device:TPU:1, one launch (start us, length us, event | category | flops | bytes accessed | tf_op | source)
XLA Modules:
  0.0 240.6 jit_solution(17800467429698426371)
XLA Ops:
  2.6 2.2 collective-permute-start.7
  4.8 2.3 collective-permute-start.11
  11.9 1.9 collective-permute-done.arrived_1_
  13.7 2.2 collective-permute-start.2
  15.9 4.2 %collective-permute-start.3 = (bf16[32,512]{1,0:T(8,128)(2,1)S(1)}, bf16[32,512]{1,0:T(8,128)(2,1)S(1)}, u32[]{:S(2)}, u32[]{:S(2)}) collective-permute-start(bf16[32,512]{1,0:T(8,128)(2,1)S(1)} %get-tuple-element.195.arrived_0_), channel_id=1, source_target_pairs={{0,4},{4,0},{8,12},{12,8},{16,20},{20,16},{24,28},{28,24},{1,5},{5... | collective-permute-start | bytes 98312 | tf_op jit(solution)/shard_map/ppermute | solution.py:137
  20.1 2.0 collective-permute-start.4
  23.3 1.6 collective-permute-start.9
  25.6 1.8 collective-permute-start.10
  28.2 1.8 collective-permute-start.14
  31.5 2.5 %collective-permute-start.17 = (bf16[144,512]{1,0:T(8,128)(2,1)S(1)}, bf16[144,512]{1,0:T(8,128)(2,1)}, u32[]{:S(2)}, u32[]{:S(2)}) collective-permute-start(bf16[144,512]{1,0:T(8,128)(2,1)S(1)} %collective-permute-done.15.near_2__0_), channel_id=1, source_target_pairs={{0,16},{4,20},{8,24},{12,28},{16,0},{20,4},{24,8},{28,12},{1,17},{... | collective-permute-start | bytes 442376 | tf_op jit(solution)/shard_map/ppermute | solution.py:134
  36.0 2.1 collective-permute-done.13.near_1__2_
  40.9 2.0 collective-permute-start.27
  43.0 1.9 collective-permute-start.20
  59.5 5.7 %message_one.1.first = f32[32,512]{1,0:T(8,128)S(1)} custom-call(bf16[32,512]{1,0:T(8,128)(2,1)S(1)} %get-tuple-element.195.arrived_0_, bf16[32,512]{1,0:T(8,128)(2,1)S(1)} %collective-permute-done.arrived_1_, bf16[32,512]{1,0:T(8,128)(2,1)S(1)} %collective-permute-done.1.arrived_2_, bf16[32,512]{1,0:T(8,128)(2,1)S(1)} %collective-permute-done.2.arrived_3_, ...), custom_call_target="tpu_custom_call" | custom-call | tf_op jit(solution)/shard_map/message_one/pallas_call | solution.py:69
  65.6 3.3 %feed_one.1 = (f32[32,512]{1,0:T(8,128)S(1)}, bf16[32,512]{1,0:T(8,128)(2,1)S(1)}, bf16[32,512]{1,0:T(8,128)(2,1)S(1)}, bf16[32,512]{1,0:T(8,128)(2,1)S(1)}, bf1...) custom-call(s32[4]{0:T(128)S(1)} %pad_add_fusion.spot, ...), custom_call_target="tpu_custom_call" | custom-call | tf_op jit(solution)/shard_map/feed_one/pallas_call | solution.py:69
  70.1 2.0 collective-permute-start.32
  75.8 1.7 collective-permute-start.37
  78.4 15.0 %layer_two.1 = (f32[1920,192]{1,0:T(8,128)S(1)}, bf16[1920,512]{1,0:T(8,128)(2,1)S(1)}, bf16[1920,512]{1,0:T(8,128)(2,1)S(1)}, bf16[1920,512]{1,0:T(8,128)(2,1)S...) custom-call(bf16[32,512]{1,0:T(8,128)(2,1)S(1)} %get-tuple-element.1, ...), custom_call_target="tpu_custom_call" | custom-call | tf_op jit(solution)/shard_map/layer_two/pallas_call | solution.py:69
  93.7 2.4 collective-permute-start.40
  100.3 9.5 %edge_turn.1 = (f32[1920,192]{1,0:T(8,128)}, f32[1920,192]{1,0:T(8,128)S(1)}, bf16[1920,192]{1,0:T(8,128)(2,1)S(1)}, bf16[1920,192]{1,0:T(8,128)(2,1)S(1)}, bf16...) custom-call(bf16[32,512]{1,0:T(8,128)(2,1)S(1)} %get-tuple-element.1, ...), custom_call_target="tpu_custom_call" | custom-call | tf_op jit(solution)/shard_map/edge_turn/pallas_call | solution.py:69
  112.3 1.5 collective-permute-start.46
  117.2 2.1 collective-permute-start.51
  120.5 3.0 %node_turn.1 = (bf16[32,512]{1,0:T(8,128)(2,1)S(1)}, f32[32,512]{1,0:T(8,128)S(1)}, f32[32,512]{1,0:T(8,128)S(1)}, bf16[640,512]{1,0:T(8,128)(2,1)S(1)}, bf16[640,512]{1,0:T(8,128)(2,1)S(1)}) custom-call(s32[4]{0:T(128)S(1)} %pad_add_fusion.spot, bf16[32,192]{1,0:T(8,128)(2,1)S(1)} %get-tuple-element.125.slot_0_.returned_0_, ...), custom_call_target="tpu_custom_call" | custom-call | tf_op jit(solution)/shard_map/node_turn/pallas_call | solution.py:69
  123.5 6.1 %message_turn.1 = (bf16[1920,512]{1,0:T(8,128)(2,1)S(1)}, bf16[32,512]{1,0:T(8,128)(2,1)S(1)}, bf16[32,512]{1,0:T(8,128)(2,1)S(1)}, bf16[32,512]{1,0:T(8,128)(2,...) custom-call(s32[4]{0:T(128)S(1)} %pad_add_fusion.spot, ...), custom_call_target="tpu_custom_call" | custom-call | tf_op jit(solution)/shard_map/message_turn/pallas_call | solution.py:69
  130.2 3.1 %collective-permute-start.94 = (bf16[32,512]{1,0:T(8,128)(2,1)S(1)}, bf16[32,512]{1,0:T(8,128)(2,1)S(1)}, u32[]{:S(2)}, u32[]{:S(2)}) collective-permute-start(bf16[32,512]{1,0:T(8,128)(2,1)S(1)} %get-tuple-element.177.mid_0_), channel_id=1, source_target_pairs={{0,2},{1,3},{2,0},{3,1},{4,6},{5,7},{6,4},{7,5},{8,10},{9,11},{10,... | collective-permute-start | bytes 98312 | tf_op jit(solution)/shard_map/ppermute | solution.py:140
  134.7 2.5 %collective-permute-start.97 = (bf16[32,512]{1,0:T(8,128)(2,1)S(1)}, bf16[32,512]{1,0:T(8,128)(2,1)S(1)}, u32[]{:S(2)}, u32[]{:S(2)}) collective-permute-start(bf16[32,512]{1,0:T(8,128)(2,1)S(1)} %get-tuple-element.178.up_0_), channel_id=1, source_target_pairs={{0,2},{1,3},{2,0},{3,1},{4,6},{5,7},{6,4},{7,5},{8,10},{9,11},{10,... | collective-permute-start | bytes 98312 | tf_op jit(solution)/shard_map/ppermute | solution.py:140
  138.5 4.0 %collective-permute-done.98.up_3_ = bf16[32,512]{1,0:T(8,128)(2,1)S(1)} collective-permute-done((bf16[32,512]{1,0:T(8,128)(2,1)S(1)}, bf16[32,512]{1,0:T(8,128)(2,1)S(1)}, u32[]{:S(2)}, u32[]{:S(2)}) %collective-permute-start.98) | collective-permute-done | bytes 32800 | tf_op jit(solution)/shard_map/ppermute | solution.py:140
  142.5 1.5 feed_weights.1
  144.0 3.1 %collective-permute-start.99 = (bf16[512,512]{1,0:T(8,128)(2,1)S(1)}, bf16[512,512]{1,0:T(8,128)(2,1)S(1)}, u32[]{:S(2)}, u32[]{:S(2)}) collective-permute-start(bf16[512,512]{1,0:T(8,128)(2,1)S(1)} %get-tuple-element.180), channel_id=1, source_target_pairs={{0,4},{4,0},{8,12},{12,8},{16,20},{20,16},{24,28},{28,24},{1,5},{5... | collective-permute-start | bytes 1572872 | tf_op jit(solution)/shard_map/ppermute | solution.py:137
  147.7 2.2 collective-permute-done.52.returned_1_
  151.7 1.9 collective-permute-done.54.returned_3_
  153.5 2.4 collective-permute-start.56
  166.7 2.9 %collective-permute-done.79.parts_3_ = bf16[160,512]{1,0:T(8,128)(2,1)S(1)} collective-permute-done((bf16[160,512]{1,0:T(8,128)(2,1)S(1)}, bf16[160,512]{1,0:T(8,128)(2,1)S(1)}, u32[]{:S(2)}, u32[]{:S(2)}) %collective-permute-start.79) | collective-permute-done | bytes 163872 | tf_op jit(solution)/shard_map/ppermute | solution.py:134
  171.4 2.9 %collective-permute-done.101.parts_2_ = bf16[128,512]{1,0:T(8,128)(2,1)S(1)} collective-permute-done((bf16[128,512]{1,0:T(8,128)(2,1)S(1)}, bf16[128,512]{1,0:T(8,128)(2,1)S(1)}, u32[]{:S(2)}, u32[]{:S(2)}) %collective-permute-start.101) | collective-permute-done | bytes 131104 | tf_op jit(solution)/shard_map/ppermute | solution.py:134
  175.0 2.4 %collective-permute-done.80.parts_1_ = bf16[160,128]{1,0:T(8,128)(2,1)S(1)} collective-permute-done((bf16[160,128]{1,0:T(8,128)(2,1)S(1)}, bf16[160,128]{1,0:T(8,128)(2,1)S(1)}, u32[]{:S(2)}, u32[]{:S(2)}) %collective-permute-start.80) | collective-permute-done | bytes 40992 | tf_op jit(solution)/shard_map/ppermute | solution.py:140
  178.7 3.9 %collective-permute-done.82.parts_3_ = bf16[160,128]{1,0:T(8,128)(2,1)S(1)} collective-permute-done((bf16[160,128]{1,0:T(8,128)(2,1)S(1)}, bf16[160,128]{1,0:T(8,128)(2,1)S(1)}, u32[]{:S(2)}, u32[]{:S(2)}) %collective-permute-start.82) | collective-permute-done | bytes 40992 | tf_op jit(solution)/shard_map/ppermute | solution.py:140
  183.5 3.1 %collective-permute-start.85 = (bf16[160,128]{1,0:T(8,128)(2,1)S(1)}, bf16[160,128]{1,0:T(8,128)(2,1)S(1)}, u32[]{:S(2)}, u32[]{:S(2)}) collective-permute-start(bf16[160,128]{1,0:T(8,128)(2,1)S(1)} %early_sum.1.parts_0_), channel_id=1, source_target_pairs={{0,3},{1,2},{2,1},{3,0},{4,7},{5,6},{6,5},{7,4},{8,11},{9,10},{10,... | collective-permute-start | bytes 122888 | tf_op jit(solution)/shard_map/ppermute | solution.py:140
  188.5 2.9 %collective-permute-start.65 = (bf16[224,128]{1,0:T(8,128)(2,1)S(1)}, bf16[224,128]{1,0:T(8,128)(2,1)S(1)}, u32[]{:S(2)}, u32[]{:S(2)}) collective-permute-start(bf16[224,128]{1,0:T(8,128)(2,1)S(1)} %get-tuple-element.161), channel_id=1, source_target_pairs={{0,3},{1,2},{2,1},{3,0},{4,7},{5,6},{6,5},{7,4},{8,11},{9,10},{10,... | collective-permute-start | bytes 172040 | tf_op jit(solution)/shard_map/ppermute | solution.py:140
  192.0 2.2 collective-permute-start.105
  194.3 6.9 %collective-permute-start.106 = (bf16[128,512]{1,0:T(8,128)(2,1)S(1)}, bf16[128,512]{1,0:T(8,128)(2,1)S(1)}, u32[]{:S(2)}, u32[]{:S(2)}) collective-permute-start(bf16[128,512]{1,0:T(8,128)(2,1)S(1)} %feed_sum.1.parts_0_), channel_id=1, source_target_pairs={{0,4},{4,0},{8,12},{12,8},{16,20},{20,16},{24,28},{28,24},{1,5},{5... | collective-permute-start | bytes 393224 | tf_op jit(solution)/shard_map/ppermute | solution.py:137
  207.3 2.6 %collective-permute-start.68 = (bf16[224,128]{1,0:T(8,128)(2,1)S(1)}, bf16[224,128]{1,0:T(8,128)(2,1)S(1)}, u32[]{:S(2)}, u32[]{:S(2)}) collective-permute-start(bf16[224,128]{1,0:T(8,128)(2,1)S(1)} %late_sum.1.parts_0_), channel_id=1, source_target_pairs={{0,3},{1,2},{2,1},{3,0},{4,7},{5,6},{6,5},{7,4},{8,11},{9,10},{10,... | collective-permute-start | bytes 172040 | tf_op jit(solution)/shard_map/ppermute | solution.py:140
  209.9 4.1 %collective-permute-start.109 = (bf16[128,512]{1,0:T(8,128)(2,1)S(1)}, bf16[128,512]{1,0:T(8,128)(2,1)S(1)}, u32[]{:S(2)}, u32[]{:S(2)}) collective-permute-start(bf16[128,512]{1,0:T(8,128)(2,1)S(1)} %collective-permute-done.105.parts_3_), channel_id=1, source_target_pairs={{0,4},{4,0},{8,12},{12,8},{16,20},{20,16},{24,28},{28,24},{1,5},{5... | collective-permute-start | bytes 393224 | tf_op jit(solution)/shard_map/ppermute | solution.py:137
  214.8 2.1 collective-permute-start.90
  223.0 1.5 copy-done.12
  224.7 2.9 %edge_end.1 = f32[1920,192]{1,0:T(8,128)} custom-call(f32[1920,192]{1,0:T(8,128)S(1)} %copy-done.10, bf16[1920,512]{1,0:T(8,128)(2,1)S(1)} %copy-done.12, bf16[1216,512]{1,0:T(8,128)(2,1)S(1)} %copy-done), custom_call_target="tpu_custom_call" | custom-call | tf_op jit(solution)/shard_map/edge_end/pallas_call | solution.py:69
  228.9 2.1 unpack_feed.1
  231.0 2.8 %unpack_early.1 = (f32[192,1216]{1,0:T(8,128)}, f32[192,192]{1,0:T(8,128)}, f32[192,192]{1,0:T(8,128)}, f32[512,512]{1,0:T(8,128)}, f32[32,512]{1,0:T(8,128)S(1)}) custom-call(s32[4]{0:T(128)S(1)} %pad_add_fusion.spot, bf16[160,512]{1,0:T(8,128)(2,1)S(1)} %copy-done.15, bf16[160,512]{1,0:T(8,128)(2,1)S(1)} %copy-done.21, ...), custom_call_target="tpu_custom_call" | custom-call | tf_op jit(solution)/shard_map/unpack_early/pallas_call | solution.py:69
  236.6 3.4 %unpack_late.1 = (f32[1216,512]{1,0:T(8,128)}, f32[512,512]{1,0:T(8,128)}, f32[16,512]{1,0:T(8,128)S(1)}) custom-call(s32[4]{0:T(128)S(1)} %pad_add_fusion.spot, bf16[224,512]{1,0:T(8,128)(2,1)S(1)} %late_join.1.parts_0_, bf16[224,512]{1,0:T(8,128)(2,1)} %collective-permute-done.69.parts_1_, bf16[224,512]{1,0:T(8,128)(2,1)} %collective-permute-done.70.parts_2_, ...), custom_call_target="tpu_custom_call" | custom-call | tf_op jit(solution)/shard_map/unpack_late/pallas_call | solution.py:69
  (407 shorter events, 88.7 us)
Async XLA Ops:
  4.8 22.5 %collective-permute-start.11 = (bf16[144,512]{1,0:T(8,128)(2,1)S(1)}, bf16[144,512]{1,0:T(8,128)(2,1)S(1)}, u32[]{:S(2)}, u32[]{:S(2)}) collective-permute-start(bf16[144,512]{1,0:T(8,128)(2,1)S(1)} %concatenate.3), channel_id=1, source_target_pairs={{0,2},{1,3},{2,0},{3,1},{4,6},{5,7},{6,4},{7,5},{8,10},{9,11},{10,... | collective-permute-start | bytes 442376 | tf_op jit(solution)/shard_map/ppermute | solution.py:140
  7.1 20.5 %collective-permute-start.15 = (bf16[144,512]{1,0:T(8,128)(2,1)S(1)}, bf16[144,512]{1,0:T(8,128)(2,1)S(1)}, u32[]{:S(2)}, u32[]{:S(2)}) collective-permute-start(bf16[144,512]{1,0:T(8,128)(2,1)S(1)} %concatenate.3), channel_id=1, source_target_pairs={{0,3},{1,2},{2,1},{3,0},{4,7},{5,6},{6,5},{7,4},{8,11},{9,10},{10,... | collective-permute-start | bytes 442376 | tf_op jit(solution)/shard_map/ppermute | solution.py:140
  9.0 19.2 %collective-permute-start.8 = (bf16[144,512]{1,0:T(8,128)(2,1)S(1)}, bf16[144,512]{1,0:T(8,128)(2,1)S(1)}, u32[]{:S(2)}, u32[]{:S(2)}) collective-permute-start(bf16[144,512]{1,0:T(8,128)(2,1)S(1)} %collective-permute-done.7.near_0__0_), channel_id=1, source_target_pairs={{0,8},{4,12},{8,0},{12,4},{16,24},{20,28},{24,16},{28,20},{1,9},{5... | collective-permute-start | bytes 442376 | tf_op jit(solution)/shard_map/ppermute | solution.py:134
  23.3 7.6 %collective-permute-start.9 = (bf16[144,512]{1,0:T(8,128)(2,1)S(1)}, bf16[144,512]{1,0:T(8,128)(2,1)S(1)}, u32[]{:S(2)}, u32[]{:S(2)}) collective-permute-start(bf16[144,512]{1,0:T(8,128)(2,1)S(1)} %collective-permute-done.7.near_0__0_), channel_id=1, source_target_pairs={{0,16},{4,20},{8,24},{12,28},{16,0},{20,4},{24,8},{28,12},{1,17},{... | collective-permute-start | bytes 442376 | tf_op jit(solution)/shard_map/ppermute | solution.py:134
  27.4 7.2 %collective-permute-start.12 = (bf16[144,512]{1,0:T(8,128)(2,1)S(1)}, bf16[144,512]{1,0:T(8,128)(2,1)S(1)}, u32[]{:S(2)}, u32[]{:S(2)}) collective-permute-start(bf16[144,512]{1,0:T(8,128)(2,1)S(1)} %collective-permute-done.11.near_1__0_), channel_id=1, source_target_pairs={{0,8},{4,12},{8,0},{12,4},{16,24},{20,28},{24,16},{28,20},{1,9},{5... | collective-permute-start | bytes 442376 | tf_op jit(solution)/shard_map/ppermute | solution.py:134
  27.6 10.5 %collective-permute-start.13 = (bf16[144,512]{1,0:T(8,128)(2,1)S(1)}, bf16[144,512]{1,0:T(8,128)(2,1)}, u32[]{:S(2)}, u32[]{:S(2)}) collective-permute-start(bf16[144,512]{1,0:T(8,128)(2,1)S(1)} %collective-permute-done.11.near_1__0_), channel_id=1, source_target_pairs={{0,16},{4,20},{8,24},{12,28},{16,0},{20,4},{24,8},{28,12},{1,17},{... | collective-permute-start | bytes 442376 | tf_op jit(solution)/shard_map/ppermute | solution.py:134
  28.2 10.7 %collective-permute-start.14 = (bf16[144,512]{1,0:T(8,128)(2,1)S(1)}, bf16[144,512]{1,0:T(8,128)(2,1)}, u32[]{:S(2)}, u32[]{:S(2)}) collective-permute-start(bf16[144,512]{1,0:T(8,128)(2,1)S(1)} %collective-permute-done.11.near_1__0_), channel_id=1, source_target_pairs={{0,24},{4,28},{8,16},{12,20},{16,8},{20,12},{24,0},{28,4},{1,25},{... | collective-permute-start | bytes 442376 | tf_op jit(solution)/shard_map/ppermute | solution.py:134
  30.9 10.0 %collective-permute-start.16 = (bf16[144,512]{1,0:T(8,128)(2,1)S(1)}, bf16[144,512]{1,0:T(8,128)(2,1)}, u32[]{:S(2)}, u32[]{:S(2)}) collective-permute-start(bf16[144,512]{1,0:T(8,128)(2,1)S(1)} %collective-permute-done.15.near_2__0_), channel_id=1, source_target_pairs={{0,8},{4,12},{8,0},{12,4},{16,24},{20,28},{24,16},{28,20},{1,9},{5... | collective-permute-start | bytes 442376 | tf_op jit(solution)/shard_map/ppermute | solution.py:134
  31.5 11.5 %collective-permute-start.17 = (bf16[144,512]{1,0:T(8,128)(2,1)S(1)}, bf16[144,512]{1,0:T(8,128)(2,1)}, u32[]{:S(2)}, u32[]{:S(2)}) collective-permute-start(bf16[144,512]{1,0:T(8,128)(2,1)S(1)} %collective-permute-done.15.near_2__0_), channel_id=1, source_target_pairs={{0,16},{4,20},{8,24},{12,28},{16,0},{20,4},{24,8},{28,12},{1,17},{... | collective-permute-start | bytes 442376 | tf_op jit(solution)/shard_map/ppermute | solution.py:134
  34.5 10.3 %collective-permute-start.18 = (bf16[144,512]{1,0:T(8,128)(2,1)S(1)}, bf16[144,512]{1,0:T(8,128)(2,1)}, u32[]{:S(2)}, u32[]{:S(2)}) collective-permute-start(bf16[144,512]{1,0:T(8,128)(2,1)S(1)} %collective-permute-done.15.near_2__0_), channel_id=1, source_target_pairs={{0,24},{4,28},{8,16},{12,20},{16,8},{20,12},{24,0},{28,4},{1,25},{... | collective-permute-start | bytes 442376 | tf_op jit(solution)/shard_map/ppermute | solution.py:134
  38.1 7.6 %collective-permute-start.19 = (bf16[144,512]{1,0:T(8,128)(2,1)S(1)}, bf16[144,512]{1,0:T(8,128)(2,1)S(1)}, u32[]{:S(2)}, u32[]{:S(2)}) collective-permute-start(bf16[144,512]{1,0:T(8,128)(2,1)S(1)} %collective-permute-done.7.near_0__0_), channel_id=1, source_target_pairs={{0,4},{4,0},{8,12},{12,8},{16,20},{20,16},{24,28},{28,24},{1,5},{5... | collective-permute-start | bytes 442376 | tf_op jit(solution)/shard_map/ppermute | solution.py:137
  38.9 7.4 %collective-permute-start.23 = (bf16[144,512]{1,0:T(8,128)(2,1)S(1)}, bf16[144,512]{1,0:T(8,128)(2,1)S(1)}, u32[]{:S(2)}, u32[]{:S(2)}) collective-permute-start(bf16[144,512]{1,0:T(8,128)(2,1)S(1)} %collective-permute-done.11.near_1__0_), channel_id=1, source_target_pairs={{0,4},{4,0},{8,12},{12,8},{16,20},{20,16},{24,28},{28,24},{1,5},{5... | collective-permute-start | bytes 442376 | tf_op jit(solution)/shard_map/ppermute | solution.py:137
  48.3 17.0 %collective-permute-start.25 = (bf16[144,512]{1,0:T(8,128)(2,1)}, bf16[144,512]{1,0:T(8,128)(2,1)}, u32[]{:S(2)}, u32[]{:S(2)}) collective-permute-start(bf16[144,512]{1,0:T(8,128)(2,1)} %collective-permute-done.13.near_1__2_), channel_id=1, source_target_pairs={{0,4},{4,0},{8,12},{12,8},{16,20},{20,16},{24,28},{28,24},{1,5},{5... | collective-permute-start | bytes 442376 | tf_op jit(solution)/shard_map/ppermute | solution.py:137
  48.9 16.3 %collective-permute-start.26 = (bf16[144,512]{1,0:T(8,128)(2,1)}, bf16[144,512]{1,0:T(8,128)(2,1)}, u32[]{:S(2)}, u32[]{:S(2)}) collective-permute-start(bf16[144,512]{1,0:T(8,128)(2,1)} %collective-permute-done.14.near_1__3_), channel_id=1, source_target_pairs={{0,4},{4,0},{8,12},{12,8},{16,20},{20,16},{24,28},{28,24},{1,5},{5... | collective-permute-start | bytes 442376 | tf_op jit(solution)/shard_map/ppermute | solution.py:137
  50.1 15.1 %collective-permute-start.28 = (bf16[144,512]{1,0:T(8,128)(2,1)}, bf16[144,512]{1,0:T(8,128)(2,1)}, u32[]{:S(2)}, u32[]{:S(2)}) collective-permute-start(bf16[144,512]{1,0:T(8,128)(2,1)} %collective-permute-done.16.near_2__1_), channel_id=1, source_target_pairs={{0,4},{4,0},{8,12},{12,8},{16,20},{20,16},{24,28},{28,24},{1,5},{5... | collective-permute-start | bytes 442376 | tf_op jit(solution)/shard_map/ppermute | solution.py:137
  50.8 14.5 %collective-permute-start.29 = (bf16[144,512]{1,0:T(8,128)(2,1)}, bf16[144,512]{1,0:T(8,128)(2,1)}, u32[]{:S(2)}, u32[]{:S(2)}) collective-permute-start(bf16[144,512]{1,0:T(8,128)(2,1)} %collective-permute-done.17.near_2__2_), channel_id=1, source_target_pairs={{0,4},{4,0},{8,12},{12,8},{16,20},{20,16},{24,28},{28,24},{1,5},{5... | collective-permute-start | bytes 442376 | tf_op jit(solution)/shard_map/ppermute | solution.py:137
  51.9 13.3 %collective-permute-start.30 = (bf16[144,512]{1,0:T(8,128)(2,1)}, bf16[144,512]{1,0:T(8,128)(2,1)}, u32[]{:S(2)}, u32[]{:S(2)}) collective-permute-start(bf16[144,512]{1,0:T(8,128)(2,1)} %collective-permute-done.18.near_2__3_), channel_id=1, source_target_pairs={{0,4},{4,0},{8,12},{12,8},{16,20},{20,16},{24,28},{28,24},{1,5},{5... | collective-permute-start | bytes 442376 | tf_op jit(solution)/shard_map/ppermute | solution.py:137
  129.7 33.1 %collective-permute-start.59 = (bf16[896,512]{1,0:T(8,128)(2,1)S(1)}, bf16[896,512]{1,0:T(8,128)(2,1)S(1)}, u32[]{:S(2)}, u32[]{:S(2)}) collective-permute-start(bf16[896,512]{1,0:T(8,128)(2,1)S(1)} %get-tuple-element.153), channel_id=1, source_target_pairs={{0,4},{4,0},{8,12},{12,8},{16,20},{20,16},{24,28},{28,24},{1,5},{5... | collective-permute-start | bytes 2752520 | tf_op jit(solution)/shard_map/ppermute | solution.py:137
  129.7 27.5 %collective-permute-start.76 = (bf16[640,512]{1,0:T(8,128)(2,1)S(1)}, bf16[640,512]{1,0:T(8,128)(2,1)S(1)}, u32[]{:S(2)}, u32[]{:S(2)}) collective-permute-start(bf16[640,512]{1,0:T(8,128)(2,1)S(1)} %get-tuple-element.166), channel_id=1, source_target_pairs={{0,4},{4,0},{8,12},{12,8},{16,20},{20,16},{24,28},{28,24},{1,5},{5... | collective-permute-start | bytes 1966088 | tf_op jit(solution)/shard_map/ppermute | solution.py:137
  144.0 12.0 %collective-permute-start.99 = (bf16[512,512]{1,0:T(8,128)(2,1)S(1)}, bf16[512,512]{1,0:T(8,128)(2,1)S(1)}, u32[]{:S(2)}, u32[]{:S(2)}) collective-permute-start(bf16[512,512]{1,0:T(8,128)(2,1)S(1)} %get-tuple-element.180), channel_id=1, source_target_pairs={{0,4},{4,0},{8,12},{12,8},{16,20},{20,16},{24,28},{28,24},{1,5},{5... | collective-permute-start | bytes 1572872 | tf_op jit(solution)/shard_map/ppermute | solution.py:137
  158.6 7.3 %collective-permute-start.77 = (bf16[160,512]{1,0:T(8,128)(2,1)S(1)}, bf16[160,512]{1,0:T(8,128)(2,1)S(1)}, u32[]{:S(2)}, u32[]{:S(2)}) collective-permute-start(bf16[160,512]{1,0:T(8,128)(2,1)S(1)} %get-tuple-element.168), channel_id=1, source_target_pairs={{0,8},{4,12},{8,0},{12,4},{16,24},{20,28},{24,16},{28,20},{1,9},{5... | collective-permute-start | bytes 491528 | tf_op jit(solution)/shard_map/ppermute | solution.py:134
  160.2 9.4 %collective-permute-start.79 = (bf16[160,512]{1,0:T(8,128)(2,1)S(1)}, bf16[160,512]{1,0:T(8,128)(2,1)S(1)}, u32[]{:S(2)}, u32[]{:S(2)}) collective-permute-start(bf16[160,512]{1,0:T(8,128)(2,1)S(1)} %get-tuple-element.170), channel_id=1, source_target_pairs={{0,24},{4,28},{8,16},{12,20},{16,8},{20,12},{24,0},{28,4},{1,25},{... | collective-permute-start | bytes 491528 | tf_op jit(solution)/shard_map/ppermute | solution.py:134
  162.4 11.9 %collective-permute-start.101 = (bf16[128,512]{1,0:T(8,128)(2,1)S(1)}, bf16[128,512]{1,0:T(8,128)(2,1)S(1)}, u32[]{:S(2)}, u32[]{:S(2)}) collective-permute-start(bf16[128,512]{1,0:T(8,128)(2,1)S(1)} %get-tuple-element.183), channel_id=1, source_target_pairs={{0,16},{4,20},{8,24},{12,28},{16,0},{20,4},{24,8},{28,12},{1,17},{... | collective-permute-start | bytes 393224 | tf_op jit(solution)/shard_map/ppermute | solution.py:134
  162.8 11.5 %collective-permute-start.102 = (bf16[128,512]{1,0:T(8,128)(2,1)S(1)}, bf16[128,512]{1,0:T(8,128)(2,1)S(1)}, u32[]{:S(2)}, u32[]{:S(2)}) collective-permute-start(bf16[128,512]{1,0:T(8,128)(2,1)S(1)} %get-tuple-element.184), channel_id=1, source_target_pairs={{0,24},{4,28},{8,16},{12,20},{16,8},{20,12},{24,0},{28,4},{1,25},{... | collective-permute-start | bytes 393224 | tf_op jit(solution)/shard_map/ppermute | solution.py:134
  165.9 17.0 %collective-permute-start.60 = (bf16[224,512]{1,0:T(8,128)(2,1)S(1)}, bf16[224,512]{1,0:T(8,128)(2,1)S(1)}, u32[]{:S(2)}, u32[]{:S(2)}) collective-permute-start(bf16[224,512]{1,0:T(8,128)(2,1)S(1)} %get-tuple-element.155), channel_id=1, source_target_pairs={{0,8},{4,12},{8,0},{12,4},{16,24},{20,28},{24,16},{28,20},{1,9},{5... | collective-permute-start | bytes 688136 | tf_op jit(solution)/shard_map/ppermute | solution.py:134
  166.3 17.1 %collective-permute-start.61 = (bf16[224,512]{1,0:T(8,128)(2,1)S(1)}, bf16[224,512]{1,0:T(8,128)(2,1)S(1)}, u32[]{:S(2)}, u32[]{:S(2)}) collective-permute-start(bf16[224,512]{1,0:T(8,128)(2,1)S(1)} %get-tuple-element.156), channel_id=1, source_target_pairs={{0,16},{4,20},{8,24},{12,28},{16,0},{20,4},{24,8},{28,12},{1,17},{... | collective-permute-start | bytes 688136 | tf_op jit(solution)/shard_map/ppermute | solution.py:134
  169.6 13.9 %collective-permute-start.62 = (bf16[224,512]{1,0:T(8,128)(2,1)S(1)}, bf16[224,512]{1,0:T(8,128)(2,1)S(1)}, u32[]{:S(2)}, u32[]{:S(2)}) collective-permute-start(bf16[224,512]{1,0:T(8,128)(2,1)S(1)} %get-tuple-element.157), channel_id=1, source_target_pairs={{0,24},{4,28},{8,16},{12,20},{16,8},{20,12},{24,0},{28,4},{1,25},{... | collective-permute-start | bytes 688136 | tf_op jit(solution)/shard_map/ppermute | solution.py:134
  178.4 13.6 %collective-permute-start.103 = (bf16[128,512]{1,0:T(8,128)(2,1)S(1)}, bf16[128,512]{1,0:T(8,128)(2,1)S(1)}, u32[]{:S(2)}, u32[]{:S(2)}) collective-permute-start(bf16[128,512]{1,0:T(8,128)(2,1)S(1)} %feed_sum.1.parts_0_), channel_id=1, source_target_pairs={{0,8},{4,12},{8,0},{12,4},{16,24},{20,28},{24,16},{28,20},{1,9},{5... | collective-permute-start | bytes 393224 | tf_op jit(solution)/shard_map/ppermute | solution.py:134
  182.5 9.5 %collective-permute-start.104 = (bf16[128,512]{1,0:T(8,128)(2,1)S(1)}, bf16[128,512]{1,0:T(8,128)(2,1)S(1)}, u32[]{:S(2)}, u32[]{:S(2)}) collective-permute-start(bf16[128,512]{1,0:T(8,128)(2,1)S(1)} %feed_sum.1.parts_0_), channel_id=1, source_target_pairs={{0,16},{4,20},{8,24},{12,28},{16,0},{20,4},{24,8},{28,12},{1,17},{... | collective-permute-start | bytes 393224 | tf_op jit(solution)/shard_map/ppermute | solution.py:134
  187.4 6.9 %collective-permute-start.63 = (bf16[224,128]{1,0:T(8,128)(2,1)S(1)}, bf16[224,128]{1,0:T(8,128)(2,1)S(1)}, u32[]{:S(2)}, u32[]{:S(2)}) collective-permute-start(bf16[224,128]{1,0:T(8,128)(2,1)S(1)} %get-tuple-element.159), channel_id=1, source_target_pairs={{0,1},{1,0},{2,3},{3,2},{4,5},{5,4},{6,7},{7,6},{8,9},{9,8},{10,11... | collective-permute-start | bytes 172040 | tf_op jit(solution)/shard_map/ppermute | solution.py:140
  187.5 13.7 %collective-permute-start.64 = (bf16[224,128]{1,0:T(8,128)(2,1)S(1)}, bf16[224,128]{1,0:T(8,128)(2,1)S(1)}, u32[]{:S(2)}, u32[]{:S(2)}) collective-permute-start(bf16[224,128]{1,0:T(8,128)(2,1)S(1)} %get-tuple-element.160), channel_id=1, source_target_pairs={{0,2},{1,3},{2,0},{3,1},{4,6},{5,7},{6,4},{7,5},{8,10},{9,11},{10,... | collective-permute-start | bytes 172040 | tf_op jit(solution)/shard_map/ppermute | solution.py:140
  188.5 13.4 %collective-permute-start.65 = (bf16[224,128]{1,0:T(8,128)(2,1)S(1)}, bf16[224,128]{1,0:T(8,128)(2,1)S(1)}, u32[]{:S(2)}, u32[]{:S(2)}) collective-permute-start(bf16[224,128]{1,0:T(8,128)(2,1)S(1)} %get-tuple-element.161), channel_id=1, source_target_pairs={{0,3},{1,2},{2,1},{3,0},{4,7},{5,6},{6,5},{7,4},{8,11},{9,10},{10,... | collective-permute-start | bytes 172040 | tf_op jit(solution)/shard_map/ppermute | solution.py:140
  191.9 15.4 %collective-permute-start.86 = (bf16[160,512]{1,0:T(8,128)(2,1)S(1)}, bf16[160,512]{1,0:T(8,128)(2,1)S(1)}, u32[]{:S(2)}, u32[]{:S(2)}) collective-permute-start(bf16[160,512]{1,0:T(8,128)(2,1)S(1)} %early_join.1.parts_0_), channel_id=1, source_target_pairs={{0,8},{4,12},{8,0},{12,4},{16,24},{20,28},{24,16},{28,20},{1,9},{5... | collective-permute-start | bytes 491528 | tf_op jit(solution)/shard_map/ppermute | solution.py:134
  192.0 11.0 %collective-permute-start.105 = (bf16[128,512]{1,0:T(8,128)(2,1)S(1)}, bf16[128,512]{1,0:T(8,128)(2,1)S(1)}, u32[]{:S(2)}, u32[]{:S(2)}) collective-permute-start(bf16[128,512]{1,0:T(8,128)(2,1)S(1)} %feed_sum.1.parts_0_), channel_id=1, source_target_pairs={{0,24},{4,28},{8,16},{12,20},{16,8},{20,12},{24,0},{28,4},{1,25},{... | collective-permute-start | bytes 393224 | tf_op jit(solution)/shard_map/ppermute | solution.py:134
  194.3 8.9 %collective-permute-start.106 = (bf16[128,512]{1,0:T(8,128)(2,1)S(1)}, bf16[128,512]{1,0:T(8,128)(2,1)S(1)}, u32[]{:S(2)}, u32[]{:S(2)}) collective-permute-start(bf16[128,512]{1,0:T(8,128)(2,1)S(1)} %feed_sum.1.parts_0_), channel_id=1, source_target_pairs={{0,4},{4,0},{8,12},{12,8},{16,20},{20,16},{24,28},{28,24},{1,5},{5... | collective-permute-start | bytes 393224 | tf_op jit(solution)/shard_map/ppermute | solution.py:137
  203.1 6.8 %collective-permute-start.66 = (bf16[224,128]{1,0:T(8,128)(2,1)S(1)}, bf16[224,128]{1,0:T(8,128)(2,1)S(1)}, u32[]{:S(2)}, u32[]{:S(2)}) collective-permute-start(bf16[224,128]{1,0:T(8,128)(2,1)S(1)} %late_sum.1.parts_0_), channel_id=1, source_target_pairs={{0,1},{1,0},{2,3},{3,2},{4,5},{5,4},{6,7},{7,6},{8,9},{9,8},{10,11... | collective-permute-start | bytes 172040 | tf_op jit(solution)/shard_map/ppermute | solution.py:140
  203.8 15.4 %collective-permute-start.87 = (bf16[160,512]{1,0:T(8,128)(2,1)S(1)}, bf16[160,512]{1,0:T(8,128)(2,1)}, u32[]{:S(2)}, u32[]{:S(2)}) collective-permute-start(bf16[160,512]{1,0:T(8,128)(2,1)S(1)} %early_join.1.parts_0_), channel_id=1, source_target_pairs={{0,16},{4,20},{8,24},{12,28},{16,0},{20,4},{24,8},{28,12},{1,17},{... | collective-permute-start | bytes 491528 | tf_op jit(solution)/shard_map/ppermute | solution.py:134
  204.6 15.1 %collective-permute-start.88 = (bf16[160,512]{1,0:T(8,128)(2,1)S(1)}, bf16[160,512]{1,0:T(8,128)(2,1)}, u32[]{:S(2)}, u32[]{:S(2)}) collective-permute-start(bf16[160,512]{1,0:T(8,128)(2,1)S(1)} %early_join.1.parts_0_), channel_id=1, source_target_pairs={{0,24},{4,28},{8,16},{12,20},{16,8},{20,12},{24,0},{28,4},{1,25},{... | collective-permute-start | bytes 491528 | tf_op jit(solution)/shard_map/ppermute | solution.py:134
  206.3 7.7 %collective-permute-start.67 = (bf16[224,128]{1,0:T(8,128)(2,1)S(1)}, bf16[224,128]{1,0:T(8,128)(2,1)S(1)}, u32[]{:S(2)}, u32[]{:S(2)}) collective-permute-start(bf16[224,128]{1,0:T(8,128)(2,1)S(1)} %late_sum.1.parts_0_), channel_id=1, source_target_pairs={{0,2},{1,3},{2,0},{3,1},{4,6},{5,7},{6,4},{7,5},{8,10},{9,11},{10,... | collective-permute-start | bytes 172040 | tf_op jit(solution)/shard_map/ppermute | solution.py:140
  207.3 7.4 %collective-permute-start.68 = (bf16[224,128]{1,0:T(8,128)(2,1)S(1)}, bf16[224,128]{1,0:T(8,128)(2,1)S(1)}, u32[]{:S(2)}, u32[]{:S(2)}) collective-permute-start(bf16[224,128]{1,0:T(8,128)(2,1)S(1)} %late_sum.1.parts_0_), channel_id=1, source_target_pairs={{0,3},{1,2},{2,1},{3,0},{4,7},{5,6},{6,5},{7,4},{8,11},{9,10},{10,... | collective-permute-start | bytes 172040 | tf_op jit(solution)/shard_map/ppermute | solution.py:140
  209.9 7.6 %collective-permute-start.109 = (bf16[128,512]{1,0:T(8,128)(2,1)S(1)}, bf16[128,512]{1,0:T(8,128)(2,1)S(1)}, u32[]{:S(2)}, u32[]{:S(2)}) collective-permute-start(bf16[128,512]{1,0:T(8,128)(2,1)S(1)} %collective-permute-done.105.parts_3_), channel_id=1, source_target_pairs={{0,4},{4,0},{8,12},{12,8},{16,20},{20,16},{24,28},{28,24},{1,5},{5... | collective-permute-start | bytes 393224 | tf_op jit(solution)/shard_map/ppermute | solution.py:137
  214.0 6.8 %collective-permute-start.89 = (bf16[160,512]{1,0:T(8,128)(2,1)S(1)}, bf16[160,512]{1,0:T(8,128)(2,1)S(1)}, u32[]{:S(2)}, u32[]{:S(2)}) collective-permute-start(bf16[160,512]{1,0:T(8,128)(2,1)S(1)} %early_join.1.parts_0_), channel_id=1, source_target_pairs={{0,4},{4,0},{8,12},{12,8},{16,20},{20,16},{24,28},{28,24},{1,5},{5... | collective-permute-start | bytes 491528 | tf_op jit(solution)/shard_map/ppermute | solution.py:137
  214.8 7.6 %collective-permute-start.90 = (bf16[160,512]{1,0:T(8,128)(2,1)S(1)}, bf16[160,512]{1,0:T(8,128)(2,1)S(1)}, u32[]{:S(2)}, u32[]{:S(2)}) collective-permute-start(bf16[160,512]{1,0:T(8,128)(2,1)S(1)} %collective-permute-done.86.parts_1_), channel_id=1, source_target_pairs={{0,4},{4,0},{8,12},{12,8},{16,20},{20,16},{24,28},{28,24},{1,5},{5... | collective-permute-start | bytes 491528 | tf_op jit(solution)/shard_map/ppermute | solution.py:137
  218.2 16.1 %collective-permute-start.69 = (bf16[224,512]{1,0:T(8,128)(2,1)S(1)}, bf16[224,512]{1,0:T(8,128)(2,1)}, u32[]{:S(2)}, u32[]{:S(2)}) collective-permute-start(bf16[224,512]{1,0:T(8,128)(2,1)S(1)} %late_join.1.parts_0_), channel_id=1, source_target_pairs={{0,8},{4,12},{8,0},{12,4},{16,24},{20,28},{24,16},{28,20},{1,9},{5... | collective-permute-start | bytes 688136 | tf_op jit(solution)/shard_map/ppermute | solution.py:134
  219.1 15.2 %collective-permute-start.70 = (bf16[224,512]{1,0:T(8,128)(2,1)S(1)}, bf16[224,512]{1,0:T(8,128)(2,1)}, u32[]{:S(2)}, u32[]{:S(2)}) collective-permute-start(bf16[224,512]{1,0:T(8,128)(2,1)S(1)} %late_join.1.parts_0_), channel_id=1, source_target_pairs={{0,16},{4,20},{8,24},{12,28},{16,0},{20,4},{24,8},{28,12},{1,17},{... | collective-permute-start | bytes 688136 | tf_op jit(solution)/shard_map/ppermute | solution.py:134
  219.7 15.1 %collective-permute-start.71 = (bf16[224,512]{1,0:T(8,128)(2,1)S(1)}, bf16[224,512]{1,0:T(8,128)(2,1)}, u32[]{:S(2)}, u32[]{:S(2)}) collective-permute-start(bf16[224,512]{1,0:T(8,128)(2,1)S(1)} %late_join.1.parts_0_), channel_id=1, source_target_pairs={{0,24},{4,28},{8,16},{12,20},{16,8},{20,12},{24,0},{28,4},{1,25},{... | collective-permute-start | bytes 688136 | tf_op jit(solution)/shard_map/ppermute | solution.py:134
  221.5 9.4 %collective-permute-start.91 = (bf16[160,512]{1,0:T(8,128)(2,1)}, bf16[160,512]{1,0:T(8,128)(2,1)}, u32[]{:S(2)}, u32[]{:S(2)}) collective-permute-start(bf16[160,512]{1,0:T(8,128)(2,1)} %collective-permute-done.87.parts_2_), channel_id=1, source_target_pairs={{0,4},{4,0},{8,12},{12,8},{16,20},{20,16},{24,28},{28,24},{1,5},{5... | collective-permute-start | bytes 491528 | tf_op jit(solution)/shard_map/ppermute | solution.py:137
  223.0 7.9 %collective-permute-start.92 = (bf16[160,512]{1,0:T(8,128)(2,1)}, bf16[160,512]{1,0:T(8,128)(2,1)}, u32[]{:S(2)}, u32[]{:S(2)}) collective-permute-start(bf16[160,512]{1,0:T(8,128)(2,1)} %collective-permute-done.88.parts_3_), channel_id=1, source_target_pairs={{0,4},{4,0},{8,12},{12,8},{16,20},{20,16},{24,28},{28,24},{1,5},{5... | collective-permute-start | bytes 491528 | tf_op jit(solution)/shard_map/ppermute | solution.py:137
  (156 other events, 1105.9 us)

commit v2 on v1

v2 whole, which is shorter than its diff:
```python
import jax
import jax.numpy as jnp
from jax import lax
from jax.experimental import pallas as pl
from jax.experimental.pallas import tpu as pltpu
from jax.sharding import PartitionSpec as P

BF = jnp.bfloat16
F32 = jnp.float32
LEAN = 0.7978845608028654
CUBE = LEAN * 0.044715
MIB = 1 << 20
KEEP = pl.BlockSpec(memory_space=pltpu.VMEM)


def dot(left, right):
    return jnp.dot(left, right, preferred_element_type=F32)


def dot_nt(left, right):
    return lax.dot_general(left, right, (((1,), (1,)), ((), ())), preferred_element_type=F32)


def dot_tn(left, right):
    return lax.dot_general(left, right, (((0,), (0,)), ((), ())), preferred_element_type=F32)


def smooth(v):
    t = jnp.tanh(v * (LEAN + CUBE * (v * v)))
    half = 0.5 * v
    return half + half * t


def smooth_slope(v):
    v2 = v * v
    t = jnp.tanh(v * (LEAN + CUBE * v2))
    half = 0.5 * v
    slope = (0.5 + 0.5 * t) + (half - half * (t * t)) * (LEAN + (3.0 * CUBE) * v2)
    return half + half * t, slope


def centred(x):
    center = x - jnp.mean(x, axis=-1, keepdims=True)
    rate = lax.rsqrt(jnp.mean(center * center, axis=-1, keepdims=True) + 1e-05)
    return center * rate, rate


def norm_pull(hat, rate, gain, up):
    g = up * gain
    return rate * (
        g - jnp.mean(g, axis=-1, keepdims=True) - hat * jnp.mean(g * hat, axis=-1, keepdims=True)
    )


def tiled_add(rows, part):
    n, width = part.shape
    return (rows.reshape(-1, n, width) + part[None]).reshape(rows.shape)


def over(count, chunk):
    if count == 1:
        chunk(0, 0)
    else:
        lax.fori_loop(0, count, chunk, 0)


def aligned(index, size):
    return index if isinstance(index, int) else pl.multiple_of(index, size)


def fold(rows, n):
    return jnp.sum(rows.reshape(-1, n, rows.shape[-1]), axis=0)


class Final:
    def __init__(self, *shape):
        self.shape, self.dtype = shape, F32


def call(body, outs, args, name, scratch=(), limit=28, spot=None, after=(), far=False, token=False):
    if token:
        outs = list(outs) + [pltpu.VMEM((8, 128), F32)]
    flat_outs, out_tree = jax.tree.flatten(list(outs), is_leaf=lambda v: hasattr(v, "dtype"))
    ends = [k for k, v in enumerate(flat_outs) if isinstance(v, Final)]
    held_outs = [pltpu.VMEM(flat_outs[k].shape, flat_outs[k].dtype) for k in ends]
    if ends:
        held_outs.append(pltpu.SemaphoreType.DMA((len(ends),)))
    shapes = [pltpu.HBM(v.shape, v.dtype) if isinstance(v, Final) else v for v in flat_outs]
    out_specs = [pl.BlockSpec(memory_space=pltpu.HBM) if isinstance(v, Final) else KEEP for v in flat_outs]
    space = pltpu.HBM if far else pltpu.VMEM
    args = jax.tree.map(lambda v: pltpu.with_memory_space_constraint(v, space), list(args))
    specs = jax.tree.map(lambda v: pl.BlockSpec(memory_space=space), args)
    lead = 0
    if spot is not None:
        args, specs, lead = [spot] + args, [pl.BlockSpec(memory_space=pltpu.SMEM)] + specs, 1
    n, more = len(args), len(after)
    scratch = list(scratch)
    if far:
        flat, tree = jax.tree.flatten(args[lead:])
        scratch += [pltpu.VMEM(v.shape, v.dtype) for v in flat] + [pltpu.SemaphoreType.DMA((len(flat),))]

    def run(*refs):
        given, rest = refs[:n], refs[n + more :]
        results, rest = list(jax.tree.leaves(list(rest[: len(outs)]))), rest[len(outs) :]
        targets = [results[k] for k in ends]
        if ends:
            rest, kept, out_sems = rest[: -len(ends) - 1], rest[-len(ends) - 1 : -1], rest[-1]
            for k, v in zip(ends, kept):
                results[k] = v
        if far:
            count = len(flat)
            rest, held, sems = rest[: -count - 1], rest[-count - 1 : -1], rest[-1]
            copies = [
                pltpu.make_async_copy(src, dst, sems.at[k])
                for k, (src, dst) in enumerate(zip(jax.tree.leaves(list(given[lead:])), held))
            ]
            for copy in copies:
                copy.start()
            for copy in copies:
                copy.wait()
            given = list(given[:lead]) + jax.tree.unflatten(tree, held)
        produced = list(jax.tree.unflatten(out_tree, results))
        if token:
            produced.pop()[...] = jnp.zeros((8, 128), F32)
        body(*given, *produced, *rest)
        if ends:
            copies = [
                pltpu.make_async_copy(src, dst, out_sems.at[k])
                for k, (src, dst) in enumerate(zip(kept, targets))
            ]
            for copy in copies:
                copy.start()
            for copy in copies:
                copy.wait()

    return pl.pallas_call(
        run,
        out_shape=jax.tree.unflatten(out_tree, shapes),
        in_specs=specs + [pl.BlockSpec(memory_space=pl.ANY)] * more,
        out_specs=jax.tree.unflatten(out_tree, out_specs),
        scratch_shapes=scratch + held_outs,
        compiler_params=pltpu.CompilerParams(vmem_limit_bytes=limit * MIB),
        name=name,
    )(*args, *after)


def struct(shape, dtype):
    return pltpu.VMEM(shape, dtype)


def shards(own, packed):
    if len(packed) == 3:
        we, web, wr = packed
        for h in range(we.shape[0]):
            yield we[h], web[h : h + 1, :], wr[h]
        return
    yield own[0][...], own[1][...], own[2][...]
    (ref,) = packed
    n, width = ref.shape[0] // 8, ref.shape[1] // 3
    part = n // 9 * 4
    for h in range(3):
        at = slice(h * width, (h + 1) * width)
        we = jnp.concatenate([ref[r * n : r * n + part, at] for r in range(8)], axis=0)
        wr = jnp.concatenate([ref[r * n + part : r * n + 2 * part, at] for r in range(8)], axis=0)
        bias = ref[2 * part : n, at].astype(F32)
        yield we, bias[0:1] + bias[1:2], wr


def feed(mid, own, packed, rb, slopes):
    mid_low = mid.astype(BF)
    total = mid + rb
    for h, (we, web, wr) in enumerate(shards(own, packed)):
        act, slope = smooth_slope(dot(mid_low, we) + web)
        slopes[h] = slope.astype(BF)
        total = total + dot(act.astype(BF), wr)
    return mid_low, total


def joined(parts):
    if len(parts) == 1:
        return parts[0][...]
    near, far = parts[: len(parts) // 2], parts[len(parts) // 2 :]
    rows = []
    for mine, other in zip(near, far):
        half = mine.shape[0] // 2
        rows += [mine[:half], other[half:]]
    return jnp.concatenate(rows, axis=0)


def dealt(outs, value):
    n = value.shape[0] // len(outs)
    for m, out in enumerate(outs):
        out[...] = value[m * n : (m + 1) * n].astype(out.dtype)


def halved(spot, pay, keep, send):
    n = keep.shape[0] // 4
    for m in range(4):
        chip = (spot[1] ^ m) * 2
        keep[m * n : (m + 1) * n, :] = pay[pl.ds(pl.multiple_of((chip + spot[0]) * n, n), n), :]
        send[m * n : (m + 1) * n, :] = pay[pl.ds(pl.multiple_of((chip + 1 - spot[0]) * n, n), n), :]


def message_mean(summed, counts, mt, mtb):
    mean = summed / counts
    high = mean.astype(BF)
    rest = (mean - high.astype(F32)).astype(BF)
    return dot(high, mt) + dot(rest, mt) + mtb


def solution(mesh):
    n_res, n_hid = mesh.shape["res"], mesh.shape["hid"]
    tuned = (n_res, n_hid) == (8, 4)
    pair = [(i, i ^ 1) for i in range(n_res)]

    def to_chip(v, m):
        return lax.ppermute(v, "res", [(i, i ^ (2 * m)) for i in range(n_res)])

    def to_core(v):
        return lax.ppermute(v, "res", pair)

    def to_hid(v, m):
        return lax.ppermute(v, "hid", [(i, i ^ m) for i in range(n_hid)])

    def exchange(parts):
        if not tuned:
            n, width = parts[0].shape
            blocks = parts[0].reshape(n_res, n // n_res, width)
            return [lax.all_to_all(blocks, "res", 0, 0, tiled=True).reshape(n, width)]
        near = [parts[0]] + [to_chip(parts[m], m) for m in (1, 2, 3)]
        return near + [to_core(v) for v in near]

    def prepare_send(spot, table, nodes, weights, away_out, send_out, piece_out):
        rows, width = nodes.shape
        n = table.shape[1]
        lines = lax.broadcasted_iota(jnp.int32, (rows, n), 0)
        same = lax.broadcasted_iota(jnp.int32, (rows, rows), 0) == lax.broadcasted_iota(
            jnp.int32, (rows, rows), 1
        )
        same = same.astype(F32).astype(BF)
        each = n_res // len(away_out)
        for q in range(n_res):
            line = table[pl.ds(q ^ spot[3], 1), :]
            chosen = (lines == line).astype(F32).astype(BF)
            at = slice(q % each * n, (q % each + 1) * n)
            away_out[q // each][at, :] = dot_tn(chosen, nodes[...]).astype(BF)
            send_out[q * n : (q + 1) * n, :] = dot_tn(chosen, same).astype(BF)
        if piece_out:
            (out,) = piece_out
            we, wr, bias = weights
            n = width // 8
            at = pl.ds(pl.multiple_of(spot[3] * n, n), n)
            out[:n, :] = we[at, :]
            out[n : 2 * n, :] = wr[at, :]
            high = bias[...].astype(BF).astype(F32)
            rest = jnp.concatenate([high, bias[...] - high, jnp.zeros((n // 4 - 2, width), F32)], axis=0)
            out[2 * n :, :] = rest.astype(BF)

    def prepare_rest(spot, slots, counts, vecs, edge_vecs, pick_out, counts_out, vecs_out, edge_out):
        rows, fanout = slots.shape
        lanes = lax.broadcasted_iota(jnp.int32, (rows, pick_out.shape[1]), 1)
        moved = slots[...] ^ (spot[3] * (pick_out.shape[1] // n_res))
        for k in range(fanout):
            chosen = (lanes == moved[:, k : k + 1]).astype(F32).astype(BF)
            pick_out[k * rows : (k + 1) * rows, :] = chosen
        same = lax.broadcasted_iota(jnp.int32, (rows, rows), 0) == lax.broadcasted_iota(
            jnp.int32, (rows, rows), 1
        )
        many = jnp.where(same, jnp.broadcast_to(counts[...].astype(F32), (rows, rows)), 0.0)
        counts_out[...] = jnp.sum(many, axis=1, keepdims=True)
        edge_out[...] = jnp.zeros_like(edge_out)
        for k, v in enumerate(vecs):
            vecs_out[k : k + 1, :] = v[...]
        for k, v in enumerate(edge_vecs):
            edge_out[k : k + 1, :] = v[...]

    def pass_one(rows, fanout, step):
        span = step * rows

        def kernel(
            arrived, nodes, edges, pick, counts, mf, ms, mt, vecs, mid_out, sums,
        ):
            mfb, msb, mtb, mg, msh = [vecs[k : k + 1, :] for k in range(5)]
            width = nodes.shape[1]
            query = dot(joined(arrived), mf[width : 2 * width]).astype(BF)
            part = dot(nodes[...], mf[:width]) + mfb
            lower = mf[2 * width :]
            lots = jnp.broadcast_to(counts[...], (rows, ms.shape[1]))
            sums[...] = jnp.zeros_like(sums)

            def chunk(i, carry):
                at = pl.ds(aligned(i * span, span), span)
                pre = dot(pick[at, :], query) + dot(edges[at, :], lower)
                act = smooth(tiled_add(pre, part)).astype(BF)
                act = smooth(dot(act, ms[...]) + msb)
                total = sums[...]
                for j in range(step):
                    total = total + jnp.where(
                        lots > jnp.float32(i * step + j), act[j * rows : (j + 1) * rows], 0.0
                    )
                sums[...] = total
                return carry

            over(fanout // step, chunk)
            first = nodes[...].astype(F32) + message_mean(sums[...], counts[...], mt[...], mtb)
            mid_out[...] = centred(first)[0] * mg + msh

        return kernel

    def feed_pass(mid, own, packed, vecs, send, slopes_out, second_out, new_out, low_out, away_out):
        rb, fg, fsh = [vecs[k : k + 1, :] for k in (5, 6, 7)]
        _, second = feed(mid[...], own, packed, rb, slopes_out)
        second_out[...] = second
        new = centred(second)[0] * fg + fsh
        new_out[...] = new
        low = new.astype(BF)
        low_out[...] = low
        dealt(away_out, dot(send[...], low))

    def pass_two(rows, fanout, step):
        span = step * rows

        def kernel(
            arrived, state, low, edges, pick, counts, mf, ms, mt, vecs, ef, es, et, edge_vecs,
            edge_out, act_out, slope1_out, slope2_out, first_out, summed_out, mid_out, mid_low_out, sums,
        ):
            mfb, msb, mtb, mg, msh = [vecs[k : k + 1, :] for k in range(5)]
            efb, esb, etb, eg, esh = [edge_vecs[k : k + 1, :] for k in range(5)]
            width = state.shape[1]
            received = joined(arrived)
            key = dot_nt(received, ef[:, width : 2 * width]).astype(BF)
            edge_part = dot_nt(low[...], ef[:, :width]) + efb
            edge_lower = ef[:, 2 * width :]
            query = dot(received, mf[width : 2 * width]).astype(BF)
            part = dot(low[...], mf[:width]) + mfb
            lower = mf[2 * width :]
            lots = jnp.broadcast_to(counts[...], (rows, ms.shape[1]))
            sums[...] = jnp.zeros_like(sums)

            def chunk(i, carry):
                at = pl.ds(aligned(i * span, span), span)
                chosen = pick[at, :]
                old = edges[at, :]
                pre = dot(chosen, key) + dot_nt(old, edge_lower)
                act = smooth(tiled_add(pre, edge_part)).astype(BF)
                act = smooth(dot(act, es[...]) + esb).astype(BF)
                total = old.astype(F32) + dot(act, et[...]) + etb
                fresh = centred(total)[0] * eg + esh
                edge_out[at, :] = fresh
                pre = dot(chosen, query) + dot(fresh.astype(BF), lower)
                act, slope = smooth_slope(tiled_add(pre, part))
                act = act.astype(BF)
                act_out[at, :] = act
                slope1_out[at, :] = slope.astype(BF)
                act, slope = smooth_slope(dot(act, ms[...]) + msb)
                total = sums[...]
                for j in range(step):
                    valid = lots > jnp.float32(i * step + j)
                    total = total + jnp.where(valid, act[j * rows : (j + 1) * rows], 0.0)
                    slope2_out[pl.ds(aligned(i * span + j * rows, rows), rows), :] = jnp.where(
                        valid, slope[j * rows : (j + 1) * rows], 0.0
                    ).astype(BF)
                sums[...] = total
                return carry

            over(fanout // step, chunk)
            summed_out[...] = sums[...].astype(BF)
            first = state[...] + message_mean(sums[...], counts[...], mt[...], mtb)
            first_out[...] = first
            mid = centred(first)[0] * mg + msh
            mid_out[...] = mid
            mid_low_out[...] = mid.astype(BF)

        return kernel

    def edge_turn(rows, fanout, step):
        span = step * rows

        def kernel(
            arrived, low, edges, up, pick, ef, es, et, edge_vecs,
            result_out, grad_out, act1_out, act2_out, top_out, mid_out, bottom_out,
            slot_out, node_out, vec_out, slots, node, marks,
        ):
            width = low.shape[1]
            efb, esb, etb, eg, esh = [edge_vecs[k : k + 1, :] for k in range(5)]
            key = dot_nt(joined(arrived), ef[:, width : 2 * width]).astype(BF)
            edge_part = dot_nt(low[...], ef[:, :width]) + efb
            edge_lower = ef[:, 2 * width :]
            slots[...] = jnp.zeros_like(slots)
            node[...] = jnp.zeros_like(node)
            marks[...] = jnp.zeros_like(marks)

            def chunk(i, carry):
                at = pl.ds(aligned(i * span, span), span)
                chosen = pick[at, :]
                old = edges[at, :]
                pre = dot(chosen, key) + dot_nt(old.astype(BF), edge_lower)
                act, slope1 = smooth_slope(tiled_add(pre, edge_part))
                act1 = act.astype(BF)
                act1_out[at, :] = act1
                act, slope2 = smooth_slope(dot(act1, es[...]) + esb)
                act2 = act.astype(BF)
                act2_out[at, :] = act2
                total = old + dot(act2, et[...]) + etb
                hat, rate = centred(total)
                result_out[at, :] = hat * eg + esh
                above = up[at, :].astype(F32)
                sum_grad = norm_pull(hat, rate, eg, above)
                top = sum_grad.astype(BF)
                top_out[at, :] = top
                mid = dot_nt(top, et[...]) * slope2
                mid_low = mid.astype(BF)
                mid_out[at, :] = mid_low
                bottom = dot_nt(mid_low, es[...]) * slope1
                bottom_low = bottom.astype(BF)
                bottom_out[at, :] = bottom_low
                grad_out[at, :] = sum_grad + dot(bottom_low, edge_lower)
                marks[0] += fold(above * hat, 8)
                marks[1] += fold(above, 8)
                marks[2] += fold(sum_grad, 8)
                marks[3] += fold(mid, 8)
                node[...] += fold(bottom, rows)
                slots[...] += dot_tn(chosen, bottom_low)
                return carry

            over(fanout // step, chunk)
            dealt(slot_out, slots[...])
            node_out[...] = node[...].astype(BF)
            vec_out[...] = jnp.zeros_like(vec_out)
            for j in range(4):
                vec_out[j : j + 1, :] = jnp.sum(marks[j], axis=0, keepdims=True)
            vec_out[4:5, :] = jnp.sum(node[...], axis=0, keepdims=True)

        return kernel

    def edge_weights(arrived, low, edges, act1, act2, top, mid, bottom, slot, node, pack_out):
        n, wide = act1.shape[1], low.shape[1]
        slot = jnp.concatenate([v[...] for v in slot], axis=0)
        pack_out[:n, :] = dot_tn(node[...], low[...]).astype(BF)
        pack_out[n : 2 * n, :] = dot_tn(slot, joined(arrived)).astype(BF)
        pack_out[2 * n :, :] = jnp.zeros((pack_out.shape[0] - 2 * n, wide), BF)
        pack_out[2 * n : 3 * n, :n] = dot_tn(act1[...], mid[...]).astype(BF)
        pack_out[2 * n : 3 * n, 256 : 256 + n] = dot_tn(act2[...], top[...]).astype(BF)
        lower = dot_tn(bottom[...], edges[...].astype(BF)).astype(BF)
        pack_out[3 * n :, :n] = lower[: n // 2]
        pack_out[3 * n :, 256 : 256 + n] = lower[n // 2 :]

    def node_turn(
        spot, returned, up, node, send, second, slopes, first, counts, summed, ef, mt, vecs,
        own, packed, pack, edge_vec, mid_low, pair_out, sum_out, pull_out, pay_out, pay,
    ):
        width = up.shape[1]
        key_low = dot_tn(send[...], joined(returned)).astype(BF)
        new_grad = (
            up[...].astype(F32) + dot(node[...], ef[:, :width]) + dot(key_low, ef[:, width : 2 * width])
        )
        hat, rate = centred(second[...])
        sum_grad = norm_pull(hat, rate, vecs[6:7, :], new_grad)
        marks = [sum_grad, new_grad * hat, new_grad]
        low = sum_grad.astype(BF)
        pair_out[:, :width] = mid_low[...]
        pair_out[:, width:] = low
        mid_grad = sum_grad
        bias = []
        for h, (we, _, wr) in enumerate(shards(own, packed)):
            expand = dot_nt(low, wr) * slopes[h].astype(F32)
            bias.append(jnp.sum(expand, axis=0, keepdims=True))
            mid_grad = mid_grad + dot_nt(expand.astype(BF), we)
        hat, rate = centred(first[...])
        first_grad = norm_pull(hat, rate, vecs[3:4, :], mid_grad)
        sum_out[...] = first_grad
        marks += [mid_grad * hat, mid_grad, first_grad]
        marks = [jnp.sum(v, axis=0, keepdims=True) for v in marks]
        rows_low = (first_grad / counts[...]).astype(BF)
        pull_out[...] = dot_nt(rows_low, mt[...])
        third = dot_tn(summed[...], rows_low).astype(BF)
        head, hidden = pack.shape[0], third.shape[0]
        pay[:head, :] = pack[...]
        pay[head : head + hidden, :] = third
        pay[head + hidden :, :] = jnp.zeros((pay.shape[0] - head - hidden, width), BF)
        rows = jnp.concatenate(marks + [jnp.zeros((10, width), F32)], axis=0)
        at = lax.broadcasted_iota(jnp.int32, rows.shape, 0)
        share = bias[0].shape[1]
        for h, v in enumerate(bias):
            line = 6 + ((spot[2] ^ h) if tuned else h)
            if share < width:
                v = jnp.concatenate([v, jnp.zeros((1, width - share), F32)], axis=1)
            rows = jnp.where(at == line, v, rows)
        pay[head + hidden : head + hidden + 16, :] = rows.astype(BF)
        pay[head + hidden + 16 : head + hidden + 32, : edge_vec.shape[1]] = jnp.concatenate(
            [edge_vec[...], jnp.zeros_like(edge_vec)], axis=0
        ).astype(BF)
        if len(pay_out) == 1:
            pay_out[0][...] = pay[...]
        else:
            halved(spot, pay, *pay_out)

    def message_second(rows, fanout, step):
        span = step * rows

        def kernel(pull, act, slope2, second_out, weight_out, vec_out, marks):
            marks[...] = jnp.zeros_like(marks)

            def chunk(i, carry):
                at = pl.ds(aligned(i * span, span), span)
                second = slope2[at, :].astype(F32).reshape(step, rows, -1) * pull[...][None]
                marks[...] += jnp.sum(second, axis=0)
                second_out[at, :] = second.reshape(span, -1).astype(BF)
                return carry

            over(fanout // step, chunk)
            weight_out[...] = dot_tn(act[...], second_out[...]).astype(BF)
            vec_out[...] = jnp.zeros_like(vec_out)
            vec_out[0:1, :] = jnp.sum(marks[...], axis=0, keepdims=True)

        return kernel

    def message_first(rows, fanout, step):
        span = step * rows

        def kernel(
            arrived, low, edges, pick, second, slope1, ms, weight, vec,
            first_low_out, slot_out, node_out, pay, slots, node,
        ):
            width = low.shape[1]
            slots[...] = jnp.zeros_like(slots)
            node[...] = jnp.zeros_like(node)

            def chunk(i, carry):
                at = pl.ds(aligned(i * span, span), span)
                first = dot_nt(second[at, :], ms[...]) * slope1[at, :].astype(F32)
                node[...] += fold(first, rows)
                first = first.astype(BF)
                first_low_out[at, :] = first
                slots[...] += dot_tn(pick[at, :], first)
                return carry

            over(fanout // step, chunk)
            slot = slots[...].astype(BF)
            dealt(slot_out, slot)
            node_low = node[...].astype(BF)
            node_out[...] = node_low
            hidden, last = ms.shape[0], 2 * width + edges.shape[1]
            pay[:width, :] = dot_tn(low[...], node_low).astype(BF)
            pay[width : 2 * width, :] = dot_tn(joined(arrived), slot).astype(BF)
            pay[2 * width : last, :] = dot_tn(edges[...].astype(BF), first_low_out[...]).astype(BF)
            pay[last : last + hidden, :] = weight[...]
            pay[last + hidden :, :] = jnp.zeros((pay.shape[0] - last - hidden, hidden), BF)
            vecs = [jnp.sum(node[...], axis=0, keepdims=True), vec[0:1, :], jnp.zeros((14, hidden), F32)]
            pay[last + hidden : last + hidden + 16, :] = jnp.concatenate(vecs, axis=0).astype(BF)

        return kernel

    def feed_weights(pairs, we, web, wr, pay_out):
        n, share = we.shape
        mid = jnp.concatenate([v[:, :n] for v in pairs], axis=0)
        up = jnp.concatenate([v[:, n:] for v in pairs], axis=0)
        act, slope = smooth_slope(dot(mid, we[...]) + web[...])
        expand = dot_nt(up, wr[...]) * slope
        expand = dot_tn(mid, expand.astype(BF)).astype(BF)
        reduce = dot_tn(act.astype(BF), up).astype(BF)
        if len(pay_out) == 2:
            pay_out[0][...], pay_out[1][...] = expand, reduce
        else:
            pay_out[0][:n, :] = expand
            pay_out[0][n:, :] = reduce

    def node_end(returned, send, first_grad, node, mf, out):
        width = out.shape[1]
        if len(returned) == 2:
            mine, twin = returned
            n = mine.shape[0] // 4
            rows = [v[m * n : (m + 1) * n, :] for m in range(4) for v in (mine, twin)]
            back = jnp.concatenate(rows, axis=0)
        else:
            back = joined(returned)
        query_low = dot_tn(send[...], back).astype(BF)
        out[...] = (
            first_grad[...] + dot_nt(node[...], mf[:width]) + dot_nt(query_low, mf[width : 2 * width])
        )

    def edge_end(rows, fanout, step):
        span = step * rows

        def kernel(grad, first_low, mf, out):
            lower = mf[mf.shape[0] - grad.shape[1] :]

            def chunk(i, carry):
                at = pl.ds(aligned(i * span, span), span)
                out[at, :] = grad[at, :] + dot_nt(first_low[at, :], lower)
                return carry

            over(fanout // step, chunk)

        return kernel

    def split_chips(keep, got, outs):
        n = keep.shape[0] // len(outs)
        for m, out in enumerate(outs):
            at = slice(m * n, (m + 1) * n)
            out[:n, :] = (keep[at, :].astype(F32) + got[at, :].astype(F32)).astype(BF)

    def split_chips_more(keep, got, more, outs):
        split_chips(keep, got, outs)
        for v, out in zip(more, outs):
            out[out.shape[0] - v.shape[0] :, :] = v[...]

    def add_up(parts, out):
        n = out.shape[0]
        total = parts[0][:n, :].astype(F32)
        for v in parts[1:]:
            total = total + v[:n, :].astype(F32)
        out[...] = total.astype(BF)

    def add_up_more(parts, out, mine, twin):
        add_up(parts, out)
        n = mine.shape[0] // len(parts)
        for m, v in enumerate(parts):
            at, top = slice(m * n, (m + 1) * n), out.shape[0]
            mine[at, :] = v[top : top + n, :]
            twin[at, :] = v[top + n : top + 2 * n, :]

    def add_two(left, right, more, out):
        n = left.shape[0]
        out[:n, :] = (left[...].astype(F32) + right[...].astype(F32)).astype(BF)
        if more:
            out[n:, :] = more[0][...]

    def to_chips(parts):
        return [parts[0]] + [to_chip(parts[m], m) for m in (1, 2, 3)]

    def spread(own):
        parts = [own] + [to_chip(own, m) for m in (1, 2, 3)]
        return parts + [to_core(v) for v in parts]

    def laid_out(spot, parts, total):
        n = parts[0].shape[0]
        for k, v in enumerate(parts):
            at = (2 * (spot[1] ^ (k % 4)) + (spot[0] ^ (k // 4))) * n
            total[pl.ds(pl.multiple_of(at, n), n), :] = v[...].astype(total.dtype)

    def lay_pair(spot, stacks, total, skip=0):
        n = total.shape[0] // 8
        step = stacks[0].shape[0] // 4
        for k in range(8):
            at = (2 * (spot[1] ^ (k % 4)) + (spot[0] ^ (k // 4))) * n
            top = k % 4 * step + skip
            total[pl.ds(pl.multiple_of(at, n), n), :] = stacks[k // 4][top : top + n, :].astype(total.dtype)

    def stack_up(parts, out):
        n = parts[0].shape[0]
        for m, v in enumerate(parts):
            out[m * n : (m + 1) * n, :] = v[...]

    def unpack_early(
        spot, parts, first_out, second_out, third_out, message_out, vec_out, edge_vec_out, bias_out, feed_out,
        total, rest,
    ):
        if len(parts) == 1:
            total[...] = parts[0][...]
        else:
            lay_pair(spot, parts, total)
            lay_pair(spot, parts, rest, total.shape[0] // 8)
            n = rest.shape[0] // 2
            feed_out[0][...] = rest[:n, :]
            feed_out[1][...] = rest[n:, :]
        n, wide = second_out.shape[0], message_out.shape[1]
        first_out[:, :wide] = total[:n, :]
        first_out[:, wide : 2 * wide] = total[n : 2 * n, :]
        second_out[...] = total[2 * n : 3 * n, :n]
        third_out[...] = total[2 * n : 3 * n, 256 : 256 + n]
        at = 3 * n + n // 2
        first_out[: n // 2, 2 * wide :] = total[3 * n : at, :n]
        first_out[n // 2 :, 2 * wide :] = total[3 * n : at, 256 : 256 + n]
        hidden = message_out.shape[0]
        message_out[...] = total[at : at + hidden, :]
        for k, out in enumerate(vec_out):
            out[...] = total[at + hidden + k : at + hidden + k + 1, :]
        for k, out in enumerate(edge_vec_out):
            out[...] = total[at + hidden + 16 + k : at + hidden + 17 + k, :n]
        vecs = total[at + hidden : at + hidden + 16, :]
        line = lax.broadcasted_iota(jnp.int32, vecs.shape, 0) == 6 + spot[2]
        bias = jnp.sum(jnp.where(line, vecs, 0.0), axis=0, keepdims=True)
        bias_out[...] = bias[:, : bias_out.shape[1]]

    def unpack_late(spot, parts, first_out, second_out, vec_out, total):
        if len(parts) == 1:
            total[...] = parts[0][...]
        else:
            lay_pair(spot, parts, total)
        n, hidden = first_out.shape[0], second_out.shape[0]
        first_out[...] = total[:n, :]
        second_out[...] = total[n : n + hidden, :]
        for k, out in enumerate(vec_out):
            out[...] = total[n + hidden + k : n + hidden + k + 1, :]

    def join_pieces(parts, out):
        for m, v in enumerate(parts):
            n = v.shape[1]
            out[:, m * n : (m + 1) * n] = v[...]

    def body(
        nodes, edges, send_rows, neighbor_slots, neighbor_counts, mf, mfb, ms, msb, mt, mtb, mg, msh,
        expand_weight, expand_bias, reduce_weight, rb, fg, fsh, ef, efb, es, esb, et, etb, eg, esh,
        node_up, edge_up,
    ):
        rows, fanout, edge_width = edges.shape
        width, hidden = nodes.shape[1], ms.shape[0]
        share = expand_weight.shape[1]
        n_edges = rows * fanout
        step, half_step = fanout, fanout // 2 if fanout % 2 == 0 else fanout
        slots_each = send_rows.shape[2]
        buffer = n_res * slots_each
        row = lambda v: v.reshape(1, -1)
        if tuned:
            res, hid = lax.axis_index("res"), lax.axis_index("hid")
            spot = jnp.stack([res % 2, res // 2, hid, res]).astype(jnp.int32)
        else:
            spot = jnp.stack([0, 0, lax.axis_index("hid"), 0]).astype(jnp.int32)
        edges = edges.transpose(1, 0, 2).reshape(n_edges, edge_width)
        edge_up = edge_up.transpose(1, 0, 2).reshape(n_edges, edge_width)
        ef = ef.T
        bias = row(expand_bias)
        own = (expand_weight, bias, reduce_weight)
        one = struct((rows, width), BF)
        deal = [one] * 4 if tuned else [struct((buffer, width), BF)]
        n_piece = width // 8 * 9 // 4
        away, send, piece = call(
            prepare_send,
            [deal, struct((buffer, rows), BF), [struct((n_piece, width), BF)] if tuned else []],
            (send_rows[0], nodes, (expand_weight, reduce_weight, bias) if tuned else ()),
            "prepare_send",
            spot=spot,
            far=True,
        )
        arrived = exchange(away)
        pick, counts, vecs, edge_vecs = call(
            prepare_rest,
            [
                struct((n_edges, buffer), BF),
                struct((rows, 1), F32),
                struct((8, width), F32),
                struct((8, edge_width), F32),
            ],
            (
                neighbor_slots,
                row(neighbor_counts),
                [row(v) for v in (mfb, msb, mtb, mg, msh, rb, fg, fsh)],
                [row(v) for v in (efb, esb, etb, eg, esh)],
            ),
            "prepare_rest",
            spot=spot,
            after=away[:1],
            far=True,
        )
        edge_args = (ef, es, et, edge_vecs)
        if tuned:
            pieces = [to_hid(piece[0], m) for m in (1, 2, 3)]
            (piece,) = call(
                join_pieces, [struct((n_piece, 3 * width), BF)], (pieces,), "join_pieces", after=arrived
            )
            packed, first = [piece] + [to_chip(piece, m) for m in (1, 2, 3)], [piece]
        else:
            packed, first = [
                lax.all_gather(expand_weight, "hid"),
                lax.all_gather(expand_bias, "hid"),
                lax.all_gather(reduce_weight, "hid"),
            ], []
        (mid,) = call(
            pass_one(rows, fanout, step),
            [struct((rows, width), F32)],
            (arrived, nodes, edges, pick, counts, mf, ms, mt, vecs),
            "message_one",
            [pltpu.VMEM((rows, hidden), F32)],
            after=first,
        )
        if tuned:
            (packed,) = call(
                stack_up, [struct((4 * n_piece, 3 * width), BF)], (packed,), "stack_weights", after=[mid]
            )
            (packed,) = call(
                lay_pair,
                [struct((8 * n_piece, 3 * width), BF)],
                ([packed, to_core(packed)],),
                "lay_weights",
                spot=spot,
            )
            packed = [packed]
        feed_outs = [
            struct((n_hid, rows, share), BF),
            struct((rows, width), F32),
            struct((rows, width), F32),
            one,
            deal,
        ]
        _, _, state, low, away = call(
            feed_pass, feed_outs, (mid, own, packed, vecs, send), "feed_one"
        )
        arrived2, low2 = exchange(away), low
        edge_state, act, slope1, slope2, first, summed, mid, mid_low = call(
            pass_two(rows, fanout, step),
            [
                struct((n_edges, edge_width), F32),
                struct((n_edges, hidden), BF),
                struct((n_edges, hidden), BF),
                struct((n_edges, hidden), BF),
                struct((rows, width), F32),
                struct((rows, hidden), BF),
                struct((rows, width), F32),
                one,
            ],
            (arrived2, state, low2, edges, pick, counts, mf, ms, mt, vecs, *edge_args),
            "layer_two",
            [pltpu.VMEM((rows, hidden), F32)],
        )
        feed_outs[2] = jax.ShapeDtypeStruct((rows, width), F32)
        slopes, second, node_result, low3, away = call(
            feed_pass, feed_outs, (mid, own, packed, vecs, send), "feed_two"
        )
        arrived3 = exchange(away)
        wide = lambda dtype: struct((n_edges, edge_width), dtype)
        edge_result, edge_grad, act1, act2, top, mid, bottom, slot, node, edge_vec = call(
            edge_turn(rows, fanout, half_step),
            [
                jax.ShapeDtypeStruct((n_edges, edge_width), F32),
                wide(F32), wide(BF), wide(BF), wide(BF), wide(BF), wide(BF),
                [struct((buffer // len(deal), edge_width), BF)] * len(deal),
                struct((rows, edge_width), BF),
                struct((8, edge_width), F32),
            ],
            (arrived3, low3, edge_state, edge_up, pick, *edge_args),
            "edge_turn",
            [
                pltpu.VMEM((buffer, edge_width), F32),
                pltpu.VMEM((rows, edge_width), F32),
                pltpu.VMEM((4, 8, edge_width), F32),
            ],
        )
        returned = exchange(slot)
        head = 3 * edge_width + edge_width // 2
        (pack,) = call(
            edge_weights,
            [struct((head, width), BF)],
            (arrived3, low3, edge_state, act1, act2, top, mid, bottom, slot, node),
            "edge_weights",
        )
        sized = lambda n: -(-n // 128) * 128
        n_early, n_late, n_feed = sized(head + hidden + 32), sized(mf.shape[0] + hidden + 16), 2 * width
        cut = lambda n: [struct((n // 2, width), BF)] * 2 if tuned else [struct((n, width), BF)]
        pair, first_grad, pull, early = call(
            node_turn,
            [struct((rows, 2 * width), BF), struct((rows, width), F32), struct((rows, hidden), F32), cut(n_early)],
            (
                returned, node_up, node, send, second, slopes, first, counts, summed, ef, mt, vecs,
                own, packed, pack, edge_vec, mid_low,
            ),
            "node_turn",
            [pltpu.VMEM((n_early, width), BF)],
            spot=spot,
        )
        eighth = lambda n: struct((n // 8, width), BF)
        second_low, second_weight, message_vec = call(
            message_second(rows, fanout, step),
            [struct((n_edges, hidden), BF), struct((hidden, hidden), BF), struct((8, hidden), F32)],
            (pull, act, slope2),
            "message_second",
            [pltpu.VMEM((rows, hidden), F32)],
        )
        feed_outs = [
            [struct((n_feed, width), BF)] if tuned else [struct((width, share), BF), struct((share, width), BF)]
        ]

        def feed_grads_of(pairs, after):
            return call(
                feed_weights, feed_outs, (pairs, expand_weight, bias, reduce_weight), "feed_weights", after=after
            )

        first = []
        if tuned:
            (pair,) = call(
                stack_up, [struct((2 * rows, 2 * width), BF)], ([pair, to_hid(pair, 1)],), "pair_stack",
                after=[second_weight],
            )
            (early,) = call(
                split_chips, [[eighth(n_early)] * 4], (early[0], to_core(early[1])), "early_chips",
                after=[pair],
            )
            first = early[:1]
            early = to_chips(early)
        else:
            early = lax.psum(early[0].astype(F32), ("res", "hid"))
        first_low, slot, node, late = call(
            message_first(rows, fanout, step),
            [
                struct((n_edges, hidden), BF),
                [struct((buffer // len(deal), hidden), BF)] * len(deal),
                struct((rows, hidden), BF),
                struct((n_late, hidden), BF),
            ],
            (arrived2, low2, edge_state, pick, second_low, slope1, ms, second_weight, message_vec),
            "message_first",
            [
                pltpu.VMEM((buffer, hidden), F32),
                pltpu.VMEM((rows, hidden), F32),
            ],
            after=first,
        )
        final = Final
        if tuned:
            (early,) = call(add_up, [eighth(n_early)], (early,), "early_plane", after=[node])
            ((feed_pay,),) = feed_grads_of([pair, to_hid(pair, 2)], [early])
            keep, send_late = call(halved, cut(n_late), (late,), "late_pay", spot=spot, after=[feed_pay])
            (late,) = call(
                split_chips_more,
                [[struct((n_late // 8 + rows, width), BF)] * 4],
                (keep, to_core(send_late), slot),
                "late_chips",
            )
            last = late[0]
            late = to_chips(late)
            keep, send_feed = call(halved, cut(n_feed), [feed_pay], "feed_pay", spot=spot, after=[last])
            (early,) = call(
                add_two, [eighth(n_early)], (early, to_hid(early, 1), []), "early_line", after=[keep]
            )
            (feed_parts,) = call(
                split_chips, [[eighth(n_feed)] * 4], (keep, to_core(send_feed)), "feed_chips", after=[early]
            )
            last = feed_parts[0]
            half = struct((rows * 2, width), BF)
            late, mine, twin = call(
                add_up_more, [eighth(n_late), half, half], (late,), "late_plane", after=[last]
            )
            feed_parts = to_chips(feed_parts)
            (late,) = call(add_two, [eighth(n_late)], (late, to_hid(late, 1), []), "late_line")
            (feed_own,) = call(add_up, [eighth(n_feed)], (feed_parts,), "feed_plane", after=[late])
            (early,) = call(
                add_two,
                [struct(((n_early + n_feed) // 8, width), BF)],
                (early, to_hid(early, 2), [feed_own]),
                "early_line",
            )
            last = early
            early = [early] + [to_chip(early, m) for m in (1, 2, 3)]
            edge_gradient, last = call(
                edge_end(rows, fanout, step),
                [final(n_edges, edge_width)],
                (edge_grad, first_low, mf),
                "edge_end",
                after=[last],
                token=True,
            )
            returned = [mine, to_core(twin)]
            node_gradient, last = call(
                node_end,
                [final(rows, width)],
                (returned, send, first_grad, node, mf),
                "node_end",
                after=[last],
                token=True,
            )
            (late,) = call(
                add_two, [eighth(n_late)], (late, to_hid(late, 2), []), "late_line", after=[last]
            )
            (early,) = call(
                stack_up,
                [struct(((n_early + n_feed) // 2, width), BF)],
                (early,),
                "early_stack",
                after=[late],
            )
            early = [early, to_core(early)]
            late = [late] + [to_chip(late, m) for m in (1, 2, 3)]
        else:
            late = [lax.psum(late.astype(F32), ("res", "hid"))]
            early = [early]
            pairs = [lax.all_gather(pair, "hid", axis=0, tiled=True)]
            (feed_pay,) = feed_grads_of(pairs, [node])
            returned = exchange(slot)
            (edge_gradient,) = call(
                edge_end(rows, fanout, step), [final(n_edges, edge_width)], (edge_grad, first_low, mf), "edge_end"
            )
            (node_gradient,) = call(
                node_end, [final(rows, width)], (returned, send, first_grad, node, mf), "node_end"
            )
        (
            edge_first_grad, edge_second_grad, edge_third_grad, third_grad, vec, edge_vecs, expand_bias_grad,
            feed_grads, last,
        ) = call(
            unpack_early,
            [
                final(edge_width, ef.shape[1]), final(edge_width, edge_width), final(edge_width, edge_width),
                final(hidden, width), [final(1, width)] * 6, [final(1, edge_width)] * 5, final(1, share),
                [final(width, share), final(share, width)] if tuned else [],
            ],
            (early,),
            "unpack_early",
            [pltpu.VMEM((n_early, width), F32), pltpu.VMEM((n_feed, width), F32)],
            limit=16,
            spot=spot,
            token=True,
        )
        if tuned:
            (late,) = call(
                stack_up, [struct((n_late // 2, width), BF)], (late,), "late_stack", after=[last]
            )
            late = [late, to_core(late)]
        first_weight_grad, second_weight_grad, message_vec = call(
            unpack_late,
            [final(*mf.shape), final(hidden, hidden), [final(1, hidden)] * 2],
            (late,),
            "unpack_late",
            [pltpu.VMEM((n_late, width), F32)],
            limit=16,
            spot=spot,
        )
        if tuned:
            expand_grad, reduce_grad = feed_grads
        else:
            expand_grad, reduce_grad = [lax.psum(v.astype(F32), "res") for v in feed_pay]
        vec, edge_vecs, message_vec = [[v[0] for v in group] for group in (vec, edge_vecs, message_vec)]

        back = lambda v: v.reshape(fanout, rows, edge_width).transpose(1, 0, 2)
        return (
            node_result,
            back(edge_result),
            node_gradient,
            back(edge_gradient),
            first_weight_grad,
            message_vec[0],
            second_weight_grad,
            message_vec[1],
            third_grad,
            vec[5],
            vec[3],
            vec[4],
            expand_grad,
            expand_bias_grad[0],
            reduce_grad,
            vec[0],
            vec[1],
            vec[2],
            edge_first_grad.T,
            edge_vecs[4],
            edge_second_grad,
            edge_vecs[3],
            edge_third_grad,
            edge_vecs[2],
            edge_vecs[0],
            edge_vecs[1],
        )

    both = ("res", "hid")
    rows2, rows3 = P(both, None), P(both, None, None)
    placed = (
        rows2, rows3, rows3, rows2, P(both),
        P(), P(), P(), P(), P(), P(), P(), P(),
        P(None, "hid"), P("hid"), P("hid", None),
        P(), P(), P(), P(), P(), P(), P(), P(), P(), P(), P(),
        rows2, rows3,
    )
    given = (
        rows2, rows3, rows2, rows3,
        P(), P(), P(), P(), P(), P(), P(), P(),
        P(None, "hid"), P("hid"), P("hid", None),
        P(), P(), P(), P(), P(), P(), P(), P(), P(), P(), P(),
    )
    return jax.shard_map(body, mesh=mesh, in_specs=placed, out_specs=given, check_vma=False)
```

time: 242 us -> 178 us (0.74)
  starting transfers between devices: 113 us -> 71.4 us
  local copies, waits for them, and re-layouts: 22.8 us -> 1.27 us
  waiting for transfers between devices: 35.9 us -> 52.6 us
  Pallas kernels: 62.9 us -> 50.8 us
  other arithmetic: 3.46 us -> 0.08 us
    ppermute x47 -> x23, starting transfers between devices: 51.5 us -> 29.8 us  [to_core(): return lax.ppermute(v, 'res', pair)]
    unnamed x188 -> x28, local copies, waits for them, and re-layouts: 19.5 us -> 1.27 us
    pallas_call x23 -> x34, Pallas kernels: 62.9 us -> 50.8 us  [call(): pl.pallas_call(run, out_shape=jax.tree.unflatten(out_tree, shapes), in_sp...]
    ppermute x21 -> x9, starting transfers between devices: 22.3 us -> 12.4 us  [to_hid(): return lax.ppermute(v, 'hid', [(i, i ^ m) for i in range(n_hid)])]
    ppermute x42 -> x30, starting transfers between devices: 38.7 us -> 29.1 us  [to_chip(): return lax.ppermute(v, 'res', [(i, i ^ 2 * m) for i in range(n_res)])]
    ppermute x42 -> x30, waiting for transfers between devices: 19.5 us -> 27.4 us  [to_chip(): return lax.ppermute(v, 'res', [(i, i ^ 2 * m) for i in range(n_res)])]
    ppermute x47 -> x23, waiting for transfers between devices: 3.23 us -> 10.5 us  [to_core(): return lax.ppermute(v, 'res', pair)]
    ppermute x21 -> x9, waiting for transfers between devices: 13.1 us -> 14.8 us  [to_hid(): return lax.ppermute(v, 'hid', [(i, i ^ m) for i in range(n_hid)])]
  transfers between devices with their start and end apart: 110 -> 62, of which waited for: 28 -> 24; matrix products, arithmetic and copies ran while one was open for 2% -> 0% of each run, Pallas kernels for 9% -> 10%
where the time goes in v2:
time: 178 us
  starting transfers between devices  71.4 us (40%)
  waiting for transfers between devices  52.6 us (30%)
  Pallas kernels  50.8 us (29%)
    pallas_call x34, Pallas kernels, call(): pl.pallas_call(run, out_shape=jax.tree.unflatten(out_tree, shapes), in_sp...  50.8 us
    ppermute x23, starting transfers between devices, to_core(): return lax.ppermute(v, 'res', pair)  29.8 us
    ppermute x30, starting transfers between devices, to_chip(): return lax.ppermute(v, 'res', [(i, i ^ 2 * m) for i in range(n_res)])  29.1 us
    ppermute x30, waiting for transfers between devices, to_chip(): return lax.ppermute(v, 'res', [(i, i ^ 2 * m) for i in range(n_res)])  27.4 us
    ppermute x9, waiting for transfers between devices, to_hid(): return lax.ppermute(v, 'hid', [(i, i ^ m) for i in range(n_hid)])  14.8 us
    ppermute x9, starting transfers between devices, to_hid(): return lax.ppermute(v, 'hid', [(i, i ^ m) for i in range(n_hid)])  12.4 us
    ppermute x23, waiting for transfers between devices, to_core(): return lax.ppermute(v, 'res', pair)  10.5 us
  transfers between devices with their start and end apart: 62, of which 24 were waited for; matrix products, arithmetic and copies ran while one was open for 0% of the time, Pallas kernels for 10%

profile of v2, /device:TPU:1, one launch (start us, length us, event | category | flops | bytes accessed | tf_op | source)
XLA Modules:
  0.0 177.6 jit_solution(10380019657807157915)
XLA Ops:
  0.8 2.1 %prepare_send.1 = (bf16[32,512]{1,0:T(8,128)(2,1)S(1)}, bf16[32,512]{1,0:T(8,128)(2,1)S(1)}, bf16[32,512]{1,0:T(8,128)(2,1)S(1)}, bf16[32,512]{1,0:T(8,128)(2,1)...) custom-call(s32[4]{0:T(128)S(1)} %pad_add_fusion.refs_0_, s32[8,16]{1,0:T(8,128)} %bitcast.59, ...), custom_call_target="tpu_custom_call" | custom-call | tf_op jit(solution)/shard_map/prepare_send/pallas_call | solution.py:136
  2.9 2.2 %collective-permute-start.7 = (bf16[144,512]{1,0:T(8,128)(2,1)S(1)}, bf16[144,512]{1,0:T(8,128)(2,1)S(1)}, u32[]{:S(2)}, u32[]{:S(2)}) collective-permute-start(bf16[144,512]{1,0:T(8,128)(2,1)S(1)} %get-tuple-element.139), channel_id=1, source_target_pairs={{0,1},{1,0},{2,3},{3,2},{4,5},{5,4},{6,7},{7,6},{8,9},{9,8},{10,11... | collective-permute-start | bytes 442376 | tf_op jit(solution)/shard_map/ppermute | solution.py:223
  5.1 2.3 %collective-permute-start.8 = (bf16[144,512]{1,0:T(8,128)(2,1)S(1)}, bf16[144,512]{1,0:T(8,128)(2,1)S(1)}, u32[]{:S(2)}, u32[]{:S(2)}) collective-permute-start(bf16[144,512]{1,0:T(8,128)(2,1)S(1)} %get-tuple-element.139), channel_id=1, source_target_pairs={{0,2},{1,3},{2,0},{3,1},{4,6},{5,7},{6,4},{7,5},{8,10},{9,11},{10,... | collective-permute-start | bytes 442376 | tf_op jit(solution)/shard_map/ppermute | solution.py:223
  8.7 1.4 collective-permute-start
  10.1 1.2 collective-permute-start.1
  11.7 2.4 %collective-permute-start.2 = (bf16[32,512]{1,0:T(8,128)(2,1)S(1)}, bf16[32,512]{1,0:T(8,128)(2,1)S(1)}, u32[]{:S(2)}, u32[]{:S(2)}) collective-permute-start(bf16[32,512]{1,0:T(8,128)(2,1)S(1)} %get-tuple-element.135), channel_id=1, source_target_pairs={{0,24},{4,28},{8,16},{12,20},{16,8},{20,12},{24,0},{28,4},{1,25},{... | collective-permute-start | bytes 98312 | tf_op jit(solution)/shard_map/ppermute | solution.py:217
  15.7 1.7 collective-permute-start.5
  18.6 1.5 collective-permute-start.10
  20.1 1.2 collective-permute-start.11
  21.4 2.0 %prepare_rest.1 = (bf16[1920,128]{1,0:T(8,128)(2,1)S(1)}, f32[32,1]{1,0:T(8,128)S(1)}, f32[8,512]{1,0:T(8,128)S(1)}, f32[8,192]{1,0:T(8,128)S(1)}) custom-call(s32[4]{0:T(128)S(1)} %pad_add_fusion.refs_0_, s32[32,60]{1,0:T(8,128)} %refs_1_.3, s32[1,32]{1,0:T(1,128)} %bitcast.73, f32[1,512]{1,0:T(1,128)} %bitcast.60, f32[1,512]{1,0:T(1,128)} %bitcast.61, ...), custom_call_target="tpu_custom_call" | custom-call | tf_op jit(solution)/shard_map/prepare_rest/pallas_call | solution.py:136
  24.6 4.3 %message_one.1.refs_1_.refs_0_ = f32[32,512]{1,0:T(8,128)S(1)} custom-call(bf16[32,512]{1,0:T(8,128)(2,1)S(1)} %get-tuple-element.132.refs_5_.refs_1_.refs_0__0_, bf16[32,512]{1,0:T(8,128)(2,1)S(1)} %collective-permute-done.refs_2_.refs_0__1_, bf16[32,512]{1,0:T(8,128)(2,1)S(1)} %collective-permute-done.1.refs_3_.refs_0__2_, ...), custom_call_target="tpu_custom_call" | custom-call | tf_op jit(solution)/shard_map/message_one/pallas_call | solution.py:136
  29.0 1.3 collective-permute-done.11.refs_0__2_
  30.3 9.5 %collective-permute-done.12.refs_0__3_ = bf16[144,1536]{1,0:T(8,128)(2,1)S(1)} collective-permute-done((bf16[144,1536]{1,0:T(8,128)(2,1)S(1)}, bf16[144,1536]{1,0:T(8,128)(2,1)S(1)}, u32[]{:S(2)}, u32[]{:S(2)}) %collective-permute-start.12) | collective-permute-done | bytes 442400 | tf_op jit(solution)/shard_map/ppermute | solution.py:217
  40.0 2.4 %collective-permute-start.13 = (bf16[576,1536]{1,0:T(8,128)(2,1)S(1)}, bf16[576,1536]{1,0:T(8,128)(2,1)S(1)}, u32[]{:S(2)}, u32[]{:S(2)}) collective-permute-start(bf16[576,1536]{1,0:T(8,128)(2,1)S(1)} %stack_weights.1.refs_1__0_), channel_id=1, source_target_pairs={{0,4},{4,0},{8,12},{12,8},{16,20},{20,16},{24,28},{28,24},{1,5},{5... | collective-permute-start | bytes 5308424 | tf_op jit(solution)/shard_map/ppermute | solution.py:220
  42.4 3.3 %collective-permute-done.13.refs_1__1_ = bf16[576,1536]{1,0:T(8,128)(2,1)S(1)} collective-permute-done((bf16[576,1536]{1,0:T(8,128)(2,1)S(1)}, bf16[576,1536]{1,0:T(8,128)(2,1)S(1)}, u32[]{:S(2)}, u32[]{:S(2)}) %collective-permute-start.13) | collective-permute-done | bytes 1769504 | tf_op jit(solution)/shard_map/ppermute | solution.py:220
  46.6 1.8 %feed_one.1 = (bf16[4,32,512]{2,1,0:T(8,128)(2,1)}, f32[32,512]{1,0:T(8,128)}, f32[32,512]{1,0:T(8,128)S(1)}, bf16[32,512]{1,0:T(8,128)(2,1)S(1)}, bf16[32,512]{...) custom-call(f32[32,512]{1,0:T(8,128)S(1)} %message_one.1.refs_1_.refs_0, ...), custom_call_target="tpu_custom_call" | custom-call | tf_op jit(solution)/shard_map/feed_one/pallas_call | solution.py:136
  52.7 1.2 collective-permute-start.19
  54.0 1.7 collective-permute-start.20
  56.5 10.2 %layer_two.1 = (f32[1920,192]{1,0:T(8,128)S(1)}, bf16[1920,512]{1,0:T(8,128)(2,1)S(1)}, bf16[1920,512]{1,0:T(8,128)(2,1)S(1)}, bf16[1920,512]{1,0:T(8,128)(2,1)S...) custom-call(bf16[32,512]{1,0:T(8,128)(2,1)S(1)} %get-tuple-element.1, ...), custom_call_target="tpu_custom_call" | custom-call | tf_op jit(solution)/shard_map/layer_two/pallas_call | solution.py:136
  66.8 2.0 %feed_two.1 = (bf16[4,32,512]{2,1,0:T(8,128)(2,1)S(1)}, f32[32,512]{1,0:T(8,128)S(1)}, f32[32,512]{1,0:T(8,128)}, bf16[32,512]{1,0:T(8,128)(2,1)S(1)}, bf16[32,5...) custom-call(f32[32,512]{1,0:T(8,128)S(1)} %get-tuple-element.148.ref, ...), custom_call_target="tpu_custom_call" | custom-call | tf_op jit(solution)/shard_map/feed_two/pallas_call | solution.py:136
  73.0 1.8 %collective-permute-start.26 = (bf16[32,512]{1,0:T(8,128)(2,1)S(1)}, bf16[32,512]{1,0:T(8,128)(2,1)S(1)}, u32[]{:S(2)}, u32[]{:S(2)}) collective-permute-start(bf16[32,512]{1,0:T(8,128)(2,1)S(1)} %collective-permute-done.22.refs_0__2_), channel_id=1, source_target_pairs={{0,4},{4,0},{8,12},{12,8},{16,20},{20,16},{24,28},{28,24},{1,5},{5... | collective-permute-start | bytes 98312 | tf_op jit(solution)/shard_map/ppermute | solution.py:220
  76.8 7.1 %edge_turn.1 = (f32[1920,192]{1,0:T(8,128)}, f32[1920,192]{1,0:T(8,128)S(1)}, bf16[1920,192]{1,0:T(8,128)(2,1)S(1)}, bf16[1920,192]{1,0:T(8,128)(2,1)S(1)}, bf16...) custom-call(bf16[32,512]{1,0:T(8,128)(2,1)S(1)} %get-tuple-element.1, ...), custom_call_target="tpu_custom_call" | custom-call | tf_op jit(solution)/shard_map/edge_turn/pallas_call | solution.py:136
  89.2 1.7 collective-permute-start.34
  92.2 3.0 %node_turn.1 = (bf16[32,1024]{1,0:T(8,128)(2,1)S(1)}, f32[32,512]{1,0:T(8,128)S(1)}, f32[32,512]{1,0:T(8,128)S(1)}, bf16[640,512]{1,0:T(8,128)(2,1)S(1)}, bf16[640,512]{1,0:T(8,128)(2,1)S(1)}) custom-call(s32[4]{0:T(128)S(1)} %pad_add_fusion.refs_0_, bf16[32,192]{1,0:T(8,128)(2,1)S(1)} %get-tuple-element.157.refs_8__0_.refs_1__0_, ...), custom_call_target="tpu_custom_call" | custom-call | tf_op jit(solution)/shard_map/node_turn/pallas_call | solution.py:136
  95.3 1.5 collective-permute-start.36
  96.7 1.3 message_second.1
  98.6 1.3 collective-permute-start.38
  101.3 2.6 %collective-permute-start.37 = (bf16[64,1024]{1,0:T(8,128)(2,1)S(1)}, bf16[64,1024]{1,0:T(8,128)(2,1)S(1)}, u32[]{:S(2)}, u32[]{:S(2)}) collective-permute-start(bf16[64,1024]{1,0:T(8,128)(2,1)S(1)} %pair_stack.1.refs_2_.refs_0__0_), channel_id=1, source_target_pairs={{0,2},{1,3},{2,0},{3,1},{4,6},{5,7},{6,4},{7,5},{8,10},{9,11},{10,... | collective-permute-start | bytes 393224 | tf_op jit(solution)/shard_map/ppermute | solution.py:223
  104.0 2.4 %message_first.1 = (bf16[1920,512]{1,0:T(8,128)(2,1)S(1)}, bf16[32,512]{1,0:T(8,128)(2,1)S(1)}, bf16[32,512]{1,0:T(8,128)(2,1)S(1)}, bf16[32,512]{1,0:T(8,128)(2...) custom-call(bf16[32,512]{1,0:T(8,128)(2,1)S(1)} %get-tuple-element.141.refs_0__0_, ...), custom_call_target="tpu_custom_call" | custom-call | tf_op jit(solution)/shard_map/message_first/pallas_call | solution.py:136
  106.7 1.4 collective-permute-done.37.refs_0__1_
  109.7 3.1 %collective-permute-start.41 = (bf16[896,512]{1,0:T(8,128)(2,1)S(1)}, bf16[896,512]{1,0:T(8,128)(2,1)S(1)}, u32[]{:S(2)}, u32[]{:S(2)}) collective-permute-start(bf16[896,512]{1,0:T(8,128)(2,1)S(1)} %get-tuple-element.190), channel_id=1, source_target_pairs={{0,4},{4,0},{8,12},{12,8},{16,20},{20,16},{24,28},{28,24},{1,5},{5... | collective-permute-start | bytes 2752520 | tf_op jit(solution)/shard_map/ppermute | solution.py:220
  112.8 2.1 %collective-permute-done.41.refs_1_ = bf16[896,512]{1,0:T(8,128)(2,1)S(1)} collective-permute-done((bf16[896,512]{1,0:T(8,128)(2,1)S(1)}, bf16[896,512]{1,0:T(8,128)(2,1)S(1)}, u32[]{:S(2)}, u32[]{:S(2)}) %collective-permute-start.41) | collective-permute-done | bytes 917536 | tf_op jit(solution)/shard_map/ppermute | solution.py:220
  119.2 4.4 %collective-permute-done.46.refs_1_ = bf16[160,512]{1,0:T(8,128)(2,1)S(1)} collective-permute-done((bf16[160,512]{1,0:T(8,128)(2,1)S(1)}, bf16[160,512]{1,0:T(8,128)(2,1)S(1)}, u32[]{:S(2)}, u32[]{:S(2)}) %collective-permute-start.46) | collective-permute-done | bytes 163872 | tf_op jit(solution)/shard_map/ppermute | solution.py:223
  125.1 5.2 %collective-permute-done.44.refs_0__3_ = bf16[256,512]{1,0:T(8,128)(2,1)S(1)} collective-permute-done((bf16[256,512]{1,0:T(8,128)(2,1)S(1)}, bf16[256,512]{1,0:T(8,128)(2,1)S(1)}, u32[]{:S(2)}, u32[]{:S(2)}) %collective-permute-start.44) | collective-permute-done | bytes 262176 | tf_op jit(solution)/shard_map/ppermute | solution.py:217
  130.8 3.1 %collective-permute-start.48 = (bf16[160,512]{1,0:T(8,128)(2,1)S(1)}, bf16[160,512]{1,0:T(8,128)(2,1)S(1)}, u32[]{:S(2)}, u32[]{:S(2)}) collective-permute-start(bf16[160,512]{1,0:T(8,128)(2,1)S(1)} %early_line.2.refs_2_.refs_0_), channel_id=1, source_target_pairs={{0,2},{1,3},{2,0},{3,1},{4,6},{5,7},{6,4},{7,5},{8,10},{9,11},{10,... | collective-permute-start | bytes 491528 | tf_op jit(solution)/shard_map/ppermute | solution.py:223
  136.5 3.0 %collective-permute-done.52.refs_1_ = bf16[224,512]{1,0:T(8,128)(2,1)S(1)} collective-permute-done((bf16[224,512]{1,0:T(8,128)(2,1)S(1)}, bf16[224,512]{1,0:T(8,128)(2,1)S(1)}, u32[]{:S(2)}, u32[]{:S(2)}) %collective-permute-start.52) | collective-permute-done | bytes 229408 | tf_op jit(solution)/shard_map/ppermute | solution.py:223
  139.6 2.3 %collective-permute-done.51.refs_0__3_ = bf16[128,512]{1,0:T(8,128)(2,1)S(1)} collective-permute-done((bf16[128,512]{1,0:T(8,128)(2,1)S(1)}, bf16[128,512]{1,0:T(8,128)(2,1)S(1)}, u32[]{:S(2)}, u32[]{:S(2)}) %collective-permute-start.51) | collective-permute-done | bytes 131104 | tf_op jit(solution)/shard_map/ppermute | solution.py:217
  143.0 1.7 collective-permute-start.59
  144.7 3.1 %collective-permute-start.47 = (bf16[64,512]{1,0:T(8,128)(2,1)S(1)}, bf16[64,512]{1,0:T(8,128)(2,1)S(1)}, u32[]{:S(2)}, u32[]{:S(2)}) collective-permute-start(bf16[64,512]{1,0:T(8,128)(2,1)S(1)} %get-tuple-element.203), channel_id=1, source_target_pairs={{0,4},{4,0},{8,12},{12,8},{16,20},{20,16},{24,28},{28,24},{1,5},{5... | collective-permute-start | bytes 196616 | tf_op jit(solution)/shard_map/ppermute | solution.py:220
  147.8 2.0 %edge_end.1 = (f32[1920,192]{1,0:T(8,128)}, f32[8,128]{1,0:T(8,128)S(1)}) custom-call(f32[1920,192]{1,0:T(8,128)S(1)} %get-tuple-element.205.refs_0_, bf16[1920,512]{1,0:T(8,128)(2,1)S(1)} %get-tuple-element.206.refs_1_, bf16[1216,512]{1,0:T(8,128)(2,1)S(1)} %copy-done, bf16[288,512]{1,0:T(8,128)(2,1)S(1)} %early_line.3.refs_3_.refs_0__0_), custom_call_target="tpu_custom_call" | custom-call | tf_op jit(solution)/shard_map/edge_end/pallas_call | solution.py:136
  150.9 5.6 %collective-permute-done.53.refs_1_ = bf16[224,512]{1,0:T(8,128)(2,1)S(1)} collective-permute-done((bf16[224,512]{1,0:T(8,128)(2,1)S(1)}, bf16[224,512]{1,0:T(8,128)(2,1)S(1)}, u32[]{:S(2)}, u32[]{:S(2)}) %collective-permute-start.53) | collective-permute-done | bytes 229408 | tf_op jit(solution)/shard_map/ppermute | solution.py:223
  156.7 1.7 collective-permute-start.60
  159.8 1.3 collective-permute-start.56
  161.0 3.4 %unpack_early.1 = (f32[192,1216]{1,0:T(8,128)}, f32[192,192]{1,0:T(8,128)}, f32[192,192]{1,0:T(8,128)}, f32[512,512]{1,0:T(8,128)}, f32[1,512]{1,0:T(1,128)}, /*...) custom-call(s32[4]{0:T(128)S(1)} %pad_add_fusion.refs_0_, ...), custom_call_target="tpu_custom_call" | custom-call | tf_op jit(solution)/shard_map/unpack_early/pallas_call | solution.py:136
  166.5 4.5 %collective-permute-done.56.refs_0__3_ = bf16[224,512]{1,0:T(8,128)(2,1)S(1)} collective-permute-done((bf16[224,512]{1,0:T(8,128)(2,1)S(1)}, bf16[224,512]{1,0:T(8,128)(2,1)S(1)}, u32[]{:S(2)}, u32[]{:S(2)}) %collective-permute-start.56) | collective-permute-done | bytes 229408 | tf_op jit(solution)/shard_map/ppermute | solution.py:217
  171.1 1.4 collective-permute-start.61
  172.5 2.1 %collective-permute-done.61.refs_1__1_ = bf16[896,512]{1,0:T(8,128)(2,1)S(1)} collective-permute-done((bf16[896,512]{1,0:T(8,128)(2,1)S(1)}, bf16[896,512]{1,0:T(8,128)(2,1)S(1)}, u32[]{:S(2)}, u32[]{:S(2)}) %collective-permute-start.61) | collective-permute-done | bytes 917536 | tf_op jit(solution)/shard_map/ppermute | solution.py:220
  174.6 2.8 %unpack_late.1 = (f32[1216,512]{1,0:T(8,128)}, f32[512,512]{1,0:T(8,128)}, f32[1,512]{1,0:T(1,128)}, f32[1,512]{1,0:T(1,128)}) custom-call(s32[4]{0:T(128)S(1)} %pad_add_fusion.refs_0_, bf16[896,512]{1,0:T(8,128)(2,1)S(1)} %late_stack.1.refs_1__0_, bf16[896,512]{1,0:T(8,128)(2,1)S(1)} %collective-permute-done.61.refs_1__1_), custom_call_target="tpu_custom_call" | custom-call | tf_op jit(solution)/shard_map/unpack_late/pallas_call | solution.py:136
  (139 shorter events, 43.4 us)
Async XLA Ops:
  2.9 15.7 %collective-permute-start.7 = (bf16[144,512]{1,0:T(8,128)(2,1)S(1)}, bf16[144,512]{1,0:T(8,128)(2,1)S(1)}, u32[]{:S(2)}, u32[]{:S(2)}) collective-permute-start(bf16[144,512]{1,0:T(8,128)(2,1)S(1)} %get-tuple-element.139), channel_id=1, source_target_pairs={{0,1},{1,0},{2,3},{3,2},{4,5},{5,4},{6,7},{7,6},{8,9},{9,8},{10,11... | collective-permute-start | bytes 442376 | tf_op jit(solution)/shard_map/ppermute | solution.py:223
  5.1 13.5 %collective-permute-start.8 = (bf16[144,512]{1,0:T(8,128)(2,1)S(1)}, bf16[144,512]{1,0:T(8,128)(2,1)S(1)}, u32[]{:S(2)}, u32[]{:S(2)}) collective-permute-start(bf16[144,512]{1,0:T(8,128)(2,1)S(1)} %get-tuple-element.139), channel_id=1, source_target_pairs={{0,2},{1,3},{2,0},{3,1},{4,6},{5,7},{6,4},{7,5},{8,10},{9,11},{10,... | collective-permute-start | bytes 442376 | tf_op jit(solution)/shard_map/ppermute | solution.py:223
  7.4 11.2 %collective-permute-start.9 = (bf16[144,512]{1,0:T(8,128)(2,1)S(1)}, bf16[144,512]{1,0:T(8,128)(2,1)S(1)}, u32[]{:S(2)}, u32[]{:S(2)}) collective-permute-start(bf16[144,512]{1,0:T(8,128)(2,1)S(1)} %get-tuple-element.139), channel_id=1, source_target_pairs={{0,3},{1,2},{2,1},{3,0},{4,7},{5,6},{6,5},{7,4},{8,11},{9,10},{10,... | collective-permute-start | bytes 442376 | tf_op jit(solution)/shard_map/ppermute | solution.py:223
  10.1 4.0 %collective-permute-start.1 = (bf16[32,512]{1,0:T(8,128)(2,1)S(1)}, bf16[32,512]{1,0:T(8,128)(2,1)S(1)}, u32[]{:S(2)}, u32[]{:S(2)}) collective-permute-start(bf16[32,512]{1,0:T(8,128)(2,1)S(1)} %get-tuple-element.134), channel_id=1, source_target_pairs={{0,16},{4,20},{8,24},{12,28},{16,0},{20,4},{24,8},{28,12},{1,17},{... | collective-permute-start | bytes 98312 | tf_op jit(solution)/shard_map/ppermute | solution.py:217
  11.7 4.0 %collective-permute-start.2 = (bf16[32,512]{1,0:T(8,128)(2,1)S(1)}, bf16[32,512]{1,0:T(8,128)(2,1)S(1)}, u32[]{:S(2)}, u32[]{:S(2)}) collective-permute-start(bf16[32,512]{1,0:T(8,128)(2,1)S(1)} %get-tuple-element.135), channel_id=1, source_target_pairs={{0,24},{4,28},{8,16},{12,20},{16,8},{20,12},{24,0},{28,4},{1,25},{... | collective-permute-start | bytes 98312 | tf_op jit(solution)/shard_map/ppermute | solution.py:217
  18.6 10.3 %collective-permute-start.10 = (bf16[144,1536]{1,0:T(8,128)(2,1)S(1)}, bf16[144,1536]{1,0:T(8,128)(2,1)S(1)}, u32[]{:S(2)}, u32[]{:S(2)}) collective-permute-start(bf16[144,1536]{1,0:T(8,128)(2,1)S(1)} %join_pieces.1.refs_9_.refs_0__0_), channel_id=1, source_target_pairs={{0,8},{4,12},{8,0},{12,4},{16,24},{20,28},{24,16},{28,20},{1,9},{5... | collective-permute-start | bytes 1327112 | tf_op jit(solution)/shard_map/ppermute | solution.py:217
  20.1 10.2 %collective-permute-start.11 = (bf16[144,1536]{1,0:T(8,128)(2,1)S(1)}, bf16[144,1536]{1,0:T(8,128)(2,1)S(1)}, u32[]{:S(2)}, u32[]{:S(2)}) collective-permute-start(bf16[144,1536]{1,0:T(8,128)(2,1)S(1)} %join_pieces.1.refs_9_.refs_0__0_), channel_id=1, source_target_pairs={{0,16},{4,20},{8,24},{12,28},{16,0},{20,4},{24,8},{28,12},{1,17},{... | collective-permute-start | bytes 1327112 | tf_op jit(solution)/shard_map/ppermute | solution.py:217
  21.4 18.5 %collective-permute-start.12 = (bf16[144,1536]{1,0:T(8,128)(2,1)S(1)}, bf16[144,1536]{1,0:T(8,128)(2,1)S(1)}, u32[]{:S(2)}, u32[]{:S(2)}) collective-permute-start(bf16[144,1536]{1,0:T(8,128)(2,1)S(1)} %join_pieces.1.refs_9_.refs_0__0_), channel_id=1, source_target_pairs={{0,24},{4,28},{8,16},{12,20},{16,8},{20,12},{24,0},{28,4},{1,25},{... | collective-permute-start | bytes 1327112 | tf_op jit(solution)/shard_map/ppermute | solution.py:217
  40.0 5.7 %collective-permute-start.13 = (bf16[576,1536]{1,0:T(8,128)(2,1)S(1)}, bf16[576,1536]{1,0:T(8,128)(2,1)S(1)}, u32[]{:S(2)}, u32[]{:S(2)}) collective-permute-start(bf16[576,1536]{1,0:T(8,128)(2,1)S(1)} %stack_weights.1.refs_1__0_), channel_id=1, source_target_pairs={{0,4},{4,0},{8,12},{12,8},{16,20},{20,16},{24,28},{28,24},{1,5},{5... | collective-permute-start | bytes 5308424 | tf_op jit(solution)/shard_map/ppermute | solution.py:220
  48.4 3.9 %collective-permute-start.14 = (bf16[32,512]{1,0:T(8,128)(2,1)S(1)}, bf16[32,512]{1,0:T(8,128)(2,1)S(1)}, u32[]{:S(2)}, u32[]{:S(2)}) collective-permute-start(bf16[32,512]{1,0:T(8,128)(2,1)S(1)} %get-tuple-element.142), channel_id=1, source_target_pairs={{0,8},{4,12},{8,0},{12,4},{16,24},{20,28},{24,16},{28,20},{1,9},{5... | collective-permute-start | bytes 98312 | tf_op jit(solution)/shard_map/ppermute | solution.py:217
  49.4 3.3 %collective-permute-start.15 = (bf16[32,512]{1,0:T(8,128)(2,1)S(1)}, bf16[32,512]{1,0:T(8,128)(2,1)S(1)}, u32[]{:S(2)}, u32[]{:S(2)}) collective-permute-start(bf16[32,512]{1,0:T(8,128)(2,1)S(1)} %get-tuple-element.143), channel_id=1, source_target_pairs={{0,16},{4,20},{8,24},{12,28},{16,0},{20,4},{24,8},{28,12},{1,17},{... | collective-permute-start | bytes 98312 | tf_op jit(solution)/shard_map/ppermute | solution.py:217
  49.9 4.0 %collective-permute-start.16 = (bf16[32,512]{1,0:T(8,128)(2,1)S(1)}, bf16[32,512]{1,0:T(8,128)(2,1)S(1)}, u32[]{:S(2)}, u32[]{:S(2)}) collective-permute-start(bf16[32,512]{1,0:T(8,128)(2,1)S(1)} %get-tuple-element.144), channel_id=1, source_target_pairs={{0,24},{4,28},{8,16},{12,20},{16,8},{20,12},{24,0},{28,4},{1,25},{... | collective-permute-start | bytes 98312 | tf_op jit(solution)/shard_map/ppermute | solution.py:217
  51.1 4.6 %collective-permute-start.17 = (bf16[32,512]{1,0:T(8,128)(2,1)S(1)}, bf16[32,512]{1,0:T(8,128)(2,1)S(1)}, u32[]{:S(2)}, u32[]{:S(2)}) collective-permute-start(bf16[32,512]{1,0:T(8,128)(2,1)S(1)} %get-tuple-element.141.refs_0__0_), channel_id=1, source_target_pairs={{0,4},{4,0},{8,12},{12,8},{16,20},{20,16},{24,28},{28,24},{1,5},{5... | collective-permute-start | bytes 98312 | tf_op jit(solution)/shard_map/ppermute | solution.py:220
  52.3 3.4 %collective-permute-start.18 = (bf16[32,512]{1,0:T(8,128)(2,1)S(1)}, bf16[32,512]{1,0:T(8,128)(2,1)S(1)}, u32[]{:S(2)}, u32[]{:S(2)}) collective-permute-start(bf16[32,512]{1,0:T(8,128)(2,1)S(1)} %collective-permute-done.14.refs_0__1_), channel_id=1, source_target_pairs={{0,4},{4,0},{8,12},{12,8},{16,20},{20,16},{24,28},{28,24},{1,5},{5... | collective-permute-start | bytes 98312 | tf_op jit(solution)/shard_map/ppermute | solution.py:220
  68.7 3.8 %collective-permute-start.21 = (bf16[32,512]{1,0:T(8,128)(2,1)S(1)}, bf16[32,512]{1,0:T(8,128)(2,1)S(1)}, u32[]{:S(2)}, u32[]{:S(2)}) collective-permute-start(bf16[32,512]{1,0:T(8,128)(2,1)S(1)} %get-tuple-element.151), channel_id=1, source_target_pairs={{0,8},{4,12},{8,0},{12,4},{16,24},{20,28},{24,16},{28,20},{1,9},{5... | collective-permute-start | bytes 98312 | tf_op jit(solution)/shard_map/ppermute | solution.py:217
  70.2 4.7 %collective-permute-start.23 = (bf16[32,512]{1,0:T(8,128)(2,1)S(1)}, bf16[32,512]{1,0:T(8,128)(2,1)S(1)}, u32[]{:S(2)}, u32[]{:S(2)}) collective-permute-start(bf16[32,512]{1,0:T(8,128)(2,1)S(1)} %get-tuple-element.153), channel_id=1, source_target_pairs={{0,24},{4,28},{8,16},{12,20},{16,8},{20,12},{24,0},{28,4},{1,25},{... | collective-permute-start | bytes 98312 | tf_op jit(solution)/shard_map/ppermute | solution.py:217
  71.4 4.5 %collective-permute-start.24 = (bf16[32,512]{1,0:T(8,128)(2,1)S(1)}, bf16[32,512]{1,0:T(8,128)(2,1)S(1)}, u32[]{:S(2)}, u32[]{:S(2)}) collective-permute-start(bf16[32,512]{1,0:T(8,128)(2,1)S(1)} %get-tuple-element.150.refs_0__0_), channel_id=1, source_target_pairs={{0,4},{4,0},{8,12},{12,8},{16,20},{20,16},{24,28},{28,24},{1,5},{5... | collective-permute-start | bytes 98312 | tf_op jit(solution)/shard_map/ppermute | solution.py:220
  72.6 3.3 %collective-permute-start.25 = (bf16[32,512]{1,0:T(8,128)(2,1)S(1)}, bf16[32,512]{1,0:T(8,128)(2,1)S(1)}, u32[]{:S(2)}, u32[]{:S(2)}) collective-permute-start(bf16[32,512]{1,0:T(8,128)(2,1)S(1)} %collective-permute-done.21.refs_0__1_), channel_id=1, source_target_pairs={{0,4},{4,0},{8,12},{12,8},{16,20},{20,16},{24,28},{28,24},{1,5},{5... | collective-permute-start | bytes 98312 | tf_op jit(solution)/shard_map/ppermute | solution.py:220
  83.9 3.8 %collective-permute-start.28 = (bf16[32,192]{1,0:T(8,128)(2,1)S(1)}, bf16[32,192]{1,0:T(8,128)(2,1)S(1)}, u32[]{:S(2)}, u32[]{:S(2)}) collective-permute-start(bf16[32,192]{1,0:T(8,128)(2,1)S(1)} %get-tuple-element.158.refs_8__1_), channel_id=1, source_target_pairs={{0,8},{4,12},{8,0},{12,4},{16,24},{20,28},{24,16},{28,20},{1,9},{5... | collective-permute-start | bytes 36872 | tf_op jit(solution)/shard_map/ppermute | solution.py:217
  85.4 3.8 %collective-permute-start.30 = (bf16[32,192]{1,0:T(8,128)(2,1)S(1)}, bf16[32,192]{1,0:T(8,128)(2,1)S(1)}, u32[]{:S(2)}, u32[]{:S(2)}) collective-permute-start(bf16[32,192]{1,0:T(8,128)(2,1)S(1)} %get-tuple-element.160.refs_8__3_), channel_id=1, source_target_pairs={{0,24},{4,28},{8,16},{12,20},{16,8},{20,12},{24,0},{28,4},{1,25},{... | collective-permute-start | bytes 36872 | tf_op jit(solution)/shard_map/ppermute | solution.py:217
  86.6 5.6 %collective-permute-start.31 = (bf16[32,192]{1,0:T(8,128)(2,1)S(1)}, bf16[32,192]{1,0:T(8,128)(2,1)S(1)}, u32[]{:S(2)}, u32[]{:S(2)}) collective-permute-start(bf16[32,192]{1,0:T(8,128)(2,1)S(1)} %get-tuple-element.157.refs_8__0_.refs_1__0_), channel_id=1, source_target_pairs={{0,4},{4,0},{8,12},{12,8},{16,20},{20,16},{24,28},{28,24},{1,5},{5... | collective-permute-start | bytes 36872 | tf_op jit(solution)/shard_map/ppermute | solution.py:220
  87.8 4.4 %collective-permute-start.32 = (bf16[32,192]{1,0:T(8,128)(2,1)S(1)}, bf16[32,192]{1,0:T(8,128)(2,1)S(1)}, u32[]{:S(2)}, u32[]{:S(2)}) collective-permute-start(bf16[32,192]{1,0:T(8,128)(2,1)S(1)} %collective-permute-done.28.refs_1__1_), channel_id=1, source_target_pairs={{0,4},{4,0},{8,12},{12,8},{16,20},{20,16},{24,28},{28,24},{1,5},{5... | collective-permute-start | bytes 36872 | tf_op jit(solution)/shard_map/ppermute | solution.py:220
  88.0 4.1 %collective-permute-start.33 = (bf16[32,192]{1,0:T(8,128)(2,1)S(1)}, bf16[32,192]{1,0:T(8,128)(2,1)S(1)}, u32[]{:S(2)}, u32[]{:S(2)}) collective-permute-start(bf16[32,192]{1,0:T(8,128)(2,1)S(1)} %collective-permute-done.29.refs_1__2_), channel_id=1, source_target_pairs={{0,4},{4,0},{8,12},{12,8},{16,20},{20,16},{24,28},{28,24},{1,5},{5... | collective-permute-start | bytes 36872 | tf_op jit(solution)/shard_map/ppermute | solution.py:220
  98.6 7.7 %collective-permute-start.38 = (bf16[160,512]{1,0:T(8,128)(2,1)S(1)}, bf16[160,512]{1,0:T(8,128)(2,1)S(1)}, u32[]{:S(2)}, u32[]{:S(2)}) collective-permute-start(bf16[160,512]{1,0:T(8,128)(2,1)S(1)} %get-tuple-element.185), channel_id=1, source_target_pairs={{0,8},{4,12},{8,0},{12,4},{16,24},{20,28},{24,16},{28,20},{1,9},{5... | collective-permute-start | bytes 491528 | tf_op jit(solution)/shard_map/ppermute | solution.py:217
  99.9 6.4 %collective-permute-start.39 = (bf16[160,512]{1,0:T(8,128)(2,1)S(1)}, bf16[160,512]{1,0:T(8,128)(2,1)S(1)}, u32[]{:S(2)}, u32[]{:S(2)}) collective-permute-start(bf16[160,512]{1,0:T(8,128)(2,1)S(1)} %get-tuple-element.186), channel_id=1, source_target_pairs={{0,16},{4,20},{8,24},{12,28},{16,0},{20,4},{24,8},{28,12},{1,17},{... | collective-permute-start | bytes 491528 | tf_op jit(solution)/shard_map/ppermute | solution.py:217
  100.1 6.5 %collective-permute-start.40 = (bf16[160,512]{1,0:T(8,128)(2,1)S(1)}, bf16[160,512]{1,0:T(8,128)(2,1)S(1)}, u32[]{:S(2)}, u32[]{:S(2)}) collective-permute-start(bf16[160,512]{1,0:T(8,128)(2,1)S(1)} %get-tuple-element.187), channel_id=1, source_target_pairs={{0,24},{4,28},{8,16},{12,20},{16,8},{20,12},{24,0},{28,4},{1,25},{... | collective-permute-start | bytes 491528 | tf_op jit(solution)/shard_map/ppermute | solution.py:217
  101.3 6.8 %collective-permute-start.37 = (bf16[64,1024]{1,0:T(8,128)(2,1)S(1)}, bf16[64,1024]{1,0:T(8,128)(2,1)S(1)}, u32[]{:S(2)}, u32[]{:S(2)}) collective-permute-start(bf16[64,1024]{1,0:T(8,128)(2,1)S(1)} %pair_stack.1.refs_2_.refs_0__0_), channel_id=1, source_target_pairs={{0,2},{1,3},{2,0},{3,1},{4,6},{5,7},{6,4},{7,5},{8,10},{9,11},{10,... | collective-permute-start | bytes 393224 | tf_op jit(solution)/shard_map/ppermute | solution.py:223
  109.7 5.2 %collective-permute-start.41 = (bf16[896,512]{1,0:T(8,128)(2,1)S(1)}, bf16[896,512]{1,0:T(8,128)(2,1)S(1)}, u32[]{:S(2)}, u32[]{:S(2)}) collective-permute-start(bf16[896,512]{1,0:T(8,128)(2,1)S(1)} %get-tuple-element.190), channel_id=1, source_target_pairs={{0,4},{4,0},{8,12},{12,8},{16,20},{20,16},{24,28},{28,24},{1,5},{5... | collective-permute-start | bytes 2752520 | tf_op jit(solution)/shard_map/ppermute | solution.py:220
  115.8 7.8 %collective-permute-start.45 = (bf16[512,512]{1,0:T(8,128)(2,1)S(1)}, bf16[512,512]{1,0:T(8,128)(2,1)S(1)}, u32[]{:S(2)}, u32[]{:S(2)}) collective-permute-start(bf16[512,512]{1,0:T(8,128)(2,1)S(1)} %get-tuple-element.200), channel_id=1, source_target_pairs={{0,4},{4,0},{8,12},{12,8},{16,20},{20,16},{24,28},{28,24},{1,5},{5... | collective-permute-start | bytes 1572872 | tf_op jit(solution)/shard_map/ppermute | solution.py:220
  116.2 7.8 %collective-permute-start.42 = (bf16[256,512]{1,0:T(8,128)(2,1)S(1)}, bf16[256,512]{1,0:T(8,128)(2,1)S(1)}, u32[]{:S(2)}, u32[]{:S(2)}) collective-permute-start(bf16[256,512]{1,0:T(8,128)(2,1)S(1)} %get-tuple-element.196), channel_id=1, source_target_pairs={{0,8},{4,12},{8,0},{12,4},{16,24},{20,28},{24,16},{28,20},{1,9},{5... | collective-permute-start | bytes 786440 | tf_op jit(solution)/shard_map/ppermute | solution.py:217
  117.4 7.7 %collective-permute-start.43 = (bf16[256,512]{1,0:T(8,128)(2,1)S(1)}, bf16[256,512]{1,0:T(8,128)(2,1)S(1)}, u32[]{:S(2)}, u32[]{:S(2)}) collective-permute-start(bf16[256,512]{1,0:T(8,128)(2,1)S(1)} %get-tuple-element.197), channel_id=1, source_target_pairs={{0,16},{4,20},{8,24},{12,28},{16,0},{20,4},{24,8},{28,12},{1,17},{... | collective-permute-start | bytes 786440 | tf_op jit(solution)/shard_map/ppermute | solution.py:217
  117.6 12.6 %collective-permute-start.44 = (bf16[256,512]{1,0:T(8,128)(2,1)S(1)}, bf16[256,512]{1,0:T(8,128)(2,1)S(1)}, u32[]{:S(2)}, u32[]{:S(2)}) collective-permute-start(bf16[256,512]{1,0:T(8,128)(2,1)S(1)} %get-tuple-element.198), channel_id=1, source_target_pairs={{0,24},{4,28},{8,16},{12,20},{16,8},{20,12},{24,0},{28,4},{1,25},{... | collective-permute-start | bytes 786440 | tf_op jit(solution)/shard_map/ppermute | solution.py:217
  118.9 4.7 %collective-permute-start.46 = (bf16[160,512]{1,0:T(8,128)(2,1)S(1)}, bf16[160,512]{1,0:T(8,128)(2,1)S(1)}, u32[]{:S(2)}, u32[]{:S(2)}) collective-permute-start(bf16[160,512]{1,0:T(8,128)(2,1)S(1)} %early_plane.1.refs_4_.refs_0_), channel_id=1, source_target_pairs={{0,1},{1,0},{2,3},{3,2},{4,5},{5,4},{6,7},{7,6},{8,9},{9,8},{10,11... | collective-permute-start | bytes 491528 | tf_op jit(solution)/shard_map/ppermute | solution.py:223
  130.4 9.2 %collective-permute-start.52 = (bf16[224,512]{1,0:T(8,128)(2,1)S(1)}, bf16[224,512]{1,0:T(8,128)(2,1)S(1)}, u32[]{:S(2)}, u32[]{:S(2)}) collective-permute-start(bf16[224,512]{1,0:T(8,128)(2,1)S(1)} %get-tuple-element.210.refs_0_), channel_id=1, source_target_pairs={{0,1},{1,0},{2,3},{3,2},{4,5},{5,4},{6,7},{7,6},{8,9},{9,8},{10,11... | collective-permute-start | bytes 688136 | tf_op jit(solution)/shard_map/ppermute | solution.py:223
  130.8 11.2 %collective-permute-start.48 = (bf16[160,512]{1,0:T(8,128)(2,1)S(1)}, bf16[160,512]{1,0:T(8,128)(2,1)S(1)}, u32[]{:S(2)}, u32[]{:S(2)}) collective-permute-start(bf16[160,512]{1,0:T(8,128)(2,1)S(1)} %early_line.2.refs_2_.refs_0_), channel_id=1, source_target_pairs={{0,2},{1,3},{2,0},{3,1},{4,6},{5,7},{6,4},{7,5},{8,10},{9,11},{10,... | collective-permute-start | bytes 491528 | tf_op jit(solution)/shard_map/ppermute | solution.py:223
  133.9 5.7 %collective-permute-start.49 = (bf16[128,512]{1,0:T(8,128)(2,1)S(1)}, bf16[128,512]{1,0:T(8,128)(2,1)S(1)}, u32[]{:S(2)}, u32[]{:S(2)}) collective-permute-start(bf16[128,512]{1,0:T(8,128)(2,1)S(1)} %get-tuple-element.207), channel_id=1, source_target_pairs={{0,8},{4,12},{8,0},{12,4},{16,24},{20,28},{24,16},{28,20},{1,9},{5... | collective-permute-start | bytes 393224 | tf_op jit(solution)/shard_map/ppermute | solution.py:217
  134.4 5.2 %collective-permute-start.50 = (bf16[128,512]{1,0:T(8,128)(2,1)S(1)}, bf16[128,512]{1,0:T(8,128)(2,1)S(1)}, u32[]{:S(2)}, u32[]{:S(2)}) collective-permute-start(bf16[128,512]{1,0:T(8,128)(2,1)S(1)} %get-tuple-element.208), channel_id=1, source_target_pairs={{0,16},{4,20},{8,24},{12,28},{16,0},{20,4},{24,8},{28,12},{1,17},{... | collective-permute-start | bytes 393224 | tf_op jit(solution)/shard_map/ppermute | solution.py:217
  135.6 6.3 %collective-permute-start.51 = (bf16[128,512]{1,0:T(8,128)(2,1)S(1)}, bf16[128,512]{1,0:T(8,128)(2,1)S(1)}, u32[]{:S(2)}, u32[]{:S(2)}) collective-permute-start(bf16[128,512]{1,0:T(8,128)(2,1)S(1)} %get-tuple-element.209), channel_id=1, source_target_pairs={{0,24},{4,28},{8,16},{12,20},{16,8},{20,12},{24,0},{28,4},{1,25},{... | collective-permute-start | bytes 393224 | tf_op jit(solution)/shard_map/ppermute | solution.py:217
  142.0 14.6 %collective-permute-start.57 = (bf16[288,512]{1,0:T(8,128)(2,1)S(1)}, bf16[288,512]{1,0:T(8,128)(2,1)S(1)}, u32[]{:S(2)}, u32[]{:S(2)}) collective-permute-start(bf16[288,512]{1,0:T(8,128)(2,1)S(1)} %early_line.3.refs_3_.refs_0__0_), channel_id=1, source_target_pairs={{0,8},{4,12},{8,0},{12,4},{16,24},{20,28},{24,16},{28,20},{1,9},{5... | collective-permute-start | bytes 884744 | tf_op jit(solution)/shard_map/ppermute | solution.py:217
  142.1 14.5 %collective-permute-start.58 = (bf16[288,512]{1,0:T(8,128)(2,1)S(1)}, bf16[288,512]{1,0:T(8,128)(2,1)S(1)}, u32[]{:S(2)}, u32[]{:S(2)}) collective-permute-start(bf16[288,512]{1,0:T(8,128)(2,1)S(1)} %early_line.3.refs_3_.refs_0__0_), channel_id=1, source_target_pairs={{0,16},{4,20},{8,24},{12,28},{16,0},{20,4},{24,8},{28,12},{1,17},{... | collective-permute-start | bytes 884744 | tf_op jit(solution)/shard_map/ppermute | solution.py:217
  143.0 13.6 %collective-permute-start.59 = (bf16[288,512]{1,0:T(8,128)(2,1)S(1)}, bf16[288,512]{1,0:T(8,128)(2,1)S(1)}, u32[]{:S(2)}, u32[]{:S(2)}) collective-permute-start(bf16[288,512]{1,0:T(8,128)(2,1)S(1)} %early_line.3.refs_3_.refs_0__0_), channel_id=1, source_target_pairs={{0,24},{4,28},{8,16},{12,20},{16,8},{20,12},{24,0},{28,4},{1,25},{... | collective-permute-start | bytes 884744 | tf_op jit(solution)/shard_map/ppermute | solution.py:217
  144.7 11.8 %collective-permute-start.53 = (bf16[224,512]{1,0:T(8,128)(2,1)S(1)}, bf16[224,512]{1,0:T(8,128)(2,1)S(1)}, u32[]{:S(2)}, u32[]{:S(2)}) collective-permute-start(bf16[224,512]{1,0:T(8,128)(2,1)S(1)} %late_line.2.refs_1_.refs_0_), channel_id=1, source_target_pairs={{0,2},{1,3},{2,0},{3,1},{4,6},{5,7},{6,4},{7,5},{8,10},{9,11},{10,... | collective-permute-start | bytes 688136 | tf_op jit(solution)/shard_map/ppermute | solution.py:223
  144.7 5.1 %collective-permute-start.47 = (bf16[64,512]{1,0:T(8,128)(2,1)S(1)}, bf16[64,512]{1,0:T(8,128)(2,1)S(1)}, u32[]{:S(2)}, u32[]{:S(2)}) collective-permute-start(bf16[64,512]{1,0:T(8,128)(2,1)S(1)} %get-tuple-element.203), channel_id=1, source_target_pairs={{0,4},{4,0},{8,12},{12,8},{16,20},{20,16},{24,28},{28,24},{1,5},{5... | collective-permute-start | bytes 196616 | tf_op jit(solution)/shard_map/ppermute | solution.py:220
  156.7 4.3 %collective-permute-start.60 = (bf16[1152,512]{1,0:T(8,128)(2,1)S(1)}, bf16[1152,512]{1,0:T(8,128)(2,1)S(1)}, u32[]{:S(2)}, u32[]{:S(2)}) collective-permute-start(bf16[1152,512]{1,0:T(8,128)(2,1)S(1)} %early_stack.1.refs_1__0_), channel_id=1, source_target_pairs={{0,4},{4,0},{8,12},{12,8},{16,20},{20,16},{24,28},{28,24},{1,5},{5... | collective-permute-start | bytes 3538952 | tf_op jit(solution)/shard_map/ppermute | solution.py:220
  158.4 7.2 %collective-permute-start.54 = (bf16[224,512]{1,0:T(8,128)(2,1)S(1)}, bf16[224,512]{1,0:T(8,128)(2,1)S(1)}, u32[]{:S(2)}, u32[]{:S(2)}) collective-permute-start(bf16[224,512]{1,0:T(8,128)(2,1)S(1)} %late_line.3.refs_1_.refs_0__0_), channel_id=1, source_target_pairs={{0,8},{4,12},{8,0},{12,4},{16,24},{20,28},{24,16},{28,20},{1,9},{5... | collective-permute-start | bytes 688136 | tf_op jit(solution)/shard_map/ppermute | solution.py:217
  159.4 7.1 %collective-permute-start.55 = (bf16[224,512]{1,0:T(8,128)(2,1)S(1)}, bf16[224,512]{1,0:T(8,128)(2,1)S(1)}, u32[]{:S(2)}, u32[]{:S(2)}) collective-permute-start(bf16[224,512]{1,0:T(8,128)(2,1)S(1)} %late_line.3.refs_1_.refs_0__0_), channel_id=1, source_target_pairs={{0,16},{4,20},{8,24},{12,28},{16,0},{20,4},{24,8},{28,12},{1,17},{... | collective-permute-start | bytes 688136 | tf_op jit(solution)/shard_map/ppermute | solution.py:217
  159.8 11.2 %collective-permute-start.56 = (bf16[224,512]{1,0:T(8,128)(2,1)S(1)}, bf16[224,512]{1,0:T(8,128)(2,1)S(1)}, u32[]{:S(2)}, u32[]{:S(2)}) collective-permute-start(bf16[224,512]{1,0:T(8,128)(2,1)S(1)} %late_line.3.refs_1_.refs_0__0_), channel_id=1, source_target_pairs={{0,24},{4,28},{8,16},{12,20},{16,8},{20,12},{24,0},{28,4},{1,25},{... | collective-permute-start | bytes 688136 | tf_op jit(solution)/shard_map/ppermute | solution.py:217
  171.1 3.5 %collective-permute-start.61 = (bf16[896,512]{1,0:T(8,128)(2,1)S(1)}, bf16[896,512]{1,0:T(8,128)(2,1)S(1)}, u32[]{:S(2)}, u32[]{:S(2)}) collective-permute-start(bf16[896,512]{1,0:T(8,128)(2,1)S(1)} %late_stack.1.refs_1__0_), channel_id=1, source_target_pairs={{0,4},{4,0},{8,12},{12,8},{16,20},{20,16},{24,28},{28,24},{1,5},{5... | collective-permute-start | bytes 2752520 | tf_op jit(solution)/shard_map/ppermute | solution.py:220
  (28 other events, 201.5 us)

commit v3 on v2

--- a/solution.py
+++ b/solution.py
@@ -39,6 +39,22 @@
     return half + half * t, slope
 
 
+def smooth_low(v):
+    v = v.astype(BF)
+    t = jnp.tanh(v * (BF(LEAN) + BF(CUBE) * (v * v)))
+    half = BF(0.5) * v
+    return half + half * t
+
+
+def smooth_slope_low(v):
+    v = v.astype(BF)
+    v2 = v * v
+    t = jnp.tanh(v * (BF(LEAN) + BF(CUBE) * v2))
+    half = BF(0.5) * v
+    slope = (BF(0.5) + BF(0.5) * t) + (half - half * (t * t)) * (BF(LEAN) + BF(3.0 * CUBE) * v2)
+    return half + half * t, slope
+
+
 def centred(x):
     center = x - jnp.mean(x, axis=-1, keepdims=True)
     rate = lax.rsqrt(jnp.mean(center * center, axis=-1, keepdims=True) + 1e-05)
@@ -77,12 +93,21 @@
         self.shape, self.dtype = shape, F32
 
 
+class Cut(Final):
+    def __init__(self, n, width, stop, start=0):
+        super().__init__(stop - start, width)
+        self.whole, self.start = (n, width), start
+
+
 def call(body, outs, args, name, scratch=(), limit=28, spot=None, after=(), far=False, token=False):
     if token:
         outs = list(outs) + [pltpu.VMEM((8, 128), F32)]
     flat_outs, out_tree = jax.tree.flatten(list(outs), is_leaf=lambda v: hasattr(v, "dtype"))
     ends = [k for k, v in enumerate(flat_outs) if isinstance(v, Final)]
-    held_outs = [pltpu.VMEM(flat_outs[k].shape, flat_outs[k].dtype) for k in ends]
+    cuts = [v for v in flat_outs if isinstance(v, Cut)]
+    held_outs = [pltpu.VMEM(flat_outs[k].shape, flat_outs[k].dtype) for k in ends if not cuts]
+    if cuts:
+        held_outs = [pltpu.VMEM(cuts[0].whole, F32)]
     if ends:
         held_outs.append(pltpu.SemaphoreType.DMA((len(ends),)))
     shapes = [pltpu.HBM(v.shape, v.dtype) if isinstance(v, Final) else v for v in flat_outs]
@@ -104,7 +129,8 @@
         results, rest = list(jax.tree.leaves(list(rest[: len(outs)]))), rest[len(outs) :]
         targets = [results[k] for k in ends]
         if ends:
-            rest, kept, out_sems = rest[: -len(ends) - 1], rest[-len(ends) - 1 : -1], rest[-1]
+            count = len(held_outs)
+            rest, kept, out_sems = rest[:-count], rest[-count:-1], rest[-1]
             for k, v in zip(ends, kept):
                 results[k] = v
         if far:
@@ -122,7 +148,11 @@
         produced = list(jax.tree.unflatten(out_tree, results))
         if token:
             produced.pop()[...] = jnp.zeros((8, 128), F32)
+        if cuts:
+            produced = [kept[0]]
         body(*given, *produced, *rest)
+        if cuts:
+            kept = [kept[0].at[v.start : v.start + v.shape[0], :] for v in cuts]
         if ends:
             copies = [
                 pltpu.make_async_copy(src, dst, out_sems.at[k])
@@ -179,6 +209,9 @@
 def joined(parts):
     if len(parts) == 1:
         return parts[0][...]
+    if len(parts) == 2:
+        n = parts[0].shape[0] // 4
+        return jnp.concatenate([v[m * n : (m + 1) * n] for m in range(4) for v in parts], axis=0)
     near, far = parts[: len(parts) // 2], parts[len(parts) // 2 :]
     rows = []
     for mine, other in zip(near, far):
@@ -256,7 +289,10 @@
             rest = jnp.concatenate([high, bias[...] - high, jnp.zeros((n // 4 - 2, width), F32)], axis=0)
             out[2 * n :, :] = rest.astype(BF)
 
-    def prepare_rest(spot, slots, counts, vecs, edge_vecs, pick_out, counts_out, vecs_out, edge_out):
+    def prepare_rest(
+        spot, slots, counts, vecs, edge_vecs, edges, pick_out, counts_out, vecs_out, edge_out, edges_out
+    ):
+        edges_out[...] = edges[...]
         rows, fanout = slots.shape
         lanes = lax.broadcasted_iota(jnp.int32, (rows, pick_out.shape[1]), 1)
         moved = slots[...] ^ (spot[3] * (pick_out.shape[1] // n_res))
@@ -278,7 +314,7 @@
         span = step * rows
 
         def kernel(
-            arrived, nodes, edges, pick, counts, mf, ms, mt, vecs, mid_out, sums,
+            arrived, nodes, edges, pick, counts, mf, ms, mt, vecs, mid_out, mid_low_out, sums,
         ):
             mfb, msb, mtb, mg, msh = [vecs[k : k + 1, :] for k in range(5)]
             width = nodes.shape[1]
@@ -291,8 +327,8 @@
             def chunk(i, carry):
                 at = pl.ds(aligned(i * span, span), span)
                 pre = dot(pick[at, :], query) + dot(edges[at, :], lower)
-                act = smooth(tiled_add(pre, part)).astype(BF)
-                act = smooth(dot(act, ms[...]) + msb)
+                act = smooth_low(tiled_add(pre, part)).astype(BF)
+                act = smooth_low(dot(act, ms[...]) + msb)
                 total = sums[...]
                 for j in range(step):
                     total = total + jnp.where(
@@ -303,9 +339,27 @@
 
             over(fanout // step, chunk)
             first = nodes[...].astype(F32) + message_mean(sums[...], counts[...], mt[...], mtb)
-            mid_out[...] = centred(first)[0] * mg + msh
+            mid = centred(first)[0] * mg + msh
+            mid_out[...] = mid
+            mid_low_out[...] = mid.astype(BF)
 
         return kernel
+
+    def feed_shard(mids, we, web, wr, outs):
+        mid = jnp.concatenate([v[...] for v in mids], axis=0)
+        act = smooth(dot(mid, we[...]) + web[...]).astype(BF)
+        dealt(outs, dot(act, wr[...]))
+
+    def feed_end(mid, parts, vecs, send, new_out, low_out, away_out):
+        rb, fg, fsh = [vecs[k : k + 1, :] for k in (5, 6, 7)]
+        second = mid[...] + rb
+        for v in parts:
+            second = second + v[...].astype(F32)
+        new = centred(second)[0] * fg + fsh
+        new_out[...] = new
+        low = new.astype(BF)
+        low_out[...] = low
+        dealt(away_out, dot(send[...], low))
 
     def feed_pass(mid, own, packed, vecs, send, slopes_out, second_out, new_out, low_out, away_out):
         rb, fg, fsh = [vecs[k : k + 1, :] for k in (5, 6, 7)]
@@ -342,17 +396,17 @@
                 chosen = pick[at, :]
                 old = edges[at, :]
                 pre = dot(chosen, key) + dot_nt(old, edge_lower)
-                act = smooth(tiled_add(pre, edge_part)).astype(BF)
-                act = smooth(dot(act, es[...]) + esb).astype(BF)
+                act = smooth_low(tiled_add(pre, edge_part)).astype(BF)
+                act = smooth_low(dot(act, es[...]) + esb).astype(BF)
                 total = old.astype(F32) + dot(act, et[...]) + etb
                 fresh = centred(total)[0] * eg + esh
                 edge_out[at, :] = fresh
                 pre = dot(chosen, query) + dot(fresh.astype(BF), lower)
-                act, slope = smooth_slope(tiled_add(pre, part))
+                act, slope = smooth_slope_low(tiled_add(pre, part))
                 act = act.astype(BF)
                 act_out[at, :] = act
                 slope1_out[at, :] = slope.astype(BF)
-                act, slope = smooth_slope(dot(act, ms[...]) + msb)
+                act, slope = smooth_slope_low(dot(act, ms[...]) + msb)
                 total = sums[...]
                 for j in range(step):
                     valid = lots > jnp.float32(i * step + j)
@@ -395,10 +449,10 @@
                 chosen = pick[at, :]
                 old = edges[at, :]
                 pre = dot(chosen, key) + dot_nt(old.astype(BF), edge_lower)
-                act, slope1 = smooth_slope(tiled_add(pre, edge_part))
+                act, slope1 = smooth_slope_low(tiled_add(pre, edge_part))
                 act1 = act.astype(BF)
                 act1_out[at, :] = act1
-                act, slope2 = smooth_slope(dot(act1, es[...]) + esb)
+                act, slope2 = smooth_slope_low(dot(act1, es[...]) + esb)
                 act2 = act.astype(BF)
                 act2_out[at, :] = act2
                 total = old + dot(act2, et[...]) + etb
@@ -551,30 +605,24 @@
 
         return kernel
 
-    def feed_weights(pairs, we, web, wr, pay_out):
-        n, share = we.shape
+    def feed_products(pairs, we, web, wr):
+        n = we.shape[0]
         mid = jnp.concatenate([v[:, :n] for v in pairs], axis=0)
         up = jnp.concatenate([v[:, n:] for v in pairs], axis=0)
-        act, slope = smooth_slope(dot(mid, we[...]) + web[...])
+        act, slope = smooth_slope_low(dot(mid, we[...]) + web[...])
         expand = dot_nt(up, wr[...]) * slope
-        expand = dot_tn(mid, expand.astype(BF)).astype(BF)
-        reduce = dot_tn(act.astype(BF), up).astype(BF)
-        if len(pay_out) == 2:
-            pay_out[0][...], pay_out[1][...] = expand, reduce
-        else:
-            pay_out[0][:n, :] = expand
-            pay_out[0][n:, :] = reduce
+        return dot_tn(mid, expand.astype(BF)), dot_tn(act, up)
+
+    def feed_weights(pairs, we, web, wr, expand_out, reduce_out):
+        expand_out[...], reduce_out[...] = feed_products(pairs, we, web, wr)
+
+    def feed_weights_more(pairs, we, web, wr, expand, reduce, expand_out, reduce_out):
+        left, right = feed_products(pairs, we, web, wr)
+        expand_out[...], reduce_out[...] = expand[...] + left, reduce[...] + right
 
     def node_end(returned, send, first_grad, node, mf, out):
         width = out.shape[1]
-        if len(returned) == 2:
-            mine, twin = returned
-            n = mine.shape[0] // 4
-            rows = [v[m * n : (m + 1) * n, :] for m in range(4) for v in (mine, twin)]
-            back = jnp.concatenate(rows, axis=0)
-        else:
-            back = joined(returned)
-        query_low = dot_tn(send[...], back).astype(BF)
+        query_low = dot_tn(send[...], joined(returned)).astype(BF)
         out[...] = (
             first_grad[...] + dot_nt(node[...], mf[:width]) + dot_nt(query_low, mf[width : 2 * width])
         )
@@ -620,6 +668,33 @@
             mine[at, :] = v[top : top + n, :]
             twin[at, :] = v[top + n : top + 2 * n, :]
 
+    def add_up_join(parts, more, out):
+        n = more.shape[0]
+        out[:n, :] = more[...]
+        total = parts[0][...].astype(F32)
+        for v in parts[1:]:
+            total = total + v[...].astype(F32)
+        out[n:, :] = total.astype(BF)
+
+    def add_up_sides(spot, parts, pay, keep, send, pay_keep, pay_send, total):
+        add_up(parts, total)
+        halved(spot, pay, pay_keep, pay_send)
+        n, side = keep.shape[1], spot[2] // 2
+        keep[...] = total[:, pl.ds(pl.multiple_of(side * n, n), n)]
+        send[...] = total[:, pl.ds(pl.multiple_of((1 - side) * n, n), n)]
+
+    def join_sides(spot, mine, other, out):
+        n, side = mine.shape[1], spot[2] // 2
+        out[:, pl.ds(pl.multiple_of(side * n, n), n)] = mine[...]
+        out[:, pl.ds(pl.multiple_of((1 - side) * n, n), n)] = other[...]
+
+    def sort_cores(parts, mine, twin):
+        n = mine.shape[0] // len(parts)
+        for m, v in enumerate(parts):
+            at = slice(m * n, (m + 1) * n)
+            mine[at, :] = v[:n, :]
+            twin[at, :] = v[n : 2 * n, :]
+
     def add_two(left, right, more, out):
         n = left.shape[0]
         out[:n, :] = (left[...].astype(F32) + right[...].astype(F32)).astype(BF)
@@ -639,12 +714,11 @@
             at = (2 * (spot[1] ^ (k % 4)) + (spot[0] ^ (k // 4))) * n
             total[pl.ds(pl.multiple_of(at, n), n), :] = v[...].astype(total.dtype)
 
-    def lay_pair(spot, stacks, total, skip=0):
+    def lay_pair(spot, stacks, total):
         n = total.shape[0] // 8
-        step = stacks[0].shape[0] // 4
         for k in range(8):
             at = (2 * (spot[1] ^ (k % 4)) + (spot[0] ^ (k // 4))) * n
-            top = k % 4 * step + skip
+            top = k % 4 * n
             total[pl.ds(pl.multiple_of(at, n), n), :] = stacks[k // 4][top : top + n, :].astype(total.dtype)
 
     def stack_up(parts, out):
@@ -653,17 +727,12 @@
             out[m * n : (m + 1) * n, :] = v[...]
 
     def unpack_early(
-        spot, parts, first_out, second_out, third_out, message_out, vec_out, edge_vec_out, bias_out, feed_out,
-        total, rest,
+        spot, parts, first_out, second_out, third_out, message_out, vec_out, edge_vec_out, bias_out, total,
     ):
         if len(parts) == 1:
             total[...] = parts[0][...]
         else:
             lay_pair(spot, parts, total)
-            lay_pair(spot, parts, rest, total.shape[0] // 8)
-            n = rest.shape[0] // 2
-            feed_out[0][...] = rest[:n, :]
-            feed_out[1][...] = rest[n:, :]
         n, wide = second_out.shape[0], message_out.shape[1]
         first_out[:, :wide] = total[:n, :]
         first_out[:, wide : 2 * wide] = total[n : 2 * n, :]
@@ -683,16 +752,23 @@
         bias = jnp.sum(jnp.where(line, vecs, 0.0), axis=0, keepdims=True)
         bias_out[...] = bias[:, : bias_out.shape[1]]
 
-    def unpack_late(spot, parts, first_out, second_out, vec_out, total):
+    def unpack_late(spot, parts, total):
         if len(parts) == 1:
             total[...] = parts[0][...]
         else:
             lay_pair(spot, parts, total)
-        n, hidden = first_out.shape[0], second_out.shape[0]
-        first_out[...] = total[:n, :]
-        second_out[...] = total[n : n + hidden, :]
-        for k, out in enumerate(vec_out):
-            out[...] = total[n + hidden + k : n + hidden + k + 1, :]
+
+    def split_relay(left, right, left_out, right_out):
+        n = left_out.shape[1]
+        left_out[...] = left[:, :n]
+        right_out[...] = right[:, n:]
+
+    def stack_relay(parts, left, right, out):
+        n, half = left.shape
+        for m, v in enumerate(parts):
+            out[m * n : (m + 1) * n, :] = v[...]
+        out[len(parts) * n :, :half] = left[...]
+        out[len(parts) * n :, half:] = right[...]
 
     def join_pieces(parts, out):
         for m, v in enumerate(parts):
@@ -708,7 +784,7 @@
         width, hidden = nodes.shape[1], ms.shape[0]
         share = expand_weight.shape[1]
         n_edges = rows * fanout
-        step, half_step = fanout, fanout // 2 if fanout % 2 == 0 else fanout
+        step = fanout
         slots_each = send_rows.shape[2]
         buffer = n_res * slots_each
         row = lambda v: v.reshape(1, -1)
@@ -733,70 +809,92 @@
             spot=spot,
             far=True,
         )
-        arrived = exchange(away)
-        pick, counts, vecs, edge_vecs = call(
+        pick, counts, vecs, edge_vecs, edges = call(
             prepare_rest,
             [
                 struct((n_edges, buffer), BF),
                 struct((rows, 1), F32),
                 struct((8, width), F32),
                 struct((8, edge_width), F32),
+                struct((n_edges, edge_width), BF),
             ],
             (
                 neighbor_slots,
                 row(neighbor_counts),
                 [row(v) for v in (mfb, msb, mtb, mg, msh, rb, fg, fsh)],
                 [row(v) for v in (efb, esb, etb, eg, esh)],
+                edges,
             ),
             "prepare_rest",
             spot=spot,
             after=away[:1],
             far=True,
         )
+        if tuned:
+            half = struct((rows * 2, width), BF)
+            mine, twin = call(sort_cores, [half, half], (to_chips(away),), "first_sort", after=[counts])
+            arrived = [mine, to_core(twin)]
+        else:
+            arrived = exchange(away)
         edge_args = (ef, es, et, edge_vecs)
         if tuned:
             pieces = [to_hid(piece[0], m) for m in (1, 2, 3)]
             (piece,) = call(
-                join_pieces, [struct((n_piece, 3 * width), BF)], (pieces,), "join_pieces", after=arrived
-            )
-            packed, first = [piece] + [to_chip(piece, m) for m in (1, 2, 3)], [piece]
+                join_pieces, [struct((n_piece, 3 * width), BF)], (pieces,), "join_pieces", after=[counts] + arrived
+            )
+            packed, first = [piece] + [to_chip(piece, m) for m in (1, 2)], [piece]
         else:
             packed, first = [
                 lax.all_gather(expand_weight, "hid"),
                 lax.all_gather(expand_bias, "hid"),
                 lax.all_gather(reduce_weight, "hid"),
             ], []
-        (mid,) = call(
+        mid, mid_low = call(
             pass_one(rows, fanout, step),
-            [struct((rows, width), F32)],
+            [struct((rows, width), F32), one],
             (arrived, nodes, edges, pick, counts, mf, ms, mt, vecs),
             "message_one",
             [pltpu.VMEM((rows, hidden), F32)],
             after=first,
         )
         if tuned:
+            mids = [mid_low] + [to_hid(mid_low, m) for m in (1, 2, 3)]
+            (parts,) = call(
+                feed_shard, [[one] * 4], (mids, expand_weight, bias, reduce_weight), "feed_shard"
+            )
+            relay = struct((n_piece, 3 * width // 2), BF)
+            left, right = call(
+                split_relay, [relay, relay], tuple(packed[1:]), "split_weights", after=parts[:1]
+            )
+            parts = [parts[0]] + [to_hid(parts[m], m) for m in (1, 2, 3)]
+        else:
+            mids = [lax.all_gather(mid_low, "hid", axis=0, tiled=True)]
+            (part,) = call(
+                feed_shard,
+                [[struct((n_hid * rows, width), BF)]],
+                (mids, expand_weight, bias, reduce_weight),
+                "feed_shard",
+            )
+            parts = [lax.psum_scatter(part[0], "hid", scatter_dimension=0, tiled=True)]
+        state, low, away = call(
+            feed_end, [struct((rows, width), F32), one, deal], (mid, parts, vecs, send), "feed_one"
+        )
+        if tuned:
             (packed,) = call(
-                stack_up, [struct((4 * n_piece, 3 * width), BF)], (packed,), "stack_weights", after=[mid]
-            )
+                stack_relay,
+                [struct((4 * n_piece, 3 * width), BF)],
+                (packed, to_chip(left, 2), to_chip(right, 1)),
+                "stack_weights",
+                after=[low],
+            )
+            packed = [packed, to_core(packed)]
+        arrived2, low2 = exchange(away), low
+        first = []
+        if tuned:
             (packed,) = call(
-                lay_pair,
-                [struct((8 * n_piece, 3 * width), BF)],
-                ([packed, to_core(packed)],),
-                "lay_weights",
-                spot=spot,
-            )
-            packed = [packed]
-        feed_outs = [
-            struct((n_hid, rows, share), BF),
-            struct((rows, width), F32),
-            struct((rows, width), F32),
-            one,
-            deal,
-        ]
-        _, _, state, low, away = call(
-            feed_pass, feed_outs, (mid, own, packed, vecs, send), "feed_one"
-        )
-        arrived2, low2 = exchange(away), low
+                lay_pair, [struct((8 * n_piece, 3 * width), BF)], (packed,), "lay_weights", spot=spot
+            )
+            first = packed = [packed]
         edge_state, act, slope1, slope2, first, summed, mid, mid_low = call(
             pass_two(rows, fanout, step),
             [
@@ -812,15 +910,22 @@
             (arrived2, state, low2, edges, pick, counts, mf, ms, mt, vecs, *edge_args),
             "layer_two",
             [pltpu.VMEM((rows, hidden), F32)],
-        )
-        feed_outs[2] = jax.ShapeDtypeStruct((rows, width), F32)
+            after=first,
+        )
+        feed_outs = [
+            struct((n_hid, rows, share), BF),
+            struct((rows, width), F32),
+            jax.ShapeDtypeStruct((rows, width), F32),
+            one,
+            deal,
+        ]
         slopes, second, node_result, low3, away = call(
             feed_pass, feed_outs, (mid, own, packed, vecs, send), "feed_two"
         )
         arrived3 = exchange(away)
         wide = lambda dtype: struct((n_edges, edge_width), dtype)
         edge_result, edge_grad, act1, act2, top, mid, bottom, slot, node, edge_vec = call(
-            edge_turn(rows, fanout, half_step),
+            edge_turn(rows, fanout, step),
             [
                 jax.ShapeDtypeStruct((n_edges, edge_width), F32),
                 wide(F32), wide(BF), wide(BF), wide(BF), wide(BF), wide(BF),
@@ -836,7 +941,6 @@
                 pltpu.VMEM((4, 8, edge_width), F32),
             ],
         )
-        returned = exchange(slot)
         head = 3 * edge_width + edge_width // 2
         (pack,) = call(
             edge_weights,
@@ -844,8 +948,14 @@
             (arrived3, low3, edge_state, act1, act2, top, mid, bottom, slot, node),
             "edge_weights",
         )
+        if tuned:
+            half = struct((rows * 2, edge_width), BF)
+            mine, twin = call(sort_cores, [half, half], (to_chips(slot),), "edge_sort", after=[pack])
+            returned = [mine, to_core(twin)]
+        else:
+            returned = exchange(slot)
         sized = lambda n: -(-n // 128) * 128
-        n_early, n_late, n_feed = sized(head + hidden + 32), sized(mf.shape[0] + hidden + 16), 2 * width
+        n_early, n_late = sized(head + hidden + 32), sized(mf.shape[0] + hidden + 16)
         cut = lambda n: [struct((n // 2, width), BF)] * 2 if tuned else [struct((n, width), BF)]
         pair, first_grad, pull, early = call(
             node_turn,
@@ -866,24 +976,13 @@
             "message_second",
             [pltpu.VMEM((rows, hidden), F32)],
         )
-        feed_outs = [
-            [struct((n_feed, width), BF)] if tuned else [struct((width, share), BF), struct((share, width), BF)]
-        ]
-
-        def feed_grads_of(pairs, after):
-            return call(
-                feed_weights, feed_outs, (pairs, expand_weight, bias, reduce_weight), "feed_weights", after=after
-            )
+        feed_own = (expand_weight, bias, reduce_weight)
 
         first = []
         if tuned:
-            (pair,) = call(
-                stack_up, [struct((2 * rows, 2 * width), BF)], ([pair, to_hid(pair, 1)],), "pair_stack",
-                after=[second_weight],
-            )
             (early,) = call(
                 split_chips, [[eighth(n_early)] * 4], (early[0], to_core(early[1])), "early_chips",
-                after=[pair],
+                after=[second_weight],
             )
             first = early[:1]
             early = to_chips(early)
@@ -907,9 +1006,15 @@
         )
         final = Final
         if tuned:
-            (early,) = call(add_up, [eighth(n_early)], (early,), "early_plane", after=[node])
-            ((feed_pay,),) = feed_grads_of([pair, to_hid(pair, 2)], [early])
-            keep, send_late = call(halved, cut(n_late), (late,), "late_pay", spot=spot, after=[feed_pay])
+            (pair,) = call(
+                stack_up, [struct((2 * rows, 2 * width), BF)], ([pair, to_hid(pair, 2)],), "pair_stack",
+                after=[node],
+            )
+            side = struct((n_early // 8, width // 2), BF)
+            early, other, keep, send_late = call(
+                add_up_sides, [side, side] + cut(n_late), (early, late), "early_plane",
+                [pltpu.VMEM((n_early // 8, width), BF)], spot=spot, after=[pair],
+            )
             (late,) = call(
                 split_chips_more,
                 [[struct((n_late // 8 + rows, width), BF)] * 4],
@@ -918,28 +1023,25 @@
             )
             last = late[0]
             late = to_chips(late)
-            keep, send_feed = call(halved, cut(n_feed), [feed_pay], "feed_pay", spot=spot, after=[last])
-            (early,) = call(
-                add_two, [eighth(n_early)], (early, to_hid(early, 1), []), "early_line", after=[keep]
-            )
-            (feed_parts,) = call(
-                split_chips, [[eighth(n_feed)] * 4], (keep, to_core(send_feed)), "feed_chips", after=[early]
-            )
-            last = feed_parts[0]
+            (early,) = call(add_two, [side], (early, to_hid(other, 2), []), "early_line", after=[last])
+            (early,) = call(add_two, [side], (early, to_hid(early, 1), []), "early_line")
+            (pair,) = call(
+                stack_up, [struct((4 * rows, 2 * width), BF)], ([pair, to_hid(pair, 1)],), "pair_stack",
+                after=[early],
+            )
             half = struct((rows * 2, width), BF)
             late, mine, twin = call(
-                add_up_more, [eighth(n_late), half, half], (late,), "late_plane", after=[last]
-            )
-            feed_parts = to_chips(feed_parts)
+                add_up_more, [eighth(n_late), half, half], (late,), "late_plane", after=[pair]
+            )
+            pairs = [pair] + [to_chip(pair, m) for m in (1, 2, 3)]
             (late,) = call(add_two, [eighth(n_late)], (late, to_hid(late, 1), []), "late_line")
-            (feed_own,) = call(add_up, [eighth(n_feed)], (feed_parts,), "feed_plane", after=[late])
             (early,) = call(
-                add_two,
-                [struct(((n_early + n_feed) // 8, width), BF)],
-                (early, to_hid(early, 2), [feed_own]),
-                "early_line",
-            )
-            last = early
+                join_sides, [eighth(n_early)], (early, to_hid(early, 2)), "early_line", spot=spot, after=[late]
+            )
+            (pair,) = call(
+                stack_up, [struct((16 * rows, 2 * width), BF)], (pairs,), "pair_stack", after=[early]
+            )
+            last = pair
             early = [early] + [to_chip(early, m) for m in (1, 2, 3)]
             edge_gradient, last = call(
                 edge_end(rows, fanout, step),
@@ -962,19 +1064,22 @@
                 add_two, [eighth(n_late)], (late, to_hid(late, 2), []), "late_line", after=[last]
             )
             (early,) = call(
-                stack_up,
-                [struct(((n_early + n_feed) // 2, width), BF)],
-                (early,),
-                "early_stack",
-                after=[late],
+                stack_up, [struct((n_early // 2, width), BF)], (early,), "early_stack", after=[late]
             )
             early = [early, to_core(early)]
             late = [late] + [to_chip(late, m) for m in (1, 2, 3)]
+            pairs = [pair, to_core(pair)]
         else:
             late = [lax.psum(late.astype(F32), ("res", "hid"))]
             early = [early]
             pairs = [lax.all_gather(pair, "hid", axis=0, tiled=True)]
-            (feed_pay,) = feed_grads_of(pairs, [node])
+            expand_grad, reduce_grad = call(
+                feed_weights,
+                [struct((width, share), F32), struct((share, width), F32)],
+                (pairs, *feed_own),
+                "feed_weights",
+                after=[node],
+            )
             returned = exchange(slot)
             (edge_gradient,) = call(
                 edge_end(rows, fanout, step), [final(n_edges, edge_width)], (edge_grad, first_low, mf), "edge_end"
@@ -984,39 +1089,59 @@
             )
         (
             edge_first_grad, edge_second_grad, edge_third_grad, third_grad, vec, edge_vecs, expand_bias_grad,
-            feed_grads, last,
+            last,
         ) = call(
             unpack_early,
             [
                 final(edge_width, ef.shape[1]), final(edge_width, edge_width), final(edge_width, edge_width),
                 final(hidden, width), [final(1, width)] * 6, [final(1, edge_width)] * 5, final(1, share),
-                [final(width, share), final(share, width)] if tuned else [],
             ],
             (early,),
             "unpack_early",
-            [pltpu.VMEM((n_early, width), F32), pltpu.VMEM((n_feed, width), F32)],
+            [pltpu.VMEM((n_early, width), F32)],
             limit=16,
             spot=spot,
             token=True,
         )
         if tuned:
+            expand_grad, reduce_grad = call(
+                feed_weights,
+                [struct((width, share), F32), struct((share, width), F32)],
+                (pairs[:1], *feed_own),
+                "feed_weights",
+                after=[last],
+            )
             (late,) = call(
-                stack_up, [struct((n_late // 2, width), BF)], (late,), "late_stack", after=[last]
-            )
+                stack_up, [struct((n_late // 2, width), BF)], (late,), "late_stack", after=[expand_grad]
+            )
+            last = late
             late = [late, to_core(late)]
+            expand_grad, reduce_grad, last = call(
+                feed_weights_more,
+                [Final(width, share), Final(share, width)],
+                (pairs[1:], *feed_own, expand_grad, reduce_grad),
+                "feed_weights_more",
+                after=[last],
+                token=True,
+            )
+            last = [last]
+        else:
+            last = []
+        c = mf.shape[0]
         first_weight_grad, second_weight_grad, message_vec = call(
             unpack_late,
-            [final(*mf.shape), final(hidden, hidden), [final(1, hidden)] * 2],
+            [
+                Cut(n_late, width, c),
+                Cut(n_late, width, c + hidden, c),
+                [Cut(n_late, width, c + hidden + k + 1, c + hidden + k) for k in range(2)],
+            ],
             (late,),
             "unpack_late",
-            [pltpu.VMEM((n_late, width), F32)],
-            limit=16,
             spot=spot,
-        )
-        if tuned:
-            expand_grad, reduce_grad = feed_grads
-        else:
-            expand_grad, reduce_grad = [lax.psum(v.astype(F32), "res") for v in feed_pay]
+            after=last,
+        )
+        if not tuned:
+            expand_grad, reduce_grad = [lax.psum(v, "res") for v in (expand_grad, reduce_grad)]
         vec, edge_vecs, message_vec = [[v[0] for v in group] for group in (vec, edge_vecs, message_vec)]
 
         back = lambda v: v.reshape(fanout, rows, edge_width).transpose(1, 0, 2)

time: 178 us -> 164 us (0.921)
  waiting for transfers between devices: 52.6 us -> 35.9 us
  starting transfers between devices: 71.4 us -> 79 us
  Pallas kernels: 50.8 us -> 47.5 us
    ppermute x30 -> x31, waiting for transfers between devices: 27.4 us -> 14 us  [to_chip(): return lax.ppermute(v, 'res', [(i, i ^ 2 * m) for i in range(n_res)])]
    ppermute x9 -> x16, starting transfers between devices: 12.4 us -> 18.5 us  [to_hid(): return lax.ppermute(v, 'hid', [(i, i ^ m) for i in range(n_hid)])]
    ppermute x23 -> x17, waiting for transfers between devices: 10.5 us -> 5.21 us  [to_core(): return lax.ppermute(v, 'res', pair)]
    pallas_call x34 -> x38, Pallas kernels: 50.8 us -> 47.5 us  [call(): pl.pallas_call(run, out_shape=jax.tree.unflatten(out_tree, shapes), in_sp...]
    ppermute x9 -> x16, waiting for transfers between devices: 14.8 us -> 16.7 us  [to_hid(): return lax.ppermute(v, 'hid', [(i, i ^ m) for i in range(n_hid)])]
    ppermute x23 -> x17, starting transfers between devices: 29.8 us -> 31.6 us  [to_core(): return lax.ppermute(v, 'res', pair)]
    ppermute x30 -> x31, starting transfers between devices: 29.1 us -> 29 us  [to_chip(): return lax.ppermute(v, 'res', [(i, i ^ 2 * m) for i in range(n_res)])]
  transfers between devices with their start and end apart: 62 -> 64, of which waited for: 24 -> 22; matrix products, arithmetic and copies ran while one was open for 0% -> 0% of each run, Pallas kernels for 10% -> 14%
where the time goes in v3:
time: 164 us
  starting transfers between devices  79 us (48%)
  Pallas kernels  47.5 us (29%)
  waiting for transfers between devices  35.9 us (22%)
    pallas_call x38, Pallas kernels, call(): pl.pallas_call(run, out_shape=jax.tree.unflatten(out_tree, shapes), in_sp...  47.5 us
    ppermute x17, starting transfers between devices, to_core(): return lax.ppermute(v, 'res', pair)  31.6 us
    ppermute x31, starting transfers between devices, to_chip(): return lax.ppermute(v, 'res', [(i, i ^ 2 * m) for i in range(n_res)])  29 us
    ppermute x16, starting transfers between devices, to_hid(): return lax.ppermute(v, 'hid', [(i, i ^ m) for i in range(n_hid)])  18.5 us
    ppermute x16, waiting for transfers between devices, to_hid(): return lax.ppermute(v, 'hid', [(i, i ^ m) for i in range(n_hid)])  16.7 us
    ppermute x31, waiting for transfers between devices, to_chip(): return lax.ppermute(v, 'res', [(i, i ^ 2 * m) for i in range(n_res)])  14 us
    ppermute x17, waiting for transfers between devices, to_core(): return lax.ppermute(v, 'res', pair)  5.21 us
  transfers between devices with their start and end apart: 64, of which 22 were waited for; matrix products, arithmetic and copies ran while one was open for 0% of the time, Pallas kernels for 14%

profile of v3, /device:TPU:1, one launch (start us, length us, event | category | flops | bytes accessed | tf_op | source)
XLA Modules:
  0.0 164.0 jit_solution(9529797266413854932)
XLA Ops:
  0.8 2.1 %prepare_send.1 = (bf16[32,512]{1,0:T(8,128)(2,1)S(1)}, bf16[32,512]{1,0:T(8,128)(2,1)S(1)}, bf16[32,512]{1,0:T(8,128)(2,1)S(1)}, bf16[32,512]{1,0:T(8,128)(2,1)...) custom-call(s32[4]{0:T(128)S(1)} %pad_add_fusion.refs_0_, s32[8,16]{1,0:T(8,128)} %bitcast.59, ...), custom_call_target="tpu_custom_call" | custom-call | tf_op jit(solution)/shard_map/prepare_send/pallas_call | solution.py:166
  2.9 2.2 %collective-permute-start.4 = (bf16[144,512]{1,0:T(8,128)(2,1)S(1)}, bf16[144,512]{1,0:T(8,128)(2,1)S(1)}, u32[]{:S(2)}, u32[]{:S(2)}) collective-permute-start(bf16[144,512]{1,0:T(8,128)(2,1)S(1)} %get-tuple-element.154), channel_id=1, source_target_pairs={{0,1},{1,0},{2,3},{3,2},{4,5},{5,4},{6,7},{7,6},{8,9},{9,8},{10,11... | collective-permute-start | bytes 442376 | tf_op jit(solution)/shard_map/ppermute | solution.py:256
  5.1 2.3 %collective-permute-start.5 = (bf16[144,512]{1,0:T(8,128)(2,1)S(1)}, bf16[144,512]{1,0:T(8,128)(2,1)S(1)}, u32[]{:S(2)}, u32[]{:S(2)}) collective-permute-start(bf16[144,512]{1,0:T(8,128)(2,1)S(1)} %get-tuple-element.154), channel_id=1, source_target_pairs={{0,2},{1,3},{2,0},{3,1},{4,6},{5,7},{6,4},{7,5},{8,10},{9,11},{10,... | collective-permute-start | bytes 442376 | tf_op jit(solution)/shard_map/ppermute | solution.py:256
  10.5 2.2 %collective-permute-start.2 = (bf16[32,512]{1,0:T(8,128)(2,1)S(1)}, bf16[32,512]{1,0:T(8,128)(2,1)S(1)}, u32[]{:S(2)}, u32[]{:S(2)}) collective-permute-start(bf16[32,512]{1,0:T(8,128)(2,1)S(1)} %get-tuple-element.147), channel_id=1, source_target_pairs={{0,24},{4,28},{8,16},{12,20},{16,8},{20,12},{24,0},{28,4},{1,25},{... | collective-permute-start | bytes 98312 | tf_op jit(solution)/shard_map/ppermute | solution.py:250
  12.6 2.6 %prepare_rest.1 = (bf16[1920,128]{1,0:T(8,128)(2,1)S(1)}, f32[32,1]{1,0:T(8,128)S(1)}, f32[8,512]{1,0:T(8,128)S(1)}, f32[8,192]{1,0:T(8,128)S(1)}, bf16[1920,192]{1,0:T(8,128)(2,1)S(1)}) custom-call(s32[4]{0:T(128)S(1)} %pad_add_fusion.refs_0_, s32[32,60]{1,0:T(8,128)} %refs_1_.5, s32[1,32]{1,0:T(1,128)} %bitcast.73, f32[1,512]{1,0:T(1,128)} %bitcast.60, ...), custom_call_target="tpu_custom_call" | custom-call | tf_op jit(solution)/shard_map/prepare_rest/pallas_call | solution.py:166
  15.3 2.7 %collective-permute-start.3 = (bf16[64,512]{1,0:T(8,128)(2,1)S(1)}, bf16[64,512]{1,0:T(8,128)(2,1)S(1)}, u32[]{:S(2)}, u32[]{:S(2)}) collective-permute-start(bf16[64,512]{1,0:T(8,128)(2,1)S(1)} %get-tuple-element.150), channel_id=1, source_target_pairs={{0,4},{4,0},{8,12},{12,8},{16,20},{20,16},{24,28},{28,24},{1,5},{5... | collective-permute-start | bytes 196616 | tf_op jit(solution)/shard_map/ppermute | solution.py:253
  21.2 3.6 %message_one.1 = (f32[32,512]{1,0:T(8,128)S(1)}, bf16[32,512]{1,0:T(8,128)(2,1)S(1)}) custom-call(bf16[64,512]{1,0:T(8,128)(2,1)S(1)} %get-tuple-element.149.refs_2_.refs_0__0_, bf16[64,512]{1,0:T(8,128)(2,1)S(1)} %collective-permute-done.3.refs_3_.refs_0__1_, bf16[32,512]{1,0:T(8,128)(2,1)S(1)} %copy-done.9, ...), custom_call_target="tpu_custom_call" | custom-call | tf_op jit(solution)/shard_map/message_one/pallas_call | solution.py:166
  24.8 1.7 %collective-permute-start.7 = (bf16[32,512]{1,0:T(8,128)(2,1)S(1)}, bf16[32,512]{1,0:T(8,128)(2,1)S(1)}, u32[]{:S(2)}, u32[]{:S(2)}) collective-permute-start(bf16[32,512]{1,0:T(8,128)(2,1)S(1)} %get-tuple-element.156.refs_0__0_), channel_id=1, source_target_pairs={{0,1},{1,0},{2,3},{3,2},{4,5},{5,4},{6,7},{7,6},{8,9},{9,8},{10,11... | collective-permute-start | bytes 98312 | tf_op jit(solution)/shard_map/ppermute | solution.py:256
  26.5 2.0 %collective-permute-start.8 = (bf16[32,512]{1,0:T(8,128)(2,1)S(1)}, bf16[32,512]{1,0:T(8,128)(2,1)S(1)}, u32[]{:S(2)}, u32[]{:S(2)}) collective-permute-start(bf16[32,512]{1,0:T(8,128)(2,1)S(1)} %get-tuple-element.156.refs_0__0_), channel_id=1, source_target_pairs={{0,2},{1,3},{2,0},{3,1},{4,6},{5,7},{6,4},{7,5},{8,10},{9,11},{10,... | collective-permute-start | bytes 98312 | tf_op jit(solution)/shard_map/ppermute | solution.py:256
  28.9 1.3 collective-permute-done.8.refs_0__2_
  30.2 3.3 %collective-permute-done.9.refs_0__3_ = bf16[32,512]{1,0:T(8,128)(2,1)S(1)} collective-permute-done((bf16[32,512]{1,0:T(8,128)(2,1)S(1)}, bf16[32,512]{1,0:T(8,128)(2,1)S(1)}, u32[]{:S(2)}, u32[]{:S(2)}) %collective-permute-start.9) | collective-permute-done | bytes 32800 | tf_op jit(solution)/shard_map/ppermute | solution.py:256
  34.7 1.6 collective-permute-start.11
  36.3 2.0 %collective-permute-start.12 = (bf16[32,512]{1,0:T(8,128)(2,1)S(1)}, bf16[32,512]{1,0:T(8,128)(2,1)S(1)}, u32[]{:S(2)}, u32[]{:S(2)}) collective-permute-start(bf16[32,512]{1,0:T(8,128)(2,1)S(1)} %get-tuple-element.160), channel_id=1, source_target_pairs={{0,3},{1,2},{2,1},{3,0},{4,7},{5,6},{6,5},{7,4},{8,11},{9,10},{10,... | collective-permute-start | bytes 98312 | tf_op jit(solution)/shard_map/ppermute | solution.py:256
  38.4 2.5 %collective-permute-done.12.refs_1__3_ = bf16[32,512]{1,0:T(8,128)(2,1)S(1)} collective-permute-done((bf16[32,512]{1,0:T(8,128)(2,1)S(1)}, bf16[32,512]{1,0:T(8,128)(2,1)S(1)}, u32[]{:S(2)}, u32[]{:S(2)}) %collective-permute-start.12) | collective-permute-done | bytes 32800 | tf_op jit(solution)/shard_map/ppermute | solution.py:256
  41.3 4.5 %collective-permute-start.24 = (bf16[576,1536]{1,0:T(8,128)(2,1)S(1)}, bf16[576,1536]{1,0:T(8,128)(2,1)S(1)}, u32[]{:S(2)}, u32[]{:S(2)}) collective-permute-start(bf16[576,1536]{1,0:T(8,128)(2,1)S(1)} %stack_weights.1.refs_1__0_), channel_id=1, source_target_pairs={{0,4},{4,0},{8,12},{12,8},{16,20},{20,16},{24,28},{28,24},{1,5},{5... | collective-permute-start | bytes 5308424 | tf_op jit(solution)/shard_map/ppermute | solution.py:253
  49.9 1.5 collective-permute-start.18
  52.0 1.8 %collective-permute-start.19 = (bf16[32,512]{1,0:T(8,128)(2,1)S(1)}, bf16[32,512]{1,0:T(8,128)(2,1)S(1)}, u32[]{:S(2)}, u32[]{:S(2)}) collective-permute-start(bf16[32,512]{1,0:T(8,128)(2,1)S(1)} %collective-permute-done.15.refs_0__3_), channel_id=1, source_target_pairs={{0,4},{4,0},{8,12},{12,8},{16,20},{20,16},{24,28},{28,24},{1,5},{5... | collective-permute-start | bytes 98312 | tf_op jit(solution)/shard_map/ppermute | solution.py:253
  54.7 7.4 %layer_two.1 = (f32[1920,192]{1,0:T(8,128)S(1)}, bf16[1920,512]{1,0:T(8,128)(2,1)S(1)}, bf16[1920,512]{1,0:T(8,128)(2,1)S(1)}, bf16[1920,512]{1,0:T(8,128)(2,1)S...) custom-call(bf16[32,512]{1,0:T(8,128)(2,1)S(1)} %get-tuple-element.1, ...), custom_call_target="tpu_custom_call" | custom-call | tf_op jit(solution)/shard_map/layer_two/pallas_call | solution.py:166
  62.1 2.0 %feed_two.1 = (bf16[4,32,512]{2,1,0:T(8,128)(2,1)S(1)}, f32[32,512]{1,0:T(8,128)S(1)}, f32[32,512]{1,0:T(8,128)}, bf16[32,512]{1,0:T(8,128)(2,1)S(1)}, bf16[32,5...) custom-call(f32[32,512]{1,0:T(8,128)S(1)} %get-tuple-element.171.ref, ...), custom_call_target="tpu_custom_call" | custom-call | tf_op jit(solution)/shard_map/feed_two/pallas_call | solution.py:166
  64.6 2.2 %collective-permute-start.27 = (bf16[32,512]{1,0:T(8,128)(2,1)S(1)}, bf16[32,512]{1,0:T(8,128)(2,1)S(1)}, u32[]{:S(2)}, u32[]{:S(2)}) collective-permute-start(bf16[32,512]{1,0:T(8,128)(2,1)S(1)} %get-tuple-element.176), channel_id=1, source_target_pairs={{0,24},{4,28},{8,16},{12,20},{16,8},{20,12},{24,0},{28,4},{1,25},{... | collective-permute-start | bytes 98312 | tf_op jit(solution)/shard_map/ppermute | solution.py:250
  71.2 5.8 %edge_turn.1 = (f32[1920,192]{1,0:T(8,128)}, f32[1920,192]{1,0:T(8,128)S(1)}, bf16[1920,192]{1,0:T(8,128)(2,1)S(1)}, bf16[1920,192]{1,0:T(8,128)(2,1)S(1)}, bf16...) custom-call(bf16[32,512]{1,0:T(8,128)(2,1)S(1)} %get-tuple-element.1, ...), custom_call_target="tpu_custom_call" | custom-call | tf_op jit(solution)/shard_map/edge_turn/pallas_call | solution.py:166
  80.8 2.1 %collective-permute-done.34.refs_0__3_ = bf16[32,192]{1,0:T(8,128)(2,1)S(1)} collective-permute-done((bf16[32,192]{1,0:T(8,128)(2,1)S(1)}, bf16[32,192]{1,0:T(8,128)(2,1)S(1)}, u32[]{:S(2)}, u32[]{:S(2)}) %collective-permute-start.34) | collective-permute-done | bytes 12320 | tf_op jit(solution)/shard_map/ppermute | solution.py:250
  82.9 2.1 %collective-permute-start.35 = (bf16[64,192]{1,0:T(8,128)(2,1)S(1)}, bf16[64,192]{1,0:T(8,128)(2,1)S(1)}, u32[]{:S(2)}, u32[]{:S(2)}) collective-permute-start(bf16[64,192]{1,0:T(8,128)(2,1)S(1)} %get-tuple-element.191), channel_id=1, source_target_pairs={{0,4},{4,0},{8,12},{12,8},{16,20},{20,16},{24,28},{28,24},{1,5},{5... | collective-permute-start | bytes 73736 | tf_op jit(solution)/shard_map/ppermute | solution.py:253
  85.9 3.0 %node_turn.1 = (bf16[32,1024]{1,0:T(8,128)(2,1)S(1)}, f32[32,512]{1,0:T(8,128)S(1)}, f32[32,512]{1,0:T(8,128)S(1)}, bf16[640,512]{1,0:T(8,128)(2,1)S(1)}, bf16[640,512]{1,0:T(8,128)(2,1)S(1)}) custom-call(s32[4]{0:T(128)S(1)} %pad_add_fusion.refs_0_, bf16[64,192]{1,0:T(8,128)(2,1)S(1)} %get-tuple-element.190.refs_1__0_, ...), custom_call_target="tpu_custom_call" | custom-call | tf_op jit(solution)/shard_map/node_turn/pallas_call | solution.py:166
  89.2 1.3 message_second.1
  91.7 2.2 %collective-permute-start.39 = (bf16[160,512]{1,0:T(8,128)(2,1)S(1)}, bf16[160,512]{1,0:T(8,128)(2,1)S(1)}, u32[]{:S(2)}, u32[]{:S(2)}) collective-permute-start(bf16[160,512]{1,0:T(8,128)(2,1)S(1)} %get-tuple-element.207), channel_id=1, source_target_pairs={{0,24},{4,28},{8,16},{12,20},{16,8},{20,12},{24,0},{28,4},{1,25},{... | collective-permute-start | bytes 491528 | tf_op jit(solution)/shard_map/ppermute | solution.py:250
  93.9 2.6 %message_first.1 = (bf16[1920,512]{1,0:T(8,128)(2,1)S(1)}, bf16[32,512]{1,0:T(8,128)(2,1)S(1)}, bf16[32,512]{1,0:T(8,128)(2,1)S(1)}, bf16[32,512]{1,0:T(8,128)(2...) custom-call(bf16[32,512]{1,0:T(8,128)(2,1)S(1)} %get-tuple-element.162.refs_0__0_, ...), custom_call_target="tpu_custom_call" | custom-call | tf_op jit(solution)/shard_map/message_first/pallas_call | solution.py:166
  96.5 2.2 %collective-permute-done.40.refs_0__1_ = bf16[32,1024]{1,0:T(8,128)(2,1)S(1)} collective-permute-done((bf16[32,1024]{1,0:T(8,128)(2,1)S(1)}, bf16[32,1024]{1,0:T(8,128)(2,1)S(1)}, u32[]{:S(2)}, u32[]{:S(2)}) %collective-permute-start.40) | collective-permute-done | bytes 65568 | tf_op jit(solution)/shard_map/ppermute | solution.py:256
  98.7 1.4 collective-permute-done.39.refs_1__3_
  100.9 1.5 collective-permute-start.41
  102.4 2.1 %collective-permute-done.41.refs_1_ = bf16[896,512]{1,0:T(8,128)(2,1)S(1)} collective-permute-done((bf16[896,512]{1,0:T(8,128)(2,1)S(1)}, bf16[896,512]{1,0:T(8,128)(2,1)S(1)}, u32[]{:S(2)}, u32[]{:S(2)}) %collective-permute-start.41) | collective-permute-done | bytes 917536 | tf_op jit(solution)/shard_map/ppermute | solution.py:253
  104.8 1.3 collective-permute-start.42
  107.5 2.4 %collective-permute-start.45 = (bf16[64,1024]{1,0:T(8,128)(2,1)S(1)}, bf16[64,1024]{1,0:T(8,128)(2,1)S(1)}, u32[]{:S(2)}, u32[]{:S(2)}) collective-permute-start(bf16[64,1024]{1,0:T(8,128)(2,1)S(1)} %pair_stack.3.refs_3_.refs_0__0_), channel_id=1, source_target_pairs={{0,1},{1,0},{2,3},{3,2},{4,5},{5,4},{6,7},{7,6},{8,9},{9,8},{10,11... | collective-permute-start | bytes 393224 | tf_op jit(solution)/shard_map/ppermute | solution.py:256
  109.9 3.2 %collective-permute-done.46.refs_1_ = bf16[160,256]{1,0:T(8,128)(2,1)S(1)} collective-permute-done((bf16[160,256]{1,0:T(8,128)(2,1)S(1)}, bf16[160,256]{1,0:T(8,128)(2,1)S(1)}, u32[]{:S(2)}, u32[]{:S(2)}) %collective-permute-start.46) | collective-permute-done | bytes 81952 | tf_op jit(solution)/shard_map/ppermute | solution.py:256
  113.2 3.6 %collective-permute-done.47.refs_1_ = bf16[160,256]{1,0:T(8,128)(2,1)S(1)} collective-permute-done((bf16[160,256]{1,0:T(8,128)(2,1)S(1)}, bf16[160,256]{1,0:T(8,128)(2,1)S(1)}, u32[]{:S(2)}, u32[]{:S(2)}) %collective-permute-start.47) | collective-permute-done | bytes 81952 | tf_op jit(solution)/shard_map/ppermute | solution.py:256
  116.9 1.8 %collective-permute-done.44.refs_0__3_ = bf16[256,512]{1,0:T(8,128)(2,1)S(1)} collective-permute-done((bf16[256,512]{1,0:T(8,128)(2,1)S(1)}, bf16[256,512]{1,0:T(8,128)(2,1)S(1)}, u32[]{:S(2)}, u32[]{:S(2)}) %collective-permute-start.44) | collective-permute-done | bytes 262176 | tf_op jit(solution)/shard_map/ppermute | solution.py:250
  121.5 2.4 %collective-permute-start.52 = (bf16[160,256]{1,0:T(8,128)(2,1)S(1)}, bf16[160,256]{1,0:T(8,128)(2,1)S(1)}, u32[]{:S(2)}, u32[]{:S(2)}) collective-permute-start(bf16[160,256]{1,0:T(8,128)(2,1)S(1)} %early_line.4.refs_1_), channel_id=1, source_target_pairs={{0,2},{1,3},{2,0},{3,1},{4,6},{5,7},{6,4},{7,5},{8,10},{9,11},{10,... | collective-permute-start | bytes 245768 | tf_op jit(solution)/shard_map/ppermute | solution.py:256
  124.2 1.3 collective-permute-start.54
  127.0 1.5 collective-permute-start.59
  129.1 2.1 %collective-permute-done.51.refs_0__3_ = bf16[128,1024]{1,0:T(8,128)(2,1)S(1)} collective-permute-done((bf16[128,1024]{1,0:T(8,128)(2,1)S(1)}, bf16[128,1024]{1,0:T(8,128)(2,1)S(1)}, u32[]{:S(2)}, u32[]{:S(2)}) %collective-permute-start.51) | collective-permute-done | bytes 262176 | tf_op jit(solution)/shard_map/ppermute | solution.py:250
  131.2 9.0 %collective-permute-start.48 = (bf16[64,512]{1,0:T(8,128)(2,1)S(1)}, bf16[64,512]{1,0:T(8,128)(2,1)S(1)}, u32[]{:S(2)}, u32[]{:S(2)}) collective-permute-start(bf16[64,512]{1,0:T(8,128)(2,1)S(1)} %get-tuple-element.227), channel_id=1, source_target_pairs={{0,4},{4,0},{8,12},{12,8},{16,20},{20,16},{24,28},{28,24},{1,5},{5... | collective-permute-start | bytes 196616 | tf_op jit(solution)/shard_map/ppermute | solution.py:253
  140.3 2.0 %edge_end.1 = (f32[1920,192]{1,0:T(8,128)}, f32[8,128]{1,0:T(8,128)S(1)}) custom-call(f32[1920,192]{1,0:T(8,128)S(1)} %get-tuple-element.229.refs_0_, bf16[1920,512]{1,0:T(8,128)(2,1)S(1)} %get-tuple-element.230.refs_1_, bf16[1216,512]{1,0:T(8,128)(2,1)S(1)} %copy-done, bf16[512,1024]{1,0:T(8,128)(2,1)S(1)} %pair_stack.5.refs_3_.refs_0__0_), custom_call_target="tpu_custom_call" | custom-call | tf_op jit(solution)/shard_map/edge_end/pallas_call | solution.py:166
  148.2 2.4 %unpack_early.1 = (f32[192,1216]{1,0:T(8,128)}, f32[192,192]{1,0:T(8,128)}, f32[192,192]{1,0:T(8,128)}, f32[512,512]{1,0:T(8,128)}, f32[1,512]{1,0:T(1,128)}, /*...) custom-call(s32[4]{0:T(128)S(1)} %pad_add_fusion.refs_0_, ...), custom_call_target="tpu_custom_call" | custom-call | tf_op jit(solution)/shard_map/unpack_early/pallas_call | solution.py:166
  150.6 1.4 feed_weights.1
  152.6 4.7 %collective-permute-done.57.refs_0__3_ = bf16[224,512]{1,0:T(8,128)(2,1)S(1)} collective-permute-done((bf16[224,512]{1,0:T(8,128)(2,1)S(1)}, bf16[224,512]{1,0:T(8,128)(2,1)S(1)}, u32[]{:S(2)}, u32[]{:S(2)}) %collective-permute-start.57) | collective-permute-done | bytes 229408 | tf_op jit(solution)/shard_map/ppermute | solution.py:250
  157.4 1.3 collective-permute-start.62
  158.7 2.5 %feed_weights_more.1 = (f32[512,512]{1,0:T(8,128)}, f32[512,512]{1,0:T(8,128)}, f32[8,128]{1,0:T(8,128)S(1)}) custom-call(bf16[512,1024]{1,0:T(8,128)(2,1)S(1)} %collective-permute-done.63.refs_0__0_, bf16[512,512]{1,0:T(8,128)(2,1)S(1)} %copy-done.1, f32[1,512]{1,0:T(1,128)S(1)} %bitcast.57, bf16[512,512]{1,0:T(8,128)(2,1)S(1)} %copy-done.2, ...), custom_call_target="tpu_custom_call" | custom-call | tf_op jit(solution)/shard_map/feed_weights_more/pallas_call | solution.py:166
  161.2 2.6 %unpack_late.1 = (f32[1216,512]{1,0:T(8,128)}, f32[512,512]{1,0:T(8,128)}, f32[1,512]{1,0:T(1,128)}, f32[1,512]{1,0:T(1,128)}) custom-call(s32[4]{0:T(128)S(1)} %pad_add_fusion.refs_0_, bf16[896,512]{1,0:T(8,128)(2,1)S(1)} %late_stack.1.refs_6_.refs_1__0_, bf16[896,512]{1,0:T(8,128)(2,1)S(1)} %collective-permute-done.62.refs_1__1_, ...), custom_call_target="tpu_custom_call" | custom-call | tf_op jit(solution)/shard_map/unpack_late/pallas_call | solution.py:166
  (143 shorter events, 39.6 us)
Async XLA Ops:
  2.9 15.9 %collective-permute-start.4 = (bf16[144,512]{1,0:T(8,128)(2,1)S(1)}, bf16[144,512]{1,0:T(8,128)(2,1)S(1)}, u32[]{:S(2)}, u32[]{:S(2)}) collective-permute-start(bf16[144,512]{1,0:T(8,128)(2,1)S(1)} %get-tuple-element.154), channel_id=1, source_target_pairs={{0,1},{1,0},{2,3},{3,2},{4,5},{5,4},{6,7},{7,6},{8,9},{9,8},{10,11... | collective-permute-start | bytes 442376 | tf_op jit(solution)/shard_map/ppermute | solution.py:256
  5.1 13.7 %collective-permute-start.5 = (bf16[144,512]{1,0:T(8,128)(2,1)S(1)}, bf16[144,512]{1,0:T(8,128)(2,1)S(1)}, u32[]{:S(2)}, u32[]{:S(2)}) collective-permute-start(bf16[144,512]{1,0:T(8,128)(2,1)S(1)} %get-tuple-element.154), channel_id=1, source_target_pairs={{0,2},{1,3},{2,0},{3,1},{4,6},{5,7},{6,4},{7,5},{8,10},{9,11},{10,... | collective-permute-start | bytes 442376 | tf_op jit(solution)/shard_map/ppermute | solution.py:256
  7.4 11.4 %collective-permute-start.6 = (bf16[144,512]{1,0:T(8,128)(2,1)S(1)}, bf16[144,512]{1,0:T(8,128)(2,1)S(1)}, u32[]{:S(2)}, u32[]{:S(2)}) collective-permute-start(bf16[144,512]{1,0:T(8,128)(2,1)S(1)} %get-tuple-element.154), channel_id=1, source_target_pairs={{0,3},{1,2},{2,1},{3,0},{4,7},{5,6},{6,5},{7,4},{8,11},{9,10},{10,... | collective-permute-start | bytes 442376 | tf_op jit(solution)/shard_map/ppermute | solution.py:256
  8.6 6.6 %collective-permute-start.1 = (bf16[32,512]{1,0:T(8,128)(2,1)S(1)}, bf16[32,512]{1,0:T(8,128)(2,1)S(1)}, u32[]{:S(2)}, u32[]{:S(2)}) collective-permute-start(bf16[32,512]{1,0:T(8,128)(2,1)S(1)} %get-tuple-element.146), channel_id=1, source_target_pairs={{0,16},{4,20},{8,24},{12,28},{16,0},{20,4},{24,8},{28,12},{1,17},{... | collective-permute-start | bytes 98312 | tf_op jit(solution)/shard_map/ppermute | solution.py:250
  10.5 4.8 %collective-permute-start.2 = (bf16[32,512]{1,0:T(8,128)(2,1)S(1)}, bf16[32,512]{1,0:T(8,128)(2,1)S(1)}, u32[]{:S(2)}, u32[]{:S(2)}) collective-permute-start(bf16[32,512]{1,0:T(8,128)(2,1)S(1)} %get-tuple-element.147), channel_id=1, source_target_pairs={{0,24},{4,28},{8,16},{12,20},{16,8},{20,12},{24,0},{28,4},{1,25},{... | collective-permute-start | bytes 98312 | tf_op jit(solution)/shard_map/ppermute | solution.py:250
  18.9 15.1 %collective-permute-start.20 = (bf16[144,1536]{1,0:T(8,128)(2,1)S(1)}, bf16[144,1536]{1,0:T(8,128)(2,1)S(1)}, u32[]{:S(2)}, u32[]{:S(2)}) collective-permute-start(bf16[144,1536]{1,0:T(8,128)(2,1)S(1)} %join_pieces.1.refs_9_.refs_0__0_), channel_id=1, source_target_pairs={{0,8},{4,12},{8,0},{12,4},{16,24},{20,28},{24,16},{28,20},{1,9},{5... | collective-permute-start | bytes 1327112 | tf_op jit(solution)/shard_map/ppermute | solution.py:250
  19.9 14.1 %collective-permute-start.21 = (bf16[144,1536]{1,0:T(8,128)(2,1)S(1)}, bf16[144,1536]{1,0:T(8,128)(2,1)S(1)}, u32[]{:S(2)}, u32[]{:S(2)}) collective-permute-start(bf16[144,1536]{1,0:T(8,128)(2,1)S(1)} %join_pieces.1.refs_9_.refs_0__0_), channel_id=1, source_target_pairs={{0,16},{4,20},{8,24},{12,28},{16,0},{20,4},{24,8},{28,12},{1,17},{... | collective-permute-start | bytes 1327112 | tf_op jit(solution)/shard_map/ppermute | solution.py:250
  24.8 4.1 %collective-permute-start.7 = (bf16[32,512]{1,0:T(8,128)(2,1)S(1)}, bf16[32,512]{1,0:T(8,128)(2,1)S(1)}, u32[]{:S(2)}, u32[]{:S(2)}) collective-permute-start(bf16[32,512]{1,0:T(8,128)(2,1)S(1)} %get-tuple-element.156.refs_0__0_), channel_id=1, source_target_pairs={{0,1},{1,0},{2,3},{3,2},{4,5},{5,4},{6,7},{7,6},{8,9},{9,8},{10,11... | collective-permute-start | bytes 98312 | tf_op jit(solution)/shard_map/ppermute | solution.py:256
  26.5 3.7 %collective-permute-start.8 = (bf16[32,512]{1,0:T(8,128)(2,1)S(1)}, bf16[32,512]{1,0:T(8,128)(2,1)S(1)}, u32[]{:S(2)}, u32[]{:S(2)}) collective-permute-start(bf16[32,512]{1,0:T(8,128)(2,1)S(1)} %get-tuple-element.156.refs_0__0_), channel_id=1, source_target_pairs={{0,2},{1,3},{2,0},{3,1},{4,6},{5,7},{6,4},{7,5},{8,10},{9,11},{10,... | collective-permute-start | bytes 98312 | tf_op jit(solution)/shard_map/ppermute | solution.py:256
  28.5 5.0 %collective-permute-start.9 = (bf16[32,512]{1,0:T(8,128)(2,1)S(1)}, bf16[32,512]{1,0:T(8,128)(2,1)S(1)}, u32[]{:S(2)}, u32[]{:S(2)}) collective-permute-start(bf16[32,512]{1,0:T(8,128)(2,1)S(1)} %get-tuple-element.156.refs_0__0_), channel_id=1, source_target_pairs={{0,3},{1,2},{2,1},{3,0},{4,7},{5,6},{6,5},{7,4},{8,11},{9,10},{10,... | collective-permute-start | bytes 98312 | tf_op jit(solution)/shard_map/ppermute | solution.py:256
  34.0 7.2 %collective-permute-start.22 = (bf16[144,768]{1,0:T(8,128)(2,1)S(1)}, bf16[144,768]{1,0:T(8,128)(2,1)S(1)}, u32[]{:S(2)}, u32[]{:S(2)}) collective-permute-start(bf16[144,768]{1,0:T(8,128)(2,1)S(1)} %get-tuple-element.169), channel_id=1, source_target_pairs={{0,16},{4,20},{8,24},{12,28},{16,0},{20,4},{24,8},{28,12},{1,17},{... | collective-permute-start | bytes 663560 | tf_op jit(solution)/shard_map/ppermute | solution.py:250
  34.3 6.9 %collective-permute-start.23 = (bf16[144,768]{1,0:T(8,128)(2,1)S(1)}, bf16[144,768]{1,0:T(8,128)(2,1)S(1)}, u32[]{:S(2)}, u32[]{:S(2)}) collective-permute-start(bf16[144,768]{1,0:T(8,128)(2,1)S(1)} %get-tuple-element.170), channel_id=1, source_target_pairs={{0,8},{4,12},{8,0},{12,4},{16,24},{20,28},{24,16},{28,20},{1,9},{5... | collective-permute-start | bytes 663560 | tf_op jit(solution)/shard_map/ppermute | solution.py:250
  34.7 3.7 %collective-permute-start.11 = (bf16[32,512]{1,0:T(8,128)(2,1)S(1)}, bf16[32,512]{1,0:T(8,128)(2,1)S(1)}, u32[]{:S(2)}, u32[]{:S(2)}) collective-permute-start(bf16[32,512]{1,0:T(8,128)(2,1)S(1)} %get-tuple-element.159), channel_id=1, source_target_pairs={{0,2},{1,3},{2,0},{3,1},{4,6},{5,7},{6,4},{7,5},{8,10},{9,11},{10,... | collective-permute-start | bytes 98312 | tf_op jit(solution)/shard_map/ppermute | solution.py:256
  36.3 4.6 %collective-permute-start.12 = (bf16[32,512]{1,0:T(8,128)(2,1)S(1)}, bf16[32,512]{1,0:T(8,128)(2,1)S(1)}, u32[]{:S(2)}, u32[]{:S(2)}) collective-permute-start(bf16[32,512]{1,0:T(8,128)(2,1)S(1)} %get-tuple-element.160), channel_id=1, source_target_pairs={{0,3},{1,2},{2,1},{3,0},{4,7},{5,6},{6,5},{7,4},{8,11},{9,10},{10,... | collective-permute-start | bytes 98312 | tf_op jit(solution)/shard_map/ppermute | solution.py:256
  41.3 12.4 %collective-permute-start.24 = (bf16[576,1536]{1,0:T(8,128)(2,1)S(1)}, bf16[576,1536]{1,0:T(8,128)(2,1)S(1)}, u32[]{:S(2)}, u32[]{:S(2)}) collective-permute-start(bf16[576,1536]{1,0:T(8,128)(2,1)S(1)} %stack_weights.1.refs_1__0_), channel_id=1, source_target_pairs={{0,4},{4,0},{8,12},{12,8},{16,20},{20,16},{24,28},{28,24},{1,5},{5... | collective-permute-start | bytes 5308424 | tf_op jit(solution)/shard_map/ppermute | solution.py:253
  48.3 3.7 %collective-permute-start.15 = (bf16[32,512]{1,0:T(8,128)(2,1)S(1)}, bf16[32,512]{1,0:T(8,128)(2,1)S(1)}, u32[]{:S(2)}, u32[]{:S(2)}) collective-permute-start(bf16[32,512]{1,0:T(8,128)(2,1)S(1)} %get-tuple-element.165), channel_id=1, source_target_pairs={{0,24},{4,28},{8,16},{12,20},{16,8},{20,12},{24,0},{28,4},{1,25},{... | collective-permute-start | bytes 98312 | tf_op jit(solution)/shard_map/ppermute | solution.py:250
  48.5 6.0 %collective-permute-start.16 = (bf16[32,512]{1,0:T(8,128)(2,1)S(1)}, bf16[32,512]{1,0:T(8,128)(2,1)S(1)}, u32[]{:S(2)}, u32[]{:S(2)}) collective-permute-start(bf16[32,512]{1,0:T(8,128)(2,1)S(1)} %get-tuple-element.162.refs_0__0_), channel_id=1, source_target_pairs={{0,4},{4,0},{8,12},{12,8},{16,20},{20,16},{24,28},{28,24},{1,5},{5... | collective-permute-start | bytes 98312 | tf_op jit(solution)/shard_map/ppermute | solution.py:253
  49.5 5.1 %collective-permute-start.17 = (bf16[32,512]{1,0:T(8,128)(2,1)S(1)}, bf16[32,512]{1,0:T(8,128)(2,1)S(1)}, u32[]{:S(2)}, u32[]{:S(2)}) collective-permute-start(bf16[32,512]{1,0:T(8,128)(2,1)S(1)} %collective-permute-done.13.refs_0__1_), channel_id=1, source_target_pairs={{0,4},{4,0},{8,12},{12,8},{16,20},{20,16},{24,28},{28,24},{1,5},{5... | collective-permute-start | bytes 98312 | tf_op jit(solution)/shard_map/ppermute | solution.py:253
  49.9 4.7 %collective-permute-start.18 = (bf16[32,512]{1,0:T(8,128)(2,1)S(1)}, bf16[32,512]{1,0:T(8,128)(2,1)S(1)}, u32[]{:S(2)}, u32[]{:S(2)}) collective-permute-start(bf16[32,512]{1,0:T(8,128)(2,1)S(1)} %collective-permute-done.14.refs_0__2_), channel_id=1, source_target_pairs={{0,4},{4,0},{8,12},{12,8},{16,20},{20,16},{24,28},{28,24},{1,5},{5... | collective-permute-start | bytes 98312 | tf_op jit(solution)/shard_map/ppermute | solution.py:253
  64.1 3.8 %collective-permute-start.25 = (bf16[32,512]{1,0:T(8,128)(2,1)S(1)}, bf16[32,512]{1,0:T(8,128)(2,1)S(1)}, u32[]{:S(2)}, u32[]{:S(2)}) collective-permute-start(bf16[32,512]{1,0:T(8,128)(2,1)S(1)} %get-tuple-element.174), channel_id=1, source_target_pairs={{0,8},{4,12},{8,0},{12,4},{16,24},{20,28},{24,16},{28,20},{1,9},{5... | collective-permute-start | bytes 98312 | tf_op jit(solution)/shard_map/ppermute | solution.py:250
  64.4 4.0 %collective-permute-start.26 = (bf16[32,512]{1,0:T(8,128)(2,1)S(1)}, bf16[32,512]{1,0:T(8,128)(2,1)S(1)}, u32[]{:S(2)}, u32[]{:S(2)}) collective-permute-start(bf16[32,512]{1,0:T(8,128)(2,1)S(1)} %get-tuple-element.175), channel_id=1, source_target_pairs={{0,16},{4,20},{8,24},{12,28},{16,0},{20,4},{24,8},{28,12},{1,17},{... | collective-permute-start | bytes 98312 | tf_op jit(solution)/shard_map/ppermute | solution.py:250
  64.6 4.7 %collective-permute-start.27 = (bf16[32,512]{1,0:T(8,128)(2,1)S(1)}, bf16[32,512]{1,0:T(8,128)(2,1)S(1)}, u32[]{:S(2)}, u32[]{:S(2)}) collective-permute-start(bf16[32,512]{1,0:T(8,128)(2,1)S(1)} %get-tuple-element.176), channel_id=1, source_target_pairs={{0,24},{4,28},{8,16},{12,20},{16,8},{20,12},{24,0},{28,4},{1,25},{... | collective-permute-start | bytes 98312 | tf_op jit(solution)/shard_map/ppermute | solution.py:250
  77.0 3.8 %collective-permute-start.32 = (bf16[32,192]{1,0:T(8,128)(2,1)S(1)}, bf16[32,192]{1,0:T(8,128)(2,1)S(1)}, u32[]{:S(2)}, u32[]{:S(2)}) collective-permute-start(bf16[32,192]{1,0:T(8,128)(2,1)S(1)} %get-tuple-element.181.refs_8__1_), channel_id=1, source_target_pairs={{0,8},{4,12},{8,0},{12,4},{16,24},{20,28},{24,16},{28,20},{1,9},{5... | collective-permute-start | bytes 36872 | tf_op jit(solution)/shard_map/ppermute | solution.py:250
  91.1 7.6 %collective-permute-start.37 = (bf16[160,512]{1,0:T(8,128)(2,1)S(1)}, bf16[160,512]{1,0:T(8,128)(2,1)S(1)}, u32[]{:S(2)}, u32[]{:S(2)}) collective-permute-start(bf16[160,512]{1,0:T(8,128)(2,1)S(1)} %get-tuple-element.205), channel_id=1, source_target_pairs={{0,8},{4,12},{8,0},{12,4},{16,24},{20,28},{24,16},{28,20},{1,9},{5... | collective-permute-start | bytes 491528 | tf_op jit(solution)/shard_map/ppermute | solution.py:250
  91.5 7.2 %collective-permute-start.38 = (bf16[160,512]{1,0:T(8,128)(2,1)S(1)}, bf16[160,512]{1,0:T(8,128)(2,1)S(1)}, u32[]{:S(2)}, u32[]{:S(2)}) collective-permute-start(bf16[160,512]{1,0:T(8,128)(2,1)S(1)} %get-tuple-element.206), channel_id=1, source_target_pairs={{0,16},{4,20},{8,24},{12,28},{16,0},{20,4},{24,8},{28,12},{1,17},{... | collective-permute-start | bytes 491528 | tf_op jit(solution)/shard_map/ppermute | solution.py:250
  91.7 8.5 %collective-permute-start.39 = (bf16[160,512]{1,0:T(8,128)(2,1)S(1)}, bf16[160,512]{1,0:T(8,128)(2,1)S(1)}, u32[]{:S(2)}, u32[]{:S(2)}) collective-permute-start(bf16[160,512]{1,0:T(8,128)(2,1)S(1)} %get-tuple-element.207), channel_id=1, source_target_pairs={{0,24},{4,28},{8,16},{12,20},{16,8},{20,12},{24,0},{28,4},{1,25},{... | collective-permute-start | bytes 491528 | tf_op jit(solution)/shard_map/ppermute | solution.py:250
  93.9 4.8 %collective-permute-start.40 = (bf16[32,1024]{1,0:T(8,128)(2,1)S(1)}, bf16[32,1024]{1,0:T(8,128)(2,1)S(1)}, u32[]{:S(2)}, u32[]{:S(2)}) collective-permute-start(bf16[32,1024]{1,0:T(8,128)(2,1)S(1)} %get-tuple-element.212.refs_0__0_), channel_id=1, source_target_pairs={{0,2},{1,3},{2,0},{3,1},{4,6},{5,7},{6,4},{7,5},{8,10},{9,11},{10,... | collective-permute-start | bytes 196616 | tf_op jit(solution)/shard_map/ppermute | solution.py:256
  104.8 12.1 %collective-permute-start.42 = (bf16[256,512]{1,0:T(8,128)(2,1)S(1)}, bf16[256,512]{1,0:T(8,128)(2,1)S(1)}, u32[]{:S(2)}, u32[]{:S(2)}) collective-permute-start(bf16[256,512]{1,0:T(8,128)(2,1)S(1)} %get-tuple-element.221), channel_id=1, source_target_pairs={{0,8},{4,12},{8,0},{12,4},{16,24},{20,28},{24,16},{28,20},{1,9},{5... | collective-permute-start | bytes 786440 | tf_op jit(solution)/shard_map/ppermute | solution.py:250
  106.0 10.8 %collective-permute-start.43 = (bf16[256,512]{1,0:T(8,128)(2,1)S(1)}, bf16[256,512]{1,0:T(8,128)(2,1)S(1)}, u32[]{:S(2)}, u32[]{:S(2)}) collective-permute-start(bf16[256,512]{1,0:T(8,128)(2,1)S(1)} %get-tuple-element.222), channel_id=1, source_target_pairs={{0,16},{4,20},{8,24},{12,28},{16,0},{20,4},{24,8},{28,12},{1,17},{... | collective-permute-start | bytes 786440 | tf_op jit(solution)/shard_map/ppermute | solution.py:250
  106.3 12.4 %collective-permute-start.44 = (bf16[256,512]{1,0:T(8,128)(2,1)S(1)}, bf16[256,512]{1,0:T(8,128)(2,1)S(1)}, u32[]{:S(2)}, u32[]{:S(2)}) collective-permute-start(bf16[256,512]{1,0:T(8,128)(2,1)S(1)} %get-tuple-element.223), channel_id=1, source_target_pairs={{0,24},{4,28},{8,16},{12,20},{16,8},{20,12},{24,0},{28,4},{1,25},{... | collective-permute-start | bytes 786440 | tf_op jit(solution)/shard_map/ppermute | solution.py:250
  107.5 5.6 %collective-permute-start.46 = (bf16[160,256]{1,0:T(8,128)(2,1)S(1)}, bf16[160,256]{1,0:T(8,128)(2,1)S(1)}, u32[]{:S(2)}, u32[]{:S(2)}) collective-permute-start(bf16[160,256]{1,0:T(8,128)(2,1)S(1)} %get-tuple-element.225), channel_id=1, source_target_pairs={{0,2},{1,3},{2,0},{3,1},{4,6},{5,7},{6,4},{7,5},{8,10},{9,11},{10,... | collective-permute-start | bytes 245768 | tf_op jit(solution)/shard_map/ppermute | solution.py:256
  107.5 9.3 %collective-permute-start.45 = (bf16[64,1024]{1,0:T(8,128)(2,1)S(1)}, bf16[64,1024]{1,0:T(8,128)(2,1)S(1)}, u32[]{:S(2)}, u32[]{:S(2)}) collective-permute-start(bf16[64,1024]{1,0:T(8,128)(2,1)S(1)} %pair_stack.3.refs_3_.refs_0__0_), channel_id=1, source_target_pairs={{0,1},{1,0},{2,3},{3,2},{4,5},{5,4},{6,7},{7,6},{8,9},{9,8},{10,11... | collective-permute-start | bytes 393224 | tf_op jit(solution)/shard_map/ppermute | solution.py:256
  118.8 5.4 %collective-permute-start.53 = (bf16[224,512]{1,0:T(8,128)(2,1)S(1)}, bf16[224,512]{1,0:T(8,128)(2,1)S(1)}, u32[]{:S(2)}, u32[]{:S(2)}) collective-permute-start(bf16[224,512]{1,0:T(8,128)(2,1)S(1)} %get-tuple-element.231.refs_0_), channel_id=1, source_target_pairs={{0,1},{1,0},{2,3},{3,2},{4,5},{5,4},{6,7},{7,6},{8,9},{9,8},{10,11... | collective-permute-start | bytes 688136 | tf_op jit(solution)/shard_map/ppermute | solution.py:256
  118.8 8.2 %collective-permute-start.49 = (bf16[128,1024]{1,0:T(8,128)(2,1)S(1)}, bf16[128,1024]{1,0:T(8,128)(2,1)S(1)}, u32[]{:S(2)}, u32[]{:S(2)}) collective-permute-start(bf16[128,1024]{1,0:T(8,128)(2,1)S(1)} %pair_stack.4.refs_1_.refs_0__0_), channel_id=1, source_target_pairs={{0,8},{4,12},{8,0},{12,4},{16,24},{20,28},{24,16},{28,20},{1,9},{5... | collective-permute-start | bytes 786440 | tf_op jit(solution)/shard_map/ppermute | solution.py:250
  119.4 9.1 %collective-permute-start.50 = (bf16[128,1024]{1,0:T(8,128)(2,1)S(1)}, bf16[128,1024]{1,0:T(8,128)(2,1)S(1)}, u32[]{:S(2)}, u32[]{:S(2)}) collective-permute-start(bf16[128,1024]{1,0:T(8,128)(2,1)S(1)} %pair_stack.4.refs_1_.refs_0__0_), channel_id=1, source_target_pairs={{0,16},{4,20},{8,24},{12,28},{16,0},{20,4},{24,8},{28,12},{1,17},{... | collective-permute-start | bytes 786440 | tf_op jit(solution)/shard_map/ppermute | solution.py:250
  120.6 10.6 %collective-permute-start.51 = (bf16[128,1024]{1,0:T(8,128)(2,1)S(1)}, bf16[128,1024]{1,0:T(8,128)(2,1)S(1)}, u32[]{:S(2)}, u32[]{:S(2)}) collective-permute-start(bf16[128,1024]{1,0:T(8,128)(2,1)S(1)} %pair_stack.4.refs_1_.refs_0__0_), channel_id=1, source_target_pairs={{0,24},{4,28},{8,16},{12,20},{16,8},{20,12},{24,0},{28,4},{1,25},{... | collective-permute-start | bytes 786440 | tf_op jit(solution)/shard_map/ppermute | solution.py:250
  121.5 4.3 %collective-permute-start.52 = (bf16[160,256]{1,0:T(8,128)(2,1)S(1)}, bf16[160,256]{1,0:T(8,128)(2,1)S(1)}, u32[]{:S(2)}, u32[]{:S(2)}) collective-permute-start(bf16[160,256]{1,0:T(8,128)(2,1)S(1)} %early_line.4.refs_1_), channel_id=1, source_target_pairs={{0,2},{1,3},{2,0},{3,1},{4,6},{5,7},{6,4},{7,5},{8,10},{9,11},{10,... | collective-permute-start | bytes 245768 | tf_op jit(solution)/shard_map/ppermute | solution.py:256
  124.2 19.2 %collective-permute-start.54 = (bf16[224,512]{1,0:T(8,128)(2,1)S(1)}, bf16[224,512]{1,0:T(8,128)(2,1)S(1)}, u32[]{:S(2)}, u32[]{:S(2)}) collective-permute-start(bf16[224,512]{1,0:T(8,128)(2,1)S(1)} %late_line.2.refs_3_.refs_0_), channel_id=1, source_target_pairs={{0,2},{1,3},{2,0},{3,1},{4,6},{5,7},{6,4},{7,5},{8,10},{9,11},{10,... | collective-permute-start | bytes 688136 | tf_op jit(solution)/shard_map/ppermute | solution.py:256
  126.4 17.0 %collective-permute-start.58 = (bf16[160,512]{1,0:T(8,128)(2,1)S(1)}, bf16[160,512]{1,0:T(8,128)(2,1)S(1)}, u32[]{:S(2)}, u32[]{:S(2)}) collective-permute-start(bf16[160,512]{1,0:T(8,128)(2,1)S(1)} %early_line.5.refs_1_.refs_0__0_), channel_id=1, source_target_pairs={{0,8},{4,12},{8,0},{12,4},{16,24},{20,28},{24,16},{28,20},{1,9},{5... | collective-permute-start | bytes 491528 | tf_op jit(solution)/shard_map/ppermute | solution.py:250
  127.0 16.5 %collective-permute-start.59 = (bf16[160,512]{1,0:T(8,128)(2,1)S(1)}, bf16[160,512]{1,0:T(8,128)(2,1)S(1)}, u32[]{:S(2)}, u32[]{:S(2)}) collective-permute-start(bf16[160,512]{1,0:T(8,128)(2,1)S(1)} %early_line.5.refs_1_.refs_0__0_), channel_id=1, source_target_pairs={{0,16},{4,20},{8,24},{12,28},{16,0},{20,4},{24,8},{28,12},{1,17},{... | collective-permute-start | bytes 491528 | tf_op jit(solution)/shard_map/ppermute | solution.py:250
  128.5 15.0 %collective-permute-start.60 = (bf16[160,512]{1,0:T(8,128)(2,1)S(1)}, bf16[160,512]{1,0:T(8,128)(2,1)S(1)}, u32[]{:S(2)}, u32[]{:S(2)}) collective-permute-start(bf16[160,512]{1,0:T(8,128)(2,1)S(1)} %early_line.5.refs_1_.refs_0__0_), channel_id=1, source_target_pairs={{0,24},{4,28},{8,16},{12,20},{16,8},{20,12},{24,0},{28,4},{1,25},{... | collective-permute-start | bytes 491528 | tf_op jit(solution)/shard_map/ppermute | solution.py:250
  131.2 11.0 %collective-permute-start.48 = (bf16[64,512]{1,0:T(8,128)(2,1)S(1)}, bf16[64,512]{1,0:T(8,128)(2,1)S(1)}, u32[]{:S(2)}, u32[]{:S(2)}) collective-permute-start(bf16[64,512]{1,0:T(8,128)(2,1)S(1)} %get-tuple-element.227), channel_id=1, source_target_pairs={{0,4},{4,0},{8,12},{12,8},{16,20},{20,16},{24,28},{28,24},{1,5},{5... | collective-permute-start | bytes 196616 | tf_op jit(solution)/shard_map/ppermute | solution.py:253
  143.6 4.6 %collective-permute-start.61 = (bf16[640,512]{1,0:T(8,128)(2,1)S(1)}, bf16[640,512]{1,0:T(8,128)(2,1)S(1)}, u32[]{:S(2)}, u32[]{:S(2)}) collective-permute-start(bf16[640,512]{1,0:T(8,128)(2,1)S(1)} %early_stack.1.refs_1__0_), channel_id=1, source_target_pairs={{0,4},{4,0},{8,12},{12,8},{16,20},{20,16},{24,28},{28,24},{1,5},{5... | collective-permute-start | bytes 1966088 | tf_op jit(solution)/shard_map/ppermute | solution.py:253
  144.6 7.4 %collective-permute-start.55 = (bf16[224,512]{1,0:T(8,128)(2,1)S(1)}, bf16[224,512]{1,0:T(8,128)(2,1)S(1)}, u32[]{:S(2)}, u32[]{:S(2)}) collective-permute-start(bf16[224,512]{1,0:T(8,128)(2,1)S(1)} %late_line.3.refs_1_.refs_0__0_), channel_id=1, source_target_pairs={{0,8},{4,12},{8,0},{12,4},{16,24},{20,28},{24,16},{28,20},{1,9},{5... | collective-permute-start | bytes 688136 | tf_op jit(solution)/shard_map/ppermute | solution.py:250
  145.7 7.0 %collective-permute-start.56 = (bf16[224,512]{1,0:T(8,128)(2,1)S(1)}, bf16[224,512]{1,0:T(8,128)(2,1)S(1)}, u32[]{:S(2)}, u32[]{:S(2)}) collective-permute-start(bf16[224,512]{1,0:T(8,128)(2,1)S(1)} %late_line.3.refs_1_.refs_0__0_), channel_id=1, source_target_pairs={{0,16},{4,20},{8,24},{12,28},{16,0},{20,4},{24,8},{28,12},{1,17},{... | collective-permute-start | bytes 688136 | tf_op jit(solution)/shard_map/ppermute | solution.py:250
  146.6 10.8 %collective-permute-start.57 = (bf16[224,512]{1,0:T(8,128)(2,1)S(1)}, bf16[224,512]{1,0:T(8,128)(2,1)S(1)}, u32[]{:S(2)}, u32[]{:S(2)}) collective-permute-start(bf16[224,512]{1,0:T(8,128)(2,1)S(1)} %late_line.3.refs_1_.refs_0__0_), channel_id=1, source_target_pairs={{0,24},{4,28},{8,16},{12,20},{16,8},{20,12},{24,0},{28,4},{1,25},{... | collective-permute-start | bytes 688136 | tf_op jit(solution)/shard_map/ppermute | solution.py:250
  147.3 11.5 %collective-permute-start.63 = (bf16[512,1024]{1,0:T(8,128)(2,1)S(1)}, bf16[512,1024]{1,0:T(8,128)(2,1)S(1)}, u32[]{:S(2)}, u32[]{:S(2)}) collective-permute-start(bf16[512,1024]{1,0:T(8,128)(2,1)S(1)} %pair_stack.5.refs_3_.refs_0__0_), channel_id=1, source_target_pairs={{0,4},{4,0},{8,12},{12,8},{16,20},{20,16},{24,28},{28,24},{1,5},{5... | collective-permute-start | bytes 3145736 | tf_op jit(solution)/shard_map/ppermute | solution.py:253
  157.4 3.8 %collective-permute-start.62 = (bf16[896,512]{1,0:T(8,128)(2,1)S(1)}, bf16[896,512]{1,0:T(8,128)(2,1)S(1)}, u32[]{:S(2)}, u32[]{:S(2)}) collective-permute-start(bf16[896,512]{1,0:T(8,128)(2,1)S(1)} %late_stack.1.refs_6_.refs_1__0_), channel_id=1, source_target_pairs={{0,4},{4,0},{8,12},{12,8},{16,20},{20,16},{24,28},{28,24},{1,5},{5... | collective-permute-start | bytes 2752520 | tf_op jit(solution)/shard_map/ppermute | solution.py:253
  (28 other events, 199.9 us)

commit v4 on v3

--- a/solution.py
+++ b/solution.py
@@ -660,8 +660,11 @@
             total = total + v[:n, :].astype(F32)
         out[...] = total.astype(BF)
 
-    def add_up_more(parts, out, mine, twin):
+    def add_up_more(spot, parts, keep, send, mine, twin, out):
         add_up(parts, out)
+        n, side = keep.shape[1], spot[2] % 2
+        keep[...] = out[:, pl.ds(pl.multiple_of(side * n, n), n)]
+        send[...] = out[:, pl.ds(pl.multiple_of((1 - side) * n, n), n)]
         n = mine.shape[0] // len(parts)
         for m, v in enumerate(parts):
             at, top = slice(m * n, (m + 1) * n), out.shape[0]
@@ -683,8 +686,14 @@
         keep[...] = total[:, pl.ds(pl.multiple_of(side * n, n), n)]
         send[...] = total[:, pl.ds(pl.multiple_of((1 - side) * n, n), n)]
 
-    def join_sides(spot, mine, other, out):
-        n, side = mine.shape[1], spot[2] // 2
+    def join_near(spot, mine, other, out):
+        join_sides(spot, mine, other, out, spot[2] % 2)
+
+    def join_far(spot, mine, other, out):
+        join_sides(spot, mine, other, out, spot[2] // 2)
+
+    def join_sides(spot, mine, other, out, side):
+        n = mine.shape[1]
         out[:, pl.ds(pl.multiple_of(side * n, n), n)] = mine[...]
         out[:, pl.ds(pl.multiple_of((1 - side) * n, n), n)] = other[...]
 
@@ -1030,27 +1039,21 @@
                 after=[early],
             )
             half = struct((rows * 2, width), BF)
-            late, mine, twin = call(
-                add_up_more, [eighth(n_late), half, half], (late,), "late_plane", after=[pair]
+            late_side = struct((n_late // 8, width // 2), BF)
+            late, other, mine, twin = call(
+                add_up_more, [late_side, late_side, half, half], (late,), "late_plane",
+                [pltpu.VMEM((n_late // 8, width), BF)], spot=spot, after=[pair],
             )
             pairs = [pair] + [to_chip(pair, m) for m in (1, 2, 3)]
-            (late,) = call(add_two, [eighth(n_late)], (late, to_hid(late, 1), []), "late_line")
+            (late,) = call(add_two, [late_side], (late, to_hid(other, 1), []), "late_line")
             (early,) = call(
-                join_sides, [eighth(n_early)], (early, to_hid(early, 2)), "early_line", spot=spot, after=[late]
+                join_far, [eighth(n_early)], (early, to_hid(early, 2)), "early_line", spot=spot, after=[late]
             )
             (pair,) = call(
                 stack_up, [struct((16 * rows, 2 * width), BF)], (pairs,), "pair_stack", after=[early]
             )
             last = pair
-            early = [early] + [to_chip(early, m) for m in (1, 2, 3)]
-            edge_gradient, last = call(
-                edge_end(rows, fanout, step),
-                [final(n_edges, edge_width)],
-                (edge_grad, first_low, mf),
-                "edge_end",
-                after=[last],
-                token=True,
-            )
+            early = [early] + [to_chip(early, m) for m in (1, 2)]
             returned = [mine, to_core(twin)]
             node_gradient, last = call(
                 node_end,
@@ -1061,10 +1064,26 @@
                 token=True,
             )
             (late,) = call(
-                add_two, [eighth(n_late)], (late, to_hid(late, 2), []), "late_line", after=[last]
+                add_two, [late_side], (late, to_hid(late, 2), []), "late_line", after=[last]
+            )
+            left, right = call(split_relay, [side, side], tuple(early[1:]), "early_split", after=[late])
+            edge_gradient, last = call(
+                edge_end(rows, fanout, step),
+                [final(n_edges, edge_width)],
+                (edge_grad, first_low, mf),
+                "edge_end",
+                after=[left],
+                token=True,
+            )
+            (late,) = call(
+                join_near, [eighth(n_late)], (late, to_hid(late, 1)), "late_join", spot=spot, after=[last]
             )
             (early,) = call(
-                stack_up, [struct((n_early // 2, width), BF)], (early,), "early_stack", after=[late]
+                stack_relay,
+                [struct((n_early // 2, width), BF)],
+                (early, to_chip(left, 2), to_chip(right, 1)),
+                "early_stack",
+                after=[late],
             )
             early = [early, to_core(early)]
             late = [late] + [to_chip(late, m) for m in (1, 2, 3)]

time: 164 us -> 163 us (level)
  starting transfers between devices: 79 us -> 75.3 us
    ppermute x17, starting transfers between devices: 31.6 us -> 27.7 us  [to_core(): return lax.ppermute(v, 'res', pair)]
    ppermute x31 -> x32, starting transfers between devices: 29 us -> 30.5 us  [to_chip(): return lax.ppermute(v, 'res', [(i, i ^ 2 * m) for i in range(n_res)])]
    ppermute x16 -> x17, starting transfers between devices: 18.5 us -> 17.2 us  [to_hid(): return lax.ppermute(v, 'hid', [(i, i ^ m) for i in range(n_hid)])]
    pallas_call x38 -> x40, Pallas kernels: 47.5 us -> 48.7 us  [call(): pl.pallas_call(run, out_shape=jax.tree.unflatten(out_tree, shapes), in_sp...]
    ppermute x16 -> x17, waiting for transfers between devices: 16.7 us -> 17.6 us  [to_hid(): return lax.ppermute(v, 'hid', [(i, i ^ m) for i in range(n_hid)])]
    ppermute x31 -> x32, waiting for transfers between devices: 14 us -> 13.2 us  [to_chip(): return lax.ppermute(v, 'res', [(i, i ^ 2 * m) for i in range(n_res)])]
  transfers between devices with their start and end apart: 64 -> 66, of which waited for: 22 -> 24; matrix products, arithmetic and copies ran while one was open for 0% -> 0% of each run, Pallas kernels for 14% -> 15%
where the time goes in v4:
time: 163 us; the launch traced here: 162 us
  starting transfers between devices  75.3 us (46%)
  Pallas kernels  48.7 us (30%)
  waiting for transfers between devices  36.8 us (23%)
    pallas_call x40, Pallas kernels, call(): pl.pallas_call(run, out_shape=jax.tree.unflatten(out_tree, shapes), in_sp...  48.7 us
    ppermute x32, starting transfers between devices, to_chip(): return lax.ppermute(v, 'res', [(i, i ^ 2 * m) for i in range(n_res)])  30.5 us
    ppermute x17, starting transfers between devices, to_core(): return lax.ppermute(v, 'res', pair)  27.7 us
    ppermute x17, waiting for transfers between devices, to_hid(): return lax.ppermute(v, 'hid', [(i, i ^ m) for i in range(n_hid)])  17.6 us
    ppermute x17, starting transfers between devices, to_hid(): return lax.ppermute(v, 'hid', [(i, i ^ m) for i in range(n_hid)])  17.2 us
    ppermute x32, waiting for transfers between devices, to_chip(): return lax.ppermute(v, 'res', [(i, i ^ 2 * m) for i in range(n_res)])  13.2 us
    ppermute x17, waiting for transfers between devices, to_core(): return lax.ppermute(v, 'res', pair)  6.03 us
  transfers between devices with their start and end apart: 66, of which 24 were waited for; matrix products, arithmetic and copies ran while one was open for 0% of the time, Pallas kernels for 15%

profile of v4, /device:TPU:1, one launch (start us, length us, event | category | flops | bytes accessed | tf_op | source)
XLA Modules:
  0.0 162.4 jit_solution(7850392890870876629)
XLA Ops:
  0.8 2.1 %prepare_send.1 = (bf16[32,512]{1,0:T(8,128)(2,1)S(1)}, bf16[32,512]{1,0:T(8,128)(2,1)S(1)}, bf16[32,512]{1,0:T(8,128)(2,1)S(1)}, bf16[32,512]{1,0:T(8,128)(2,1)...) custom-call(s32[4]{0:T(128)S(1)} %pad_add_fusion.refs_0_, s32[8,16]{1,0:T(8,128)} %bitcast.59, ...), custom_call_target="tpu_custom_call" | custom-call | tf_op jit(solution)/shard_map/prepare_send/pallas_call | solution.py:166
  2.9 2.2 %collective-permute-start.4 = (bf16[144,512]{1,0:T(8,128)(2,1)S(1)}, bf16[144,512]{1,0:T(8,128)(2,1)S(1)}, u32[]{:S(2)}, u32[]{:S(2)}) collective-permute-start(bf16[144,512]{1,0:T(8,128)(2,1)S(1)} %get-tuple-element.157), channel_id=1, source_target_pairs={{0,1},{1,0},{2,3},{3,2},{4,5},{5,4},{6,7},{7,6},{8,9},{9,8},{10,11... | collective-permute-start | bytes 442376 | tf_op jit(solution)/shard_map/ppermute | solution.py:256
  5.1 2.3 %collective-permute-start.5 = (bf16[144,512]{1,0:T(8,128)(2,1)S(1)}, bf16[144,512]{1,0:T(8,128)(2,1)S(1)}, u32[]{:S(2)}, u32[]{:S(2)}) collective-permute-start(bf16[144,512]{1,0:T(8,128)(2,1)S(1)} %get-tuple-element.157), channel_id=1, source_target_pairs={{0,2},{1,3},{2,0},{3,1},{4,6},{5,7},{6,4},{7,5},{8,10},{9,11},{10,... | collective-permute-start | bytes 442376 | tf_op jit(solution)/shard_map/ppermute | solution.py:256
  10.5 2.2 %collective-permute-start.2 = (bf16[32,512]{1,0:T(8,128)(2,1)S(1)}, bf16[32,512]{1,0:T(8,128)(2,1)S(1)}, u32[]{:S(2)}, u32[]{:S(2)}) collective-permute-start(bf16[32,512]{1,0:T(8,128)(2,1)S(1)} %get-tuple-element.150), channel_id=1, source_target_pairs={{0,24},{4,28},{8,16},{12,20},{16,8},{20,12},{24,0},{28,4},{1,25},{... | collective-permute-start | bytes 98312 | tf_op jit(solution)/shard_map/ppermute | solution.py:250
  12.6 2.6 %prepare_rest.1 = (bf16[1920,128]{1,0:T(8,128)(2,1)S(1)}, f32[32,1]{1,0:T(8,128)S(1)}, f32[8,512]{1,0:T(8,128)S(1)}, f32[8,192]{1,0:T(8,128)S(1)}, bf16[1920,192]{1,0:T(8,128)(2,1)S(1)}) custom-call(s32[4]{0:T(128)S(1)} %pad_add_fusion.refs_0_, s32[32,60]{1,0:T(8,128)} %refs_1_.5, s32[1,32]{1,0:T(1,128)} %bitcast.73, f32[1,512]{1,0:T(1,128)} %bitcast.60, ...), custom_call_target="tpu_custom_call" | custom-call | tf_op jit(solution)/shard_map/prepare_rest/pallas_call | solution.py:166
  15.3 2.7 %collective-permute-start.3 = (bf16[64,512]{1,0:T(8,128)(2,1)S(1)}, bf16[64,512]{1,0:T(8,128)(2,1)S(1)}, u32[]{:S(2)}, u32[]{:S(2)}) collective-permute-start(bf16[64,512]{1,0:T(8,128)(2,1)S(1)} %get-tuple-element.153), channel_id=1, source_target_pairs={{0,4},{4,0},{8,12},{12,8},{16,20},{20,16},{24,28},{28,24},{1,5},{5... | collective-permute-start | bytes 196616 | tf_op jit(solution)/shard_map/ppermute | solution.py:253
  21.2 3.6 %message_one.1 = (f32[32,512]{1,0:T(8,128)S(1)}, bf16[32,512]{1,0:T(8,128)(2,1)S(1)}) custom-call(bf16[64,512]{1,0:T(8,128)(2,1)S(1)} %get-tuple-element.152.refs_2_.refs_0__0_, bf16[64,512]{1,0:T(8,128)(2,1)S(1)} %collective-permute-done.3.refs_3_.refs_0__1_, bf16[32,512]{1,0:T(8,128)(2,1)S(1)} %copy-done.9, ...), custom_call_target="tpu_custom_call" | custom-call | tf_op jit(solution)/shard_map/message_one/pallas_call | solution.py:166
  24.8 1.7 %collective-permute-start.7 = (bf16[32,512]{1,0:T(8,128)(2,1)S(1)}, bf16[32,512]{1,0:T(8,128)(2,1)S(1)}, u32[]{:S(2)}, u32[]{:S(2)}) collective-permute-start(bf16[32,512]{1,0:T(8,128)(2,1)S(1)} %get-tuple-element.159.refs_0__0_), channel_id=1, source_target_pairs={{0,1},{1,0},{2,3},{3,2},{4,5},{5,4},{6,7},{7,6},{8,9},{9,8},{10,11... | collective-permute-start | bytes 98312 | tf_op jit(solution)/shard_map/ppermute | solution.py:256
  26.5 2.0 %collective-permute-start.8 = (bf16[32,512]{1,0:T(8,128)(2,1)S(1)}, bf16[32,512]{1,0:T(8,128)(2,1)S(1)}, u32[]{:S(2)}, u32[]{:S(2)}) collective-permute-start(bf16[32,512]{1,0:T(8,128)(2,1)S(1)} %get-tuple-element.159.refs_0__0_), channel_id=1, source_target_pairs={{0,2},{1,3},{2,0},{3,1},{4,6},{5,7},{6,4},{7,5},{8,10},{9,11},{10,... | collective-permute-start | bytes 98312 | tf_op jit(solution)/shard_map/ppermute | solution.py:256
  28.9 1.3 collective-permute-done.8.refs_0__2_
  30.2 3.3 %collective-permute-done.9.refs_0__3_ = bf16[32,512]{1,0:T(8,128)(2,1)S(1)} collective-permute-done((bf16[32,512]{1,0:T(8,128)(2,1)S(1)}, bf16[32,512]{1,0:T(8,128)(2,1)S(1)}, u32[]{:S(2)}, u32[]{:S(2)}) %collective-permute-start.9) | collective-permute-done | bytes 32800 | tf_op jit(solution)/shard_map/ppermute | solution.py:256
  34.7 1.6 collective-permute-start.11
  36.3 2.0 %collective-permute-start.12 = (bf16[32,512]{1,0:T(8,128)(2,1)S(1)}, bf16[32,512]{1,0:T(8,128)(2,1)S(1)}, u32[]{:S(2)}, u32[]{:S(2)}) collective-permute-start(bf16[32,512]{1,0:T(8,128)(2,1)S(1)} %get-tuple-element.163), channel_id=1, source_target_pairs={{0,3},{1,2},{2,1},{3,0},{4,7},{5,6},{6,5},{7,4},{8,11},{9,10},{10,... | collective-permute-start | bytes 98312 | tf_op jit(solution)/shard_map/ppermute | solution.py:256
  38.4 2.5 %collective-permute-done.12.refs_1__3_ = bf16[32,512]{1,0:T(8,128)(2,1)S(1)} collective-permute-done((bf16[32,512]{1,0:T(8,128)(2,1)S(1)}, bf16[32,512]{1,0:T(8,128)(2,1)S(1)}, u32[]{:S(2)}, u32[]{:S(2)}) %collective-permute-start.12) | collective-permute-done | bytes 32800 | tf_op jit(solution)/shard_map/ppermute | solution.py:256
  41.3 4.5 %collective-permute-start.24 = (bf16[576,1536]{1,0:T(8,128)(2,1)S(1)}, bf16[576,1536]{1,0:T(8,128)(2,1)S(1)}, u32[]{:S(2)}, u32[]{:S(2)}) collective-permute-start(bf16[576,1536]{1,0:T(8,128)(2,1)S(1)} %stack_weights.1.refs_1__0_), channel_id=1, source_target_pairs={{0,4},{4,0},{8,12},{12,8},{16,20},{20,16},{24,28},{28,24},{1,5},{5... | collective-permute-start | bytes 5308424 | tf_op jit(solution)/shard_map/ppermute | solution.py:253
  49.9 1.5 collective-permute-start.18
  52.0 1.8 %collective-permute-start.19 = (bf16[32,512]{1,0:T(8,128)(2,1)S(1)}, bf16[32,512]{1,0:T(8,128)(2,1)S(1)}, u32[]{:S(2)}, u32[]{:S(2)}) collective-permute-start(bf16[32,512]{1,0:T(8,128)(2,1)S(1)} %collective-permute-done.15.refs_0__3_), channel_id=1, source_target_pairs={{0,4},{4,0},{8,12},{12,8},{16,20},{20,16},{24,28},{28,24},{1,5},{5... | collective-permute-start | bytes 98312 | tf_op jit(solution)/shard_map/ppermute | solution.py:253
  54.7 7.4 %layer_two.1 = (f32[1920,192]{1,0:T(8,128)S(1)}, bf16[1920,512]{1,0:T(8,128)(2,1)S(1)}, bf16[1920,512]{1,0:T(8,128)(2,1)S(1)}, bf16[1920,512]{1,0:T(8,128)(2,1)S...) custom-call(bf16[32,512]{1,0:T(8,128)(2,1)S(1)} %get-tuple-element.1, ...), custom_call_target="tpu_custom_call" | custom-call | tf_op jit(solution)/shard_map/layer_two/pallas_call | solution.py:166
  62.1 2.0 %feed_two.1 = (bf16[4,32,512]{2,1,0:T(8,128)(2,1)S(1)}, f32[32,512]{1,0:T(8,128)S(1)}, f32[32,512]{1,0:T(8,128)}, bf16[32,512]{1,0:T(8,128)(2,1)S(1)}, bf16[32,5...) custom-call(f32[32,512]{1,0:T(8,128)S(1)} %get-tuple-element.174.ref, ...), custom_call_target="tpu_custom_call" | custom-call | tf_op jit(solution)/shard_map/feed_two/pallas_call | solution.py:166
  64.6 2.2 %collective-permute-start.27 = (bf16[32,512]{1,0:T(8,128)(2,1)S(1)}, bf16[32,512]{1,0:T(8,128)(2,1)S(1)}, u32[]{:S(2)}, u32[]{:S(2)}) collective-permute-start(bf16[32,512]{1,0:T(8,128)(2,1)S(1)} %get-tuple-element.179), channel_id=1, source_target_pairs={{0,24},{4,28},{8,16},{12,20},{16,8},{20,12},{24,0},{28,4},{1,25},{... | collective-permute-start | bytes 98312 | tf_op jit(solution)/shard_map/ppermute | solution.py:250
  71.2 5.8 %edge_turn.1 = (f32[1920,192]{1,0:T(8,128)}, f32[1920,192]{1,0:T(8,128)S(1)}, bf16[1920,192]{1,0:T(8,128)(2,1)S(1)}, bf16[1920,192]{1,0:T(8,128)(2,1)S(1)}, bf16...) custom-call(bf16[32,512]{1,0:T(8,128)(2,1)S(1)} %get-tuple-element.1, ...), custom_call_target="tpu_custom_call" | custom-call | tf_op jit(solution)/shard_map/edge_turn/pallas_call | solution.py:166
  80.8 2.1 %collective-permute-done.34.refs_0__3_ = bf16[32,192]{1,0:T(8,128)(2,1)S(1)} collective-permute-done((bf16[32,192]{1,0:T(8,128)(2,1)S(1)}, bf16[32,192]{1,0:T(8,128)(2,1)S(1)}, u32[]{:S(2)}, u32[]{:S(2)}) %collective-permute-start.34) | collective-permute-done | bytes 12320 | tf_op jit(solution)/shard_map/ppermute | solution.py:250
  82.9 2.1 %collective-permute-start.35 = (bf16[64,192]{1,0:T(8,128)(2,1)S(1)}, bf16[64,192]{1,0:T(8,128)(2,1)S(1)}, u32[]{:S(2)}, u32[]{:S(2)}) collective-permute-start(bf16[64,192]{1,0:T(8,128)(2,1)S(1)} %get-tuple-element.194), channel_id=1, source_target_pairs={{0,4},{4,0},{8,12},{12,8},{16,20},{20,16},{24,28},{28,24},{1,5},{5... | collective-permute-start | bytes 73736 | tf_op jit(solution)/shard_map/ppermute | solution.py:253
  85.9 3.0 %node_turn.1 = (bf16[32,1024]{1,0:T(8,128)(2,1)S(1)}, f32[32,512]{1,0:T(8,128)S(1)}, f32[32,512]{1,0:T(8,128)S(1)}, bf16[640,512]{1,0:T(8,128)(2,1)S(1)}, bf16[640,512]{1,0:T(8,128)(2,1)S(1)}) custom-call(s32[4]{0:T(128)S(1)} %pad_add_fusion.refs_0_, bf16[64,192]{1,0:T(8,128)(2,1)S(1)} %get-tuple-element.193.refs_1__0_, ...), custom_call_target="tpu_custom_call" | custom-call | tf_op jit(solution)/shard_map/node_turn/pallas_call | solution.py:166
  89.2 1.3 message_second.1
  91.7 2.2 %collective-permute-start.39 = (bf16[160,512]{1,0:T(8,128)(2,1)S(1)}, bf16[160,512]{1,0:T(8,128)(2,1)S(1)}, u32[]{:S(2)}, u32[]{:S(2)}) collective-permute-start(bf16[160,512]{1,0:T(8,128)(2,1)S(1)} %get-tuple-element.210), channel_id=1, source_target_pairs={{0,24},{4,28},{8,16},{12,20},{16,8},{20,12},{24,0},{28,4},{1,25},{... | collective-permute-start | bytes 491528 | tf_op jit(solution)/shard_map/ppermute | solution.py:250
  93.8 2.6 %message_first.1 = (bf16[1920,512]{1,0:T(8,128)(2,1)S(1)}, bf16[32,512]{1,0:T(8,128)(2,1)S(1)}, bf16[32,512]{1,0:T(8,128)(2,1)S(1)}, bf16[32,512]{1,0:T(8,128)(2...) custom-call(bf16[32,512]{1,0:T(8,128)(2,1)S(1)} %get-tuple-element.165.refs_0__0_, ...), custom_call_target="tpu_custom_call" | custom-call | tf_op jit(solution)/shard_map/message_first/pallas_call | solution.py:166
  96.5 2.2 %collective-permute-done.40.refs_0__1_ = bf16[32,1024]{1,0:T(8,128)(2,1)S(1)} collective-permute-done((bf16[32,1024]{1,0:T(8,128)(2,1)S(1)}, bf16[32,1024]{1,0:T(8,128)(2,1)S(1)}, u32[]{:S(2)}, u32[]{:S(2)}) %collective-permute-start.40) | collective-permute-done | bytes 65568 | tf_op jit(solution)/shard_map/ppermute | solution.py:256
  98.7 1.4 collective-permute-done.39.refs_1__3_
  100.9 1.5 collective-permute-start.41
  102.4 2.1 %collective-permute-done.41.refs_1_ = bf16[896,512]{1,0:T(8,128)(2,1)S(1)} collective-permute-done((bf16[896,512]{1,0:T(8,128)(2,1)S(1)}, bf16[896,512]{1,0:T(8,128)(2,1)S(1)}, u32[]{:S(2)}, u32[]{:S(2)}) %collective-permute-start.41) | collective-permute-done | bytes 917536 | tf_op jit(solution)/shard_map/ppermute | solution.py:253
  104.7 1.3 collective-permute-start.42
  107.8 1.5 collective-permute-done.46.refs_1_
  109.4 4.4 %collective-permute-done.47.refs_1_ = bf16[160,256]{1,0:T(8,128)(2,1)S(1)} collective-permute-done((bf16[160,256]{1,0:T(8,128)(2,1)S(1)}, bf16[160,256]{1,0:T(8,128)(2,1)S(1)}, u32[]{:S(2)}, u32[]{:S(2)}) %collective-permute-start.47) | collective-permute-done | bytes 81952 | tf_op jit(solution)/shard_map/ppermute | solution.py:256
  113.9 1.3 collective-permute-start.49
  116.6 2.0 %collective-permute-done.44.refs_1__3_ = bf16[256,512]{1,0:T(8,128)(2,1)S(1)} collective-permute-done((bf16[256,512]{1,0:T(8,128)(2,1)S(1)}, bf16[256,512]{1,0:T(8,128)(2,1)S(1)}, u32[]{:S(2)}, u32[]{:S(2)}) %collective-permute-start.44) | collective-permute-done | bytes 262176 | tf_op jit(solution)/shard_map/ppermute | solution.py:250
  119.8 2.1 %collective-permute-start.52 = (bf16[160,256]{1,0:T(8,128)(2,1)S(1)}, bf16[160,256]{1,0:T(8,128)(2,1)S(1)}, u32[]{:S(2)}, u32[]{:S(2)}) collective-permute-start(bf16[160,256]{1,0:T(8,128)(2,1)S(1)} %early_line.4.refs_1_), channel_id=1, source_target_pairs={{0,2},{1,3},{2,0},{3,1},{4,6},{5,7},{6,4},{7,5},{8,10},{9,11},{10,... | collective-permute-start | bytes 245768 | tf_op jit(solution)/shard_map/ppermute | solution.py:256
  121.9 1.5 collective-permute-done.53.refs_1_
  125.2 2.2 %collective-permute-start.55 = (bf16[160,512]{1,0:T(8,128)(2,1)S(1)}, bf16[160,512]{1,0:T(8,128)(2,1)S(1)}, u32[]{:S(2)}, u32[]{:S(2)}) collective-permute-start(bf16[160,512]{1,0:T(8,128)(2,1)S(1)} %early_line.5.refs_1_.refs_0__0_), channel_id=1, source_target_pairs={{0,16},{4,20},{8,24},{12,28},{16,0},{20,4},{24,8},{28,12},{1,17},{... | collective-permute-start | bytes 491528 | tf_op jit(solution)/shard_map/ppermute | solution.py:250
  127.4 1.9 %collective-permute-start.56 = (bf16[224,256]{1,0:T(8,128)(2,1)S(1)}, bf16[224,256]{1,0:T(8,128)(2,1)S(1)}, u32[]{:S(2)}, u32[]{:S(2)}) collective-permute-start(bf16[224,256]{1,0:T(8,128)(2,1)S(1)} %late_line.2.refs_3_.refs_0_), channel_id=1, source_target_pairs={{0,2},{1,3},{2,0},{3,1},{4,6},{5,7},{6,4},{7,5},{8,10},{9,11},{10,... | collective-permute-start | bytes 344072 | tf_op jit(solution)/shard_map/ppermute | solution.py:256
  130.0 2.7 %collective-permute-start.48 = (bf16[64,512]{1,0:T(8,128)(2,1)S(1)}, bf16[64,512]{1,0:T(8,128)(2,1)S(1)}, u32[]{:S(2)}, u32[]{:S(2)}) collective-permute-start(bf16[64,512]{1,0:T(8,128)(2,1)S(1)} %get-tuple-element.230), channel_id=1, source_target_pairs={{0,4},{4,0},{8,12},{12,8},{16,20},{20,16},{24,28},{28,24},{1,5},{5... | collective-permute-start | bytes 196616 | tf_op jit(solution)/shard_map/ppermute | solution.py:253
  136.4 2.0 %edge_end.1 = (f32[1920,192]{1,0:T(8,128)}, f32[8,128]{1,0:T(8,128)S(1)}) custom-call(f32[1920,192]{1,0:T(8,128)S(1)} %get-tuple-element.235.refs_0_, bf16[1920,512]{1,0:T(8,128)(2,1)S(1)} %get-tuple-element.236.refs_1_, bf16[1216,512]{1,0:T(8,128)(2,1)S(1)} %copy-done, bf16[160,256]{1,0:T(8,128)(2,1)S(1)} %get-tuple-element.238.refs_3_), custom_call_target="tpu_custom_call" | custom-call | tf_op jit(solution)/shard_map/edge_end/pallas_call | solution.py:166
  139.2 3.7 %collective-permute-start.63 = (bf16[640,512]{1,0:T(8,128)(2,1)S(1)}, bf16[640,512]{1,0:T(8,128)(2,1)S(1)}, u32[]{:S(2)}, u32[]{:S(2)}) collective-permute-start(bf16[640,512]{1,0:T(8,128)(2,1)S(1)} %early_stack.1.refs_1__0_), channel_id=1, source_target_pairs={{0,4},{4,0},{8,12},{12,8},{16,20},{20,16},{24,28},{28,24},{1,5},{5... | collective-permute-start | bytes 1966088 | tf_op jit(solution)/shard_map/ppermute | solution.py:253
  146.5 2.4 %unpack_early.1 = (f32[192,1216]{1,0:T(8,128)}, f32[192,192]{1,0:T(8,128)}, f32[192,192]{1,0:T(8,128)}, f32[512,512]{1,0:T(8,128)}, f32[1,512]{1,0:T(1,128)}, /*...) custom-call(s32[4]{0:T(128)S(1)} %pad_add_fusion.refs_0_, ...), custom_call_target="tpu_custom_call" | custom-call | tf_op jit(solution)/shard_map/unpack_early/pallas_call | solution.py:166
  148.9 1.4 feed_weights.1
  150.8 5.1 %collective-permute-done.60.refs_0__3_ = bf16[224,512]{1,0:T(8,128)(2,1)S(1)} collective-permute-done((bf16[224,512]{1,0:T(8,128)(2,1)S(1)}, bf16[224,512]{1,0:T(8,128)(2,1)S(1)}, u32[]{:S(2)}, u32[]{:S(2)}) %collective-permute-start.60) | collective-permute-done | bytes 229408 | tf_op jit(solution)/shard_map/ppermute | solution.py:250
  157.1 2.5 %feed_weights_more.1 = (f32[512,512]{1,0:T(8,128)}, f32[512,512]{1,0:T(8,128)}, f32[8,128]{1,0:T(8,128)S(1)}) custom-call(bf16[512,1024]{1,0:T(8,128)(2,1)S(1)} %collective-permute-done.65.refs_0__0_, bf16[512,512]{1,0:T(8,128)(2,1)S(1)} %copy-done.1, f32[1,512]{1,0:T(1,128)S(1)} %bitcast.57, bf16[512,512]{1,0:T(8,128)(2,1)S(1)} %copy-done.2, ...), custom_call_target="tpu_custom_call" | custom-call | tf_op jit(solution)/shard_map/feed_weights_more/pallas_call | solution.py:166
  159.6 2.6 %unpack_late.1 = (f32[1216,512]{1,0:T(8,128)}, f32[512,512]{1,0:T(8,128)}, f32[1,512]{1,0:T(1,128)}, f32[1,512]{1,0:T(1,128)}) custom-call(s32[4]{0:T(128)S(1)} %pad_add_fusion.refs_0_, bf16[896,512]{1,0:T(8,128)(2,1)S(1)} %late_stack.1.refs_6_.refs_1__0_, bf16[896,512]{1,0:T(8,128)(2,1)S(1)} %collective-permute-done.64.refs_1__1_, ...), custom_call_target="tpu_custom_call" | custom-call | tf_op jit(solution)/shard_map/unpack_late/pallas_call | solution.py:166
  (149 shorter events, 42.8 us)
Async XLA Ops:
  2.9 15.9 %collective-permute-start.4 = (bf16[144,512]{1,0:T(8,128)(2,1)S(1)}, bf16[144,512]{1,0:T(8,128)(2,1)S(1)}, u32[]{:S(2)}, u32[]{:S(2)}) collective-permute-start(bf16[144,512]{1,0:T(8,128)(2,1)S(1)} %get-tuple-element.157), channel_id=1, source_target_pairs={{0,1},{1,0},{2,3},{3,2},{4,5},{5,4},{6,7},{7,6},{8,9},{9,8},{10,11... | collective-permute-start | bytes 442376 | tf_op jit(solution)/shard_map/ppermute | solution.py:256
  5.1 13.7 %collective-permute-start.5 = (bf16[144,512]{1,0:T(8,128)(2,1)S(1)}, bf16[144,512]{1,0:T(8,128)(2,1)S(1)}, u32[]{:S(2)}, u32[]{:S(2)}) collective-permute-start(bf16[144,512]{1,0:T(8,128)(2,1)S(1)} %get-tuple-element.157), channel_id=1, source_target_pairs={{0,2},{1,3},{2,0},{3,1},{4,6},{5,7},{6,4},{7,5},{8,10},{9,11},{10,... | collective-permute-start | bytes 442376 | tf_op jit(solution)/shard_map/ppermute | solution.py:256
  7.4 11.4 %collective-permute-start.6 = (bf16[144,512]{1,0:T(8,128)(2,1)S(1)}, bf16[144,512]{1,0:T(8,128)(2,1)S(1)}, u32[]{:S(2)}, u32[]{:S(2)}) collective-permute-start(bf16[144,512]{1,0:T(8,128)(2,1)S(1)} %get-tuple-element.157), channel_id=1, source_target_pairs={{0,3},{1,2},{2,1},{3,0},{4,7},{5,6},{6,5},{7,4},{8,11},{9,10},{10,... | collective-permute-start | bytes 442376 | tf_op jit(solution)/shard_map/ppermute | solution.py:256
  8.6 6.6 %collective-permute-start.1 = (bf16[32,512]{1,0:T(8,128)(2,1)S(1)}, bf16[32,512]{1,0:T(8,128)(2,1)S(1)}, u32[]{:S(2)}, u32[]{:S(2)}) collective-permute-start(bf16[32,512]{1,0:T(8,128)(2,1)S(1)} %get-tuple-element.149), channel_id=1, source_target_pairs={{0,16},{4,20},{8,24},{12,28},{16,0},{20,4},{24,8},{28,12},{1,17},{... | collective-permute-start | bytes 98312 | tf_op jit(solution)/shard_map/ppermute | solution.py:250
  10.5 4.8 %collective-permute-start.2 = (bf16[32,512]{1,0:T(8,128)(2,1)S(1)}, bf16[32,512]{1,0:T(8,128)(2,1)S(1)}, u32[]{:S(2)}, u32[]{:S(2)}) collective-permute-start(bf16[32,512]{1,0:T(8,128)(2,1)S(1)} %get-tuple-element.150), channel_id=1, source_target_pairs={{0,24},{4,28},{8,16},{12,20},{16,8},{20,12},{24,0},{28,4},{1,25},{... | collective-permute-start | bytes 98312 | tf_op jit(solution)/shard_map/ppermute | solution.py:250
  18.9 15.1 %collective-permute-start.20 = (bf16[144,1536]{1,0:T(8,128)(2,1)S(1)}, bf16[144,1536]{1,0:T(8,128)(2,1)S(1)}, u32[]{:S(2)}, u32[]{:S(2)}) collective-permute-start(bf16[144,1536]{1,0:T(8,128)(2,1)S(1)} %join_pieces.1.refs_9_.refs_0__0_), channel_id=1, source_target_pairs={{0,8},{4,12},{8,0},{12,4},{16,24},{20,28},{24,16},{28,20},{1,9},{5... | collective-permute-start | bytes 1327112 | tf_op jit(solution)/shard_map/ppermute | solution.py:250
  19.9 14.1 %collective-permute-start.21 = (bf16[144,1536]{1,0:T(8,128)(2,1)S(1)}, bf16[144,1536]{1,0:T(8,128)(2,1)S(1)}, u32[]{:S(2)}, u32[]{:S(2)}) collective-permute-start(bf16[144,1536]{1,0:T(8,128)(2,1)S(1)} %join_pieces.1.refs_9_.refs_0__0_), channel_id=1, source_target_pairs={{0,16},{4,20},{8,24},{12,28},{16,0},{20,4},{24,8},{28,12},{1,17},{... | collective-permute-start | bytes 1327112 | tf_op jit(solution)/shard_map/ppermute | solution.py:250
  24.8 4.1 %collective-permute-start.7 = (bf16[32,512]{1,0:T(8,128)(2,1)S(1)}, bf16[32,512]{1,0:T(8,128)(2,1)S(1)}, u32[]{:S(2)}, u32[]{:S(2)}) collective-permute-start(bf16[32,512]{1,0:T(8,128)(2,1)S(1)} %get-tuple-element.159.refs_0__0_), channel_id=1, source_target_pairs={{0,1},{1,0},{2,3},{3,2},{4,5},{5,4},{6,7},{7,6},{8,9},{9,8},{10,11... | collective-permute-start | bytes 98312 | tf_op jit(solution)/shard_map/ppermute | solution.py:256
  26.5 3.7 %collective-permute-start.8 = (bf16[32,512]{1,0:T(8,128)(2,1)S(1)}, bf16[32,512]{1,0:T(8,128)(2,1)S(1)}, u32[]{:S(2)}, u32[]{:S(2)}) collective-permute-start(bf16[32,512]{1,0:T(8,128)(2,1)S(1)} %get-tuple-element.159.refs_0__0_), channel_id=1, source_target_pairs={{0,2},{1,3},{2,0},{3,1},{4,6},{5,7},{6,4},{7,5},{8,10},{9,11},{10,... | collective-permute-start | bytes 98312 | tf_op jit(solution)/shard_map/ppermute | solution.py:256
  28.5 5.0 %collective-permute-start.9 = (bf16[32,512]{1,0:T(8,128)(2,1)S(1)}, bf16[32,512]{1,0:T(8,128)(2,1)S(1)}, u32[]{:S(2)}, u32[]{:S(2)}) collective-permute-start(bf16[32,512]{1,0:T(8,128)(2,1)S(1)} %get-tuple-element.159.refs_0__0_), channel_id=1, source_target_pairs={{0,3},{1,2},{2,1},{3,0},{4,7},{5,6},{6,5},{7,4},{8,11},{9,10},{10,... | collective-permute-start | bytes 98312 | tf_op jit(solution)/shard_map/ppermute | solution.py:256
  34.0 7.2 %collective-permute-start.22 = (bf16[144,768]{1,0:T(8,128)(2,1)S(1)}, bf16[144,768]{1,0:T(8,128)(2,1)S(1)}, u32[]{:S(2)}, u32[]{:S(2)}) collective-permute-start(bf16[144,768]{1,0:T(8,128)(2,1)S(1)} %get-tuple-element.172), channel_id=1, source_target_pairs={{0,16},{4,20},{8,24},{12,28},{16,0},{20,4},{24,8},{28,12},{1,17},{... | collective-permute-start | bytes 663560 | tf_op jit(solution)/shard_map/ppermute | solution.py:250
  34.3 6.9 %collective-permute-start.23 = (bf16[144,768]{1,0:T(8,128)(2,1)S(1)}, bf16[144,768]{1,0:T(8,128)(2,1)S(1)}, u32[]{:S(2)}, u32[]{:S(2)}) collective-permute-start(bf16[144,768]{1,0:T(8,128)(2,1)S(1)} %get-tuple-element.173), channel_id=1, source_target_pairs={{0,8},{4,12},{8,0},{12,4},{16,24},{20,28},{24,16},{28,20},{1,9},{5... | collective-permute-start | bytes 663560 | tf_op jit(solution)/shard_map/ppermute | solution.py:250
  34.7 3.7 %collective-permute-start.11 = (bf16[32,512]{1,0:T(8,128)(2,1)S(1)}, bf16[32,512]{1,0:T(8,128)(2,1)S(1)}, u32[]{:S(2)}, u32[]{:S(2)}) collective-permute-start(bf16[32,512]{1,0:T(8,128)(2,1)S(1)} %get-tuple-element.162), channel_id=1, source_target_pairs={{0,2},{1,3},{2,0},{3,1},{4,6},{5,7},{6,4},{7,5},{8,10},{9,11},{10,... | collective-permute-start | bytes 98312 | tf_op jit(solution)/shard_map/ppermute | solution.py:256
  36.3 4.6 %collective-permute-start.12 = (bf16[32,512]{1,0:T(8,128)(2,1)S(1)}, bf16[32,512]{1,0:T(8,128)(2,1)S(1)}, u32[]{:S(2)}, u32[]{:S(2)}) collective-permute-start(bf16[32,512]{1,0:T(8,128)(2,1)S(1)} %get-tuple-element.163), channel_id=1, source_target_pairs={{0,3},{1,2},{2,1},{3,0},{4,7},{5,6},{6,5},{7,4},{8,11},{9,10},{10,... | collective-permute-start | bytes 98312 | tf_op jit(solution)/shard_map/ppermute | solution.py:256
  41.3 12.4 %collective-permute-start.24 = (bf16[576,1536]{1,0:T(8,128)(2,1)S(1)}, bf16[576,1536]{1,0:T(8,128)(2,1)S(1)}, u32[]{:S(2)}, u32[]{:S(2)}) collective-permute-start(bf16[576,1536]{1,0:T(8,128)(2,1)S(1)} %stack_weights.1.refs_1__0_), channel_id=1, source_target_pairs={{0,4},{4,0},{8,12},{12,8},{16,20},{20,16},{24,28},{28,24},{1,5},{5... | collective-permute-start | bytes 5308424 | tf_op jit(solution)/shard_map/ppermute | solution.py:253
  48.5 6.0 %collective-permute-start.16 = (bf16[32,512]{1,0:T(8,128)(2,1)S(1)}, bf16[32,512]{1,0:T(8,128)(2,1)S(1)}, u32[]{:S(2)}, u32[]{:S(2)}) collective-permute-start(bf16[32,512]{1,0:T(8,128)(2,1)S(1)} %get-tuple-element.165.refs_0__0_), channel_id=1, source_target_pairs={{0,4},{4,0},{8,12},{12,8},{16,20},{20,16},{24,28},{28,24},{1,5},{5... | collective-permute-start | bytes 98312 | tf_op jit(solution)/shard_map/ppermute | solution.py:253
  49.5 5.1 %collective-permute-start.17 = (bf16[32,512]{1,0:T(8,128)(2,1)S(1)}, bf16[32,512]{1,0:T(8,128)(2,1)S(1)}, u32[]{:S(2)}, u32[]{:S(2)}) collective-permute-start(bf16[32,512]{1,0:T(8,128)(2,1)S(1)} %collective-permute-done.13.refs_0__1_), channel_id=1, source_target_pairs={{0,4},{4,0},{8,12},{12,8},{16,20},{20,16},{24,28},{28,24},{1,5},{5... | collective-permute-start | bytes 98312 | tf_op jit(solution)/shard_map/ppermute | solution.py:253
  49.9 4.7 %collective-permute-start.18 = (bf16[32,512]{1,0:T(8,128)(2,1)S(1)}, bf16[32,512]{1,0:T(8,128)(2,1)S(1)}, u32[]{:S(2)}, u32[]{:S(2)}) collective-permute-start(bf16[32,512]{1,0:T(8,128)(2,1)S(1)} %collective-permute-done.14.refs_0__2_), channel_id=1, source_target_pairs={{0,4},{4,0},{8,12},{12,8},{16,20},{20,16},{24,28},{28,24},{1,5},{5... | collective-permute-start | bytes 98312 | tf_op jit(solution)/shard_map/ppermute | solution.py:253
  64.1 3.8 %collective-permute-start.25 = (bf16[32,512]{1,0:T(8,128)(2,1)S(1)}, bf16[32,512]{1,0:T(8,128)(2,1)S(1)}, u32[]{:S(2)}, u32[]{:S(2)}) collective-permute-start(bf16[32,512]{1,0:T(8,128)(2,1)S(1)} %get-tuple-element.177), channel_id=1, source_target_pairs={{0,8},{4,12},{8,0},{12,4},{16,24},{20,28},{24,16},{28,20},{1,9},{5... | collective-permute-start | bytes 98312 | tf_op jit(solution)/shard_map/ppermute | solution.py:250
  64.4 4.0 %collective-permute-start.26 = (bf16[32,512]{1,0:T(8,128)(2,1)S(1)}, bf16[32,512]{1,0:T(8,128)(2,1)S(1)}, u32[]{:S(2)}, u32[]{:S(2)}) collective-permute-start(bf16[32,512]{1,0:T(8,128)(2,1)S(1)} %get-tuple-element.178), channel_id=1, source_target_pairs={{0,16},{4,20},{8,24},{12,28},{16,0},{20,4},{24,8},{28,12},{1,17},{... | collective-permute-start | bytes 98312 | tf_op jit(solution)/shard_map/ppermute | solution.py:250
  64.6 4.7 %collective-permute-start.27 = (bf16[32,512]{1,0:T(8,128)(2,1)S(1)}, bf16[32,512]{1,0:T(8,128)(2,1)S(1)}, u32[]{:S(2)}, u32[]{:S(2)}) collective-permute-start(bf16[32,512]{1,0:T(8,128)(2,1)S(1)} %get-tuple-element.179), channel_id=1, source_target_pairs={{0,24},{4,28},{8,16},{12,20},{16,8},{20,12},{24,0},{28,4},{1,25},{... | collective-permute-start | bytes 98312 | tf_op jit(solution)/shard_map/ppermute | solution.py:250
  77.0 3.8 %collective-permute-start.32 = (bf16[32,192]{1,0:T(8,128)(2,1)S(1)}, bf16[32,192]{1,0:T(8,128)(2,1)S(1)}, u32[]{:S(2)}, u32[]{:S(2)}) collective-permute-start(bf16[32,192]{1,0:T(8,128)(2,1)S(1)} %get-tuple-element.184.refs_8__1_), channel_id=1, source_target_pairs={{0,8},{4,12},{8,0},{12,4},{16,24},{20,28},{24,16},{28,20},{1,9},{5... | collective-permute-start | bytes 36872 | tf_op jit(solution)/shard_map/ppermute | solution.py:250
  91.1 7.6 %collective-permute-start.37 = (bf16[160,512]{1,0:T(8,128)(2,1)S(1)}, bf16[160,512]{1,0:T(8,128)(2,1)S(1)}, u32[]{:S(2)}, u32[]{:S(2)}) collective-permute-start(bf16[160,512]{1,0:T(8,128)(2,1)S(1)} %get-tuple-element.208), channel_id=1, source_target_pairs={{0,8},{4,12},{8,0},{12,4},{16,24},{20,28},{24,16},{28,20},{1,9},{5... | collective-permute-start | bytes 491528 | tf_op jit(solution)/shard_map/ppermute | solution.py:250
  91.4 7.3 %collective-permute-start.38 = (bf16[160,512]{1,0:T(8,128)(2,1)S(1)}, bf16[160,512]{1,0:T(8,128)(2,1)S(1)}, u32[]{:S(2)}, u32[]{:S(2)}) collective-permute-start(bf16[160,512]{1,0:T(8,128)(2,1)S(1)} %get-tuple-element.209), channel_id=1, source_target_pairs={{0,16},{4,20},{8,24},{12,28},{16,0},{20,4},{24,8},{28,12},{1,17},{... | collective-permute-start | bytes 491528 | tf_op jit(solution)/shard_map/ppermute | solution.py:250
  91.7 8.5 %collective-permute-start.39 = (bf16[160,512]{1,0:T(8,128)(2,1)S(1)}, bf16[160,512]{1,0:T(8,128)(2,1)S(1)}, u32[]{:S(2)}, u32[]{:S(2)}) collective-permute-start(bf16[160,512]{1,0:T(8,128)(2,1)S(1)} %get-tuple-element.210), channel_id=1, source_target_pairs={{0,24},{4,28},{8,16},{12,20},{16,8},{20,12},{24,0},{28,4},{1,25},{... | collective-permute-start | bytes 491528 | tf_op jit(solution)/shard_map/ppermute | solution.py:250
  93.8 4.8 %collective-permute-start.40 = (bf16[32,1024]{1,0:T(8,128)(2,1)S(1)}, bf16[32,1024]{1,0:T(8,128)(2,1)S(1)}, u32[]{:S(2)}, u32[]{:S(2)}) collective-permute-start(bf16[32,1024]{1,0:T(8,128)(2,1)S(1)} %get-tuple-element.215.refs_0__0_), channel_id=1, source_target_pairs={{0,2},{1,3},{2,0},{3,1},{4,6},{5,7},{6,4},{7,5},{8,10},{9,11},{10,... | collective-permute-start | bytes 196616 | tf_op jit(solution)/shard_map/ppermute | solution.py:256
  102.4 6.9 %collective-permute-start.46 = (bf16[160,256]{1,0:T(8,128)(2,1)S(1)}, bf16[160,256]{1,0:T(8,128)(2,1)S(1)}, u32[]{:S(2)}, u32[]{:S(2)}) collective-permute-start(bf16[160,256]{1,0:T(8,128)(2,1)S(1)} %get-tuple-element.228), channel_id=1, source_target_pairs={{0,2},{1,3},{2,0},{3,1},{4,6},{5,7},{6,4},{7,5},{8,10},{9,11},{10,... | collective-permute-start | bytes 245768 | tf_op jit(solution)/shard_map/ppermute | solution.py:256
  104.7 10.7 %collective-permute-start.42 = (bf16[256,512]{1,0:T(8,128)(2,1)S(1)}, bf16[256,512]{1,0:T(8,128)(2,1)S(1)}, u32[]{:S(2)}, u32[]{:S(2)}) collective-permute-start(bf16[256,512]{1,0:T(8,128)(2,1)S(1)} %get-tuple-element.224), channel_id=1, source_target_pairs={{0,8},{4,12},{8,0},{12,4},{16,24},{20,28},{24,16},{28,20},{1,9},{5... | collective-permute-start | bytes 786440 | tf_op jit(solution)/shard_map/ppermute | solution.py:250
  106.0 10.6 %collective-permute-start.43 = (bf16[256,512]{1,0:T(8,128)(2,1)S(1)}, bf16[256,512]{1,0:T(8,128)(2,1)S(1)}, u32[]{:S(2)}, u32[]{:S(2)}) collective-permute-start(bf16[256,512]{1,0:T(8,128)(2,1)S(1)} %get-tuple-element.225), channel_id=1, source_target_pairs={{0,16},{4,20},{8,24},{12,28},{16,0},{20,4},{24,8},{28,12},{1,17},{... | collective-permute-start | bytes 786440 | tf_op jit(solution)/shard_map/ppermute | solution.py:250
  106.2 12.4 %collective-permute-start.44 = (bf16[256,512]{1,0:T(8,128)(2,1)S(1)}, bf16[256,512]{1,0:T(8,128)(2,1)S(1)}, u32[]{:S(2)}, u32[]{:S(2)}) collective-permute-start(bf16[256,512]{1,0:T(8,128)(2,1)S(1)} %get-tuple-element.226), channel_id=1, source_target_pairs={{0,24},{4,28},{8,16},{12,20},{16,8},{20,12},{24,0},{28,4},{1,25},{... | collective-permute-start | bytes 786440 | tf_op jit(solution)/shard_map/ppermute | solution.py:250
  107.4 6.4 %collective-permute-start.45 = (bf16[64,1024]{1,0:T(8,128)(2,1)S(1)}, bf16[64,1024]{1,0:T(8,128)(2,1)S(1)}, u32[]{:S(2)}, u32[]{:S(2)}) collective-permute-start(bf16[64,1024]{1,0:T(8,128)(2,1)S(1)} %pair_stack.3.refs_3_.refs_0__0_), channel_id=1, source_target_pairs={{0,1},{1,0},{2,3},{3,2},{4,5},{5,4},{6,7},{7,6},{8,9},{9,8},{10,11... | collective-permute-start | bytes 393224 | tf_op jit(solution)/shard_map/ppermute | solution.py:256
  109.3 4.5 %collective-permute-start.47 = (bf16[160,256]{1,0:T(8,128)(2,1)S(1)}, bf16[160,256]{1,0:T(8,128)(2,1)S(1)}, u32[]{:S(2)}, u32[]{:S(2)}) collective-permute-start(bf16[160,256]{1,0:T(8,128)(2,1)S(1)} %early_line.3.refs_0_), channel_id=1, source_target_pairs={{0,1},{1,0},{2,3},{3,2},{4,5},{5,4},{6,7},{7,6},{8,9},{9,8},{10,11... | collective-permute-start | bytes 245768 | tf_op jit(solution)/shard_map/ppermute | solution.py:256
  113.9 13.5 %collective-permute-start.49 = (bf16[128,1024]{1,0:T(8,128)(2,1)S(1)}, bf16[128,1024]{1,0:T(8,128)(2,1)S(1)}, u32[]{:S(2)}, u32[]{:S(2)}) collective-permute-start(bf16[128,1024]{1,0:T(8,128)(2,1)S(1)} %pair_stack.4.refs_2_.refs_0__0_), channel_id=1, source_target_pairs={{0,8},{4,12},{8,0},{12,4},{16,24},{20,28},{24,16},{28,20},{1,9},{5... | collective-permute-start | bytes 786440 | tf_op jit(solution)/shard_map/ppermute | solution.py:250
  115.2 14.9 %collective-permute-start.50 = (bf16[128,1024]{1,0:T(8,128)(2,1)S(1)}, bf16[128,1024]{1,0:T(8,128)(2,1)S(1)}, u32[]{:S(2)}, u32[]{:S(2)}) collective-permute-start(bf16[128,1024]{1,0:T(8,128)(2,1)S(1)} %pair_stack.4.refs_2_.refs_0__0_), channel_id=1, source_target_pairs={{0,16},{4,20},{8,24},{12,28},{16,0},{20,4},{24,8},{28,12},{1,17},{... | collective-permute-start | bytes 786440 | tf_op jit(solution)/shard_map/ppermute | solution.py:250
  115.4 17.4 %collective-permute-start.51 = (bf16[128,1024]{1,0:T(8,128)(2,1)S(1)}, bf16[128,1024]{1,0:T(8,128)(2,1)S(1)}, u32[]{:S(2)}, u32[]{:S(2)}) collective-permute-start(bf16[128,1024]{1,0:T(8,128)(2,1)S(1)} %pair_stack.4.refs_2_.refs_0__0_), channel_id=1, source_target_pairs={{0,24},{4,28},{8,16},{12,20},{16,8},{20,12},{24,0},{28,4},{1,25},{... | collective-permute-start | bytes 786440 | tf_op jit(solution)/shard_map/ppermute | solution.py:250
  119.4 4.0 %collective-permute-start.53 = (bf16[224,256]{1,0:T(8,128)(2,1)S(1)}, bf16[224,256]{1,0:T(8,128)(2,1)S(1)}, u32[]{:S(2)}, u32[]{:S(2)}) collective-permute-start(bf16[224,256]{1,0:T(8,128)(2,1)S(1)} %get-tuple-element.233), channel_id=1, source_target_pairs={{0,1},{1,0},{2,3},{3,2},{4,5},{5,4},{6,7},{7,6},{8,9},{9,8},{10,11... | collective-permute-start | bytes 344072 | tf_op jit(solution)/shard_map/ppermute | solution.py:256
  119.8 4.2 %collective-permute-start.52 = (bf16[160,256]{1,0:T(8,128)(2,1)S(1)}, bf16[160,256]{1,0:T(8,128)(2,1)S(1)}, u32[]{:S(2)}, u32[]{:S(2)}) collective-permute-start(bf16[160,256]{1,0:T(8,128)(2,1)S(1)} %early_line.4.refs_1_), channel_id=1, source_target_pairs={{0,2},{1,3},{2,0},{3,1},{4,6},{5,7},{6,4},{7,5},{8,10},{9,11},{10,... | collective-permute-start | bytes 245768 | tf_op jit(solution)/shard_map/ppermute | solution.py:256
  124.6 10.4 %collective-permute-start.54 = (bf16[160,512]{1,0:T(8,128)(2,1)S(1)}, bf16[160,512]{1,0:T(8,128)(2,1)S(1)}, u32[]{:S(2)}, u32[]{:S(2)}) collective-permute-start(bf16[160,512]{1,0:T(8,128)(2,1)S(1)} %early_line.5.refs_1_.refs_0__0_), channel_id=1, source_target_pairs={{0,8},{4,12},{8,0},{12,4},{16,24},{20,28},{24,16},{28,20},{1,9},{5... | collective-permute-start | bytes 491528 | tf_op jit(solution)/shard_map/ppermute | solution.py:250
  125.2 9.8 %collective-permute-start.55 = (bf16[160,512]{1,0:T(8,128)(2,1)S(1)}, bf16[160,512]{1,0:T(8,128)(2,1)S(1)}, u32[]{:S(2)}, u32[]{:S(2)}) collective-permute-start(bf16[160,512]{1,0:T(8,128)(2,1)S(1)} %early_line.5.refs_1_.refs_0__0_), channel_id=1, source_target_pairs={{0,16},{4,20},{8,24},{12,28},{16,0},{20,4},{24,8},{28,12},{1,17},{... | collective-permute-start | bytes 491528 | tf_op jit(solution)/shard_map/ppermute | solution.py:250
  127.4 7.4 %collective-permute-start.56 = (bf16[224,256]{1,0:T(8,128)(2,1)S(1)}, bf16[224,256]{1,0:T(8,128)(2,1)S(1)}, u32[]{:S(2)}, u32[]{:S(2)}) collective-permute-start(bf16[224,256]{1,0:T(8,128)(2,1)S(1)} %late_line.2.refs_3_.refs_0_), channel_id=1, source_target_pairs={{0,2},{1,3},{2,0},{3,1},{4,6},{5,7},{6,4},{7,5},{8,10},{9,11},{10,... | collective-permute-start | bytes 344072 | tf_op jit(solution)/shard_map/ppermute | solution.py:256
  134.8 3.7 %collective-permute-start.57 = (bf16[224,256]{1,0:T(8,128)(2,1)S(1)}, bf16[224,256]{1,0:T(8,128)(2,1)S(1)}, u32[]{:S(2)}, u32[]{:S(2)}) collective-permute-start(bf16[224,256]{1,0:T(8,128)(2,1)S(1)} %late_line.3.refs_2_.refs_1_), channel_id=1, source_target_pairs={{0,1},{1,0},{2,3},{3,2},{4,5},{5,4},{6,7},{7,6},{8,9},{9,8},{10,11... | collective-permute-start | bytes 344072 | tf_op jit(solution)/shard_map/ppermute | solution.py:256
  135.0 4.1 %collective-permute-start.61 = (bf16[160,256]{1,0:T(8,128)(2,1)S(1)}, bf16[160,256]{1,0:T(8,128)(2,1)S(1)}, u32[]{:S(2)}, u32[]{:S(2)}) collective-permute-start(bf16[160,256]{1,0:T(8,128)(2,1)S(1)} %get-tuple-element.238.refs_3_), channel_id=1, source_target_pairs={{0,16},{4,20},{8,24},{12,28},{16,0},{20,4},{24,8},{28,12},{1,17},{... | collective-permute-start | bytes 245768 | tf_op jit(solution)/shard_map/ppermute | solution.py:250
  135.3 3.8 %collective-permute-start.62 = (bf16[160,256]{1,0:T(8,128)(2,1)S(1)}, bf16[160,256]{1,0:T(8,128)(2,1)S(1)}, u32[]{:S(2)}, u32[]{:S(2)}) collective-permute-start(bf16[160,256]{1,0:T(8,128)(2,1)S(1)} %get-tuple-element.241), channel_id=1, source_target_pairs={{0,8},{4,12},{8,0},{12,4},{16,24},{20,28},{24,16},{28,20},{1,9},{5... | collective-permute-start | bytes 245768 | tf_op jit(solution)/shard_map/ppermute | solution.py:250
  139.2 7.3 %collective-permute-start.63 = (bf16[640,512]{1,0:T(8,128)(2,1)S(1)}, bf16[640,512]{1,0:T(8,128)(2,1)S(1)}, u32[]{:S(2)}, u32[]{:S(2)}) collective-permute-start(bf16[640,512]{1,0:T(8,128)(2,1)S(1)} %early_stack.1.refs_1__0_), channel_id=1, source_target_pairs={{0,4},{4,0},{8,12},{12,8},{16,20},{20,16},{24,28},{28,24},{1,5},{5... | collective-permute-start | bytes 1966088 | tf_op jit(solution)/shard_map/ppermute | solution.py:253
  142.9 7.4 %collective-permute-start.58 = (bf16[224,512]{1,0:T(8,128)(2,1)S(1)}, bf16[224,512]{1,0:T(8,128)(2,1)S(1)}, u32[]{:S(2)}, u32[]{:S(2)}) collective-permute-start(bf16[224,512]{1,0:T(8,128)(2,1)S(1)} %late_join.1.refs_3_.refs_0__0_), channel_id=1, source_target_pairs={{0,8},{4,12},{8,0},{12,4},{16,24},{20,28},{24,16},{28,20},{1,9},{5... | collective-permute-start | bytes 688136 | tf_op jit(solution)/shard_map/ppermute | solution.py:250
  144.0 6.8 %collective-permute-start.59 = (bf16[224,512]{1,0:T(8,128)(2,1)S(1)}, bf16[224,512]{1,0:T(8,128)(2,1)S(1)}, u32[]{:S(2)}, u32[]{:S(2)}) collective-permute-start(bf16[224,512]{1,0:T(8,128)(2,1)S(1)} %late_join.1.refs_3_.refs_0__0_), channel_id=1, source_target_pairs={{0,16},{4,20},{8,24},{12,28},{16,0},{20,4},{24,8},{28,12},{1,17},{... | collective-permute-start | bytes 688136 | tf_op jit(solution)/shard_map/ppermute | solution.py:250
  144.4 11.6 %collective-permute-start.60 = (bf16[224,512]{1,0:T(8,128)(2,1)S(1)}, bf16[224,512]{1,0:T(8,128)(2,1)S(1)}, u32[]{:S(2)}, u32[]{:S(2)}) collective-permute-start(bf16[224,512]{1,0:T(8,128)(2,1)S(1)} %late_join.1.refs_3_.refs_0__0_), channel_id=1, source_target_pairs={{0,24},{4,28},{8,16},{12,20},{16,8},{20,12},{24,0},{28,4},{1,25},{... | collective-permute-start | bytes 688136 | tf_op jit(solution)/shard_map/ppermute | solution.py:250
  145.6 11.5 %collective-permute-start.65 = (bf16[512,1024]{1,0:T(8,128)(2,1)S(1)}, bf16[512,1024]{1,0:T(8,128)(2,1)S(1)}, u32[]{:S(2)}, u32[]{:S(2)}) collective-permute-start(bf16[512,1024]{1,0:T(8,128)(2,1)S(1)} %pair_stack.5.refs_5_.refs_0__0_), channel_id=1, source_target_pairs={{0,4},{4,0},{8,12},{12,8},{16,20},{20,16},{24,28},{28,24},{1,5},{5... | collective-permute-start | bytes 3145736 | tf_op jit(solution)/shard_map/ppermute | solution.py:253
  (30 other events, 207.1 us)

commit v5 on v4

--- a/solution.py
+++ b/solution.py
@@ -42,17 +42,16 @@
 def smooth_low(v):
     v = v.astype(BF)
     t = jnp.tanh(v * (BF(LEAN) + BF(CUBE) * (v * v)))
-    half = BF(0.5) * v
-    return half + half * t
+    return v * (BF(0.5) + BF(0.5) * t)
 
 
 def smooth_slope_low(v):
     v = v.astype(BF)
     v2 = v * v
     t = jnp.tanh(v * (BF(LEAN) + BF(CUBE) * v2))
-    half = BF(0.5) * v
-    slope = (BF(0.5) + BF(0.5) * t) + (half - half * (t * t)) * (BF(LEAN) + BF(3.0 * CUBE) * v2)
-    return half + half * t, slope
+    s = BF(0.5) + BF(0.5) * t
+    act = v * s
+    return act, s + (act * (BF(1.0) - s)) * (BF(2.0 * LEAN) + BF(6.0 * CUBE) * v2)
 
 
 def centred(x):

time: 163 us -> 162 us (level)
  no operation moved by 1% of the time
where the time goes in v5:
time: 162 us
  starting transfers between devices  75.3 us (46%)
  Pallas kernels  48.3 us (30%)
  waiting for transfers between devices  36.8 us (23%)
    pallas_call x40, Pallas kernels, call(): pl.pallas_call(run, out_shape=jax.tree.unflatten(out_tree, shapes), in_sp...  48.3 us
    ppermute x32, starting transfers between devices, to_chip(): return lax.ppermute(v, 'res', [(i, i ^ 2 * m) for i in range(n_res)])  30.4 us
    ppermute x17, starting transfers between devices, to_core(): return lax.ppermute(v, 'res', pair)  27.6 us
    ppermute x17, waiting for transfers between devices, to_hid(): return lax.ppermute(v, 'hid', [(i, i ^ m) for i in range(n_hid)])  17.6 us
    ppermute x17, starting transfers between devices, to_hid(): return lax.ppermute(v, 'hid', [(i, i ^ m) for i in range(n_hid)])  17.3 us
    ppermute x32, waiting for transfers between devices, to_chip(): return lax.ppermute(v, 'res', [(i, i ^ 2 * m) for i in range(n_res)])  13.2 us
    ppermute x17, waiting for transfers between devices, to_core(): return lax.ppermute(v, 'res', pair)  6.03 us
  transfers between devices with their start and end apart: 66, of which 24 were waited for; matrix products, arithmetic and copies ran while one was open for 0% of the time, Pallas kernels for 15%

profile of v5, /device:TPU:1, one launch (start us, length us, event | category | flops | bytes accessed | tf_op | source)
XLA Modules:
  0.0 162.0 jit_solution(6855792859744875762)
XLA Ops:
  0.8 2.1 %prepare_send.1 = (bf16[32,512]{1,0:T(8,128)(2,1)S(1)}, bf16[32,512]{1,0:T(8,128)(2,1)S(1)}, bf16[32,512]{1,0:T(8,128)(2,1)S(1)}, bf16[32,512]{1,0:T(8,128)(2,1)...) custom-call(s32[4]{0:T(128)S(1)} %pad_add_fusion.refs_0_, s32[8,16]{1,0:T(8,128)} %bitcast.59, ...), custom_call_target="tpu_custom_call" | custom-call | tf_op jit(solution)/shard_map/prepare_send/pallas_call | solution.py:165
  2.9 2.2 %collective-permute-start.4 = (bf16[144,512]{1,0:T(8,128)(2,1)S(1)}, bf16[144,512]{1,0:T(8,128)(2,1)S(1)}, u32[]{:S(2)}, u32[]{:S(2)}) collective-permute-start(bf16[144,512]{1,0:T(8,128)(2,1)S(1)} %get-tuple-element.157), channel_id=1, source_target_pairs={{0,1},{1,0},{2,3},{3,2},{4,5},{5,4},{6,7},{7,6},{8,9},{9,8},{10,11... | collective-permute-start | bytes 442376 | tf_op jit(solution)/shard_map/ppermute | solution.py:255
  5.1 2.3 %collective-permute-start.5 = (bf16[144,512]{1,0:T(8,128)(2,1)S(1)}, bf16[144,512]{1,0:T(8,128)(2,1)S(1)}, u32[]{:S(2)}, u32[]{:S(2)}) collective-permute-start(bf16[144,512]{1,0:T(8,128)(2,1)S(1)} %get-tuple-element.157), channel_id=1, source_target_pairs={{0,2},{1,3},{2,0},{3,1},{4,6},{5,7},{6,4},{7,5},{8,10},{9,11},{10,... | collective-permute-start | bytes 442376 | tf_op jit(solution)/shard_map/ppermute | solution.py:255
  10.5 2.2 %collective-permute-start.2 = (bf16[32,512]{1,0:T(8,128)(2,1)S(1)}, bf16[32,512]{1,0:T(8,128)(2,1)S(1)}, u32[]{:S(2)}, u32[]{:S(2)}) collective-permute-start(bf16[32,512]{1,0:T(8,128)(2,1)S(1)} %get-tuple-element.150), channel_id=1, source_target_pairs={{0,24},{4,28},{8,16},{12,20},{16,8},{20,12},{24,0},{28,4},{1,25},{... | collective-permute-start | bytes 98312 | tf_op jit(solution)/shard_map/ppermute | solution.py:249
  12.6 2.6 %prepare_rest.1 = (bf16[1920,128]{1,0:T(8,128)(2,1)S(1)}, f32[32,1]{1,0:T(8,128)S(1)}, f32[8,512]{1,0:T(8,128)S(1)}, f32[8,192]{1,0:T(8,128)S(1)}, bf16[1920,192]{1,0:T(8,128)(2,1)S(1)}) custom-call(s32[4]{0:T(128)S(1)} %pad_add_fusion.refs_0_, s32[32,60]{1,0:T(8,128)} %refs_1_.5, s32[1,32]{1,0:T(1,128)} %bitcast.73, f32[1,512]{1,0:T(1,128)} %bitcast.60, ...), custom_call_target="tpu_custom_call" | custom-call | tf_op jit(solution)/shard_map/prepare_rest/pallas_call | solution.py:165
  15.3 2.7 %collective-permute-start.3 = (bf16[64,512]{1,0:T(8,128)(2,1)S(1)}, bf16[64,512]{1,0:T(8,128)(2,1)S(1)}, u32[]{:S(2)}, u32[]{:S(2)}) collective-permute-start(bf16[64,512]{1,0:T(8,128)(2,1)S(1)} %get-tuple-element.153), channel_id=1, source_target_pairs={{0,4},{4,0},{8,12},{12,8},{16,20},{20,16},{24,28},{28,24},{1,5},{5... | collective-permute-start | bytes 196616 | tf_op jit(solution)/shard_map/ppermute | solution.py:252
  21.2 3.6 %message_one.1 = (f32[32,512]{1,0:T(8,128)S(1)}, bf16[32,512]{1,0:T(8,128)(2,1)S(1)}) custom-call(bf16[64,512]{1,0:T(8,128)(2,1)S(1)} %get-tuple-element.152.refs_2_.refs_0__0_, bf16[64,512]{1,0:T(8,128)(2,1)S(1)} %collective-permute-done.3.refs_3_.refs_0__1_, bf16[32,512]{1,0:T(8,128)(2,1)S(1)} %copy-done.9, ...), custom_call_target="tpu_custom_call" | custom-call | tf_op jit(solution)/shard_map/message_one/pallas_call | solution.py:165
  24.8 1.7 %collective-permute-start.7 = (bf16[32,512]{1,0:T(8,128)(2,1)S(1)}, bf16[32,512]{1,0:T(8,128)(2,1)S(1)}, u32[]{:S(2)}, u32[]{:S(2)}) collective-permute-start(bf16[32,512]{1,0:T(8,128)(2,1)S(1)} %get-tuple-element.159.refs_0__0_), channel_id=1, source_target_pairs={{0,1},{1,0},{2,3},{3,2},{4,5},{5,4},{6,7},{7,6},{8,9},{9,8},{10,11... | collective-permute-start | bytes 98312 | tf_op jit(solution)/shard_map/ppermute | solution.py:255
  26.6 2.0 %collective-permute-start.8 = (bf16[32,512]{1,0:T(8,128)(2,1)S(1)}, bf16[32,512]{1,0:T(8,128)(2,1)S(1)}, u32[]{:S(2)}, u32[]{:S(2)}) collective-permute-start(bf16[32,512]{1,0:T(8,128)(2,1)S(1)} %get-tuple-element.159.refs_0__0_), channel_id=1, source_target_pairs={{0,2},{1,3},{2,0},{3,1},{4,6},{5,7},{6,4},{7,5},{8,10},{9,11},{10,... | collective-permute-start | bytes 98312 | tf_op jit(solution)/shard_map/ppermute | solution.py:255
  28.9 1.3 collective-permute-done.8.refs_0__2_
  30.2 3.3 %collective-permute-done.9.refs_0__3_ = bf16[32,512]{1,0:T(8,128)(2,1)S(1)} collective-permute-done((bf16[32,512]{1,0:T(8,128)(2,1)S(1)}, bf16[32,512]{1,0:T(8,128)(2,1)S(1)}, u32[]{:S(2)}, u32[]{:S(2)}) %collective-permute-start.9) | collective-permute-done | bytes 32800 | tf_op jit(solution)/shard_map/ppermute | solution.py:255
  34.7 1.5 collective-permute-start.11
  36.3 2.0 %collective-permute-start.12 = (bf16[32,512]{1,0:T(8,128)(2,1)S(1)}, bf16[32,512]{1,0:T(8,128)(2,1)S(1)}, u32[]{:S(2)}, u32[]{:S(2)}) collective-permute-start(bf16[32,512]{1,0:T(8,128)(2,1)S(1)} %get-tuple-element.163), channel_id=1, source_target_pairs={{0,3},{1,2},{2,1},{3,0},{4,7},{5,6},{6,5},{7,4},{8,11},{9,10},{10,... | collective-permute-start | bytes 98312 | tf_op jit(solution)/shard_map/ppermute | solution.py:255
  38.4 2.5 %collective-permute-done.12.refs_1__3_ = bf16[32,512]{1,0:T(8,128)(2,1)S(1)} collective-permute-done((bf16[32,512]{1,0:T(8,128)(2,1)S(1)}, bf16[32,512]{1,0:T(8,128)(2,1)S(1)}, u32[]{:S(2)}, u32[]{:S(2)}) %collective-permute-start.12) | collective-permute-done | bytes 32800 | tf_op jit(solution)/shard_map/ppermute | solution.py:255
  41.3 4.5 %collective-permute-start.24 = (bf16[576,1536]{1,0:T(8,128)(2,1)S(1)}, bf16[576,1536]{1,0:T(8,128)(2,1)S(1)}, u32[]{:S(2)}, u32[]{:S(2)}) collective-permute-start(bf16[576,1536]{1,0:T(8,128)(2,1)S(1)} %stack_weights.1.refs_1__0_), channel_id=1, source_target_pairs={{0,4},{4,0},{8,12},{12,8},{16,20},{20,16},{24,28},{28,24},{1,5},{5... | collective-permute-start | bytes 5308424 | tf_op jit(solution)/shard_map/ppermute | solution.py:252
  49.9 1.5 collective-permute-start.18
  52.0 1.8 %collective-permute-start.19 = (bf16[32,512]{1,0:T(8,128)(2,1)S(1)}, bf16[32,512]{1,0:T(8,128)(2,1)S(1)}, u32[]{:S(2)}, u32[]{:S(2)}) collective-permute-start(bf16[32,512]{1,0:T(8,128)(2,1)S(1)} %collective-permute-done.15.refs_0__3_), channel_id=1, source_target_pairs={{0,4},{4,0},{8,12},{12,8},{16,20},{20,16},{24,28},{28,24},{1,5},{5... | collective-permute-start | bytes 98312 | tf_op jit(solution)/shard_map/ppermute | solution.py:252
  54.7 7.0 %layer_two.1 = (f32[1920,192]{1,0:T(8,128)S(1)}, bf16[1920,512]{1,0:T(8,128)(2,1)S(1)}, bf16[1920,512]{1,0:T(8,128)(2,1)S(1)}, bf16[1920,512]{1,0:T(8,128)(2,1)S...) custom-call(bf16[32,512]{1,0:T(8,128)(2,1)S(1)} %get-tuple-element.1, ...), custom_call_target="tpu_custom_call" | custom-call | tf_op jit(solution)/shard_map/layer_two/pallas_call | solution.py:165
  61.7 2.0 %feed_two.1 = (bf16[4,32,512]{2,1,0:T(8,128)(2,1)S(1)}, f32[32,512]{1,0:T(8,128)S(1)}, f32[32,512]{1,0:T(8,128)}, bf16[32,512]{1,0:T(8,128)(2,1)S(1)}, bf16[32,5...) custom-call(f32[32,512]{1,0:T(8,128)S(1)} %get-tuple-element.174.ref, ...), custom_call_target="tpu_custom_call" | custom-call | tf_op jit(solution)/shard_map/feed_two/pallas_call | solution.py:165
  64.1 2.2 %collective-permute-start.27 = (bf16[32,512]{1,0:T(8,128)(2,1)S(1)}, bf16[32,512]{1,0:T(8,128)(2,1)S(1)}, u32[]{:S(2)}, u32[]{:S(2)}) collective-permute-start(bf16[32,512]{1,0:T(8,128)(2,1)S(1)} %get-tuple-element.179), channel_id=1, source_target_pairs={{0,24},{4,28},{8,16},{12,20},{16,8},{20,12},{24,0},{28,4},{1,25},{... | collective-permute-start | bytes 98312 | tf_op jit(solution)/shard_map/ppermute | solution.py:249
  70.7 5.8 %edge_turn.1 = (f32[1920,192]{1,0:T(8,128)}, f32[1920,192]{1,0:T(8,128)S(1)}, bf16[1920,192]{1,0:T(8,128)(2,1)S(1)}, bf16[1920,192]{1,0:T(8,128)(2,1)S(1)}, bf16...) custom-call(bf16[32,512]{1,0:T(8,128)(2,1)S(1)} %get-tuple-element.1, ...), custom_call_target="tpu_custom_call" | custom-call | tf_op jit(solution)/shard_map/edge_turn/pallas_call | solution.py:165
  80.4 2.1 %collective-permute-done.34.refs_0__3_ = bf16[32,192]{1,0:T(8,128)(2,1)S(1)} collective-permute-done((bf16[32,192]{1,0:T(8,128)(2,1)S(1)}, bf16[32,192]{1,0:T(8,128)(2,1)S(1)}, u32[]{:S(2)}, u32[]{:S(2)}) %collective-permute-start.34) | collective-permute-done | bytes 12320 | tf_op jit(solution)/shard_map/ppermute | solution.py:249
  82.5 2.1 %collective-permute-start.35 = (bf16[64,192]{1,0:T(8,128)(2,1)S(1)}, bf16[64,192]{1,0:T(8,128)(2,1)S(1)}, u32[]{:S(2)}, u32[]{:S(2)}) collective-permute-start(bf16[64,192]{1,0:T(8,128)(2,1)S(1)} %get-tuple-element.194), channel_id=1, source_target_pairs={{0,4},{4,0},{8,12},{12,8},{16,20},{20,16},{24,28},{28,24},{1,5},{5... | collective-permute-start | bytes 73736 | tf_op jit(solution)/shard_map/ppermute | solution.py:252
  85.4 3.0 %node_turn.1 = (bf16[32,1024]{1,0:T(8,128)(2,1)S(1)}, f32[32,512]{1,0:T(8,128)S(1)}, f32[32,512]{1,0:T(8,128)S(1)}, bf16[640,512]{1,0:T(8,128)(2,1)S(1)}, bf16[640,512]{1,0:T(8,128)(2,1)S(1)}) custom-call(s32[4]{0:T(128)S(1)} %pad_add_fusion.refs_0_, bf16[64,192]{1,0:T(8,128)(2,1)S(1)} %get-tuple-element.193.refs_1__0_, ...), custom_call_target="tpu_custom_call" | custom-call | tf_op jit(solution)/shard_map/node_turn/pallas_call | solution.py:165
  88.8 1.3 message_second.1
  91.2 2.2 %collective-permute-start.39 = (bf16[160,512]{1,0:T(8,128)(2,1)S(1)}, bf16[160,512]{1,0:T(8,128)(2,1)S(1)}, u32[]{:S(2)}, u32[]{:S(2)}) collective-permute-start(bf16[160,512]{1,0:T(8,128)(2,1)S(1)} %get-tuple-element.210), channel_id=1, source_target_pairs={{0,24},{4,28},{8,16},{12,20},{16,8},{20,12},{24,0},{28,4},{1,25},{... | collective-permute-start | bytes 491528 | tf_op jit(solution)/shard_map/ppermute | solution.py:249
  93.4 2.6 %message_first.1 = (bf16[1920,512]{1,0:T(8,128)(2,1)S(1)}, bf16[32,512]{1,0:T(8,128)(2,1)S(1)}, bf16[32,512]{1,0:T(8,128)(2,1)S(1)}, bf16[32,512]{1,0:T(8,128)(2...) custom-call(bf16[32,512]{1,0:T(8,128)(2,1)S(1)} %get-tuple-element.165.refs_0__0_, ...), custom_call_target="tpu_custom_call" | custom-call | tf_op jit(solution)/shard_map/message_first/pallas_call | solution.py:165
  96.0 2.2 %collective-permute-done.40.refs_0__1_ = bf16[32,1024]{1,0:T(8,128)(2,1)S(1)} collective-permute-done((bf16[32,1024]{1,0:T(8,128)(2,1)S(1)}, bf16[32,1024]{1,0:T(8,128)(2,1)S(1)}, u32[]{:S(2)}, u32[]{:S(2)}) %collective-permute-start.40) | collective-permute-done | bytes 65568 | tf_op jit(solution)/shard_map/ppermute | solution.py:255
  98.3 1.4 collective-permute-done.39.refs_1__3_
  100.5 1.5 collective-permute-start.41
  102.0 2.1 %collective-permute-done.41.refs_1_ = bf16[896,512]{1,0:T(8,128)(2,1)S(1)} collective-permute-done((bf16[896,512]{1,0:T(8,128)(2,1)S(1)}, bf16[896,512]{1,0:T(8,128)(2,1)S(1)}, u32[]{:S(2)}, u32[]{:S(2)}) %collective-permute-start.41) | collective-permute-done | bytes 917536 | tf_op jit(solution)/shard_map/ppermute | solution.py:252
  104.3 1.3 collective-permute-start.42
  107.4 1.5 collective-permute-done.46.refs_1_
  109.0 4.4 %collective-permute-done.47.refs_1_ = bf16[160,256]{1,0:T(8,128)(2,1)S(1)} collective-permute-done((bf16[160,256]{1,0:T(8,128)(2,1)S(1)}, bf16[160,256]{1,0:T(8,128)(2,1)S(1)}, u32[]{:S(2)}, u32[]{:S(2)}) %collective-permute-start.47) | collective-permute-done | bytes 81952 | tf_op jit(solution)/shard_map/ppermute | solution.py:255
  113.5 1.3 collective-permute-start.49
  116.2 2.0 %collective-permute-done.44.refs_1__3_ = bf16[256,512]{1,0:T(8,128)(2,1)S(1)} collective-permute-done((bf16[256,512]{1,0:T(8,128)(2,1)S(1)}, bf16[256,512]{1,0:T(8,128)(2,1)S(1)}, u32[]{:S(2)}, u32[]{:S(2)}) %collective-permute-start.44) | collective-permute-done | bytes 262176 | tf_op jit(solution)/shard_map/ppermute | solution.py:249
  119.4 2.1 %collective-permute-start.52 = (bf16[160,256]{1,0:T(8,128)(2,1)S(1)}, bf16[160,256]{1,0:T(8,128)(2,1)S(1)}, u32[]{:S(2)}, u32[]{:S(2)}) collective-permute-start(bf16[160,256]{1,0:T(8,128)(2,1)S(1)} %early_line.4.refs_1_), channel_id=1, source_target_pairs={{0,2},{1,3},{2,0},{3,1},{4,6},{5,7},{6,4},{7,5},{8,10},{9,11},{10,... | collective-permute-start | bytes 245768 | tf_op jit(solution)/shard_map/ppermute | solution.py:255
  121.5 1.5 collective-permute-done.53.refs_1_
  124.8 2.1 %collective-permute-start.55 = (bf16[160,512]{1,0:T(8,128)(2,1)S(1)}, bf16[160,512]{1,0:T(8,128)(2,1)S(1)}, u32[]{:S(2)}, u32[]{:S(2)}) collective-permute-start(bf16[160,512]{1,0:T(8,128)(2,1)S(1)} %early_line.5.refs_1_.refs_0__0_), channel_id=1, source_target_pairs={{0,16},{4,20},{8,24},{12,28},{16,0},{20,4},{24,8},{28,12},{1,17},{... | collective-permute-start | bytes 491528 | tf_op jit(solution)/shard_map/ppermute | solution.py:249
  126.9 2.0 %collective-permute-start.56 = (bf16[224,256]{1,0:T(8,128)(2,1)S(1)}, bf16[224,256]{1,0:T(8,128)(2,1)S(1)}, u32[]{:S(2)}, u32[]{:S(2)}) collective-permute-start(bf16[224,256]{1,0:T(8,128)(2,1)S(1)} %late_line.2.refs_3_.refs_0_), channel_id=1, source_target_pairs={{0,2},{1,3},{2,0},{3,1},{4,6},{5,7},{6,4},{7,5},{8,10},{9,11},{10,... | collective-permute-start | bytes 344072 | tf_op jit(solution)/shard_map/ppermute | solution.py:255
  129.6 2.7 %collective-permute-start.48 = (bf16[64,512]{1,0:T(8,128)(2,1)S(1)}, bf16[64,512]{1,0:T(8,128)(2,1)S(1)}, u32[]{:S(2)}, u32[]{:S(2)}) collective-permute-start(bf16[64,512]{1,0:T(8,128)(2,1)S(1)} %get-tuple-element.230), channel_id=1, source_target_pairs={{0,4},{4,0},{8,12},{12,8},{16,20},{20,16},{24,28},{28,24},{1,5},{5... | collective-permute-start | bytes 196616 | tf_op jit(solution)/shard_map/ppermute | solution.py:252
  136.0 2.0 %edge_end.1 = (f32[1920,192]{1,0:T(8,128)}, f32[8,128]{1,0:T(8,128)S(1)}) custom-call(f32[1920,192]{1,0:T(8,128)S(1)} %get-tuple-element.235.refs_0_, bf16[1920,512]{1,0:T(8,128)(2,1)S(1)} %get-tuple-element.236.refs_1_, bf16[1216,512]{1,0:T(8,128)(2,1)S(1)} %copy-done, bf16[160,256]{1,0:T(8,128)(2,1)S(1)} %get-tuple-element.238.refs_3_), custom_call_target="tpu_custom_call" | custom-call | tf_op jit(solution)/shard_map/edge_end/pallas_call | solution.py:165
  138.8 3.7 %collective-permute-start.63 = (bf16[640,512]{1,0:T(8,128)(2,1)S(1)}, bf16[640,512]{1,0:T(8,128)(2,1)S(1)}, u32[]{:S(2)}, u32[]{:S(2)}) collective-permute-start(bf16[640,512]{1,0:T(8,128)(2,1)S(1)} %early_stack.1.refs_1__0_), channel_id=1, source_target_pairs={{0,4},{4,0},{8,12},{12,8},{16,20},{20,16},{24,28},{28,24},{1,5},{5... | collective-permute-start | bytes 1966088 | tf_op jit(solution)/shard_map/ppermute | solution.py:252
  146.0 2.4 %unpack_early.1 = (f32[192,1216]{1,0:T(8,128)}, f32[192,192]{1,0:T(8,128)}, f32[192,192]{1,0:T(8,128)}, f32[512,512]{1,0:T(8,128)}, f32[1,512]{1,0:T(1,128)}, /*...) custom-call(s32[4]{0:T(128)S(1)} %pad_add_fusion.refs_0_, ...), custom_call_target="tpu_custom_call" | custom-call | tf_op jit(solution)/shard_map/unpack_early/pallas_call | solution.py:165
  148.4 1.5 feed_weights.1
  150.4 5.1 %collective-permute-done.60.refs_0__3_ = bf16[224,512]{1,0:T(8,128)(2,1)S(1)} collective-permute-done((bf16[224,512]{1,0:T(8,128)(2,1)S(1)}, bf16[224,512]{1,0:T(8,128)(2,1)S(1)}, u32[]{:S(2)}, u32[]{:S(2)}) %collective-permute-start.60) | collective-permute-done | bytes 229408 | tf_op jit(solution)/shard_map/ppermute | solution.py:249
  156.6 2.5 %feed_weights_more.1 = (f32[512,512]{1,0:T(8,128)}, f32[512,512]{1,0:T(8,128)}, f32[8,128]{1,0:T(8,128)S(1)}) custom-call(bf16[512,1024]{1,0:T(8,128)(2,1)S(1)} %collective-permute-done.65.refs_0__0_, bf16[512,512]{1,0:T(8,128)(2,1)S(1)} %copy-done.1, f32[1,512]{1,0:T(1,128)S(1)} %bitcast.57, bf16[512,512]{1,0:T(8,128)(2,1)S(1)} %copy-done.2, ...), custom_call_target="tpu_custom_call" | custom-call | tf_op jit(solution)/shard_map/feed_weights_more/pallas_call | solution.py:165
  159.2 2.6 %unpack_late.1 = (f32[1216,512]{1,0:T(8,128)}, f32[512,512]{1,0:T(8,128)}, f32[1,512]{1,0:T(1,128)}, f32[1,512]{1,0:T(1,128)}) custom-call(s32[4]{0:T(128)S(1)} %pad_add_fusion.refs_0_, bf16[896,512]{1,0:T(8,128)(2,1)S(1)} %late_stack.1.refs_6_.refs_1__0_, bf16[896,512]{1,0:T(8,128)(2,1)S(1)} %collective-permute-done.64.refs_1__1_, ...), custom_call_target="tpu_custom_call" | custom-call | tf_op jit(solution)/shard_map/unpack_late/pallas_call | solution.py:165
  (149 shorter events, 42.8 us)
Async XLA Ops:
  2.9 15.9 %collective-permute-start.4 = (bf16[144,512]{1,0:T(8,128)(2,1)S(1)}, bf16[144,512]{1,0:T(8,128)(2,1)S(1)}, u32[]{:S(2)}, u32[]{:S(2)}) collective-permute-start(bf16[144,512]{1,0:T(8,128)(2,1)S(1)} %get-tuple-element.157), channel_id=1, source_target_pairs={{0,1},{1,0},{2,3},{3,2},{4,5},{5,4},{6,7},{7,6},{8,9},{9,8},{10,11... | collective-permute-start | bytes 442376 | tf_op jit(solution)/shard_map/ppermute | solution.py:255
  5.1 13.7 %collective-permute-start.5 = (bf16[144,512]{1,0:T(8,128)(2,1)S(1)}, bf16[144,512]{1,0:T(8,128)(2,1)S(1)}, u32[]{:S(2)}, u32[]{:S(2)}) collective-permute-start(bf16[144,512]{1,0:T(8,128)(2,1)S(1)} %get-tuple-element.157), channel_id=1, source_target_pairs={{0,2},{1,3},{2,0},{3,1},{4,6},{5,7},{6,4},{7,5},{8,10},{9,11},{10,... | collective-permute-start | bytes 442376 | tf_op jit(solution)/shard_map/ppermute | solution.py:255
  7.4 11.4 %collective-permute-start.6 = (bf16[144,512]{1,0:T(8,128)(2,1)S(1)}, bf16[144,512]{1,0:T(8,128)(2,1)S(1)}, u32[]{:S(2)}, u32[]{:S(2)}) collective-permute-start(bf16[144,512]{1,0:T(8,128)(2,1)S(1)} %get-tuple-element.157), channel_id=1, source_target_pairs={{0,3},{1,2},{2,1},{3,0},{4,7},{5,6},{6,5},{7,4},{8,11},{9,10},{10,... | collective-permute-start | bytes 442376 | tf_op jit(solution)/shard_map/ppermute | solution.py:255
  8.6 6.6 %collective-permute-start.1 = (bf16[32,512]{1,0:T(8,128)(2,1)S(1)}, bf16[32,512]{1,0:T(8,128)(2,1)S(1)}, u32[]{:S(2)}, u32[]{:S(2)}) collective-permute-start(bf16[32,512]{1,0:T(8,128)(2,1)S(1)} %get-tuple-element.149), channel_id=1, source_target_pairs={{0,16},{4,20},{8,24},{12,28},{16,0},{20,4},{24,8},{28,12},{1,17},{... | collective-permute-start | bytes 98312 | tf_op jit(solution)/shard_map/ppermute | solution.py:249
  10.5 4.8 %collective-permute-start.2 = (bf16[32,512]{1,0:T(8,128)(2,1)S(1)}, bf16[32,512]{1,0:T(8,128)(2,1)S(1)}, u32[]{:S(2)}, u32[]{:S(2)}) collective-permute-start(bf16[32,512]{1,0:T(8,128)(2,1)S(1)} %get-tuple-element.150), channel_id=1, source_target_pairs={{0,24},{4,28},{8,16},{12,20},{16,8},{20,12},{24,0},{28,4},{1,25},{... | collective-permute-start | bytes 98312 | tf_op jit(solution)/shard_map/ppermute | solution.py:249
  18.9 15.1 %collective-permute-start.20 = (bf16[144,1536]{1,0:T(8,128)(2,1)S(1)}, bf16[144,1536]{1,0:T(8,128)(2,1)S(1)}, u32[]{:S(2)}, u32[]{:S(2)}) collective-permute-start(bf16[144,1536]{1,0:T(8,128)(2,1)S(1)} %join_pieces.1.refs_9_.refs_0__0_), channel_id=1, source_target_pairs={{0,8},{4,12},{8,0},{12,4},{16,24},{20,28},{24,16},{28,20},{1,9},{5... | collective-permute-start | bytes 1327112 | tf_op jit(solution)/shard_map/ppermute | solution.py:249
  19.9 14.1 %collective-permute-start.21 = (bf16[144,1536]{1,0:T(8,128)(2,1)S(1)}, bf16[144,1536]{1,0:T(8,128)(2,1)S(1)}, u32[]{:S(2)}, u32[]{:S(2)}) collective-permute-start(bf16[144,1536]{1,0:T(8,128)(2,1)S(1)} %join_pieces.1.refs_9_.refs_0__0_), channel_id=1, source_target_pairs={{0,16},{4,20},{8,24},{12,28},{16,0},{20,4},{24,8},{28,12},{1,17},{... | collective-permute-start | bytes 1327112 | tf_op jit(solution)/shard_map/ppermute | solution.py:249
  24.8 4.1 %collective-permute-start.7 = (bf16[32,512]{1,0:T(8,128)(2,1)S(1)}, bf16[32,512]{1,0:T(8,128)(2,1)S(1)}, u32[]{:S(2)}, u32[]{:S(2)}) collective-permute-start(bf16[32,512]{1,0:T(8,128)(2,1)S(1)} %get-tuple-element.159.refs_0__0_), channel_id=1, source_target_pairs={{0,1},{1,0},{2,3},{3,2},{4,5},{5,4},{6,7},{7,6},{8,9},{9,8},{10,11... | collective-permute-start | bytes 98312 | tf_op jit(solution)/shard_map/ppermute | solution.py:255
  26.6 3.7 %collective-permute-start.8 = (bf16[32,512]{1,0:T(8,128)(2,1)S(1)}, bf16[32,512]{1,0:T(8,128)(2,1)S(1)}, u32[]{:S(2)}, u32[]{:S(2)}) collective-permute-start(bf16[32,512]{1,0:T(8,128)(2,1)S(1)} %get-tuple-element.159.refs_0__0_), channel_id=1, source_target_pairs={{0,2},{1,3},{2,0},{3,1},{4,6},{5,7},{6,4},{7,5},{8,10},{9,11},{10,... | collective-permute-start | bytes 98312 | tf_op jit(solution)/shard_map/ppermute | solution.py:255
  28.5 5.0 %collective-permute-start.9 = (bf16[32,512]{1,0:T(8,128)(2,1)S(1)}, bf16[32,512]{1,0:T(8,128)(2,1)S(1)}, u32[]{:S(2)}, u32[]{:S(2)}) collective-permute-start(bf16[32,512]{1,0:T(8,128)(2,1)S(1)} %get-tuple-element.159.refs_0__0_), channel_id=1, source_target_pairs={{0,3},{1,2},{2,1},{3,0},{4,7},{5,6},{6,5},{7,4},{8,11},{9,10},{10,... | collective-permute-start | bytes 98312 | tf_op jit(solution)/shard_map/ppermute | solution.py:255
  34.1 7.1 %collective-permute-start.22 = (bf16[144,768]{1,0:T(8,128)(2,1)S(1)}, bf16[144,768]{1,0:T(8,128)(2,1)S(1)}, u32[]{:S(2)}, u32[]{:S(2)}) collective-permute-start(bf16[144,768]{1,0:T(8,128)(2,1)S(1)} %get-tuple-element.172), channel_id=1, source_target_pairs={{0,16},{4,20},{8,24},{12,28},{16,0},{20,4},{24,8},{28,12},{1,17},{... | collective-permute-start | bytes 663560 | tf_op jit(solution)/shard_map/ppermute | solution.py:249
  34.3 6.9 %collective-permute-start.23 = (bf16[144,768]{1,0:T(8,128)(2,1)S(1)}, bf16[144,768]{1,0:T(8,128)(2,1)S(1)}, u32[]{:S(2)}, u32[]{:S(2)}) collective-permute-start(bf16[144,768]{1,0:T(8,128)(2,1)S(1)} %get-tuple-element.173), channel_id=1, source_target_pairs={{0,8},{4,12},{8,0},{12,4},{16,24},{20,28},{24,16},{28,20},{1,9},{5... | collective-permute-start | bytes 663560 | tf_op jit(solution)/shard_map/ppermute | solution.py:249
  34.7 3.7 %collective-permute-start.11 = (bf16[32,512]{1,0:T(8,128)(2,1)S(1)}, bf16[32,512]{1,0:T(8,128)(2,1)S(1)}, u32[]{:S(2)}, u32[]{:S(2)}) collective-permute-start(bf16[32,512]{1,0:T(8,128)(2,1)S(1)} %get-tuple-element.162), channel_id=1, source_target_pairs={{0,2},{1,3},{2,0},{3,1},{4,6},{5,7},{6,4},{7,5},{8,10},{9,11},{10,... | collective-permute-start | bytes 98312 | tf_op jit(solution)/shard_map/ppermute | solution.py:255
  36.3 4.6 %collective-permute-start.12 = (bf16[32,512]{1,0:T(8,128)(2,1)S(1)}, bf16[32,512]{1,0:T(8,128)(2,1)S(1)}, u32[]{:S(2)}, u32[]{:S(2)}) collective-permute-start(bf16[32,512]{1,0:T(8,128)(2,1)S(1)} %get-tuple-element.163), channel_id=1, source_target_pairs={{0,3},{1,2},{2,1},{3,0},{4,7},{5,6},{6,5},{7,4},{8,11},{9,10},{10,... | collective-permute-start | bytes 98312 | tf_op jit(solution)/shard_map/ppermute | solution.py:255
  41.3 12.5 %collective-permute-start.24 = (bf16[576,1536]{1,0:T(8,128)(2,1)S(1)}, bf16[576,1536]{1,0:T(8,128)(2,1)S(1)}, u32[]{:S(2)}, u32[]{:S(2)}) collective-permute-start(bf16[576,1536]{1,0:T(8,128)(2,1)S(1)} %stack_weights.1.refs_1__0_), channel_id=1, source_target_pairs={{0,4},{4,0},{8,12},{12,8},{16,20},{20,16},{24,28},{28,24},{1,5},{5... | collective-permute-start | bytes 5308424 | tf_op jit(solution)/shard_map/ppermute | solution.py:252
  48.6 6.0 %collective-permute-start.16 = (bf16[32,512]{1,0:T(8,128)(2,1)S(1)}, bf16[32,512]{1,0:T(8,128)(2,1)S(1)}, u32[]{:S(2)}, u32[]{:S(2)}) collective-permute-start(bf16[32,512]{1,0:T(8,128)(2,1)S(1)} %get-tuple-element.165.refs_0__0_), channel_id=1, source_target_pairs={{0,4},{4,0},{8,12},{12,8},{16,20},{20,16},{24,28},{28,24},{1,5},{5... | collective-permute-start | bytes 98312 | tf_op jit(solution)/shard_map/ppermute | solution.py:252
  49.5 5.1 %collective-permute-start.17 = (bf16[32,512]{1,0:T(8,128)(2,1)S(1)}, bf16[32,512]{1,0:T(8,128)(2,1)S(1)}, u32[]{:S(2)}, u32[]{:S(2)}) collective-permute-start(bf16[32,512]{1,0:T(8,128)(2,1)S(1)} %collective-permute-done.13.refs_0__1_), channel_id=1, source_target_pairs={{0,4},{4,0},{8,12},{12,8},{16,20},{20,16},{24,28},{28,24},{1,5},{5... | collective-permute-start | bytes 98312 | tf_op jit(solution)/shard_map/ppermute | solution.py:252
  49.9 4.7 %collective-permute-start.18 = (bf16[32,512]{1,0:T(8,128)(2,1)S(1)}, bf16[32,512]{1,0:T(8,128)(2,1)S(1)}, u32[]{:S(2)}, u32[]{:S(2)}) collective-permute-start(bf16[32,512]{1,0:T(8,128)(2,1)S(1)} %collective-permute-done.14.refs_0__2_), channel_id=1, source_target_pairs={{0,4},{4,0},{8,12},{12,8},{16,20},{20,16},{24,28},{28,24},{1,5},{5... | collective-permute-start | bytes 98312 | tf_op jit(solution)/shard_map/ppermute | solution.py:252
  63.7 3.8 %collective-permute-start.25 = (bf16[32,512]{1,0:T(8,128)(2,1)S(1)}, bf16[32,512]{1,0:T(8,128)(2,1)S(1)}, u32[]{:S(2)}, u32[]{:S(2)}) collective-permute-start(bf16[32,512]{1,0:T(8,128)(2,1)S(1)} %get-tuple-element.177), channel_id=1, source_target_pairs={{0,8},{4,12},{8,0},{12,4},{16,24},{20,28},{24,16},{28,20},{1,9},{5... | collective-permute-start | bytes 98312 | tf_op jit(solution)/shard_map/ppermute | solution.py:249
  63.9 4.0 %collective-permute-start.26 = (bf16[32,512]{1,0:T(8,128)(2,1)S(1)}, bf16[32,512]{1,0:T(8,128)(2,1)S(1)}, u32[]{:S(2)}, u32[]{:S(2)}) collective-permute-start(bf16[32,512]{1,0:T(8,128)(2,1)S(1)} %get-tuple-element.178), channel_id=1, source_target_pairs={{0,16},{4,20},{8,24},{12,28},{16,0},{20,4},{24,8},{28,12},{1,17},{... | collective-permute-start | bytes 98312 | tf_op jit(solution)/shard_map/ppermute | solution.py:249
  64.1 4.7 %collective-permute-start.27 = (bf16[32,512]{1,0:T(8,128)(2,1)S(1)}, bf16[32,512]{1,0:T(8,128)(2,1)S(1)}, u32[]{:S(2)}, u32[]{:S(2)}) collective-permute-start(bf16[32,512]{1,0:T(8,128)(2,1)S(1)} %get-tuple-element.179), channel_id=1, source_target_pairs={{0,24},{4,28},{8,16},{12,20},{16,8},{20,12},{24,0},{28,4},{1,25},{... | collective-permute-start | bytes 98312 | tf_op jit(solution)/shard_map/ppermute | solution.py:249
  76.5 3.8 %collective-permute-start.32 = (bf16[32,192]{1,0:T(8,128)(2,1)S(1)}, bf16[32,192]{1,0:T(8,128)(2,1)S(1)}, u32[]{:S(2)}, u32[]{:S(2)}) collective-permute-start(bf16[32,192]{1,0:T(8,128)(2,1)S(1)} %get-tuple-element.184.refs_8__1_), channel_id=1, source_target_pairs={{0,8},{4,12},{8,0},{12,4},{16,24},{20,28},{24,16},{28,20},{1,9},{5... | collective-permute-start | bytes 36872 | tf_op jit(solution)/shard_map/ppermute | solution.py:249
  90.7 7.6 %collective-permute-start.37 = (bf16[160,512]{1,0:T(8,128)(2,1)S(1)}, bf16[160,512]{1,0:T(8,128)(2,1)S(1)}, u32[]{:S(2)}, u32[]{:S(2)}) collective-permute-start(bf16[160,512]{1,0:T(8,128)(2,1)S(1)} %get-tuple-element.208), channel_id=1, source_target_pairs={{0,8},{4,12},{8,0},{12,4},{16,24},{20,28},{24,16},{28,20},{1,9},{5... | collective-permute-start | bytes 491528 | tf_op jit(solution)/shard_map/ppermute | solution.py:249
  91.0 7.3 %collective-permute-start.38 = (bf16[160,512]{1,0:T(8,128)(2,1)S(1)}, bf16[160,512]{1,0:T(8,128)(2,1)S(1)}, u32[]{:S(2)}, u32[]{:S(2)}) collective-permute-start(bf16[160,512]{1,0:T(8,128)(2,1)S(1)} %get-tuple-element.209), channel_id=1, source_target_pairs={{0,16},{4,20},{8,24},{12,28},{16,0},{20,4},{24,8},{28,12},{1,17},{... | collective-permute-start | bytes 491528 | tf_op jit(solution)/shard_map/ppermute | solution.py:249
  91.2 8.5 %collective-permute-start.39 = (bf16[160,512]{1,0:T(8,128)(2,1)S(1)}, bf16[160,512]{1,0:T(8,128)(2,1)S(1)}, u32[]{:S(2)}, u32[]{:S(2)}) collective-permute-start(bf16[160,512]{1,0:T(8,128)(2,1)S(1)} %get-tuple-element.210), channel_id=1, source_target_pairs={{0,24},{4,28},{8,16},{12,20},{16,8},{20,12},{24,0},{28,4},{1,25},{... | collective-permute-start | bytes 491528 | tf_op jit(solution)/shard_map/ppermute | solution.py:249
  93.4 4.8 %collective-permute-start.40 = (bf16[32,1024]{1,0:T(8,128)(2,1)S(1)}, bf16[32,1024]{1,0:T(8,128)(2,1)S(1)}, u32[]{:S(2)}, u32[]{:S(2)}) collective-permute-start(bf16[32,1024]{1,0:T(8,128)(2,1)S(1)} %get-tuple-element.215.refs_0__0_), channel_id=1, source_target_pairs={{0,2},{1,3},{2,0},{3,1},{4,6},{5,7},{6,4},{7,5},{8,10},{9,11},{10,... | collective-permute-start | bytes 196616 | tf_op jit(solution)/shard_map/ppermute | solution.py:255
  102.0 6.9 %collective-permute-start.46 = (bf16[160,256]{1,0:T(8,128)(2,1)S(1)}, bf16[160,256]{1,0:T(8,128)(2,1)S(1)}, u32[]{:S(2)}, u32[]{:S(2)}) collective-permute-start(bf16[160,256]{1,0:T(8,128)(2,1)S(1)} %get-tuple-element.228), channel_id=1, source_target_pairs={{0,2},{1,3},{2,0},{3,1},{4,6},{5,7},{6,4},{7,5},{8,10},{9,11},{10,... | collective-permute-start | bytes 245768 | tf_op jit(solution)/shard_map/ppermute | solution.py:255
  104.3 10.7 %collective-permute-start.42 = (bf16[256,512]{1,0:T(8,128)(2,1)S(1)}, bf16[256,512]{1,0:T(8,128)(2,1)S(1)}, u32[]{:S(2)}, u32[]{:S(2)}) collective-permute-start(bf16[256,512]{1,0:T(8,128)(2,1)S(1)} %get-tuple-element.224), channel_id=1, source_target_pairs={{0,8},{4,12},{8,0},{12,4},{16,24},{20,28},{24,16},{28,20},{1,9},{5... | collective-permute-start | bytes 786440 | tf_op jit(solution)/shard_map/ppermute | solution.py:249
  105.6 10.6 %collective-permute-start.43 = (bf16[256,512]{1,0:T(8,128)(2,1)S(1)}, bf16[256,512]{1,0:T(8,128)(2,1)S(1)}, u32[]{:S(2)}, u32[]{:S(2)}) collective-permute-start(bf16[256,512]{1,0:T(8,128)(2,1)S(1)} %get-tuple-element.225), channel_id=1, source_target_pairs={{0,16},{4,20},{8,24},{12,28},{16,0},{20,4},{24,8},{28,12},{1,17},{... | collective-permute-start | bytes 786440 | tf_op jit(solution)/shard_map/ppermute | solution.py:249
  105.8 12.4 %collective-permute-start.44 = (bf16[256,512]{1,0:T(8,128)(2,1)S(1)}, bf16[256,512]{1,0:T(8,128)(2,1)S(1)}, u32[]{:S(2)}, u32[]{:S(2)}) collective-permute-start(bf16[256,512]{1,0:T(8,128)(2,1)S(1)} %get-tuple-element.226), channel_id=1, source_target_pairs={{0,24},{4,28},{8,16},{12,20},{16,8},{20,12},{24,0},{28,4},{1,25},{... | collective-permute-start | bytes 786440 | tf_op jit(solution)/shard_map/ppermute | solution.py:249
  107.0 6.4 %collective-permute-start.45 = (bf16[64,1024]{1,0:T(8,128)(2,1)S(1)}, bf16[64,1024]{1,0:T(8,128)(2,1)S(1)}, u32[]{:S(2)}, u32[]{:S(2)}) collective-permute-start(bf16[64,1024]{1,0:T(8,128)(2,1)S(1)} %pair_stack.3.refs_3_.refs_0__0_), channel_id=1, source_target_pairs={{0,1},{1,0},{2,3},{3,2},{4,5},{5,4},{6,7},{7,6},{8,9},{9,8},{10,11... | collective-permute-start | bytes 393224 | tf_op jit(solution)/shard_map/ppermute | solution.py:255
  108.9 4.5 %collective-permute-start.47 = (bf16[160,256]{1,0:T(8,128)(2,1)S(1)}, bf16[160,256]{1,0:T(8,128)(2,1)S(1)}, u32[]{:S(2)}, u32[]{:S(2)}) collective-permute-start(bf16[160,256]{1,0:T(8,128)(2,1)S(1)} %early_line.3.refs_0_), channel_id=1, source_target_pairs={{0,1},{1,0},{2,3},{3,2},{4,5},{5,4},{6,7},{7,6},{8,9},{9,8},{10,11... | collective-permute-start | bytes 245768 | tf_op jit(solution)/shard_map/ppermute | solution.py:255
  113.5 13.4 %collective-permute-start.49 = (bf16[128,1024]{1,0:T(8,128)(2,1)S(1)}, bf16[128,1024]{1,0:T(8,128)(2,1)S(1)}, u32[]{:S(2)}, u32[]{:S(2)}) collective-permute-start(bf16[128,1024]{1,0:T(8,128)(2,1)S(1)} %pair_stack.4.refs_2_.refs_0__0_), channel_id=1, source_target_pairs={{0,8},{4,12},{8,0},{12,4},{16,24},{20,28},{24,16},{28,20},{1,9},{5... | collective-permute-start | bytes 786440 | tf_op jit(solution)/shard_map/ppermute | solution.py:249
  114.8 14.9 %collective-permute-start.50 = (bf16[128,1024]{1,0:T(8,128)(2,1)S(1)}, bf16[128,1024]{1,0:T(8,128)(2,1)S(1)}, u32[]{:S(2)}, u32[]{:S(2)}) collective-permute-start(bf16[128,1024]{1,0:T(8,128)(2,1)S(1)} %pair_stack.4.refs_2_.refs_0__0_), channel_id=1, source_target_pairs={{0,16},{4,20},{8,24},{12,28},{16,0},{20,4},{24,8},{28,12},{1,17},{... | collective-permute-start | bytes 786440 | tf_op jit(solution)/shard_map/ppermute | solution.py:249
  115.0 17.4 %collective-permute-start.51 = (bf16[128,1024]{1,0:T(8,128)(2,1)S(1)}, bf16[128,1024]{1,0:T(8,128)(2,1)S(1)}, u32[]{:S(2)}, u32[]{:S(2)}) collective-permute-start(bf16[128,1024]{1,0:T(8,128)(2,1)S(1)} %pair_stack.4.refs_2_.refs_0__0_), channel_id=1, source_target_pairs={{0,24},{4,28},{8,16},{12,20},{16,8},{20,12},{24,0},{28,4},{1,25},{... | collective-permute-start | bytes 786440 | tf_op jit(solution)/shard_map/ppermute | solution.py:249
  119.0 4.0 %collective-permute-start.53 = (bf16[224,256]{1,0:T(8,128)(2,1)S(1)}, bf16[224,256]{1,0:T(8,128)(2,1)S(1)}, u32[]{:S(2)}, u32[]{:S(2)}) collective-permute-start(bf16[224,256]{1,0:T(8,128)(2,1)S(1)} %get-tuple-element.233), channel_id=1, source_target_pairs={{0,1},{1,0},{2,3},{3,2},{4,5},{5,4},{6,7},{7,6},{8,9},{9,8},{10,11... | collective-permute-start | bytes 344072 | tf_op jit(solution)/shard_map/ppermute | solution.py:255
  119.4 4.2 %collective-permute-start.52 = (bf16[160,256]{1,0:T(8,128)(2,1)S(1)}, bf16[160,256]{1,0:T(8,128)(2,1)S(1)}, u32[]{:S(2)}, u32[]{:S(2)}) collective-permute-start(bf16[160,256]{1,0:T(8,128)(2,1)S(1)} %early_line.4.refs_1_), channel_id=1, source_target_pairs={{0,2},{1,3},{2,0},{3,1},{4,6},{5,7},{6,4},{7,5},{8,10},{9,11},{10,... | collective-permute-start | bytes 245768 | tf_op jit(solution)/shard_map/ppermute | solution.py:255
  124.2 10.4 %collective-permute-start.54 = (bf16[160,512]{1,0:T(8,128)(2,1)S(1)}, bf16[160,512]{1,0:T(8,128)(2,1)S(1)}, u32[]{:S(2)}, u32[]{:S(2)}) collective-permute-start(bf16[160,512]{1,0:T(8,128)(2,1)S(1)} %early_line.5.refs_1_.refs_0__0_), channel_id=1, source_target_pairs={{0,8},{4,12},{8,0},{12,4},{16,24},{20,28},{24,16},{28,20},{1,9},{5... | collective-permute-start | bytes 491528 | tf_op jit(solution)/shard_map/ppermute | solution.py:249
  124.8 9.8 %collective-permute-start.55 = (bf16[160,512]{1,0:T(8,128)(2,1)S(1)}, bf16[160,512]{1,0:T(8,128)(2,1)S(1)}, u32[]{:S(2)}, u32[]{:S(2)}) collective-permute-start(bf16[160,512]{1,0:T(8,128)(2,1)S(1)} %early_line.5.refs_1_.refs_0__0_), channel_id=1, source_target_pairs={{0,16},{4,20},{8,24},{12,28},{16,0},{20,4},{24,8},{28,12},{1,17},{... | collective-permute-start | bytes 491528 | tf_op jit(solution)/shard_map/ppermute | solution.py:249
  126.9 7.5 %collective-permute-start.56 = (bf16[224,256]{1,0:T(8,128)(2,1)S(1)}, bf16[224,256]{1,0:T(8,128)(2,1)S(1)}, u32[]{:S(2)}, u32[]{:S(2)}) collective-permute-start(bf16[224,256]{1,0:T(8,128)(2,1)S(1)} %late_line.2.refs_3_.refs_0_), channel_id=1, source_target_pairs={{0,2},{1,3},{2,0},{3,1},{4,6},{5,7},{6,4},{7,5},{8,10},{9,11},{10,... | collective-permute-start | bytes 344072 | tf_op jit(solution)/shard_map/ppermute | solution.py:255
  134.4 3.7 %collective-permute-start.57 = (bf16[224,256]{1,0:T(8,128)(2,1)S(1)}, bf16[224,256]{1,0:T(8,128)(2,1)S(1)}, u32[]{:S(2)}, u32[]{:S(2)}) collective-permute-start(bf16[224,256]{1,0:T(8,128)(2,1)S(1)} %late_line.3.refs_2_.refs_1_), channel_id=1, source_target_pairs={{0,1},{1,0},{2,3},{3,2},{4,5},{5,4},{6,7},{7,6},{8,9},{9,8},{10,11... | collective-permute-start | bytes 344072 | tf_op jit(solution)/shard_map/ppermute | solution.py:255
  134.6 4.1 %collective-permute-start.61 = (bf16[160,256]{1,0:T(8,128)(2,1)S(1)}, bf16[160,256]{1,0:T(8,128)(2,1)S(1)}, u32[]{:S(2)}, u32[]{:S(2)}) collective-permute-start(bf16[160,256]{1,0:T(8,128)(2,1)S(1)} %get-tuple-element.238.refs_3_), channel_id=1, source_target_pairs={{0,16},{4,20},{8,24},{12,28},{16,0},{20,4},{24,8},{28,12},{1,17},{... | collective-permute-start | bytes 245768 | tf_op jit(solution)/shard_map/ppermute | solution.py:249
  134.9 3.8 %collective-permute-start.62 = (bf16[160,256]{1,0:T(8,128)(2,1)S(1)}, bf16[160,256]{1,0:T(8,128)(2,1)S(1)}, u32[]{:S(2)}, u32[]{:S(2)}) collective-permute-start(bf16[160,256]{1,0:T(8,128)(2,1)S(1)} %get-tuple-element.241), channel_id=1, source_target_pairs={{0,8},{4,12},{8,0},{12,4},{16,24},{20,28},{24,16},{28,20},{1,9},{5... | collective-permute-start | bytes 245768 | tf_op jit(solution)/shard_map/ppermute | solution.py:249
  138.8 7.3 %collective-permute-start.63 = (bf16[640,512]{1,0:T(8,128)(2,1)S(1)}, bf16[640,512]{1,0:T(8,128)(2,1)S(1)}, u32[]{:S(2)}, u32[]{:S(2)}) collective-permute-start(bf16[640,512]{1,0:T(8,128)(2,1)S(1)} %early_stack.1.refs_1__0_), channel_id=1, source_target_pairs={{0,4},{4,0},{8,12},{12,8},{16,20},{20,16},{24,28},{28,24},{1,5},{5... | collective-permute-start | bytes 1966088 | tf_op jit(solution)/shard_map/ppermute | solution.py:252
  142.5 7.4 %collective-permute-start.58 = (bf16[224,512]{1,0:T(8,128)(2,1)S(1)}, bf16[224,512]{1,0:T(8,128)(2,1)S(1)}, u32[]{:S(2)}, u32[]{:S(2)}) collective-permute-start(bf16[224,512]{1,0:T(8,128)(2,1)S(1)} %late_join.1.refs_3_.refs_0__0_), channel_id=1, source_target_pairs={{0,8},{4,12},{8,0},{12,4},{16,24},{20,28},{24,16},{28,20},{1,9},{5... | collective-permute-start | bytes 688136 | tf_op jit(solution)/shard_map/ppermute | solution.py:249
  143.6 6.8 %collective-permute-start.59 = (bf16[224,512]{1,0:T(8,128)(2,1)S(1)}, bf16[224,512]{1,0:T(8,128)(2,1)S(1)}, u32[]{:S(2)}, u32[]{:S(2)}) collective-permute-start(bf16[224,512]{1,0:T(8,128)(2,1)S(1)} %late_join.1.refs_3_.refs_0__0_), channel_id=1, source_target_pairs={{0,16},{4,20},{8,24},{12,28},{16,0},{20,4},{24,8},{28,12},{1,17},{... | collective-permute-start | bytes 688136 | tf_op jit(solution)/shard_map/ppermute | solution.py:249
  143.9 11.6 %collective-permute-start.60 = (bf16[224,512]{1,0:T(8,128)(2,1)S(1)}, bf16[224,512]{1,0:T(8,128)(2,1)S(1)}, u32[]{:S(2)}, u32[]{:S(2)}) collective-permute-start(bf16[224,512]{1,0:T(8,128)(2,1)S(1)} %late_join.1.refs_3_.refs_0__0_), channel_id=1, source_target_pairs={{0,24},{4,28},{8,16},{12,20},{16,8},{20,12},{24,0},{28,4},{1,25},{... | collective-permute-start | bytes 688136 | tf_op jit(solution)/shard_map/ppermute | solution.py:249
  145.1 11.5 %collective-permute-start.65 = (bf16[512,1024]{1,0:T(8,128)(2,1)S(1)}, bf16[512,1024]{1,0:T(8,128)(2,1)S(1)}, u32[]{:S(2)}, u32[]{:S(2)}) collective-permute-start(bf16[512,1024]{1,0:T(8,128)(2,1)S(1)} %pair_stack.5.refs_5_.refs_0__0_), channel_id=1, source_target_pairs={{0,4},{4,0},{8,12},{12,8},{16,20},{20,16},{24,28},{28,24},{1,5},{5... | collective-permute-start | bytes 3145736 | tf_op jit(solution)/shard_map/ppermute | solution.py:252
  (30 other events, 207.2 us)

commit v6 on v5

--- a/solution.py
+++ b/solution.py
@@ -259,7 +259,8 @@
             n, width = parts[0].shape
             blocks = parts[0].reshape(n_res, n // n_res, width)
             return [lax.all_to_all(blocks, "res", 0, 0, tiled=True).reshape(n, width)]
-        near = [parts[0]] + [to_chip(parts[m], m) for m in (1, 2, 3)]
+        far = to_chip(parts[3], 3)
+        near = [parts[0], to_chip(parts[1], 1), to_chip(parts[2], 2), far]
         return near + [to_core(v) for v in near]
 
     def prepare_send(spot, table, nodes, weights, away_out, send_out, piece_out):
@@ -710,7 +711,8 @@
             out[n:, :] = more[0][...]
 
     def to_chips(parts):
-        return [parts[0]] + [to_chip(parts[m], m) for m in (1, 2, 3)]
+        far = to_chip(parts[3], 3)
+        return [parts[0], to_chip(parts[1], 1), to_chip(parts[2], 2), far]
 
     def spread(own):
         parts = [own] + [to_chip(own, m) for m in (1, 2, 3)]

time: 162 us -> 162 us (level)
  no operation moved by 1% of the time
where the time goes in v6:
time: 162 us
  starting transfers between devices  75.3 us (46%)
  Pallas kernels  48.3 us (30%)
  waiting for transfers between devices  36.8 us (23%)
    pallas_call x40, Pallas kernels, call(): pl.pallas_call(run, out_shape=jax.tree.unflatten(out_tree, shapes), in_sp...  48.3 us
    ppermute x32, starting transfers between devices, to_chip(): return lax.ppermute(v, 'res', [(i, i ^ 2 * m) for i in range(n_res)])  30.4 us
    ppermute x17, starting transfers between devices, to_core(): return lax.ppermute(v, 'res', pair)  27.6 us
    ppermute x17, waiting for transfers between devices, to_hid(): return lax.ppermute(v, 'hid', [(i, i ^ m) for i in range(n_hid)])  17.6 us
    ppermute x17, starting transfers between devices, to_hid(): return lax.ppermute(v, 'hid', [(i, i ^ m) for i in range(n_hid)])  17.3 us
    ppermute x32, waiting for transfers between devices, to_chip(): return lax.ppermute(v, 'res', [(i, i ^ 2 * m) for i in range(n_res)])  13.2 us
    ppermute x17, waiting for transfers between devices, to_core(): return lax.ppermute(v, 'res', pair)  6.03 us
  transfers between devices with their start and end apart: 66, of which 24 were waited for; matrix products, arithmetic and copies ran while one was open for 0% of the time, Pallas kernels for 15%

profile of v6, /device:TPU:1, one launch (start us, length us, event | category | flops | bytes accessed | tf_op | source)
XLA Modules:
  0.0 162.0 jit_solution(6855792859744875762)
XLA Ops:
  0.8 2.1 %prepare_send.1 = (bf16[32,512]{1,0:T(8,128)(2,1)S(1)}, bf16[32,512]{1,0:T(8,128)(2,1)S(1)}, bf16[32,512]{1,0:T(8,128)(2,1)S(1)}, bf16[32,512]{1,0:T(8,128)(2,1)...) custom-call(s32[4]{0:T(128)S(1)} %pad_add_fusion.refs_0_, s32[8,16]{1,0:T(8,128)} %bitcast.59, ...), custom_call_target="tpu_custom_call" | custom-call | tf_op jit(solution)/shard_map/prepare_send/pallas_call | solution.py:165
  2.9 2.2 %collective-permute-start.4 = (bf16[144,512]{1,0:T(8,128)(2,1)S(1)}, bf16[144,512]{1,0:T(8,128)(2,1)S(1)}, u32[]{:S(2)}, u32[]{:S(2)}) collective-permute-start(bf16[144,512]{1,0:T(8,128)(2,1)S(1)} %get-tuple-element.157), channel_id=1, source_target_pairs={{0,1},{1,0},{2,3},{3,2},{4,5},{5,4},{6,7},{7,6},{8,9},{9,8},{10,11... | collective-permute-start | bytes 442376 | tf_op jit(solution)/shard_map/ppermute | solution.py:255
  5.1 2.3 %collective-permute-start.5 = (bf16[144,512]{1,0:T(8,128)(2,1)S(1)}, bf16[144,512]{1,0:T(8,128)(2,1)S(1)}, u32[]{:S(2)}, u32[]{:S(2)}) collective-permute-start(bf16[144,512]{1,0:T(8,128)(2,1)S(1)} %get-tuple-element.157), channel_id=1, source_target_pairs={{0,2},{1,3},{2,0},{3,1},{4,6},{5,7},{6,4},{7,5},{8,10},{9,11},{10,... | collective-permute-start | bytes 442376 | tf_op jit(solution)/shard_map/ppermute | solution.py:255
  10.5 2.2 %collective-permute-start.2 = (bf16[32,512]{1,0:T(8,128)(2,1)S(1)}, bf16[32,512]{1,0:T(8,128)(2,1)S(1)}, u32[]{:S(2)}, u32[]{:S(2)}) collective-permute-start(bf16[32,512]{1,0:T(8,128)(2,1)S(1)} %get-tuple-element.150), channel_id=1, source_target_pairs={{0,24},{4,28},{8,16},{12,20},{16,8},{20,12},{24,0},{28,4},{1,25},{... | collective-permute-start | bytes 98312 | tf_op jit(solution)/shard_map/ppermute | solution.py:249
  12.6 2.6 %prepare_rest.1 = (bf16[1920,128]{1,0:T(8,128)(2,1)S(1)}, f32[32,1]{1,0:T(8,128)S(1)}, f32[8,512]{1,0:T(8,128)S(1)}, f32[8,192]{1,0:T(8,128)S(1)}, bf16[1920,192]{1,0:T(8,128)(2,1)S(1)}) custom-call(s32[4]{0:T(128)S(1)} %pad_add_fusion.refs_0_, s32[32,60]{1,0:T(8,128)} %refs_1_.5, s32[1,32]{1,0:T(1,128)} %bitcast.73, f32[1,512]{1,0:T(1,128)} %bitcast.60, ...), custom_call_target="tpu_custom_call" | custom-call | tf_op jit(solution)/shard_map/prepare_rest/pallas_call | solution.py:165
  15.3 2.7 %collective-permute-start.3 = (bf16[64,512]{1,0:T(8,128)(2,1)S(1)}, bf16[64,512]{1,0:T(8,128)(2,1)S(1)}, u32[]{:S(2)}, u32[]{:S(2)}) collective-permute-start(bf16[64,512]{1,0:T(8,128)(2,1)S(1)} %get-tuple-element.153), channel_id=1, source_target_pairs={{0,4},{4,0},{8,12},{12,8},{16,20},{20,16},{24,28},{28,24},{1,5},{5... | collective-permute-start | bytes 196616 | tf_op jit(solution)/shard_map/ppermute | solution.py:252
  21.2 3.6 %message_one.1 = (f32[32,512]{1,0:T(8,128)S(1)}, bf16[32,512]{1,0:T(8,128)(2,1)S(1)}) custom-call(bf16[64,512]{1,0:T(8,128)(2,1)S(1)} %get-tuple-element.152.refs_2_.refs_0__0_, bf16[64,512]{1,0:T(8,128)(2,1)S(1)} %collective-permute-done.3.refs_3_.refs_0__1_, bf16[32,512]{1,0:T(8,128)(2,1)S(1)} %copy-done.9, ...), custom_call_target="tpu_custom_call" | custom-call | tf_op jit(solution)/shard_map/message_one/pallas_call | solution.py:165
  24.8 1.7 %collective-permute-start.7 = (bf16[32,512]{1,0:T(8,128)(2,1)S(1)}, bf16[32,512]{1,0:T(8,128)(2,1)S(1)}, u32[]{:S(2)}, u32[]{:S(2)}) collective-permute-start(bf16[32,512]{1,0:T(8,128)(2,1)S(1)} %get-tuple-element.159.refs_0__0_), channel_id=1, source_target_pairs={{0,1},{1,0},{2,3},{3,2},{4,5},{5,4},{6,7},{7,6},{8,9},{9,8},{10,11... | collective-permute-start | bytes 98312 | tf_op jit(solution)/shard_map/ppermute | solution.py:255
  26.6 2.0 %collective-permute-start.8 = (bf16[32,512]{1,0:T(8,128)(2,1)S(1)}, bf16[32,512]{1,0:T(8,128)(2,1)S(1)}, u32[]{:S(2)}, u32[]{:S(2)}) collective-permute-start(bf16[32,512]{1,0:T(8,128)(2,1)S(1)} %get-tuple-element.159.refs_0__0_), channel_id=1, source_target_pairs={{0,2},{1,3},{2,0},{3,1},{4,6},{5,7},{6,4},{7,5},{8,10},{9,11},{10,... | collective-permute-start | bytes 98312 | tf_op jit(solution)/shard_map/ppermute | solution.py:255
  28.9 1.3 collective-permute-done.8.refs_0__2_
  30.2 3.3 %collective-permute-done.9.refs_0__3_ = bf16[32,512]{1,0:T(8,128)(2,1)S(1)} collective-permute-done((bf16[32,512]{1,0:T(8,128)(2,1)S(1)}, bf16[32,512]{1,0:T(8,128)(2,1)S(1)}, u32[]{:S(2)}, u32[]{:S(2)}) %collective-permute-start.9) | collective-permute-done | bytes 32800 | tf_op jit(solution)/shard_map/ppermute | solution.py:255
  34.7 1.5 collective-permute-start.11
  36.3 2.0 %collective-permute-start.12 = (bf16[32,512]{1,0:T(8,128)(2,1)S(1)}, bf16[32,512]{1,0:T(8,128)(2,1)S(1)}, u32[]{:S(2)}, u32[]{:S(2)}) collective-permute-start(bf16[32,512]{1,0:T(8,128)(2,1)S(1)} %get-tuple-element.163), channel_id=1, source_target_pairs={{0,3},{1,2},{2,1},{3,0},{4,7},{5,6},{6,5},{7,4},{8,11},{9,10},{10,... | collective-permute-start | bytes 98312 | tf_op jit(solution)/shard_map/ppermute | solution.py:255
  38.4 2.5 %collective-permute-done.12.refs_1__3_ = bf16[32,512]{1,0:T(8,128)(2,1)S(1)} collective-permute-done((bf16[32,512]{1,0:T(8,128)(2,1)S(1)}, bf16[32,512]{1,0:T(8,128)(2,1)S(1)}, u32[]{:S(2)}, u32[]{:S(2)}) %collective-permute-start.12) | collective-permute-done | bytes 32800 | tf_op jit(solution)/shard_map/ppermute | solution.py:255
  41.3 4.5 %collective-permute-start.24 = (bf16[576,1536]{1,0:T(8,128)(2,1)S(1)}, bf16[576,1536]{1,0:T(8,128)(2,1)S(1)}, u32[]{:S(2)}, u32[]{:S(2)}) collective-permute-start(bf16[576,1536]{1,0:T(8,128)(2,1)S(1)} %stack_weights.1.refs_1__0_), channel_id=1, source_target_pairs={{0,4},{4,0},{8,12},{12,8},{16,20},{20,16},{24,28},{28,24},{1,5},{5... | collective-permute-start | bytes 5308424 | tf_op jit(solution)/shard_map/ppermute | solution.py:252
  49.9 1.5 collective-permute-start.18
  52.0 1.8 %collective-permute-start.19 = (bf16[32,512]{1,0:T(8,128)(2,1)S(1)}, bf16[32,512]{1,0:T(8,128)(2,1)S(1)}, u32[]{:S(2)}, u32[]{:S(2)}) collective-permute-start(bf16[32,512]{1,0:T(8,128)(2,1)S(1)} %collective-permute-done.15.refs_0__3_), channel_id=1, source_target_pairs={{0,4},{4,0},{8,12},{12,8},{16,20},{20,16},{24,28},{28,24},{1,5},{5... | collective-permute-start | bytes 98312 | tf_op jit(solution)/shard_map/ppermute | solution.py:252
  54.7 7.0 %layer_two.1 = (f32[1920,192]{1,0:T(8,128)S(1)}, bf16[1920,512]{1,0:T(8,128)(2,1)S(1)}, bf16[1920,512]{1,0:T(8,128)(2,1)S(1)}, bf16[1920,512]{1,0:T(8,128)(2,1)S...) custom-call(bf16[32,512]{1,0:T(8,128)(2,1)S(1)} %get-tuple-element.1, ...), custom_call_target="tpu_custom_call" | custom-call | tf_op jit(solution)/shard_map/layer_two/pallas_call | solution.py:165
  61.7 2.0 %feed_two.1 = (bf16[4,32,512]{2,1,0:T(8,128)(2,1)S(1)}, f32[32,512]{1,0:T(8,128)S(1)}, f32[32,512]{1,0:T(8,128)}, bf16[32,512]{1,0:T(8,128)(2,1)S(1)}, bf16[32,5...) custom-call(f32[32,512]{1,0:T(8,128)S(1)} %get-tuple-element.174.ref, ...), custom_call_target="tpu_custom_call" | custom-call | tf_op jit(solution)/shard_map/feed_two/pallas_call | solution.py:165
  64.1 2.2 %collective-permute-start.27 = (bf16[32,512]{1,0:T(8,128)(2,1)S(1)}, bf16[32,512]{1,0:T(8,128)(2,1)S(1)}, u32[]{:S(2)}, u32[]{:S(2)}) collective-permute-start(bf16[32,512]{1,0:T(8,128)(2,1)S(1)} %get-tuple-element.179), channel_id=1, source_target_pairs={{0,24},{4,28},{8,16},{12,20},{16,8},{20,12},{24,0},{28,4},{1,25},{... | collective-permute-start | bytes 98312 | tf_op jit(solution)/shard_map/ppermute | solution.py:249
  70.7 5.8 %edge_turn.1 = (f32[1920,192]{1,0:T(8,128)}, f32[1920,192]{1,0:T(8,128)S(1)}, bf16[1920,192]{1,0:T(8,128)(2,1)S(1)}, bf16[1920,192]{1,0:T(8,128)(2,1)S(1)}, bf16...) custom-call(bf16[32,512]{1,0:T(8,128)(2,1)S(1)} %get-tuple-element.1, ...), custom_call_target="tpu_custom_call" | custom-call | tf_op jit(solution)/shard_map/edge_turn/pallas_call | solution.py:165
  80.4 2.1 %collective-permute-done.34.refs_0__3_ = bf16[32,192]{1,0:T(8,128)(2,1)S(1)} collective-permute-done((bf16[32,192]{1,0:T(8,128)(2,1)S(1)}, bf16[32,192]{1,0:T(8,128)(2,1)S(1)}, u32[]{:S(2)}, u32[]{:S(2)}) %collective-permute-start.34) | collective-permute-done | bytes 12320 | tf_op jit(solution)/shard_map/ppermute | solution.py:249
  82.5 2.1 %collective-permute-start.35 = (bf16[64,192]{1,0:T(8,128)(2,1)S(1)}, bf16[64,192]{1,0:T(8,128)(2,1)S(1)}, u32[]{:S(2)}, u32[]{:S(2)}) collective-permute-start(bf16[64,192]{1,0:T(8,128)(2,1)S(1)} %get-tuple-element.194), channel_id=1, source_target_pairs={{0,4},{4,0},{8,12},{12,8},{16,20},{20,16},{24,28},{28,24},{1,5},{5... | collective-permute-start | bytes 73736 | tf_op jit(solution)/shard_map/ppermute | solution.py:252
  85.4 3.0 %node_turn.1 = (bf16[32,1024]{1,0:T(8,128)(2,1)S(1)}, f32[32,512]{1,0:T(8,128)S(1)}, f32[32,512]{1,0:T(8,128)S(1)}, bf16[640,512]{1,0:T(8,128)(2,1)S(1)}, bf16[640,512]{1,0:T(8,128)(2,1)S(1)}) custom-call(s32[4]{0:T(128)S(1)} %pad_add_fusion.refs_0_, bf16[64,192]{1,0:T(8,128)(2,1)S(1)} %get-tuple-element.193.refs_1__0_, ...), custom_call_target="tpu_custom_call" | custom-call | tf_op jit(solution)/shard_map/node_turn/pallas_call | solution.py:165
  88.8 1.3 message_second.1
  91.2 2.2 %collective-permute-start.39 = (bf16[160,512]{1,0:T(8,128)(2,1)S(1)}, bf16[160,512]{1,0:T(8,128)(2,1)S(1)}, u32[]{:S(2)}, u32[]{:S(2)}) collective-permute-start(bf16[160,512]{1,0:T(8,128)(2,1)S(1)} %get-tuple-element.210), channel_id=1, source_target_pairs={{0,24},{4,28},{8,16},{12,20},{16,8},{20,12},{24,0},{28,4},{1,25},{... | collective-permute-start | bytes 491528 | tf_op jit(solution)/shard_map/ppermute | solution.py:249
  93.4 2.6 %message_first.1 = (bf16[1920,512]{1,0:T(8,128)(2,1)S(1)}, bf16[32,512]{1,0:T(8,128)(2,1)S(1)}, bf16[32,512]{1,0:T(8,128)(2,1)S(1)}, bf16[32,512]{1,0:T(8,128)(2...) custom-call(bf16[32,512]{1,0:T(8,128)(2,1)S(1)} %get-tuple-element.165.refs_0__0_, ...), custom_call_target="tpu_custom_call" | custom-call | tf_op jit(solution)/shard_map/message_first/pallas_call | solution.py:165
  96.0 2.2 %collective-permute-done.40.refs_0__1_ = bf16[32,1024]{1,0:T(8,128)(2,1)S(1)} collective-permute-done((bf16[32,1024]{1,0:T(8,128)(2,1)S(1)}, bf16[32,1024]{1,0:T(8,128)(2,1)S(1)}, u32[]{:S(2)}, u32[]{:S(2)}) %collective-permute-start.40) | collective-permute-done | bytes 65568 | tf_op jit(solution)/shard_map/ppermute | solution.py:255
  98.3 1.4 collective-permute-done.39.refs_1__3_
  100.5 1.5 collective-permute-start.41
  102.0 2.1 %collective-permute-done.41.refs_1_ = bf16[896,512]{1,0:T(8,128)(2,1)S(1)} collective-permute-done((bf16[896,512]{1,0:T(8,128)(2,1)S(1)}, bf16[896,512]{1,0:T(8,128)(2,1)S(1)}, u32[]{:S(2)}, u32[]{:S(2)}) %collective-permute-start.41) | collective-permute-done | bytes 917536 | tf_op jit(solution)/shard_map/ppermute | solution.py:252
  104.3 1.3 collective-permute-start.42
  107.4 1.5 collective-permute-done.46.refs_1_
  109.0 4.4 %collective-permute-done.47.refs_1_ = bf16[160,256]{1,0:T(8,128)(2,1)S(1)} collective-permute-done((bf16[160,256]{1,0:T(8,128)(2,1)S(1)}, bf16[160,256]{1,0:T(8,128)(2,1)S(1)}, u32[]{:S(2)}, u32[]{:S(2)}) %collective-permute-start.47) | collective-permute-done | bytes 81952 | tf_op jit(solution)/shard_map/ppermute | solution.py:255
  113.5 1.3 collective-permute-start.49
  116.2 2.0 %collective-permute-done.44.refs_1__3_ = bf16[256,512]{1,0:T(8,128)(2,1)S(1)} collective-permute-done((bf16[256,512]{1,0:T(8,128)(2,1)S(1)}, bf16[256,512]{1,0:T(8,128)(2,1)S(1)}, u32[]{:S(2)}, u32[]{:S(2)}) %collective-permute-start.44) | collective-permute-done | bytes 262176 | tf_op jit(solution)/shard_map/ppermute | solution.py:249
  119.4 2.1 %collective-permute-start.52 = (bf16[160,256]{1,0:T(8,128)(2,1)S(1)}, bf16[160,256]{1,0:T(8,128)(2,1)S(1)}, u32[]{:S(2)}, u32[]{:S(2)}) collective-permute-start(bf16[160,256]{1,0:T(8,128)(2,1)S(1)} %early_line.4.refs_1_), channel_id=1, source_target_pairs={{0,2},{1,3},{2,0},{3,1},{4,6},{5,7},{6,4},{7,5},{8,10},{9,11},{10,... | collective-permute-start | bytes 245768 | tf_op jit(solution)/shard_map/ppermute | solution.py:255
  121.5 1.5 collective-permute-done.53.refs_1_
  124.8 2.1 %collective-permute-start.55 = (bf16[160,512]{1,0:T(8,128)(2,1)S(1)}, bf16[160,512]{1,0:T(8,128)(2,1)S(1)}, u32[]{:S(2)}, u32[]{:S(2)}) collective-permute-start(bf16[160,512]{1,0:T(8,128)(2,1)S(1)} %early_line.5.refs_1_.refs_0__0_), channel_id=1, source_target_pairs={{0,16},{4,20},{8,24},{12,28},{16,0},{20,4},{24,8},{28,12},{1,17},{... | collective-permute-start | bytes 491528 | tf_op jit(solution)/shard_map/ppermute | solution.py:249
  126.9 2.0 %collective-permute-start.56 = (bf16[224,256]{1,0:T(8,128)(2,1)S(1)}, bf16[224,256]{1,0:T(8,128)(2,1)S(1)}, u32[]{:S(2)}, u32[]{:S(2)}) collective-permute-start(bf16[224,256]{1,0:T(8,128)(2,1)S(1)} %late_line.2.refs_3_.refs_0_), channel_id=1, source_target_pairs={{0,2},{1,3},{2,0},{3,1},{4,6},{5,7},{6,4},{7,5},{8,10},{9,11},{10,... | collective-permute-start | bytes 344072 | tf_op jit(solution)/shard_map/ppermute | solution.py:255
  129.6 2.7 %collective-permute-start.48 = (bf16[64,512]{1,0:T(8,128)(2,1)S(1)}, bf16[64,512]{1,0:T(8,128)(2,1)S(1)}, u32[]{:S(2)}, u32[]{:S(2)}) collective-permute-start(bf16[64,512]{1,0:T(8,128)(2,1)S(1)} %get-tuple-element.230), channel_id=1, source_target_pairs={{0,4},{4,0},{8,12},{12,8},{16,20},{20,16},{24,28},{28,24},{1,5},{5... | collective-permute-start | bytes 196616 | tf_op jit(solution)/shard_map/ppermute | solution.py:252
  136.0 2.0 %edge_end.1 = (f32[1920,192]{1,0:T(8,128)}, f32[8,128]{1,0:T(8,128)S(1)}) custom-call(f32[1920,192]{1,0:T(8,128)S(1)} %get-tuple-element.235.refs_0_, bf16[1920,512]{1,0:T(8,128)(2,1)S(1)} %get-tuple-element.236.refs_1_, bf16[1216,512]{1,0:T(8,128)(2,1)S(1)} %copy-done, bf16[160,256]{1,0:T(8,128)(2,1)S(1)} %get-tuple-element.238.refs_3_), custom_call_target="tpu_custom_call" | custom-call | tf_op jit(solution)/shard_map/edge_end/pallas_call | solution.py:165
  138.8 3.7 %collective-permute-start.63 = (bf16[640,512]{1,0:T(8,128)(2,1)S(1)}, bf16[640,512]{1,0:T(8,128)(2,1)S(1)}, u32[]{:S(2)}, u32[]{:S(2)}) collective-permute-start(bf16[640,512]{1,0:T(8,128)(2,1)S(1)} %early_stack.1.refs_1__0_), channel_id=1, source_target_pairs={{0,4},{4,0},{8,12},{12,8},{16,20},{20,16},{24,28},{28,24},{1,5},{5... | collective-permute-start | bytes 1966088 | tf_op jit(solution)/shard_map/ppermute | solution.py:252
  146.0 2.4 %unpack_early.1 = (f32[192,1216]{1,0:T(8,128)}, f32[192,192]{1,0:T(8,128)}, f32[192,192]{1,0:T(8,128)}, f32[512,512]{1,0:T(8,128)}, f32[1,512]{1,0:T(1,128)}, /*...) custom-call(s32[4]{0:T(128)S(1)} %pad_add_fusion.refs_0_, ...), custom_call_target="tpu_custom_call" | custom-call | tf_op jit(solution)/shard_map/unpack_early/pallas_call | solution.py:165
  148.4 1.5 feed_weights.1
  150.4 5.1 %collective-permute-done.60.refs_0__3_ = bf16[224,512]{1,0:T(8,128)(2,1)S(1)} collective-permute-done((bf16[224,512]{1,0:T(8,128)(2,1)S(1)}, bf16[224,512]{1,0:T(8,128)(2,1)S(1)}, u32[]{:S(2)}, u32[]{:S(2)}) %collective-permute-start.60) | collective-permute-done | bytes 229408 | tf_op jit(solution)/shard_map/ppermute | solution.py:249
  156.6 2.5 %feed_weights_more.1 = (f32[512,512]{1,0:T(8,128)}, f32[512,512]{1,0:T(8,128)}, f32[8,128]{1,0:T(8,128)S(1)}) custom-call(bf16[512,1024]{1,0:T(8,128)(2,1)S(1)} %collective-permute-done.65.refs_0__0_, bf16[512,512]{1,0:T(8,128)(2,1)S(1)} %copy-done.1, f32[1,512]{1,0:T(1,128)S(1)} %bitcast.57, bf16[512,512]{1,0:T(8,128)(2,1)S(1)} %copy-done.2, ...), custom_call_target="tpu_custom_call" | custom-call | tf_op jit(solution)/shard_map/feed_weights_more/pallas_call | solution.py:165
  159.2 2.6 %unpack_late.1 = (f32[1216,512]{1,0:T(8,128)}, f32[512,512]{1,0:T(8,128)}, f32[1,512]{1,0:T(1,128)}, f32[1,512]{1,0:T(1,128)}) custom-call(s32[4]{0:T(128)S(1)} %pad_add_fusion.refs_0_, bf16[896,512]{1,0:T(8,128)(2,1)S(1)} %late_stack.1.refs_6_.refs_1__0_, bf16[896,512]{1,0:T(8,128)(2,1)S(1)} %collective-permute-done.64.refs_1__1_, ...), custom_call_target="tpu_custom_call" | custom-call | tf_op jit(solution)/shard_map/unpack_late/pallas_call | solution.py:165
  (149 shorter events, 42.8 us)
Async XLA Ops:
  2.9 15.9 %collective-permute-start.4 = (bf16[144,512]{1,0:T(8,128)(2,1)S(1)}, bf16[144,512]{1,0:T(8,128)(2,1)S(1)}, u32[]{:S(2)}, u32[]{:S(2)}) collective-permute-start(bf16[144,512]{1,0:T(8,128)(2,1)S(1)} %get-tuple-element.157), channel_id=1, source_target_pairs={{0,1},{1,0},{2,3},{3,2},{4,5},{5,4},{6,7},{7,6},{8,9},{9,8},{10,11... | collective-permute-start | bytes 442376 | tf_op jit(solution)/shard_map/ppermute | solution.py:255
  5.1 13.7 %collective-permute-start.5 = (bf16[144,512]{1,0:T(8,128)(2,1)S(1)}, bf16[144,512]{1,0:T(8,128)(2,1)S(1)}, u32[]{:S(2)}, u32[]{:S(2)}) collective-permute-start(bf16[144,512]{1,0:T(8,128)(2,1)S(1)} %get-tuple-element.157), channel_id=1, source_target_pairs={{0,2},{1,3},{2,0},{3,1},{4,6},{5,7},{6,4},{7,5},{8,10},{9,11},{10,... | collective-permute-start | bytes 442376 | tf_op jit(solution)/shard_map/ppermute | solution.py:255
  7.4 11.4 %collective-permute-start.6 = (bf16[144,512]{1,0:T(8,128)(2,1)S(1)}, bf16[144,512]{1,0:T(8,128)(2,1)S(1)}, u32[]{:S(2)}, u32[]{:S(2)}) collective-permute-start(bf16[144,512]{1,0:T(8,128)(2,1)S(1)} %get-tuple-element.157), channel_id=1, source_target_pairs={{0,3},{1,2},{2,1},{3,0},{4,7},{5,6},{6,5},{7,4},{8,11},{9,10},{10,... | collective-permute-start | bytes 442376 | tf_op jit(solution)/shard_map/ppermute | solution.py:255
  8.6 6.6 %collective-permute-start.1 = (bf16[32,512]{1,0:T(8,128)(2,1)S(1)}, bf16[32,512]{1,0:T(8,128)(2,1)S(1)}, u32[]{:S(2)}, u32[]{:S(2)}) collective-permute-start(bf16[32,512]{1,0:T(8,128)(2,1)S(1)} %get-tuple-element.149), channel_id=1, source_target_pairs={{0,16},{4,20},{8,24},{12,28},{16,0},{20,4},{24,8},{28,12},{1,17},{... | collective-permute-start | bytes 98312 | tf_op jit(solution)/shard_map/ppermute | solution.py:249
  10.5 4.8 %collective-permute-start.2 = (bf16[32,512]{1,0:T(8,128)(2,1)S(1)}, bf16[32,512]{1,0:T(8,128)(2,1)S(1)}, u32[]{:S(2)}, u32[]{:S(2)}) collective-permute-start(bf16[32,512]{1,0:T(8,128)(2,1)S(1)} %get-tuple-element.150), channel_id=1, source_target_pairs={{0,24},{4,28},{8,16},{12,20},{16,8},{20,12},{24,0},{28,4},{1,25},{... | collective-permute-start | bytes 98312 | tf_op jit(solution)/shard_map/ppermute | solution.py:249
  18.9 15.1 %collective-permute-start.20 = (bf16[144,1536]{1,0:T(8,128)(2,1)S(1)}, bf16[144,1536]{1,0:T(8,128)(2,1)S(1)}, u32[]{:S(2)}, u32[]{:S(2)}) collective-permute-start(bf16[144,1536]{1,0:T(8,128)(2,1)S(1)} %join_pieces.1.refs_9_.refs_0__0_), channel_id=1, source_target_pairs={{0,8},{4,12},{8,0},{12,4},{16,24},{20,28},{24,16},{28,20},{1,9},{5... | collective-permute-start | bytes 1327112 | tf_op jit(solution)/shard_map/ppermute | solution.py:249
  19.9 14.1 %collective-permute-start.21 = (bf16[144,1536]{1,0:T(8,128)(2,1)S(1)}, bf16[144,1536]{1,0:T(8,128)(2,1)S(1)}, u32[]{:S(2)}, u32[]{:S(2)}) collective-permute-start(bf16[144,1536]{1,0:T(8,128)(2,1)S(1)} %join_pieces.1.refs_9_.refs_0__0_), channel_id=1, source_target_pairs={{0,16},{4,20},{8,24},{12,28},{16,0},{20,4},{24,8},{28,12},{1,17},{... | collective-permute-start | bytes 1327112 | tf_op jit(solution)/shard_map/ppermute | solution.py:249
  24.8 4.1 %collective-permute-start.7 = (bf16[32,512]{1,0:T(8,128)(2,1)S(1)}, bf16[32,512]{1,0:T(8,128)(2,1)S(1)}, u32[]{:S(2)}, u32[]{:S(2)}) collective-permute-start(bf16[32,512]{1,0:T(8,128)(2,1)S(1)} %get-tuple-element.159.refs_0__0_), channel_id=1, source_target_pairs={{0,1},{1,0},{2,3},{3,2},{4,5},{5,4},{6,7},{7,6},{8,9},{9,8},{10,11... | collective-permute-start | bytes 98312 | tf_op jit(solution)/shard_map/ppermute | solution.py:255
  26.6 3.7 %collective-permute-start.8 = (bf16[32,512]{1,0:T(8,128)(2,1)S(1)}, bf16[32,512]{1,0:T(8,128)(2,1)S(1)}, u32[]{:S(2)}, u32[]{:S(2)}) collective-permute-start(bf16[32,512]{1,0:T(8,128)(2,1)S(1)} %get-tuple-element.159.refs_0__0_), channel_id=1, source_target_pairs={{0,2},{1,3},{2,0},{3,1},{4,6},{5,7},{6,4},{7,5},{8,10},{9,11},{10,... | collective-permute-start | bytes 98312 | tf_op jit(solution)/shard_map/ppermute | solution.py:255
  28.5 5.0 %collective-permute-start.9 = (bf16[32,512]{1,0:T(8,128)(2,1)S(1)}, bf16[32,512]{1,0:T(8,128)(2,1)S(1)}, u32[]{:S(2)}, u32[]{:S(2)}) collective-permute-start(bf16[32,512]{1,0:T(8,128)(2,1)S(1)} %get-tuple-element.159.refs_0__0_), channel_id=1, source_target_pairs={{0,3},{1,2},{2,1},{3,0},{4,7},{5,6},{6,5},{7,4},{8,11},{9,10},{10,... | collective-permute-start | bytes 98312 | tf_op jit(solution)/shard_map/ppermute | solution.py:255
  34.1 7.1 %collective-permute-start.22 = (bf16[144,768]{1,0:T(8,128)(2,1)S(1)}, bf16[144,768]{1,0:T(8,128)(2,1)S(1)}, u32[]{:S(2)}, u32[]{:S(2)}) collective-permute-start(bf16[144,768]{1,0:T(8,128)(2,1)S(1)} %get-tuple-element.172), channel_id=1, source_target_pairs={{0,16},{4,20},{8,24},{12,28},{16,0},{20,4},{24,8},{28,12},{1,17},{... | collective-permute-start | bytes 663560 | tf_op jit(solution)/shard_map/ppermute | solution.py:249
  34.3 6.9 %collective-permute-start.23 = (bf16[144,768]{1,0:T(8,128)(2,1)S(1)}, bf16[144,768]{1,0:T(8,128)(2,1)S(1)}, u32[]{:S(2)}, u32[]{:S(2)}) collective-permute-start(bf16[144,768]{1,0:T(8,128)(2,1)S(1)} %get-tuple-element.173), channel_id=1, source_target_pairs={{0,8},{4,12},{8,0},{12,4},{16,24},{20,28},{24,16},{28,20},{1,9},{5... | collective-permute-start | bytes 663560 | tf_op jit(solution)/shard_map/ppermute | solution.py:249
  34.7 3.7 %collective-permute-start.11 = (bf16[32,512]{1,0:T(8,128)(2,1)S(1)}, bf16[32,512]{1,0:T(8,128)(2,1)S(1)}, u32[]{:S(2)}, u32[]{:S(2)}) collective-permute-start(bf16[32,512]{1,0:T(8,128)(2,1)S(1)} %get-tuple-element.162), channel_id=1, source_target_pairs={{0,2},{1,3},{2,0},{3,1},{4,6},{5,7},{6,4},{7,5},{8,10},{9,11},{10,... | collective-permute-start | bytes 98312 | tf_op jit(solution)/shard_map/ppermute | solution.py:255
  36.3 4.6 %collective-permute-start.12 = (bf16[32,512]{1,0:T(8,128)(2,1)S(1)}, bf16[32,512]{1,0:T(8,128)(2,1)S(1)}, u32[]{:S(2)}, u32[]{:S(2)}) collective-permute-start(bf16[32,512]{1,0:T(8,128)(2,1)S(1)} %get-tuple-element.163), channel_id=1, source_target_pairs={{0,3},{1,2},{2,1},{3,0},{4,7},{5,6},{6,5},{7,4},{8,11},{9,10},{10,... | collective-permute-start | bytes 98312 | tf_op jit(solution)/shard_map/ppermute | solution.py:255
  41.3 12.5 %collective-permute-start.24 = (bf16[576,1536]{1,0:T(8,128)(2,1)S(1)}, bf16[576,1536]{1,0:T(8,128)(2,1)S(1)}, u32[]{:S(2)}, u32[]{:S(2)}) collective-permute-start(bf16[576,1536]{1,0:T(8,128)(2,1)S(1)} %stack_weights.1.refs_1__0_), channel_id=1, source_target_pairs={{0,4},{4,0},{8,12},{12,8},{16,20},{20,16},{24,28},{28,24},{1,5},{5... | collective-permute-start | bytes 5308424 | tf_op jit(solution)/shard_map/ppermute | solution.py:252
  48.6 6.0 %collective-permute-start.16 = (bf16[32,512]{1,0:T(8,128)(2,1)S(1)}, bf16[32,512]{1,0:T(8,128)(2,1)S(1)}, u32[]{:S(2)}, u32[]{:S(2)}) collective-permute-start(bf16[32,512]{1,0:T(8,128)(2,1)S(1)} %get-tuple-element.165.refs_0__0_), channel_id=1, source_target_pairs={{0,4},{4,0},{8,12},{12,8},{16,20},{20,16},{24,28},{28,24},{1,5},{5... | collective-permute-start | bytes 98312 | tf_op jit(solution)/shard_map/ppermute | solution.py:252
  49.5 5.1 %collective-permute-start.17 = (bf16[32,512]{1,0:T(8,128)(2,1)S(1)}, bf16[32,512]{1,0:T(8,128)(2,1)S(1)}, u32[]{:S(2)}, u32[]{:S(2)}) collective-permute-start(bf16[32,512]{1,0:T(8,128)(2,1)S(1)} %collective-permute-done.13.refs_0__1_), channel_id=1, source_target_pairs={{0,4},{4,0},{8,12},{12,8},{16,20},{20,16},{24,28},{28,24},{1,5},{5... | collective-permute-start | bytes 98312 | tf_op jit(solution)/shard_map/ppermute | solution.py:252
  49.9 4.7 %collective-permute-start.18 = (bf16[32,512]{1,0:T(8,128)(2,1)S(1)}, bf16[32,512]{1,0:T(8,128)(2,1)S(1)}, u32[]{:S(2)}, u32[]{:S(2)}) collective-permute-start(bf16[32,512]{1,0:T(8,128)(2,1)S(1)} %collective-permute-done.14.refs_0__2_), channel_id=1, source_target_pairs={{0,4},{4,0},{8,12},{12,8},{16,20},{20,16},{24,28},{28,24},{1,5},{5... | collective-permute-start | bytes 98312 | tf_op jit(solution)/shard_map/ppermute | solution.py:252
  63.7 3.8 %collective-permute-start.25 = (bf16[32,512]{1,0:T(8,128)(2,1)S(1)}, bf16[32,512]{1,0:T(8,128)(2,1)S(1)}, u32[]{:S(2)}, u32[]{:S(2)}) collective-permute-start(bf16[32,512]{1,0:T(8,128)(2,1)S(1)} %get-tuple-element.177), channel_id=1, source_target_pairs={{0,8},{4,12},{8,0},{12,4},{16,24},{20,28},{24,16},{28,20},{1,9},{5... | collective-permute-start | bytes 98312 | tf_op jit(solution)/shard_map/ppermute | solution.py:249
  63.9 4.0 %collective-permute-start.26 = (bf16[32,512]{1,0:T(8,128)(2,1)S(1)}, bf16[32,512]{1,0:T(8,128)(2,1)S(1)}, u32[]{:S(2)}, u32[]{:S(2)}) collective-permute-start(bf16[32,512]{1,0:T(8,128)(2,1)S(1)} %get-tuple-element.178), channel_id=1, source_target_pairs={{0,16},{4,20},{8,24},{12,28},{16,0},{20,4},{24,8},{28,12},{1,17},{... | collective-permute-start | bytes 98312 | tf_op jit(solution)/shard_map/ppermute | solution.py:249
  64.1 4.7 %collective-permute-start.27 = (bf16[32,512]{1,0:T(8,128)(2,1)S(1)}, bf16[32,512]{1,0:T(8,128)(2,1)S(1)}, u32[]{:S(2)}, u32[]{:S(2)}) collective-permute-start(bf16[32,512]{1,0:T(8,128)(2,1)S(1)} %get-tuple-element.179), channel_id=1, source_target_pairs={{0,24},{4,28},{8,16},{12,20},{16,8},{20,12},{24,0},{28,4},{1,25},{... | collective-permute-start | bytes 98312 | tf_op jit(solution)/shard_map/ppermute | solution.py:249
  76.5 3.8 %collective-permute-start.32 = (bf16[32,192]{1,0:T(8,128)(2,1)S(1)}, bf16[32,192]{1,0:T(8,128)(2,1)S(1)}, u32[]{:S(2)}, u32[]{:S(2)}) collective-permute-start(bf16[32,192]{1,0:T(8,128)(2,1)S(1)} %get-tuple-element.184.refs_8__1_), channel_id=1, source_target_pairs={{0,8},{4,12},{8,0},{12,4},{16,24},{20,28},{24,16},{28,20},{1,9},{5... | collective-permute-start | bytes 36872 | tf_op jit(solution)/shard_map/ppermute | solution.py:249
  90.7 7.6 %collective-permute-start.37 = (bf16[160,512]{1,0:T(8,128)(2,1)S(1)}, bf16[160,512]{1,0:T(8,128)(2,1)S(1)}, u32[]{:S(2)}, u32[]{:S(2)}) collective-permute-start(bf16[160,512]{1,0:T(8,128)(2,1)S(1)} %get-tuple-element.208), channel_id=1, source_target_pairs={{0,8},{4,12},{8,0},{12,4},{16,24},{20,28},{24,16},{28,20},{1,9},{5... | collective-permute-start | bytes 491528 | tf_op jit(solution)/shard_map/ppermute | solution.py:249
  91.0 7.3 %collective-permute-start.38 = (bf16[160,512]{1,0:T(8,128)(2,1)S(1)}, bf16[160,512]{1,0:T(8,128)(2,1)S(1)}, u32[]{:S(2)}, u32[]{:S(2)}) collective-permute-start(bf16[160,512]{1,0:T(8,128)(2,1)S(1)} %get-tuple-element.209), channel_id=1, source_target_pairs={{0,16},{4,20},{8,24},{12,28},{16,0},{20,4},{24,8},{28,12},{1,17},{... | collective-permute-start | bytes 491528 | tf_op jit(solution)/shard_map/ppermute | solution.py:249
  91.2 8.5 %collective-permute-start.39 = (bf16[160,512]{1,0:T(8,128)(2,1)S(1)}, bf16[160,512]{1,0:T(8,128)(2,1)S(1)}, u32[]{:S(2)}, u32[]{:S(2)}) collective-permute-start(bf16[160,512]{1,0:T(8,128)(2,1)S(1)} %get-tuple-element.210), channel_id=1, source_target_pairs={{0,24},{4,28},{8,16},{12,20},{16,8},{20,12},{24,0},{28,4},{1,25},{... | collective-permute-start | bytes 491528 | tf_op jit(solution)/shard_map/ppermute | solution.py:249
  93.4 4.8 %collective-permute-start.40 = (bf16[32,1024]{1,0:T(8,128)(2,1)S(1)}, bf16[32,1024]{1,0:T(8,128)(2,1)S(1)}, u32[]{:S(2)}, u32[]{:S(2)}) collective-permute-start(bf16[32,1024]{1,0:T(8,128)(2,1)S(1)} %get-tuple-element.215.refs_0__0_), channel_id=1, source_target_pairs={{0,2},{1,3},{2,0},{3,1},{4,6},{5,7},{6,4},{7,5},{8,10},{9,11},{10,... | collective-permute-start | bytes 196616 | tf_op jit(solution)/shard_map/ppermute | solution.py:255
  102.0 6.9 %collective-permute-start.46 = (bf16[160,256]{1,0:T(8,128)(2,1)S(1)}, bf16[160,256]{1,0:T(8,128)(2,1)S(1)}, u32[]{:S(2)}, u32[]{:S(2)}) collective-permute-start(bf16[160,256]{1,0:T(8,128)(2,1)S(1)} %get-tuple-element.228), channel_id=1, source_target_pairs={{0,2},{1,3},{2,0},{3,1},{4,6},{5,7},{6,4},{7,5},{8,10},{9,11},{10,... | collective-permute-start | bytes 245768 | tf_op jit(solution)/shard_map/ppermute | solution.py:255
  104.3 10.7 %collective-permute-start.42 = (bf16[256,512]{1,0:T(8,128)(2,1)S(1)}, bf16[256,512]{1,0:T(8,128)(2,1)S(1)}, u32[]{:S(2)}, u32[]{:S(2)}) collective-permute-start(bf16[256,512]{1,0:T(8,128)(2,1)S(1)} %get-tuple-element.224), channel_id=1, source_target_pairs={{0,8},{4,12},{8,0},{12,4},{16,24},{20,28},{24,16},{28,20},{1,9},{5... | collective-permute-start | bytes 786440 | tf_op jit(solution)/shard_map/ppermute | solution.py:249
  105.6 10.6 %collective-permute-start.43 = (bf16[256,512]{1,0:T(8,128)(2,1)S(1)}, bf16[256,512]{1,0:T(8,128)(2,1)S(1)}, u32[]{:S(2)}, u32[]{:S(2)}) collective-permute-start(bf16[256,512]{1,0:T(8,128)(2,1)S(1)} %get-tuple-element.225), channel_id=1, source_target_pairs={{0,16},{4,20},{8,24},{12,28},{16,0},{20,4},{24,8},{28,12},{1,17},{... | collective-permute-start | bytes 786440 | tf_op jit(solution)/shard_map/ppermute | solution.py:249
  105.8 12.4 %collective-permute-start.44 = (bf16[256,512]{1,0:T(8,128)(2,1)S(1)}, bf16[256,512]{1,0:T(8,128)(2,1)S(1)}, u32[]{:S(2)}, u32[]{:S(2)}) collective-permute-start(bf16[256,512]{1,0:T(8,128)(2,1)S(1)} %get-tuple-element.226), channel_id=1, source_target_pairs={{0,24},{4,28},{8,16},{12,20},{16,8},{20,12},{24,0},{28,4},{1,25},{... | collective-permute-start | bytes 786440 | tf_op jit(solution)/shard_map/ppermute | solution.py:249
  107.0 6.4 %collective-permute-start.45 = (bf16[64,1024]{1,0:T(8,128)(2,1)S(1)}, bf16[64,1024]{1,0:T(8,128)(2,1)S(1)}, u32[]{:S(2)}, u32[]{:S(2)}) collective-permute-start(bf16[64,1024]{1,0:T(8,128)(2,1)S(1)} %pair_stack.3.refs_3_.refs_0__0_), channel_id=1, source_target_pairs={{0,1},{1,0},{2,3},{3,2},{4,5},{5,4},{6,7},{7,6},{8,9},{9,8},{10,11... | collective-permute-start | bytes 393224 | tf_op jit(solution)/shard_map/ppermute | solution.py:255
  108.9 4.5 %collective-permute-start.47 = (bf16[160,256]{1,0:T(8,128)(2,1)S(1)}, bf16[160,256]{1,0:T(8,128)(2,1)S(1)}, u32[]{:S(2)}, u32[]{:S(2)}) collective-permute-start(bf16[160,256]{1,0:T(8,128)(2,1)S(1)} %early_line.3.refs_0_), channel_id=1, source_target_pairs={{0,1},{1,0},{2,3},{3,2},{4,5},{5,4},{6,7},{7,6},{8,9},{9,8},{10,11... | collective-permute-start | bytes 245768 | tf_op jit(solution)/shard_map/ppermute | solution.py:255
  113.5 13.4 %collective-permute-start.49 = (bf16[128,1024]{1,0:T(8,128)(2,1)S(1)}, bf16[128,1024]{1,0:T(8,128)(2,1)S(1)}, u32[]{:S(2)}, u32[]{:S(2)}) collective-permute-start(bf16[128,1024]{1,0:T(8,128)(2,1)S(1)} %pair_stack.4.refs_2_.refs_0__0_), channel_id=1, source_target_pairs={{0,8},{4,12},{8,0},{12,4},{16,24},{20,28},{24,16},{28,20},{1,9},{5... | collective-permute-start | bytes 786440 | tf_op jit(solution)/shard_map/ppermute | solution.py:249
  114.8 14.9 %collective-permute-start.50 = (bf16[128,1024]{1,0:T(8,128)(2,1)S(1)}, bf16[128,1024]{1,0:T(8,128)(2,1)S(1)}, u32[]{:S(2)}, u32[]{:S(2)}) collective-permute-start(bf16[128,1024]{1,0:T(8,128)(2,1)S(1)} %pair_stack.4.refs_2_.refs_0__0_), channel_id=1, source_target_pairs={{0,16},{4,20},{8,24},{12,28},{16,0},{20,4},{24,8},{28,12},{1,17},{... | collective-permute-start | bytes 786440 | tf_op jit(solution)/shard_map/ppermute | solution.py:249
  115.0 17.4 %collective-permute-start.51 = (bf16[128,1024]{1,0:T(8,128)(2,1)S(1)}, bf16[128,1024]{1,0:T(8,128)(2,1)S(1)}, u32[]{:S(2)}, u32[]{:S(2)}) collective-permute-start(bf16[128,1024]{1,0:T(8,128)(2,1)S(1)} %pair_stack.4.refs_2_.refs_0__0_), channel_id=1, source_target_pairs={{0,24},{4,28},{8,16},{12,20},{16,8},{20,12},{24,0},{28,4},{1,25},{... | collective-permute-start | bytes 786440 | tf_op jit(solution)/shard_map/ppermute | solution.py:249
  119.0 4.0 %collective-permute-start.53 = (bf16[224,256]{1,0:T(8,128)(2,1)S(1)}, bf16[224,256]{1,0:T(8,128)(2,1)S(1)}, u32[]{:S(2)}, u32[]{:S(2)}) collective-permute-start(bf16[224,256]{1,0:T(8,128)(2,1)S(1)} %get-tuple-element.233), channel_id=1, source_target_pairs={{0,1},{1,0},{2,3},{3,2},{4,5},{5,4},{6,7},{7,6},{8,9},{9,8},{10,11... | collective-permute-start | bytes 344072 | tf_op jit(solution)/shard_map/ppermute | solution.py:255
  119.4 4.2 %collective-permute-start.52 = (bf16[160,256]{1,0:T(8,128)(2,1)S(1)}, bf16[160,256]{1,0:T(8,128)(2,1)S(1)}, u32[]{:S(2)}, u32[]{:S(2)}) collective-permute-start(bf16[160,256]{1,0:T(8,128)(2,1)S(1)} %early_line.4.refs_1_), channel_id=1, source_target_pairs={{0,2},{1,3},{2,0},{3,1},{4,6},{5,7},{6,4},{7,5},{8,10},{9,11},{10,... | collective-permute-start | bytes 245768 | tf_op jit(solution)/shard_map/ppermute | solution.py:255
  124.2 10.4 %collective-permute-start.54 = (bf16[160,512]{1,0:T(8,128)(2,1)S(1)}, bf16[160,512]{1,0:T(8,128)(2,1)S(1)}, u32[]{:S(2)}, u32[]{:S(2)}) collective-permute-start(bf16[160,512]{1,0:T(8,128)(2,1)S(1)} %early_line.5.refs_1_.refs_0__0_), channel_id=1, source_target_pairs={{0,8},{4,12},{8,0},{12,4},{16,24},{20,28},{24,16},{28,20},{1,9},{5... | collective-permute-start | bytes 491528 | tf_op jit(solution)/shard_map/ppermute | solution.py:249
  124.8 9.8 %collective-permute-start.55 = (bf16[160,512]{1,0:T(8,128)(2,1)S(1)}, bf16[160,512]{1,0:T(8,128)(2,1)S(1)}, u32[]{:S(2)}, u32[]{:S(2)}) collective-permute-start(bf16[160,512]{1,0:T(8,128)(2,1)S(1)} %early_line.5.refs_1_.refs_0__0_), channel_id=1, source_target_pairs={{0,16},{4,20},{8,24},{12,28},{16,0},{20,4},{24,8},{28,12},{1,17},{... | collective-permute-start | bytes 491528 | tf_op jit(solution)/shard_map/ppermute | solution.py:249
  126.9 7.5 %collective-permute-start.56 = (bf16[224,256]{1,0:T(8,128)(2,1)S(1)}, bf16[224,256]{1,0:T(8,128)(2,1)S(1)}, u32[]{:S(2)}, u32[]{:S(2)}) collective-permute-start(bf16[224,256]{1,0:T(8,128)(2,1)S(1)} %late_line.2.refs_3_.refs_0_), channel_id=1, source_target_pairs={{0,2},{1,3},{2,0},{3,1},{4,6},{5,7},{6,4},{7,5},{8,10},{9,11},{10,... | collective-permute-start | bytes 344072 | tf_op jit(solution)/shard_map/ppermute | solution.py:255
  134.4 3.7 %collective-permute-start.57 = (bf16[224,256]{1,0:T(8,128)(2,1)S(1)}, bf16[224,256]{1,0:T(8,128)(2,1)S(1)}, u32[]{:S(2)}, u32[]{:S(2)}) collective-permute-start(bf16[224,256]{1,0:T(8,128)(2,1)S(1)} %late_line.3.refs_2_.refs_1_), channel_id=1, source_target_pairs={{0,1},{1,0},{2,3},{3,2},{4,5},{5,4},{6,7},{7,6},{8,9},{9,8},{10,11... | collective-permute-start | bytes 344072 | tf_op jit(solution)/shard_map/ppermute | solution.py:255
  134.6 4.1 %collective-permute-start.61 = (bf16[160,256]{1,0:T(8,128)(2,1)S(1)}, bf16[160,256]{1,0:T(8,128)(2,1)S(1)}, u32[]{:S(2)}, u32[]{:S(2)}) collective-permute-start(bf16[160,256]{1,0:T(8,128)(2,1)S(1)} %get-tuple-element.238.refs_3_), channel_id=1, source_target_pairs={{0,16},{4,20},{8,24},{12,28},{16,0},{20,4},{24,8},{28,12},{1,17},{... | collective-permute-start | bytes 245768 | tf_op jit(solution)/shard_map/ppermute | solution.py:249
  134.9 3.8 %collective-permute-start.62 = (bf16[160,256]{1,0:T(8,128)(2,1)S(1)}, bf16[160,256]{1,0:T(8,128)(2,1)S(1)}, u32[]{:S(2)}, u32[]{:S(2)}) collective-permute-start(bf16[160,256]{1,0:T(8,128)(2,1)S(1)} %get-tuple-element.241), channel_id=1, source_target_pairs={{0,8},{4,12},{8,0},{12,4},{16,24},{20,28},{24,16},{28,20},{1,9},{5... | collective-permute-start | bytes 245768 | tf_op jit(solution)/shard_map/ppermute | solution.py:249
  138.8 7.3 %collective-permute-start.63 = (bf16[640,512]{1,0:T(8,128)(2,1)S(1)}, bf16[640,512]{1,0:T(8,128)(2,1)S(1)}, u32[]{:S(2)}, u32[]{:S(2)}) collective-permute-start(bf16[640,512]{1,0:T(8,128)(2,1)S(1)} %early_stack.1.refs_1__0_), channel_id=1, source_target_pairs={{0,4},{4,0},{8,12},{12,8},{16,20},{20,16},{24,28},{28,24},{1,5},{5... | collective-permute-start | bytes 1966088 | tf_op jit(solution)/shard_map/ppermute | solution.py:252
  142.5 7.4 %collective-permute-start.58 = (bf16[224,512]{1,0:T(8,128)(2,1)S(1)}, bf16[224,512]{1,0:T(8,128)(2,1)S(1)}, u32[]{:S(2)}, u32[]{:S(2)}) collective-permute-start(bf16[224,512]{1,0:T(8,128)(2,1)S(1)} %late_join.1.refs_3_.refs_0__0_), channel_id=1, source_target_pairs={{0,8},{4,12},{8,0},{12,4},{16,24},{20,28},{24,16},{28,20},{1,9},{5... | collective-permute-start | bytes 688136 | tf_op jit(solution)/shard_map/ppermute | solution.py:249
  143.6 6.8 %collective-permute-start.59 = (bf16[224,512]{1,0:T(8,128)(2,1)S(1)}, bf16[224,512]{1,0:T(8,128)(2,1)S(1)}, u32[]{:S(2)}, u32[]{:S(2)}) collective-permute-start(bf16[224,512]{1,0:T(8,128)(2,1)S(1)} %late_join.1.refs_3_.refs_0__0_), channel_id=1, source_target_pairs={{0,16},{4,20},{8,24},{12,28},{16,0},{20,4},{24,8},{28,12},{1,17},{... | collective-permute-start | bytes 688136 | tf_op jit(solution)/shard_map/ppermute | solution.py:249
  143.9 11.6 %collective-permute-start.60 = (bf16[224,512]{1,0:T(8,128)(2,1)S(1)}, bf16[224,512]{1,0:T(8,128)(2,1)S(1)}, u32[]{:S(2)}, u32[]{:S(2)}) collective-permute-start(bf16[224,512]{1,0:T(8,128)(2,1)S(1)} %late_join.1.refs_3_.refs_0__0_), channel_id=1, source_target_pairs={{0,24},{4,28},{8,16},{12,20},{16,8},{20,12},{24,0},{28,4},{1,25},{... | collective-permute-start | bytes 688136 | tf_op jit(solution)/shard_map/ppermute | solution.py:249
  145.1 11.5 %collective-permute-start.65 = (bf16[512,1024]{1,0:T(8,128)(2,1)S(1)}, bf16[512,1024]{1,0:T(8,128)(2,1)S(1)}, u32[]{:S(2)}, u32[]{:S(2)}) collective-permute-start(bf16[512,1024]{1,0:T(8,128)(2,1)S(1)} %pair_stack.5.refs_5_.refs_0__0_), channel_id=1, source_target_pairs={{0,4},{4,0},{8,12},{12,8},{16,20},{20,16},{24,28},{28,24},{1,5},{5... | collective-permute-start | bytes 3145736 | tf_op jit(solution)/shard_map/ppermute | solution.py:252
  (30 other events, 207.2 us)
